TPU v7x, 32 devices: a whole 2x2x4 slice. The times are simulated.
32 devices in a mesh: blk: 8 (over z, y), tensor: 4 (over x, core).
Axes of the slice: x: 2, y: 2, z: 4, core: 2. Of those that a mesh axis runs over, the one named last changes fastest.
Arguments:
- tokens: bfloat16 [8, 1024, 2048], P(None, 'blk'), may hold values from -9 to 9
- cotangent: bfloat16 [8, 1024, 2048], P(None, 'blk'), may hold values from -6 to 6
- norm_gain: float32 [2, 2048], replicated, may hold values from 0.5 to 1.5
- in_weight: bfloat16 [2, 2048, 2, 4096], P(None, None, None, 'tensor'), may hold values from -0.125 to 0.125
- conv_weight: float32 [2, 4, 4096], P(None, None, 'tensor'), may hold values from -3 to 3
- conv_bias: float32 [2, 4096], P(None, 'tensor'), may hold values from -3 to 3
- x_weight: bfloat16 [2, 4096, 160], P(None, 'tensor'), may hold values from -0.1875 to 0.1875
- dt_weight: bfloat16 [2, 128, 4096], P(None, None, 'tensor'), may hold values from -0.5 to 0.5
- dt_bias: float32 [2, 4096], P(None, 'tensor'), may hold values from -6.9 to -2.3
- decay_log: float32 [2, 16, 4096], P(None, None, 'tensor'), may hold values from -10 to 4
- skip_weight: float32 [2, 4096], P(None, 'tensor'), may hold values from 0.5 to 1.5
- out_weight: bfloat16 [2, 4096, 2048], P(None, 'tensor'), may hold values from -0.1875 to 0.1875
- scan_init: float32 [2, 8, 16, 4096], P(None, None, None, 'tensor'), may hold values from -6 to 6
- conv_init: float32 [2, 8, 3, 4096], P(None, None, None, 'tensor'), may hold values from -6 to 6
Outputs:
- out: bfloat16 [8, 1024, 2048], P(None, 'blk')
- end_states: float32 [2, 8, 8, 16, 4096], P(None, None, 'blk', None, 'tensor')
- conv_tails: float32 [2, 8, 8, 3, 4096], P(None, None, 'blk', None, 'tensor')
- input_grad: bfloat16 [8, 1024, 2048], P(None, 'blk')
- scan_grads: float32 [2, 8, 8, 16, 4096], P(None, None, 'blk', None, 'tensor')
- conv_grads: float32 [2, 8, 8, 3, 4096], P(None, None, 'blk', None, 'tensor')
- norm_gain_grad: float32 [2, 2048], replicated
- in_weight_grad: float32 [2, 2048, 2, 4096], P(None, 'blk', None, 'tensor')
- conv_weight_grad: float32 [2, 4, 4096], P(None, None, 'tensor')
- conv_bias_grad: float32 [2, 4096], P(None, 'tensor')
- x_weight_grad: float32 [2, 4096, 160], P(None, 'tensor', 'blk')
- dt_weight_grad: float32 [2, 128, 4096], P(None, 'blk', 'tensor')
- dt_bias_grad: float32 [2, 4096], P(None, 'tensor')
- decay_log_grad: float32 [2, 16, 4096], P(None, None, 'tensor')
- skip_weight_grad: float32 [2, 4096], P(None, 'tensor')
- out_weight_grad: float32 [2, 4096, 2048], P(None, 'tensor', 'blk')
- rms_stats: float32 [2, 2], replicated
- input_rms: float32 [1], replicated
All inputs are finite; a program needn't handle non-finite values.
Results may differ from a plain program's by a relative error of at most 0.025.
The roundings to bfloat16 on the way count: a program that leaves them out, or rounds other values in their place, can miss the bound.
Values sent between devices are 32-bit elements; how exact they have to be, the bound alone decides.
A program may use at most 384 MiB of HBM per device.

v0:
```python
from functools import partial
import math

import jax
import jax.numpy as jnp
from jax import lax
from jax.sharding import PartitionSpec as P

STATE = 16
RANK = 128
MICRO = 2
MB_SEQS = 4


EPSILON = 1e-05
TOP_PRECISION = lax.Precision.HIGHEST


def passed_along(value, axis, steps):
    count = lax.axis_size(axis)
    first, last = (max(0, -steps), min(count, count - steps))
    return lax.ppermute(value, axis, [(source, source + steps) for source in range(first, last)])


def entering(array, axis, combine, identity, reverse):
    peers, index = (lax.axis_size(axis), lax.axis_index(axis))
    everything = jax.tree.map(lambda part: lax.all_gather(part, axis), array)
    start = jax.tree.map(
        lambda part, zero: jnp.broadcast_to(jnp.asarray(zero, part.dtype), part.shape),
        array,
        identity,
    )

    def step(k, before):
        at = peers - 1 - k if reverse else k
        reached = at > index if reverse else at < index
        new = combine(before, jax.tree.map(lambda part: part[at], everything))
        return jax.tree.map(lambda a, b: jnp.where(reached, a, b), new, before)

    return lax.fori_loop(0, peers, step, start)


def silu_slope(argument):
    sigmoid_value = jax.nn.sigmoid(argument)
    return sigmoid_value * (1.0 + argument * (1.0 - sigmoid_value))


def norm_rows(residual, gain_vector):
    mean_square = jnp.mean(residual * residual, axis=-1, keepdims=True)
    return residual * lax.rsqrt(mean_square + EPSILON) * gain_vector


def conv_local(prefix, values, kernel, conv_shift):
    window = jnp.concatenate([prefix, values], axis=1)
    length = values.shape[1]
    summed = conv_shift + kernel[0] * window[:, 0:length]
    for offset in range(1, kernel.shape[0]):
        summed = summed + kernel[offset] * window[:, offset : offset + length]
    return summed


def scan_steps(decay_rate, carried, pieces):
    step_size, inputs, write_coef, read_coef = pieces
    outputs = []
    for moment in range(step_size.shape[0]):
        carried = (
            jnp.exp(step_size[moment][:, None, :] * decay_rate) * carried
            + (step_size[moment] * inputs[moment])[:, None, :] * write_coef[moment][:, :, None]
        )
        outputs.append(jnp.sum(read_coef[moment][:, :, None] * carried, axis=1))
    return (carried, jnp.stack(outputs))


def local_scan(start_state, step_size, inputs, write_coef, read_coef, decay_log):
    decay_rate = -jnp.exp(decay_log)
    seq_count, length = (step_size.shape[0], step_size.shape[1])
    sub_length = math.gcd(length, 16)

    def arrange(array_in):
        return jnp.moveaxis(
            array_in.reshape(seq_count, length // sub_length, sub_length, array_in.shape[-1]), 0, 2
        )

    pieces = tuple((arrange(array_in) for array_in in (step_size, inputs, write_coef, read_coef)))
    final_state, outputs = lax.scan(
        jax.checkpoint(partial(scan_steps, decay_rate)), start_state, pieces
    )
    return (jnp.moveaxis(outputs, 2, 0).reshape(seq_count, length, -1), final_state)


def end_terms(step_size, inputs, write_coef, decay_rate):
    running = jnp.cumsum(step_size, axis=1)
    remain = running[:, -1:] - running
    weights = jnp.exp(remain[:, :, None, :] * decay_rate)
    local_end = jnp.sum(
        weights * (step_size * inputs)[:, :, None, :] * write_coef[:, :, :, None], axis=1
    )
    return (jnp.exp(running[:, -1][:, None, :] * decay_rate), local_end)


def start_terms(step_size, read_coef, out_grad, decay_rate):
    running = jnp.cumsum(step_size, axis=1)
    weights = jnp.exp(running[:, :, None, :] * decay_rate)
    return jnp.sum(weights * read_coef[:, :, :, None] * out_grad[:, :, None, :], axis=1)


def join_forward(earlier, following):
    return (earlier[0] * following[0], earlier[1] * following[0] + following[1])


def join_backward(earlier, following):
    return (following[0] * earlier[0], following[1] + following[0] * earlier[1])


def layer_front(residual, gain_vector, input_matrix):
    seq_count, length, model_width = residual.shape
    normalized_rows = norm_rows(residual, gain_vector).astype(jnp.bfloat16)
    mixer_output = jnp.dot(
        normalized_rows.reshape(seq_count * length, model_width),
        input_matrix.reshape(model_width, -1),
        preferred_element_type=jnp.float32,
    )
    mixer_output = mixer_output.reshape(seq_count, length, 2, -1)
    return (normalized_rows, mixer_output[:, :, 0], mixer_output[:, :, 1])


def step_sizes(projected, dt_matrix, dt_bias):
    dt_low = projected[..., :RANK].astype(jnp.bfloat16)
    write_coef = projected[..., RANK : RANK + STATE]
    read_coef = projected[..., RANK + STATE :]
    before = (
        jnp.einsum("slr,re->sle", dt_low, dt_matrix, preferred_element_type=jnp.float32) + dt_bias
    )
    return (dt_low, write_coef, read_coef, before, jax.nn.softplus(before))


def forward_layer(residual, weights, scan_start, conv_start, at_first):
    (
        gain_vector,
        input_matrix,
        kernel,
        conv_shift,
        x_matrix,
        dt_matrix,
        dt_bias,
        decay_log,
        skip_scale,
        output_matrix,
    ) = weights
    seq_count, length, model_width = residual.shape
    normalized_rows, values, gate_half = layer_front(residual, gain_vector, input_matrix)
    rim_width = kernel.shape[0] - 1
    tail_values = values[:, length - rim_width :]
    arrived = passed_along(tail_values, "blk", 1)
    prefix = jnp.where(at_first, conv_start, arrived)
    conv_out = conv_local(prefix, values, kernel, conv_shift)
    inputs = jax.nn.silu(conv_out).astype(jnp.bfloat16)
    proj_part = jnp.einsum("sle,ec->slc", inputs, x_matrix, preferred_element_type=jnp.float32)
    projected = lax.psum(proj_part, "tensor")
    dt_low, write_coef, read_coef, before, step_size = step_sizes(projected, dt_matrix, dt_bias)
    decay_rate = -jnp.exp(decay_log)
    inputs_wide = inputs.astype(jnp.float32)
    decay_prod, local_end = end_terms(step_size, inputs_wide, write_coef, decay_rate)
    identity = (jnp.ones_like(decay_prod), jnp.zeros_like(local_end))
    prior_prod, prior_state = entering(
        (decay_prod, local_end), "blk", join_forward, identity, False
    )
    start_state = prior_state + prior_prod * scan_start
    scanned, final_state = local_scan(
        start_state, step_size, inputs_wide, write_coef, read_coef, decay_log
    )
    gated_reduced = ((scanned + skip_scale * inputs_wide) * jax.nn.silu(gate_half)).astype(
        jnp.bfloat16
    )
    gated_rows = gated_reduced.reshape(seq_count * length, -1)
    residual_rows = residual.reshape(seq_count * length, model_width)
    side_branch = lax.psum(
        jnp.dot(gated_rows, output_matrix, preferred_element_type=jnp.float32), "tensor"
    )
    next_rows = residual_rows + side_branch
    squares = jnp.stack([jnp.sum(side_branch * side_branch), jnp.sum(next_rows * next_rows)])
    return (
        next_rows.reshape(residual.shape),
        (start_state, prefix, projected),
        final_state,
        tail_values,
        squares,
    )


def backward_layer(residual, grad_out, weights, saved):
    (
        gain_vector,
        input_matrix,
        kernel,
        conv_shift,
        x_matrix,
        dt_matrix,
        dt_bias,
        decay_log,
        skip_scale,
        output_matrix,
    ) = weights
    start_state, prefix, projected = saved
    seq_count, length, model_width = residual.shape
    row_count = seq_count * length
    normalized_rows, values, gate_half = layer_front(residual, gain_vector, input_matrix)
    conv_out, conv_pull = jax.vjp(conv_local, prefix, values, kernel, conv_shift)
    inputs = jax.nn.silu(conv_out).astype(jnp.bfloat16)
    inputs_wide = inputs.astype(jnp.float32)
    dt_low, write_coef, read_coef, before, step_size = step_sizes(projected, dt_matrix, dt_bias)
    (scanned, final_state), scan_pull = jax.vjp(
        local_scan, start_state, step_size, inputs_wide, write_coef, read_coef, decay_log
    )
    result = scanned + skip_scale * inputs_wide
    gate_act = jax.nn.silu(gate_half)
    gated_reduced = (result * gate_act).astype(jnp.bfloat16)
    grad_low = grad_out.astype(jnp.bfloat16).reshape(row_count, model_width)
    grad_gated = jnp.einsum(
        "rd,ed->re", grad_low, output_matrix, preferred_element_type=jnp.float32
    ).reshape(seq_count, length, -1)
    out_w_grad = jnp.einsum(
        "re,rd->ed",
        gated_reduced.reshape(row_count, -1),
        grad_low,
        preferred_element_type=jnp.float32,
    )
    grad_result = grad_gated * gate_act
    grad_gate = grad_gated * result * silu_slope(gate_half)
    skip_grad = jnp.sum(grad_result * inputs_wide, axis=(0, 1))
    decay_rate = -jnp.exp(decay_log)
    local_start = start_terms(step_size, read_coef, grad_result, decay_rate)
    decay_prod = jnp.exp(jnp.sum(step_size, axis=1)[:, None, :] * decay_rate)
    identity = (jnp.ones_like(decay_prod), jnp.zeros_like(local_start))
    later_prod, end_grad = entering((decay_prod, local_start), "blk", join_backward, identity, True)
    start_grad, step_grad, scan_input_grad, write_grad, read_grad, decay_grad = scan_pull(
        (grad_result, end_grad)
    )
    before_grad = step_grad * jax.nn.sigmoid(before)
    bias_grad = jnp.sum(before_grad, axis=(0, 1))
    before_low = before_grad.astype(jnp.bfloat16)
    dt_w_grad = jnp.einsum("slr,sle->re", dt_low, before_low, preferred_element_type=jnp.float32)
    rank_grad = jnp.einsum("sle,re->slr", before_low, dt_matrix, preferred_element_type=jnp.float32)
    proj_part = jnp.concatenate([rank_grad, write_grad, read_grad], axis=-1)
    proj_grad = lax.psum(proj_part, "tensor")
    x_w_grad = jnp.einsum("sle,slc->ec", inputs_wide, proj_grad, precision=TOP_PRECISION)
    inputs_grad = (
        grad_result * skip_scale
        + scan_input_grad
        + jnp.einsum(
            "slc,ec->sle", proj_grad, x_matrix.astype(jnp.float32), precision=TOP_PRECISION
        )
    )
    conv_grad = inputs_grad * silu_slope(conv_out)
    prefix_grad, values_grad, kernel_grad, shift_grad = conv_pull(conv_grad)
    rim_width = prefix.shape[1]
    arrived = passed_along(prefix_grad, "blk", -1)
    values_grad = values_grad.at[:, length - rim_width :].add(arrived)
    mixed_grad = (
        jnp.stack([values_grad, grad_gate], axis=2).astype(jnp.bfloat16).reshape(row_count, -1)
    )
    in_w_grad = jnp.einsum(
        "rd,rk->dk",
        normalized_rows.reshape(row_count, model_width),
        mixed_grad,
        preferred_element_type=jnp.float32,
    )
    normed_part = jnp.einsum(
        "rk,dk->rd",
        mixed_grad,
        input_matrix.reshape(model_width, -1),
        preferred_element_type=jnp.float32,
    )
    normed_grad = lax.psum(normed_part, "tensor").reshape(seq_count, length, model_width)
    normed_again, norm_pull = jax.vjp(norm_rows, residual, gain_vector)
    residual_grad, gain_grad = norm_pull(normed_grad)
    layer_grads = (
        gain_grad,
        in_w_grad.reshape(input_matrix.shape),
        kernel_grad,
        shift_grad,
        x_w_grad,
        dt_w_grad,
        bias_grad,
        decay_grad,
        skip_grad,
        out_w_grad,
    )
    return (grad_out + residual_grad, layer_grads, start_grad, prefix_grad)


def on_device(
    tokens,
    cotangent,
    norm_gain,
    in_weight,
    conv_weight,
    conv_bias,
    x_weight,
    dt_weight,
    dt_bias,
    decay_log,
    skip_weight,
    out_weight,
    scan_init,
    conv_init,
):
    at_first = lax.axis_index("blk") == 0
    layer_total = in_weight.shape[0]

    def weights_of(layer_index):
        return tuple(
            (
                weight_item[layer_index]
                for weight_item in (
                    norm_gain,
                    in_weight,
                    conv_weight,
                    conv_bias,
                    x_weight,
                    dt_weight,
                    dt_bias,
                    decay_log,
                    skip_weight,
                    out_weight,
                )
            )
        )

    grad_sums = [None] * layer_total
    square_rows = [jnp.zeros((2,), jnp.float32) for layer_index in range(layer_total)]
    input_square = jnp.zeros((1,), jnp.float32)
    finals = [[] for layer_index in range(layer_total)]
    tail_lists = [[] for layer_index in range(layer_total)]
    start_lists = [[] for layer_index in range(layer_total)]
    prefix_lists = [[] for layer_index in range(layer_total)]
    out_blocks, input_blocks = ([], [])
    for micro_index in range(MICRO):
        first_seq = micro_index * MB_SEQS
        stop_seq = first_seq + MB_SEQS
        residual = tokens[first_seq:stop_seq].astype(jnp.float32)
        input_square = input_square + jnp.sum(residual * residual)
        kept_inputs = []
        for layer_index in range(layer_total):
            next_residual, saved, final_state, tail_values, squares = forward_layer(
                residual,
                weights_of(layer_index),
                scan_init[layer_index, first_seq:stop_seq],
                conv_init[layer_index, first_seq:stop_seq],
                at_first,
            )
            kept_inputs.append((residual, saved))
            finals[layer_index].append(final_state)
            tail_lists[layer_index].append(tail_values)
            square_rows[layer_index] = square_rows[layer_index] + squares
            residual = next_residual
        out_blocks.append(residual.astype(jnp.bfloat16))
        grad_now = cotangent[first_seq:stop_seq].astype(jnp.float32)
        for layer_index in reversed(range(layer_total)):
            grad_now, layer_grads, start_grad, prefix_grad = backward_layer(
                kept_inputs[layer_index][0],
                grad_now,
                weights_of(layer_index),
                kept_inputs[layer_index][1],
            )
            start_lists[layer_index].append(start_grad)
            prefix_lists[layer_index].append(prefix_grad)
            if grad_sums[layer_index] is None:
                grad_sums[layer_index] = layer_grads
            else:
                grad_sums[layer_index] = jax.tree.map(jnp.add, grad_sums[layer_index], layer_grads)
        input_blocks.append(grad_now.astype(jnp.bfloat16))

    def stack_layers(position):
        return jnp.stack([grad_sums[layer_index][position] for layer_index in range(layer_total)])

    in_grad, out_grad, proj_w_grad, dt_w_grad = (
        lax.psum_scatter(stack_layers(1), "blk", scatter_dimension=1, tiled=True),
        lax.psum_scatter(stack_layers(9), "blk", scatter_dimension=2, tiled=True),
        lax.psum_scatter(stack_layers(4), "blk", scatter_dimension=2, tiled=True),
        lax.psum_scatter(stack_layers(5), "blk", scatter_dimension=1, tiled=True),
    )
    row_total = tokens.shape[0] * tokens.shape[1] * tokens.shape[2] * lax.axis_size("blk")
    gain_grad, kernel_grad, shift_grad, bias_grad, decay_grad, skip_grad, square_sums, input_sum = (
        lax.psum(
            (
                stack_layers(0),
                stack_layers(2),
                stack_layers(3),
                stack_layers(6),
                stack_layers(7),
                stack_layers(8),
                jnp.stack(square_rows),
                input_square,
            ),
            "blk",
        )
    )
    rms_stats = jnp.sqrt(square_sums / row_total)
    input_rms = jnp.sqrt(input_sum / row_total)

    def gather_lists(lists):
        return jnp.stack(
            [jnp.concatenate(lists[layer_index], axis=0) for layer_index in range(layer_total)]
        )[:, :, None]

    end_states = gather_lists(finals)
    conv_tails = gather_lists(tail_lists)
    scan_grads = gather_lists(start_lists)
    conv_grads = gather_lists(prefix_lists)
    return (
        jnp.concatenate(out_blocks, axis=0),
        end_states,
        conv_tails,
        jnp.concatenate(input_blocks, axis=0),
        scan_grads,
        conv_grads,
        gain_grad,
        in_grad,
        kernel_grad,
        shift_grad,
        proj_w_grad,
        dt_w_grad,
        bias_grad,
        decay_grad,
        skip_grad,
        out_grad,
        rms_stats,
        input_rms,
    )


def solution(mesh):
    placed = (
        P(None, "blk", None),
        P(None, "blk", None),
        P(),
        P(None, None, None, "tensor"),
        P(None, None, "tensor"),
        P(None, "tensor"),
        P(None, "tensor", None),
        P(None, None, "tensor"),
        P(None, "tensor"),
        P(None, None, "tensor"),
        P(None, "tensor"),
        P(None, "tensor", None),
        P(None, None, None, "tensor"),
        P(None, None, None, "tensor"),
    )
    return jax.shard_map(
        on_device,
        mesh=mesh,
        in_specs=placed,
        out_specs=(
            P(None, "blk", None),
            P(None, None, "blk", None, "tensor"),
            P(None, None, "blk", None, "tensor"),
            P(None, "blk", None),
            P(None, None, "blk", None, "tensor"),
            P(None, None, "blk", None, "tensor"),
            P(),
            P(None, "blk", None, "tensor"),
            P(None, None, "tensor"),
            P(None, "tensor"),
            P(None, "tensor", "blk"),
            P(None, "blk", "tensor"),
            P(None, "tensor"),
            P(None, None, "tensor"),
            P(None, "tensor"),
            P(None, "tensor", "blk"),
            P(),
            P(),
        ),
        check_vma=False,
    )
```

profile of v0, /device:TPU:0, one launch (start us, length us, event | category | flops | bytes accessed | tf_op | source)
XLA Modules:
  0.0 3974.3 jit_solution(16154308563870616324)
XLA Ops:
  205.7 50.5 %all-gather.25.cloned.1.call-done = f32[8,4,16,1024]{3,2,1,0:T(8,128)} async-done(((f32[1,4,16,1024]{3,2,1,0:T(8,128)}), f32[8,4,16,1024]{3,2,1,0:T(8,128)}) %all-gather.25.cloned.1.call-update) | async-done | bytes 2097168 | tf_op jit(solution)/shard_map/all_gather | solution.py:27
  275.7 55.0 %while.340 = (s32[]{:T(128)}, f32[4,16,1024]{2,1,0:T(8,128)S(1)}, f32[8,16,4,1024]{3,2,1,0:T(4,128)}, f32[8,16,4,1024]{3,2,1,0:T(4,128)}, f32[16,1024]{1,0:T(8,1...) while((s32[]{:T(128)}, f32[4,16,1024]{2,1,0:T(8,128)S(1)}, ...), condition=%wide.region_23.24_spmd, body=%wide.region_6.23_spmd.sunk | while | flops 9437201 | bytes 6139957 | solution.py:85
  338.4 60.1 %while.345 = (s32[]{:T(128)}, f32[4,16,1024]{2,1,0:T(8,128)S(1)}, f32[8,16,4,1024]{3,2,1,0:T(4,128)}, f32[8,4,16,1024]{3,2,1,0:T(8,128)}, f32[8,16,4,1024]{3,2,1...) while((s32[]{:T(128)}, f32[4,16,1024]{2,1,0:T(8,128)S(1)}, ...), condition=%wide.region_228.229_spmd, body=%wide.region_211.228_spmd.sunk | while | flops 9437201 | bytes 6664765 | solution.py:85
  435.2 61.2 %all-reduce.374.cloned.1.call-done = f32[512,2048]{1,0:T(8,128)} async-done(((f32[512,2048]{1,0:T(8,128)}), f32[512,2048]{1,0:T(8,128)}) %all-reduce.374.cloned.1.call-update) | async-done | bytes 4194320 | tf_op jit(solution)/shard_map/psum | solution.py:177
  639.0 50.2 %all-gather.27.cloned.1.call-done = f32[8,4,16,1024]{3,2,1,0:T(8,128)} async-done(((f32[1,4,16,1024]{3,2,1,0:T(8,128)}), f32[8,4,16,1024]{3,2,1,0:T(8,128)}) %all-gather.27.cloned.1.call-update) | async-done | bytes 2097168 | tf_op jit(solution)/shard_map/all_gather | solution.py:27
  739.3 50.2 %all-gather.33.cloned.1.call-done = f32[8,4,16,1024]{3,2,1,0:T(8,128)} async-done(((f32[1,4,16,1024]{3,2,1,0:T(8,128)}), f32[8,4,16,1024]{3,2,1,0:T(8,128)}) %all-gather.33.cloned.1.call-update) | async-done | bytes 2097168 | tf_op jit(solution)/shard_map/all_gather | solution.py:27
  803.1 52.7 %while.344 = (s32[]{:T(128)}, f32[4,16,1024]{2,1,0:T(8,128)S(1)}, f32[8,16,4,1024]{3,2,1,0:T(4,128)}, f32[8,4,16,1024]{3,2,1,0:T(8,128)}, f32[8,16,4,1024]{3,2,1...) while((s32[]{:T(128)}, f32[4,16,1024]{2,1,0:T(8,128)S(1)}, ...), condition=%wide.region_121.122_spmd, body=%wide.region_104.121_spmd.sunk | while | flops 9437201 | bytes 6664765 | solution.py:85
  861.0 135.0 %while.353 = (s32[]{:T(128)}, f32[16,1024]{1,0:T(8,128)}, f32[4,16,1024]{2,1,0:T(8,128)S(1)}, f32[8,16,4,1024]{3,2,1,0:T(4,128)}, f32[8,16,4,1024]{3,2,1,0:T(4,1...) while((s32[]{:T(128)}, f32[16,1024]{1,0:T(8,128)}, ...), condition=%wide.region_203.204_spmd.clone, body=%wide.region_122.203_spmd.clone.sunk | while | flops 31830020 | bytes 21284388 | solution.py:85
  1109.4 145.0 %all-reduce.394.cloned.1.call-done = (f32[512,2048]{1,0:T(8,128)}, f32[512,2048]{1,0:T(8,128)}) async-done(((f32[512,2048]{1,0:T(8,128)}, f32[512,2048]{1,0:T(8,128)}), (f32[512,2048]{1,0:T(8,128)}, f32[512,2048]{1,0:T(8,128)})) %all-reduce.394.cloned.1.call-update) | async-done | bytes 8388624 | tf_op jit(solution)/shard_map/psum | solution.py:274
  1306.0 50.7 %all-gather.45.cloned.1.call-done = f32[32,16,1024]{2,1,0:T(8,128)} async-done(((f32[4,16,1024]{2,1,0:T(8,128)}), f32[32,16,1024]{2,1,0:T(8,128)}) %all-gather.45.cloned.1.call-update) | async-done | bytes 2097168 | tf_op jit(solution)/shard_map/all_gather | solution.py:27
  1375.8 55.0 %while.342 = (s32[]{:T(128)}, f32[4,16,1024]{2,1,0:T(8,128)S(1)}, f32[8,16,4,1024]{3,2,1,0:T(4,128)}, f32[8,16,4,1024]{3,2,1,0:T(4,128)}, f32[16,1024]{1,0:T(8,1...) while((s32[]{:T(128)}, f32[4,16,1024]{2,1,0:T(8,128)S(1)}, ...), condition=%wide.region_73.74_spmd, body=%wide.region_56.73_spmd.sunk | while | flops 9437201 | bytes 6139957 | solution.py:85
  1439.3 55.9 %while.347 = (s32[]{:T(128)}, f32[4,16,1024]{2,1,0:T(8,128)S(1)}, f32[8,16,4,1024]{3,2,1,0:T(4,128)S(1)}, f32[8,4,16,1024]{3,2,1,0:T(8,128)}, f32[8,16,4,1024]{3...) while((s32[]{:T(128)}, f32[4,16,1024]{2,1,0:T(8,128)S(1)}, ...), condition=%wide.region_442.443_spmd, body=%wide.region_425.442_spmd.sunk | while | flops 9437201 | bytes 6664257 | solution.py:85
  1508.2 84.1 %all-reduce.378.cloned.1.call-done = f32[512,2048]{1,0:T(8,128)} async-done(((f32[512,2048]{1,0:T(8,128)}), f32[512,2048]{1,0:T(8,128)}) %all-reduce.378.cloned.1.call-update) | async-done | bytes 4194320 | tf_op jit(solution)/shard_map/psum | solution.py:177
  1737.4 49.8 %all-gather.37.cloned.1.call-done = f32[8,4,16,1024]{3,2,1,0:T(8,128)} async-done(((f32[1,4,16,1024]{3,2,1,0:T(8,128)}), f32[8,4,16,1024]{3,2,1,0:T(8,128)}) %all-gather.37.cloned.1.call-update) | async-done | bytes 2097168 | tf_op jit(solution)/shard_map/all_gather | solution.py:27
  1837.0 49.9 %all-gather.31.cloned.1.call-done = f32[8,4,16,1024]{3,2,1,0:T(8,128)} async-done(((f32[1,4,16,1024]{3,2,1,0:T(8,128)}), f32[8,4,16,1024]{3,2,1,0:T(8,128)}) %all-gather.31.cloned.1.call-update) | async-done | bytes 2097168 | tf_op jit(solution)/shard_map/all_gather | solution.py:27
  1901.4 52.7 %while.346 = (s32[]{:T(128)}, f32[4,16,1024]{2,1,0:T(8,128)S(1)}, f32[8,16,4,1024]{3,2,1,0:T(4,128)}, f32[8,4,16,1024]{3,2,1,0:T(8,128)}, f32[8,16,4,1024]{3,2,1...) while((s32[]{:T(128)}, f32[4,16,1024]{2,1,0:T(8,128)S(1)}, ...), condition=%wide.region_335.336_spmd, body=%wide.region_318.335_spmd.sunk | while | flops 9437201 | bytes 6664765 | solution.py:85
  1959.3 143.8 %while.357 = (s32[]{:T(128)}, f32[16,1024]{1,0:T(8,128)}, f32[4,16,1024]{2,1,0:T(8,128)S(1)}, f32[8,16,4,1024]{3,2,1,0:T(4,128)}, f32[8,16,4,1024]{3,2,1,0:T(4,1...) while((s32[]{:T(128)}, f32[16,1024]{1,0:T(8,128)}, ...), condition=%wide.region_417.418_spmd.clone, body=%wide.region_336.417_spmd.clone.sunk | while | flops 31830020 | bytes 21808732 | solution.py:85
  2253.0 144.5 %all-reduce.392.cloned.1.call-done = (f32[512,2048]{1,0:T(8,128)}, f32[512,2048]{1,0:T(8,128)}) async-done(((f32[512,2048]{1,0:T(8,128)}, f32[512,2048]{1,0:T(8,128)}), (f32[512,2048]{1,0:T(8,128)}, f32[512,2048]{1,0:T(8,128)})) %all-reduce.392.cloned.1.call-update) | async-done | bytes 8388624 | tf_op jit(solution)/shard_map/psum | solution.py:177
  2432.5 137.7 %while.355 = (s32[]{:T(128)}, f32[16,1024]{1,0:T(8,128)}, f32[4,16,1024]{2,1,0:T(8,128)S(1)}, f32[8,16,4,1024]{3,2,1,0:T(4,128)}, f32[8,16,4,1024]{3,2,1,0:T(4,1...) while((s32[]{:T(128)}, f32[16,1024]{1,0:T(8,128)}, ...), condition=%wide.region_310.311_spmd.clone, body=%wide.region_229.310_spmd.clone.sunk | while | flops 31830020 | bytes 20497876 | solution.py:85
  2612.9 120.7 %while.359 = (s32[]{:T(128)}, f32[16,1024]{1,0:T(8,128)S(1)}, f32[4,16,1024]{2,1,0:T(8,128)S(1)}, f32[8,16,4,1024]{3,2,1,0:T(4,128)}, f32[8,16,4,1024]{3,2,1,0:T...) while((s32[]{:T(128)}, f32[16,1024]{1,0:T(8,128)S(1)}, ...), condition=%wide.region_524.525_spmd.clone, body=%wide.region_443.524_spmd.clone.sunk | while | flops 31830020 | bytes 20497876 | solution.py:85
  2974.1 88.5 %all-reduce.388.cloned.1.call-done = (f32[4,128,2048]{2,1,0:T(8,128)}, f32[4,128,2048]{2,1,0:T(8,128)}) async-done(((f32[4,128,2048]{2,1,0:T(8,128)}, f32[4,128,2048]{2,1,0:T(8,128)}), (f32[4,128,2048]{2,1,0:T(8,128)}, f32[4,128,2048]{2,1,0:T(8,128)})) %all-reduce.388.cloned.1.call-update) | async-done | bytes 8388624 | tf_op jit(solution)/shard_map/psum | solution.py:274
  3123.7 488.9 %reduce-scatter.4.cloned.1.call-done = f32[2,256,2,1024]{3,1,2,0:T(8,128)} async-done(((f32[2,2048,2,1024]{3,1,2,0:T(8,128)}), f32[2,256,2,1024]{3,1,2,0:T(8,128)}) %reduce-scatter.4.cloned.1.call-update) | async-done | bytes 4194320 | tf_op jit(solution)/shard_map/reduce_scatter | solution.py:378
  3620.0 59.3 %reduce-scatter.6.cloned.1.call-done = f32[2,16,1024]{2,1,0:T(8,128)} async-done(((f32[2,128,1024]{2,1,0:T(8,128)}), f32[2,16,1024]{2,1,0:T(8,128)}) %reduce-scatter.6.cloned.1.call-update) | async-done | bytes 131088 | tf_op jit(solution)/shard_map/reduce_scatter | solution.py:381
  3679.3 286.1 %reduce-scatter.8.cloned.1.call-done = f32[2,1024,256]{2,1,0:T(8,128)} async-done(((f32[2,1024,2048]{2,1,0:T(8,128)}), f32[2,1024,256]{2,1,0:T(8,128)}) %reduce-scatter.8.cloned.1.call-update) | async-done | bytes 2097168 | tf_op jit(solution)/shard_map/reduce_scatter | solution.py:379
  (3788 shorter events, 2469.7 us)
Async XLA Ops:
  162.8 333.6 %all-reduce.374.cloned.1.call-start = ((), (), s32[]{:S(2)}) async-start(), calls=%async_computation.4 | async-start | bytes 8388608 | tf_op jit(solution)/shard_map/psum | solution.py:177
  412.3 145.5 %all-reduce.376.cloned.1.call-start = ((), (), s32[]{:S(2)}) async-start(), calls=%async_computation.5 | async-start | bytes 655360 | tf_op jit(solution)/shard_map/psum | solution.py:159
  590.5 148.8 %all-gather.49.cloned.1.call-start = ((), (), s32[]{:S(2)}) async-start(), calls=%async_computation.24 | async-start | bytes 2359296 | tf_op jit(solution)/shard_map/all_gather | solution.py:27
  591.3 198.2 %all-gather.33.cloned.1.call-start = ((), (), s32[]{:S(2)}) async-start(), calls=%async_computation.11 | async-start | bytes 2359296 | tf_op jit(solution)/shard_map/all_gather | solution.py:27
  592.0 475.0 %all-reduce.382.cloned.1.call-start = ((), (), s32[]{:S(2)}) async-start(), calls=%async_computation.12 | async-start | bytes 655360 | tf_op jit(solution)/shard_map/psum | solution.py:245
  1002.7 251.7 %all-reduce.394.cloned.1.call-start = ((), (), s32[]{:S(2)}) async-start(), calls=%async_computation.32 | async-start | bytes 16777216 | tf_op jit(solution)/shard_map/psum | solution.py:274
  1101.1 204.9 %all-gather.29.cloned.1.call-start = ((), (), s32[]{:S(2)}) async-start(), calls=%async_computation.7 | async-start | bytes 2359296 | tf_op jit(solution)/shard_map/all_gather | solution.py:27
  1109.3 247.5 %all-gather.45.cloned.1.call-start = ((), (), s32[]{:S(2)}) async-start(), calls=%async_computation.22 | async-start | bytes 2359296 | tf_op jit(solution)/shard_map/all_gather | solution.py:27
  1290.4 301.8 %all-reduce.378.cloned.1.call-start = ((), (), s32[]{:S(2)}) async-start(), calls=%async_computation.8 | async-start | bytes 8388608 | tf_op jit(solution)/shard_map/psum | solution.py:177
  1508.1 148.2 %all-reduce.380.cloned.1.call-start = ((), (), s32[]{:S(2)}) async-start(), calls=%async_computation.9 | async-start | bytes 655360 | tf_op jit(solution)/shard_map/psum | solution.py:159
  1688.9 148.1 %all-gather.47.cloned.1.call-start = ((), (), s32[]{:S(2)}) async-start(), calls=%async_computation.23 | async-start | bytes 2359296 | tf_op jit(solution)/shard_map/all_gather | solution.py:27
  1689.5 197.4 %all-gather.31.cloned.1.call-start = ((), (), s32[]{:S(2)}) async-start(), calls=%async_computation.10 | async-start | bytes 2359296 | tf_op jit(solution)/shard_map/all_gather | solution.py:27
  1690.3 485.6 %all-reduce.384.cloned.1.call-start = ((), (), s32[]{:S(2)}) async-start(), calls=%async_computation.15 | async-start | bytes 655360 | tf_op jit(solution)/shard_map/psum | solution.py:245
  2109.8 121.4 %all-gather.35.cloned.1.call-start = ((), (), s32[]{:S(2)}) async-start(), calls=%async_computation.13 | async-start | bytes 2359296 | tf_op jit(solution)/shard_map/all_gather | solution.py:27
  2110.6 132.0 %all-gather.51.cloned.1.call-start = ((), (), s32[]{:S(2)}) async-start(), calls=%async_computation.25 | async-start | bytes 2359296 | tf_op jit(solution)/shard_map/all_gather | solution.py:27
  2111.3 286.1 %all-reduce.392.cloned.1.call-start = ((), (), s32[]{:S(2)}) async-start(), calls=%async_computation.31 | async-start | bytes 16777216 | tf_op jit(solution)/shard_map/psum | solution.py:177
  2210.6 386.8 %all-gather.39.cloned.1.call-start = ((), (), s32[]{:S(2)}) async-start(), calls=%async_computation.16 | async-start | bytes 2359296 | tf_op jit(solution)/shard_map/all_gather | solution.py:27
  2211.5 385.9 %all-gather.55.cloned.1.call-start = ((), (), s32[]{:S(2)}) async-start(), calls=%async_computation.27 | async-start | bytes 2359296 | tf_op jit(solution)/shard_map/all_gather | solution.py:27
  2427.3 356.9 %all-reduce.390.cloned.1.call-start = ((), (), s32[]{:S(2)}) async-start(), calls=%async_computation.30 | async-start | bytes 1310720 | tf_op jit(solution)/shard_map/psum | solution.py:245
  2749.9 222.5 %all-reduce.386.cloned.1.call-start = ((), (), s32[]{:S(2)}) async-start(), calls=%async_computation.28 | async-start | bytes 2883584
  2816.5 246.1 %all-reduce.388.cloned.1.call-start = ((), (), s32[]{:S(2)}) async-start(), calls=%async_computation.29 | async-start | bytes 16777216 | tf_op jit(solution)/shard_map/psum | solution.py:274
  2849.0 763.6 %reduce-scatter.4.cloned.1.call-start = ((), (), s32[]{:S(2)}) async-start(), calls=%async_computation.17 | async-start | bytes 37748736 | tf_op jit(solution)/shard_map/reduce_scatter | solution.py:378
  2918.6 760.6 %reduce-scatter.6.cloned.1.call-start = ((), (), s32[]{:S(2)}) async-start(), calls=%async_computation.18 | async-start | bytes 1179648 | tf_op jit(solution)/shard_map/reduce_scatter | solution.py:381
  2936.9 1028.6 %reduce-scatter.8.cloned.1.call-start = ((), (), s32[]{:S(2)}) async-start(), calls=%async_computation.19 | async-start | bytes 18874368 | tf_op jit(solution)/shard_map/reduce_scatter | solution.py:379
  (382 other events, 6765.9 us)
Sparse Core Ops, SparseCore 0:
  156.4 49.2 all-gather.40
  208.4 47.7 all-gather.24
  412.4 83.9 all-reduce.373
  589.7 49.2 all-gather.42
  641.4 47.7 all-gather.26
  691.5 47.7 all-gather.48
  741.7 47.7 all-gather.32
  1101.3 153.0 all-reduce.393
  1256.6 49.4 all-gather.28
  1309.0 47.7 all-gather.44
  1508.2 83.9 all-reduce.377
  1688.1 49.2 all-gather.52
  1739.4 47.7 all-gather.36
  1839.1 47.7 all-gather.30
  2142.9 49.3 all-gather.34
  2194.4 48.0 all-gather.50
  2245.7 151.7 all-reduce.391
  2399.4 49.4 all-gather.38
  2451.0 47.7 all-gather.54
  2816.6 90.0 all-reduce.385
  2910.1 152.4 all-reduce.387
  3066.8 545.6 reduce-scatter.3
  3616.8 62.4 reduce-scatter.5
  3683.6 281.7 reduce-scatter.7
  (7 shorter events, 245.8 us)
where the time goes:
time: 4000 us; the launch traced here: 3970 us
  waiting for transfers between devices  2010 us (50%)
  other arithmetic  1040 us (26%)
  local copies, waits for them, and re-layouts  581 us (15%)
  matrix products  243 us (6%)
  blocking collectives  42.8 us (1%)
    all_gather x16, waiting for transfers between devices, entering(): everything = jax.tree.map(lambda part: lax.all_gather(part, axis), array)  508 us
    reduce_scatter x1, waiting for transfers between devices, on_device(): lax.psum_scatter(stack_layers(1), 'blk', scatter_dimension=1, tiled=True)  489 us
    psum x3, waiting for transfers between devices, forward_layer(): lax.psum(jnp.dot(gated_rows, output_matrix, preferred_element_type=jnp.fl...  290 us
    reduce_scatter x1, waiting for transfers between devices, on_device(): lax.psum_scatter(stack_layers(9), 'blk', scatter_dimension=2, tiled=True)  286 us
    psum x2, waiting for transfers between devices, backward_layer(): lax.psum(normed_part, 'tensor').reshape(seq_count, length, model_width)  234 us
    reduce_sum x224, other arithmetic, scan_steps(): step_size[moment][:, None, :] * decay_rate  230 us
    reduce_sum x352, other arithmetic, scan_steps(): outputs.append(jnp.sum(read_coef[moment][:, :, None] * carried, axis=1))  208 us
    squeeze x128, local copies, waits for them, and re-layouts, local_scan(): lax.scan(jax.checkpoint(partial(scan_steps, decay_rate)), start_state, pi...  106 us
  transfers between devices with their start and end apart: 39, of which 28 were waited for; matrix products, arithmetic and copies ran while one was open for 18% of the time, Pallas kernels for 0%

commit v1 on v0

v1 whole, which is shorter than its diff:
```python
import math
from functools import partial
import jax
import jax.numpy as jnp
from jax import lax
from jax.experimental import pallas as pl
from jax.experimental.pallas import tpu as pltpu

from jax.sharding import PartitionSpec as P

STATE = 16
RANK = 128
EPSILON = 1e-05
LANES=128
LOG2E=math.log2(math.e)

def cp(limit):
    return pltpu.CompilerParams(dimension_semantics=("arbitrary",), vmem_limit_bytes=limit)

def spread(ref_value, out, first):
    for t in range(out.shape[0]):
        row = ref_value[t]
        for n in range(STATE):
            out[t, n] = jnp.broadcast_to(row[:, first + n:first + n + 1], out.shape[2:])

def rates(rate_ref, lanes, n):
    return jnp.broadcast_to(rate_ref[pl.ds(n, 1), lanes], (8, LANES))

def end_body(blocks, width, step_ref, push_ref, coef_ref, rate_ref, end_ref, write):
    @pl.when(pl.program_id(0) == 0)
    def _():
        end_ref[...] = jnp.zeros_like(end_ref)
    spread(coef_ref, write, 0)
    def group(g, _):
        cols = [pl.ds(pl.multiple_of((g * width + k) * LANES, LANES), LANES) for k in range(width)]
        for low in range(0, STATE, STATE // width):
            span = range(low, low + STATE // width)
            state = {(k, n): end_ref[n, :, cols[k]] for k in range(width) for n in span}
            rate = {(k, n): rates(rate_ref, cols[k], n) for k in range(width) for n in span}
            for t in range(step_ref.shape[0]):
                step = [step_ref[t, :, c] for c in cols]
                push = [push_ref[t, :, c] for c in cols]
                for n in span:
                    w = write[t, n]
                    for k in range(width):
                        state[k, n] = jnp.exp2(step[k] * rate[k, n]) * state[k, n] + push[k] * w
            for k in range(width):
                for n in span:
                    end_ref[n, :, cols[k]] = state[k, n]
        return 0
    lax.fori_loop(0, blocks // width, group, 0)

def end_states(step, push, coef, rate, tb=8, width=2, limit=40*2**20):
    T, _, C = step.shape
    return pl.pallas_call(
        partial(end_body, C // LANES, width),
        grid=(T // tb,),
        in_specs=[pl.BlockSpec((tb, 8, C), lambda i: (i, 0, 0)), pl.BlockSpec((tb, 8, C), lambda i: (i, 0, 0)),
                  pl.BlockSpec((tb, 8, 2 * STATE), lambda i: (i, 0, 0)), pl.BlockSpec((STATE, C), lambda i: (0, 0))],
        out_specs=pl.BlockSpec((STATE, 8, C), lambda i: (0, 0, 0)),
        out_shape=jax.ShapeDtypeStruct((STATE, 8, C), jnp.float32),
        scratch_shapes=[pltpu.VMEM((tb, STATE, 8, LANES), jnp.float32)],
        compiler_params=cp(limit), name="end_states")(step, push, coef, rate)

def scan_body(blocks, width, step_ref, push_ref, coef_ref, rate_ref, start_ref, out_ref, states_ref, enter_ref, final_ref, write, read):
    @pl.when(pl.program_id(0) == 0)
    def _():
        final_ref[...] = start_ref[...]
    spread(coef_ref, write, 0)
    spread(coef_ref, read, STATE)
    enter_ref[0] = final_ref[...]
    def group(g, _):
        cols = [pl.ds(pl.multiple_of((g * width + k) * LANES, LANES), LANES) for k in range(width)]
        for low in range(0, STATE, STATE // width):
            span = range(low, low + STATE // width)
            state = {(k, n): final_ref[n, :, cols[k]] for k in range(width) for n in span}
            rate = {(k, n): rates(rate_ref, cols[k], n) for k in range(width) for n in span}
            for t in range(step_ref.shape[0]):
                step = [step_ref[t, :, c] for c in cols]
                push = [push_ref[t, :, c] for c in cols]
                total = [None] * width
                for n in span:
                    w, r = write[t, n], read[t, n]
                    for k in range(width):
                        s = jnp.exp2(step[k] * rate[k, n]) * state[k, n] + push[k] * w
                        state[k, n] = s
                        states_ref[t, n, :, cols[k]] = s
                        total[k] = r * s if total[k] is None else total[k] + r * s
                for k in range(width):
                    if low == 0:
                        out_ref[t, :, cols[k]] = total[k]
                    else:
                        out_ref[t, :, cols[k]] += total[k]
            for k in range(width):
                for n in span:
                    final_ref[n, :, cols[k]] = state[k, n]
        return 0
    lax.fori_loop(0, blocks // width, group, 0)

def scan_forward(step, push, coef, rate, start, tb=8, width=2, limit=48*2**20):
    T, _, C = step.shape
    row = pl.BlockSpec((tb, 8, C), lambda i: (i, 0, 0))
    whole = pl.BlockSpec((STATE, 8, C), lambda i: (0, 0, 0))
    f32 = jnp.float32
    return pl.pallas_call(
        partial(scan_body, C // LANES, width),
        grid=(T // tb,),
        in_specs=[row, row, pl.BlockSpec((tb, 8, 2 * STATE), lambda i: (i, 0, 0)), pl.BlockSpec((STATE, C), lambda i: (0, 0)), whole],
        out_specs=[row, pl.BlockSpec((tb, STATE, 8, C), lambda i: (i, 0, 0, 0)), pl.BlockSpec((1, STATE, 8, C), lambda i: (i, 0, 0, 0)), whole],
        out_shape=[jax.ShapeDtypeStruct((T, 8, C), f32), jax.ShapeDtypeStruct((T, STATE, 8, C), f32),
                   jax.ShapeDtypeStruct((T // tb, STATE, 8, C), f32), jax.ShapeDtypeStruct((STATE, 8, C), f32)],
        scratch_shapes=[pltpu.VMEM((tb, STATE, 8, LANES), f32)] * 2,
        compiler_params=cp(limit), name="scan_forward")(step, push, coef, rate, start)

def start_body(blocks, width, step_ref, grad_ref, coef_ref, rate_ref, start_ref, read):
    @pl.when(pl.program_id(0) == 0)
    def _():
        start_ref[...] = jnp.zeros_like(start_ref)
    spread(coef_ref, read, STATE)
    def group(g, _):
        cols = [pl.ds(pl.multiple_of((g * width + k) * LANES, LANES), LANES) for k in range(width)]
        for low in range(0, STATE, STATE // width):
            span = range(low, low + STATE // width)
            state = {(k, n): start_ref[n, :, cols[k]] for k in range(width) for n in span}
            rate = {(k, n): rates(rate_ref, cols[k], n) for k in range(width) for n in span}
            for t in reversed(range(step_ref.shape[0])):
                step = [step_ref[t, :, c] for c in cols]
                grad = [grad_ref[t, :, c] for c in cols]
                for n in span:
                    r = read[t, n]
                    for k in range(width):
                        state[k, n] = jnp.exp2(step[k] * rate[k, n]) * (state[k, n] + r * grad[k])
            for k in range(width):
                for n in span:
                    start_ref[n, :, cols[k]] = state[k, n]
        return 0
    lax.fori_loop(0, blocks // width, group, 0)

def start_grads(step, grad, coef, rate, tb=8, width=2, limit=40*2**20):
    T, _, C = step.shape
    last = T // tb - 1
    row = pl.BlockSpec((tb, 8, C), lambda i: (last - i, 0, 0))
    return pl.pallas_call(
        partial(start_body, C // LANES, width),
        grid=(T // tb,),
        in_specs=[row, row, pl.BlockSpec((tb, 8, 2 * STATE), lambda i: (last - i, 0, 0)), pl.BlockSpec((STATE, C), lambda i: (0, 0))],
        out_specs=pl.BlockSpec((STATE, 8, C), lambda i: (0, 0, 0)),
        out_shape=jax.ShapeDtypeStruct((STATE, 8, C), jnp.float32),
        scratch_shapes=[pltpu.VMEM((tb, STATE, 8, LANES), jnp.float32)],
        compiler_params=cp(limit), name="start_grads")(step, grad, coef, rate)

def back_body(blocks, width, step_ref, push_ref, grad_ref, coef_ref, rate_ref, states_ref, enter_ref, end_ref,
              decay_out, push_out, coef_out, start_ref, speed_ref, write, read, write_sum, read_sum):
    @pl.when(pl.program_id(0) == 0)
    def _():
        start_ref[...] = end_ref[...]
        speed_ref[...] = jnp.zeros_like(speed_ref)
    spread(coef_ref, write, 0)
    spread(coef_ref, read, STATE)
    tb = step_ref.shape[0]
    def group(g, first):
        cols = [pl.ds(pl.multiple_of((g * width + k) * LANES, LANES), LANES) for k in range(width)]
        for low in range(0, STATE, STATE // width):
            span = range(low, low + STATE // width)
            carry = {(k, n): start_ref[n, :, cols[k]] for k in range(width) for n in span}
            speed = {(k, n): speed_ref[n, :, cols[k]] for k in range(width) for n in span}
            rate = {(k, n): rates(rate_ref, cols[k], n) for k in range(width) for n in span}
            for t in reversed(range(tb)):
                step = [step_ref[t, :, c] for c in cols]
                push = [push_ref[t, :, c] for c in cols]
                grad = [grad_ref[t, :, c] for c in cols]
                decays = [None] * width
                pushes = [None] * width
                for n in span:
                    w, r = write[t, n], read[t, n]
                    wsum, rsum = None, None
                    for k in range(width):
                        before = states_ref[t - 1, n, :, cols[k]] if t else enter_ref[0, n, :, cols[k]]
                        back = carry[k, n] + r * grad[k]
                        held = jnp.exp2(step[k] * rate[k, n]) * back
                        carry[k, n] = held
                        q = held * before
                        speed[k, n] = speed[k, n] + step[k] * q
                        rq, bw = rate[k, n] * q, back * w
                        decays[k] = rq if decays[k] is None else decays[k] + rq
                        pushes[k] = bw if pushes[k] is None else pushes[k] + bw
                        bp, gs = back * push[k], grad[k] * states_ref[t, n, :, cols[k]]
                        wsum = bp if wsum is None else wsum + bp
                        rsum = gs if rsum is None else rsum + gs
                    if first:
                        write_sum[t, n] = wsum
                        read_sum[t, n] = rsum
                    else:
                        write_sum[t, n] += wsum
                        read_sum[t, n] += rsum
                for k in range(width):
                    if low == 0:
                        decay_out[t, :, cols[k]] = decays[k]
                        push_out[t, :, cols[k]] = pushes[k]
                    else:
                        decay_out[t, :, cols[k]] += decays[k]
                        push_out[t, :, cols[k]] += pushes[k]
            for k in range(width):
                for n in span:
                    start_ref[n, :, cols[k]] = carry[k, n]
                    speed_ref[n, :, cols[k]] = speed[k, n]
        return 0
    write_sum[...] = jnp.zeros_like(write_sum)
    read_sum[...] = jnp.zeros_like(read_sum)
    lax.fori_loop(0, blocks // width, lambda g, _: group(g, False), 0)
    lane = lax.broadcasted_iota(jnp.int32, (8, 2 * STATE), 1)
    for t in range(tb):
        row = jnp.zeros((8, 2 * STATE), jnp.float32)
        for n in range(STATE):
            row = jnp.where(lane == n, jnp.sum(write_sum[t, n], axis=-1, keepdims=True), row)
            row = jnp.where(lane == STATE + n, jnp.sum(read_sum[t, n], axis=-1, keepdims=True), row)
        coef_out[t] = row

def scan_backward(step, push, grad, coef, rate, states, enter, end, tb=8, width=2, limit=48*2**20):
    T, _, C = step.shape
    last = T // tb - 1
    f32 = jnp.float32
    row = pl.BlockSpec((tb, 8, C), lambda i: (last - i, 0, 0))
    thin = pl.BlockSpec((tb, 8, 2 * STATE), lambda i: (last - i, 0, 0))
    whole = pl.BlockSpec((STATE, 8, C), lambda i: (0, 0, 0))
    return pl.pallas_call(
        partial(back_body, C // LANES, width),
        grid=(T // tb,),
        in_specs=[row, row, row, thin, pl.BlockSpec((STATE, C), lambda i: (0, 0)),
                  pl.BlockSpec((tb, STATE, 8, C), lambda i: (last - i, 0, 0, 0)),
                  pl.BlockSpec((1, STATE, 8, C), lambda i: (last - i, 0, 0, 0)), whole],
        out_specs=[row, row, thin, whole, whole],
        out_shape=[jax.ShapeDtypeStruct((T, 8, C), f32)] * 2 + [jax.ShapeDtypeStruct((T, 8, 2 * STATE), f32)]
          + [jax.ShapeDtypeStruct((STATE, 8, C), f32)] * 2,
        scratch_shapes=[pltpu.VMEM((tb, STATE, 8, LANES), f32)] * 4,
        compiler_params=cp(limit), name="scan_backward")(step, push, grad, coef, rate, states, enter, end)


HALVES_OF_CHIP = 2


def silu_slope(argument):
    sigmoid_value = jax.nn.sigmoid(argument)
    return sigmoid_value * (1.0 + argument * (1.0 - sigmoid_value))


def half_of(array, index):
    size = array.shape[0] // 2
    return lax.dynamic_slice_in_dim(array, index * size, size, 0)


def ordered(index, mine, other):
    first = jnp.where(index == 0, mine, other)
    second = jnp.where(index == 0, other, mine)
    return jnp.concatenate([first, second], axis=0)


def tensor_sum(array):
    if lax.axis_size("tensor") != 4:
        return lax.psum(array, "tensor")
    core = lax.axis_index("tensor") % 2
    beside = [(0, 1), (1, 0), (2, 3), (3, 2)]
    across = [(0, 2), (2, 0), (1, 3), (3, 1)]
    half = half_of(array, core) + lax.ppermute(half_of(array, 1 - core), "tensor", beside)
    half = half + lax.ppermute(half, "tensor", across)
    return ordered(core, half, lax.ppermute(half, "tensor", beside))


def blk_sum(array):
    if lax.axis_size("blk") != 8:
        return lax.psum(array, "blk")
    for bit in (1, 2, 4):
        array = array + lax.ppermute(array, "blk", [(j, j ^ bit) for j in range(8)])
    return array


def blk_scatter(array):
    return lax.psum_scatter(array, "blk", scatter_dimension=0, tiled=True)


def neighbour(value, steps):
    count = lax.axis_size("blk")
    first, last = max(0, -steps), min(count, count - steps)
    return lax.ppermute(value, "blk", [(j, j + steps) for j in range(first, last)])


def entering_any(total, local, rate, first, reverse):
    peers, index = lax.axis_size("blk"), lax.axis_index("blk")
    totals, locals_ = lax.all_gather(total, "blk"), lax.all_gather(local, "blk")

    def step(k, state):
        at = peers - 1 - k if reverse else k
        reached = at > index if reverse else at < index
        return jnp.where(reached, jnp.exp2(totals[at][None] * rate) * state + locals_[at], state)

    return lax.fori_loop(0, peers, step, first)


def entering(total, local, rate, first, reverse):
    if lax.axis_size("blk") != 8:
        return entering_any(total, local, rate, first, reverse)
    index = lax.axis_index("blk")
    y, z = index % 2, index // 2
    pair = [(j, j ^ 1) for j in range(8)]
    if reverse:
        y, z = 1 - y, 3 - z
    sign = -1 if reverse else 1
    at_a = y == 0
    decay = jnp.exp2(total[None] * rate)
    own = local + jnp.where(jnp.logical_and(z == 0, at_a), decay * first, 0.0)
    mine, give = half_of(own, y), half_of(own, 1 - y)
    got = lax.ppermute(jnp.concatenate([give, total[None]], axis=0), "blk", pair)
    got, got_total = got[:-1], got[-1]
    rate_half = half_of(rate, y)
    local_a, local_b = jnp.where(at_a, mine, got), jnp.where(at_a, got, mine)
    total_a, total_b = jnp.where(at_a, total, got_total), jnp.where(at_a, got_total, total)
    joined = local_b + jnp.exp2(total_b[None] * rate_half) * local_a
    message = jnp.concatenate([joined, (total_a + total_b)[None]], axis=0)

    def along(value, pairs):
        if reverse:
            pairs = [(3 - s, 3 - d) for s, d in pairs]
        return lax.ppermute(value, "blk", [(2 * s + k, 2 * d + k) for s, d in pairs for k in (0, 1)])

    one = along(message, [(0, 1), (1, 2), (2, 3)])
    two = along(one, [(1, 2), (2, 3)])
    three = along(one[:-1], [(1, 3)])
    enter = one[:-1] + jnp.exp2(one[-1:] * rate_half) * (
        two[:-1] + jnp.exp2(two[-1:] * rate_half) * three
    )
    after_a = local_a + jnp.exp2(total_a[None] * rate_half) * enter
    other = lax.ppermute(jnp.where(at_a, after_a, enter), "blk", pair)
    state = ordered(y, jnp.where(at_a, enter, after_a), other)
    return jnp.where(jnp.logical_and(z == 0, at_a), first, state)


def rows(array):
    return array.reshape(-1, array.shape[-1])


def by_step(array):
    return array.reshape(-1, 8, array.shape[-1])


def dot32(left, right):
    return jnp.dot(left, right, preferred_element_type=jnp.float32)


def dot_t(left, right):
    return lax.dot_general(left, right, (((0,), (0,)), ((), ())), preferred_element_type=jnp.float32)


def dot_n(left, right):
    return lax.dot_general(left, right, (((1,), (1,)), ((), ())), preferred_element_type=jnp.float32)


def two_parts(array):
    high = lax.optimization_barrier(array.astype(jnp.bfloat16))
    return high, (array - high.astype(jnp.float32)).astype(jnp.bfloat16)


def split_parts(array, parts):
    return array.reshape(array.shape[:-2] + (parts, 8 // parts) + array.shape[-1:])


class Layer:
    def __init__(self, index, args):
        (norm_gain, in_weight, conv_weight, conv_bias, x_weight, dt_weight, dt_bias, decay_log,
         skip_weight, out_weight) = args
        self.gain = norm_gain[index]
        self.into = in_weight[index].reshape(in_weight.shape[1], -1)
        self.taps = conv_weight[index]
        self.shift = conv_bias[index]
        self.x = x_weight[index]
        self.dt = dt_weight[index]
        self.dt_bias = dt_bias[index]
        self.rate = -jnp.exp(decay_log[index])
        self.rate2 = self.rate * LOG2E
        self.skip = skip_weight[index]
        self.out = out_weight[index]


def forward_layer(layer, residual, scan_first, conv_first, parts, at_first):
    width = residual.shape[1]
    q = lax.rsqrt(jnp.mean(residual * residual, axis=-1, keepdims=True) + EPSILON)
    normed = (residual * q * layer.gain).astype(jnp.bfloat16)
    mixed = dot32(normed, layer.into)
    inner = mixed.shape[-1] // 2
    values, gate = mixed[:, :inner], mixed[:, inner:]
    count = values.shape[0]
    rim = layer.taps.shape[0] - 1
    tails = split_parts(by_step(values[count - 8 * rim:]), parts)
    arrived = jnp.where(at_first, conv_first, neighbour(tails[:, -1], 1))
    prefix = jnp.concatenate([arrived[:, None], tails[:, :-1]], axis=1).reshape(rim * 8, inner)
    window = jnp.concatenate([prefix, values], axis=0)
    conv_out = layer.shift + sum(layer.taps[k] * window[8 * k:8 * k + count] for k in range(rim + 1))
    inputs = lax.optimization_barrier(jax.nn.silu(conv_out).astype(jnp.bfloat16))
    projected = tensor_sum(dot32(inputs, layer.x))
    dt_low = projected[:, :RANK].astype(jnp.bfloat16)
    coef = by_step(projected[:, RANK:])
    before = dot32(dt_low, layer.dt) + layer.dt_bias
    step = jax.nn.softplus(before)
    push = step * inputs.astype(jnp.float32)
    rate = layer.rate2[:, None]
    local = split_parts(end_states(by_step(step), by_step(push), coef, layer.rate2), parts)
    totals = split_parts(jnp.sum(by_step(step), axis=0), parts)
    joined, total = local[:, 0], totals[0]
    for p in range(1, parts):
        joined = local[:, p] + jnp.exp2(totals[p][None] * rate) * joined
        total = total + totals[p]
    start = entering(total, joined, rate, scan_first, False)
    starts = [start]
    for p in range(1, parts):
        starts.append(local[:, p - 1] + jnp.exp2(totals[p - 1][None] * rate) * starts[-1])
    start = jnp.stack(starts, axis=1).reshape(STATE, 8, inner)
    scanned, states, enter, final = scan_forward(by_step(step), by_step(push), coef, layer.rate2, start)
    result = rows(scanned) + layer.skip * inputs.astype(jnp.float32)
    gated = (result * jax.nn.silu(gate)).astype(jnp.bfloat16)
    branch = tensor_sum(dot32(gated, layer.out))
    following = residual + branch
    squares = jnp.stack([jnp.sum(branch * branch), jnp.sum(following * following)])
    kept = (residual, q, normed, window, gate, conv_out, inputs, dt_low, coef, before, step, push, totals,
            result, gated, states, enter)
    return following, squares, split_parts(final, parts)[:, -1], tails[:, -1], kept


def backward_layer(layer, grad, kept, parts):
    (residual, q, normed, window, gate, conv_out, inputs, dt_low, coef, before, step, push, totals,
     result, gated, states, enter) = kept
    count, inner = gate.shape
    rim = layer.taps.shape[0] - 1
    wide = inputs.astype(jnp.float32)
    grad_low = grad.astype(jnp.bfloat16)
    grad_gated = dot_n(grad_low, layer.out)
    out_grad = dot_t(grad_low, gated)
    grad_result = grad_gated * jax.nn.silu(gate)
    grad_gate = (grad_gated * result * silu_slope(gate)).astype(jnp.bfloat16)
    skip_grad = jnp.sum(grad_result * wide, axis=0)
    gate_grad = dot_t(normed, grad_gate)
    rate = layer.rate2[:, None]
    local = split_parts(start_grads(by_step(step), by_step(grad_result), coef, layer.rate2), parts)
    joined, total = local[:, -1], totals[-1]
    for p in reversed(range(parts - 1)):
        joined = local[:, p] + jnp.exp2(totals[p][None] * rate) * joined
        total = total + totals[p]
    end = entering(total, joined, rate, jnp.zeros_like(joined), True)
    ends = [end]
    for p in reversed(range(1, parts)):
        ends.insert(0, local[:, p] + jnp.exp2(totals[p][None] * rate) * ends[0])
    end = jnp.stack(ends, axis=1).reshape(STATE, 8, inner)
    decays, pushes, coef_grad, start_grad, speed = scan_backward(
        by_step(step), by_step(push), by_step(grad_result), coef, layer.rate2, states, enter, end)
    pushes = rows(pushes)
    step_grad = rows(decays) * (1.0 / LOG2E) + wide * pushes
    before_grad = step_grad * jax.nn.sigmoid(before)
    bias_grad = jnp.sum(before_grad, axis=0)
    decay_grad = layer.rate * jnp.sum(speed, axis=1)
    before_low = before_grad.astype(jnp.bfloat16)
    dt_grad = dot_t(dt_low, before_low)
    projected_grad = tensor_sum(jnp.concatenate([dot_n(before_low, layer.dt), rows(coef_grad)], axis=-1))
    high, low = two_parts(projected_grad)
    x_grad = dot_t(high, inputs) + dot_t(low, inputs)
    through = dot_n(jnp.concatenate([high, low], axis=-1), jnp.concatenate([layer.x, layer.x], axis=-1))
    inputs_grad = grad_result * layer.skip + step * pushes + through
    conv_grad = inputs_grad * silu_slope(conv_out)
    taps_grad = jnp.stack([jnp.sum(conv_grad * window[8 * k:8 * k + count], axis=0) for k in range(rim + 1)])
    shift_grad = jnp.sum(conv_grad, axis=0)
    margin = jnp.zeros((8 * rim, inner), jnp.float32)
    padded = jnp.concatenate([margin, conv_grad, margin], axis=0)
    window_grad = sum(
        layer.taps[k] * padded[8 * (rim - k):8 * (rim - k) + count + 8 * rim] for k in range(rim + 1))
    prefix_grad = split_parts(by_step(window_grad[:8 * rim]), parts)
    arrived = neighbour(prefix_grad[:, 0], -1)
    tail_grad = jnp.concatenate([prefix_grad[:, 1:], arrived[:, None]], axis=1).reshape(8 * rim, inner)
    values_grad = jnp.concatenate([window_grad[8 * rim:count], window_grad[count:] + tail_grad], axis=0)
    values_grad = values_grad.astype(jnp.bfloat16)
    into_grad = dot_t(normed, values_grad)
    mixed_grad = jnp.concatenate([values_grad, grad_gate], axis=-1)
    normed_grad = tensor_sum(dot_n(mixed_grad, layer.into))
    gain_grad = jnp.sum(normed_grad * (residual * q), axis=0)
    scaled = normed_grad * layer.gain
    inner_mean = jnp.mean(scaled * residual, axis=-1, keepdims=True)
    passed = grad + q * scaled - residual * (q * q * q * inner_mean)
    grads = (gain_grad, into_grad, gate_grad, taps_grad, shift_grad, x_grad, dt_grad, bias_grad, decay_grad,
             skip_grad, out_grad)
    start_first = split_parts(start_grad, parts)[:, 0]
    return passed, grads, start_first, prefix_grad[:, 0]


MICRO = 1


def on_device(tokens, cotangent, *args):
    scan_init, conv_init = args[-2:]
    weights = args[:-2]
    blocks, index = lax.axis_size("blk"), lax.axis_index("blk")
    at_first = index == 0
    layer_total = weights[1].shape[0]
    seqs = tokens.shape[0] // MICRO
    parts = 8 // seqs
    length = tokens.shape[1] // parts
    width = tokens.shape[2]
    layers = [Layer(l, weights) for l in range(layer_total)]

    def arrange(array):
        return array.reshape(seqs, parts, length, width).transpose(2, 1, 0, 3).reshape(length * 8, width)

    def restore(array):
        array = array.reshape(length, parts, seqs, width).transpose(2, 1, 0, 3)
        return array.reshape(seqs, parts * length, width)

    outs, ins = [], []
    finals, tails, starts, prefixes = ([[None] * MICRO for _ in range(layer_total)] for _ in range(4))
    sums = [None] * layer_total
    squares = [0.0] * layer_total
    input_square = 0.0
    for m in range(MICRO):
        part = slice(m * seqs, (m + 1) * seqs)
        residual = arrange(tokens[part]).astype(jnp.float32)
        input_square = input_square + jnp.sum(residual * residual)
        kept = []
        for l in range(layer_total):
            residual, square, finals[l][m], tails[l][m], saved = forward_layer(
                layers[l], residual, jnp.moveaxis(scan_init[l, part], 1, 0),
                jnp.moveaxis(conv_init[l, part], 1, 0), parts, at_first)
            squares[l] = squares[l] + square
            kept.append(saved)
        outs.append(restore(residual.astype(jnp.bfloat16)))
        grad = arrange(cotangent[part]).astype(jnp.float32)
        for l in reversed(range(layer_total)):
            grad, grads, starts[l][m], prefixes[l][m] = backward_layer(layers[l], grad, kept[l], parts)
            sums[l] = grads if sums[l] is None else jax.tree.map(jnp.add, sums[l], grads)
        ins.append(restore(grad.astype(jnp.bfloat16)))

    big, small = [], []
    for l in reversed(range(layer_total)):
        (gain_grad, into_grad, gate_grad, taps_grad, shift_grad, x_grad, dt_grad, bias_grad, decay_grad,
         skip_grad, out_grad) = sums[l]
        into_part, gate_part, out_part = blk_scatter(into_grad), blk_scatter(gate_grad), blk_scatter(out_grad)
        thin = jnp.concatenate([x_grad.reshape(blocks, -1, x_grad.shape[-1]),
                                dt_grad.reshape(blocks, -1, dt_grad.shape[-1])], axis=1)
        thin = blk_scatter(thin)[0]
        cut = x_grad.shape[0] // blocks
        big.insert(0, (jnp.stack([into_part, gate_part], axis=1), out_part.T, thin[:cut].T, thin[cut:]))
        inner = taps_grad.shape[-1]
        packed = jnp.concatenate([gain_grad.reshape(-1, inner), taps_grad, shift_grad[None], bias_grad[None],
                                  skip_grad[None], decay_grad], axis=0)
        if l == 0:
            extra = jnp.concatenate([jnp.stack(squares).reshape(-1), input_square.reshape(1)])
            extra = jnp.pad(extra, (0, inner - extra.shape[0]))[None]
            packed = jnp.concatenate([packed, extra], axis=0)
        small.insert(0, blk_sum(packed))
    rows_gain = width // weights[2].shape[-1]
    taps = weights[2].shape[1]

    def unpack(first, count):
        return jnp.stack([part[first:first + count] for part in small])

    row_total = tokens.shape[0] * tokens.shape[1] * width * blocks
    last = jnp.sqrt(small[0][-1] / row_total)
    rms_stats = last[:2 * layer_total].reshape(layer_total, 2)
    input_rms = last[2 * layer_total:2 * layer_total + 1]
    gain_grad = unpack(0, rows_gain).reshape(layer_total, width)
    at = rows_gain + taps

    def stacked(lists):
        return jnp.stack([jnp.moveaxis(jnp.concatenate(parts_, axis=1), 0, 1) for parts_ in lists])[:, :, None]

    return (
        jnp.concatenate(outs, axis=0),
        stacked(finals),
        stacked(tails),
        jnp.concatenate(ins, axis=0),
        stacked(starts),
        stacked(prefixes),
        gain_grad,
        jnp.stack([part[0] for part in big]),
        unpack(rows_gain, taps),
        unpack(at, 1)[:, 0],
        jnp.stack([part[2] for part in big]),
        jnp.stack([part[3] for part in big]),
        unpack(at + 1, 1)[:, 0],
        unpack(at + 3, STATE),
        unpack(at + 2, 1)[:, 0],
        jnp.stack([part[1] for part in big]),
        rms_stats,
        input_rms,
    )


def solution(mesh):
    placed = (
        P(None, "blk", None),
        P(None, "blk", None),
        P(),
        P(None, None, None, "tensor"),
        P(None, None, "tensor"),
        P(None, "tensor"),
        P(None, "tensor", None),
        P(None, None, "tensor"),
        P(None, "tensor"),
        P(None, None, "tensor"),
        P(None, "tensor"),
        P(None, "tensor", None),
        P(None, None, None, "tensor"),
        P(None, None, None, "tensor"),
    )
    return jax.shard_map(
        on_device,
        mesh=mesh,
        in_specs=placed,
        out_specs=(
            P(None, "blk", None),
            P(None, None, "blk", None, "tensor"),
            P(None, None, "blk", None, "tensor"),
            P(None, "blk", None),
            P(None, None, "blk", None, "tensor"),
            P(None, None, "blk", None, "tensor"),
            P(),
            P(None, "blk", None, "tensor"),
            P(None, None, "tensor"),
            P(None, "tensor"),
            P(None, "tensor", "blk"),
            P(None, "blk", "tensor"),
            P(None, "tensor"),
            P(None, None, "tensor"),
            P(None, "tensor"),
            P(None, "tensor", "blk"),
            P(),
            P(),
        ),
        check_vma=False,
    )
```

time: 4000 us -> 1790 us (0.45)
  waiting for transfers between devices: 2010 us -> 939 us
  other arithmetic: 1040 us -> 184 us
  local copies, waits for them, and re-layouts: 581 us -> 115 us
  Pallas kernels: 0 us -> 248 us
  starting transfers between devices: 24.6 us -> 76.9 us
  blocking collectives: 42.8 us -> 0 us
  matrix products: 243 us -> 203 us
    psum x11 -> x0, waiting for transfers between devices: 660 us -> none  [the longest x3 290 us: forward_layer(): lax.psum(jnp.dot(gated_rows, output_matrix, preferred_element_type=jnp.fl...]
    ppermute x8 -> x54, waiting for transfers between devices: 4.24 us -> 565 us  [the longest x8 380 us: tensor_sum(): half = half + lax.ppermute(half, 'tensor', across)]
    reduce_sum x625 -> x10, other arithmetic: 568 us -> 56.1 us  [the longest x2 12.7 us: forward_layer(): jnp.mean(residual * residual, axis=-1, keepdims=True) + EPSILON]
    all_gather x16 -> x0, waiting for transfers between devices: 508 us -> none  [entering(): everything = jax.tree.map(lambda part: lax.all_gather(part, axis), array)]
    reduce_scatter x3 -> x8, waiting for transfers between devices: 834 us -> 374 us  [blk_scatter(): return lax.psum_scatter(array, 'blk', scatter_dimension=0, tiled=True)]
    pallas_call x0 -> x8, Pallas kernels: none -> 248 us  [the longest x2 115 us: scan_backward(): pl.pallas_call(partial(back_body, C // LANES, width), grid=(T // tb,), in...]
    mul x292 -> x4, other arithmetic: 113 us -> 0.08 us  [the longest x1 0.03 us: backward_layer(): decay_grad = layer.rate * jnp.sum(speed, axis=1)]
    squeeze x132 -> x1, local copies, waits for them, and re-layouts: 107 us -> 0.87 us  [__init__(): self.x = x_weight[index]]
  transfers between devices with their start and end apart: 39 -> 62, of which waited for: 28 -> 42; matrix products, arithmetic and copies ran while one was open for 18% -> 19% of each run, Pallas kernels for 0% -> 4%
where the time goes in v1:
time: 1790 us; the launch traced here: 1780 us
  waiting for transfers between devices  939 us (52%)
  Pallas kernels  248 us (14%)
  matrix products  203 us (11%)
  other arithmetic  184 us (10%)
  local copies, waits for them, and re-layouts  115 us (6%)
  starting transfers between devices  76.9 us (4%)
    ppermute x8, waiting for transfers between devices, tensor_sum(): half = half + lax.ppermute(half, 'tensor', across)  380 us
    reduce_scatter x8, waiting for transfers between devices, blk_scatter(): return lax.psum_scatter(array, 'blk', scatter_dimension=0, tiled=True)  374 us
    pallas_call x2, Pallas kernels, scan_backward(): pl.pallas_call(partial(back_body, C // LANES, width), grid=(T // tb,), in...  115 us
    ppermute x12, waiting for transfers between devices, along(): lax.ppermute(value, 'blk', [(2 * s + k, 2 * d + k) for s, d in pairs for...  79.8 us
    dot_general x8, matrix products, dot_n(): lax.dot_general(left, right, (((1,), (1,)), ((), ())), preferred_element_...  76.9 us
    dot_general x12, matrix products, dot_t(): lax.dot_general(left, right, (((0,), (0,)), ((), ())), preferred_element_...  71.3 us
    pallas_call x2, Pallas kernels, scan_forward(): pl.pallas_call(partial(scan_body, C // LANES, width), grid=(T // tb,), in...  65.8 us
    unnamed x293, local copies, waits for them, and re-layouts  65.1 us
  transfers between devices with their start and end apart: 62, of which 42 were waited for; matrix products, arithmetic and copies ran while one was open for 19% of the time, Pallas kernels for 4%

profile of v1, /device:TPU:0, one launch (start us, length us, event | category | flops | bytes accessed | tf_op | source)
XLA Modules:
  0.0 1782.3 jit_solution(18367511847112495713)
XLA Ops:
  12.6 14.1 fusion.215
  95.2 16.5 end_states.2
  140.3 32.8 %scan_forward.2 = (f32[128,8,1024]{2,1,0:T(8,128)S(1)}, f32[128,16,8,1024]{3,2,1,0:T(8,128)}, f32[16,16,8,1024]{3,2,1,0:T(8,128)}, f32[16,8,1024]{2,1,0:T(8,128)S(1)}) custom-call(f32[128,8,1024]{2,1,0:T(8,128)} %copy-done, f32[128,8,1024]{2,1,0:T(8,128)} %copy-done.4, f32[128,8,32]{2,1,0:T(8,128)S(1)} %bitcast.518, ...), custom_call_target="tpu_custom_call" | custom-call | tf_op jit(solution)/shard_map/scan_forward/pallas_call | solution.py:105
  195.1 91.1 %collective-permute-done.10 = f32[512,2048]{1,0:T(8,128)S(1)} collective-permute-done((f32[512,2048]{1,0:T(8,128)S(1)}, f32[512,2048]{1,0:T(8,128)S(1)}, u32[]{:S(2)}, u32[]{:S(2)}) %collective-permute-start.10) | collective-permute-done | bytes 4194336 | tf_op jit(solution)/shard_map/ppermute | solution.py:265
  314.5 14.5 fusion.40
  361.0 16.5 end_states.3
  378.0 14.3 collective-permute-start.16
  423.1 33.0 %scan_forward.3 = (f32[128,8,1024]{2,1,0:T(8,128)S(1)}, f32[128,16,8,1024]{3,2,1,0:T(8,128)}, f32[16,16,8,1024]{3,2,1,0:T(8,128)}, f32[16,8,1024]{2,1,0:T(8,128)S(1)}) custom-call(f32[128,8,1024]{2,1,0:T(8,128)} %copy-done.2, f32[128,8,1024]{2,1,0:T(8,128)} %copy-done.5, f32[128,8,32]{2,1,0:T(8,128)S(1)} %bitcast.522, ...), custom_call_target="tpu_custom_call" | custom-call | tf_op jit(solution)/shard_map/scan_forward/pallas_call | solution.py:105
  462.7 16.7 start_grads.2
  488.1 20.3 %collective-permute-done.25 = f32[9,8,1024]{2,1,0:T(8,128)S(1)} collective-permute-done((f32[9,8,1024]{2,1,0:T(8,128)S(1)}, f32[9,8,1024]{2,1,0:T(8,128)S(1)}, u32[]{:S(2)}, u32[]{:S(2)}) %collective-permute-start.25) | collective-permute-done | bytes 294944 | tf_op jit(solution)/shard_map/ppermute | solution.py:323
  529.0 57.8 %scan_backward.2 = (f32[128,8,1024]{2,1,0:T(8,128)}, f32[128,8,1024]{2,1,0:T(8,128)}, f32[128,8,32]{2,1,0:T(8,128)S(1)}, f32[16,8,1024]{2,1,0:T(8,128)S(1)}, f32[16,8,1024]{2,1,0:T(8,128)S(1)}) custom-call(f32[128,8,1024]{2,1,0:T(8,128)} %copy-done.2, f32[128,8,1024]{2,1,0:T(8,128)} %copy-done.5, f32[128,8,1024]{2,1,0:T(8,128)} %bitcast.514, ...), custom_call_target="tpu_custom_call" | custom-call | tf_op jit(solution)/shard_map/scan_backward/pallas_call | solution.py:226
  700.4 84.8 %collective-permute-done.22 = f32[512,2048]{1,0:T(8,128)S(1)} collective-permute-done((f32[512,2048]{1,0:T(8,128)S(1)}, f32[512,2048]{1,0:T(8,128)S(1)}, u32[]{:S(2)}, u32[]{:S(2)}) %collective-permute-start.22) | collective-permute-done | bytes 4194336 | tf_op jit(solution)/shard_map/ppermute | solution.py:265
  795.4 79.5 %collective-permute-done.34 = f32[512,2048]{1,0:T(8,128)} collective-permute-done((f32[512,2048]{1,0:T(8,128)}, f32[512,2048]{1,0:T(8,128)}, u32[]{:S(2)}, u32[]{:S(2)}) %collective-permute-start.34) | collective-permute-done | bytes 4194336 | tf_op jit(solution)/shard_map/ppermute | solution.py:265
  902.8 18.6 %fusion.33 = (f32[1024]{0:T(1024)}, f32[1024,1024]{1,0:T(8,128)}, bf16[1024,1024]{1,0:T(8,128)(2,1)}) fusion(bf16[1024,1024]{1,0:T(8,128)(2,1)} %copy-done.20, f32[1024,2048]{1,0:T(8,128)} %copy-done.38, f32[1024]{0:T(1024)S(1)} %bitcast.599, f32[128,8,1024]{2,1,0:T(8,128)} %copy-done.11, bf16[2,1024,2048]{2,1,0:T(8,128)(2,1)} %param.25, ...), kind=kOutput, calls=%fused_computation.75 | convolution fusion | flops 4329569280 | bytes 41967616 | tf_op jit(solution)/shard_map/dot_general | solution.py:354
  925.9 16.7 start_grads.3
  960.5 22.3 %collective-permute-done.37 = f32[9,8,1024]{2,1,0:T(8,128)S(1)} collective-permute-done((f32[9,8,1024]{2,1,0:T(8,128)S(1)}, f32[9,8,1024]{2,1,0:T(8,128)S(1)}, u32[]{:S(2)}, u32[]{:S(2)}) %collective-permute-start.37) | collective-permute-done | bytes 294944 | tf_op jit(solution)/shard_map/ppermute | solution.py:323
  1006.9 57.7 %scan_backward.3 = (f32[128,8,1024]{2,1,0:T(8,128)}, f32[128,8,1024]{2,1,0:T(8,128)}, f32[128,8,32]{2,1,0:T(8,128)S(1)}, f32[16,8,1024]{2,1,0:T(8,128)S(1)}, f32[16,8,1024]{2,1,0:T(8,128)S(1)}) custom-call(f32[128,8,1024]{2,1,0:T(8,128)} %copy-done, f32[128,8,1024]{2,1,0:T(8,128)} %copy-done.4, f32[128,8,1024]{2,1,0:T(8,128)} %bitcast.515, ...), custom_call_target="tpu_custom_call" | custom-call | tf_op jit(solution)/shard_map/scan_backward/pallas_call | solution.py:226
  1104.1 17.7 fusion.42
  1190.3 91.4 %collective-permute-done.46 = f32[512,2048]{1,0:T(8,128)S(1)} collective-permute-done((f32[512,2048]{1,0:T(8,128)S(1)}, f32[512,2048]{1,0:T(8,128)S(1)}, u32[]{:S(2)}, u32[]{:S(2)}) %collective-permute-start.46) | collective-permute-done | bytes 4194336 | tf_op jit(solution)/shard_map/ppermute | solution.py:265
  1345.2 15.9 collective-permute-done.49
  1361.2 16.7 fusion.43
  1389.6 74.1 %reduce-scatter.21.cloned.1.call-done = f32[256,1024]{1,0:T(8,128)} async-done(((f32[2048,1024]{1,0:T(8,128)}), f32[256,1024]{1,0:T(8,128)}) %reduce-scatter.21.cloned.1.call-update) | async-done | bytes 1048592 | tf_op jit(solution)/shard_map/reduce_scatter | solution.py:278
  1467.3 148.1 %reduce-scatter.11.cloned.1.call-done = f32[256,1024]{1,0:T(8,128)} async-done(((f32[2048,1024]{1,0:T(8,128)}), f32[256,1024]{1,0:T(8,128)}) %reduce-scatter.11.cloned.1.call-update) | async-done | bytes 1048592 | tf_op jit(solution)/shard_map/reduce_scatter | solution.py:278
  1615.4 152.1 %reduce-scatter.9.cloned.1.call-done = f32[256,1024]{1,0:T(8,128)} async-done(((f32[2048,1024]{1,0:T(8,128)}), f32[256,1024]{1,0:T(8,128)}) %reduce-scatter.9.cloned.1.call-update) | async-done | bytes 1048592 | tf_op jit(solution)/shard_map/reduce_scatter | solution.py:278
  (636 shorter events, 641.7 us)
Async XLA Ops:
  7.2 1280.0 %reduce-scatter.19.cloned.1.call-start = ((), (), s32[]{:S(2)}) async-start(), calls=%async_computation.13 | async-start | bytes 1474560 | tf_op jit(solution)/shard_map/reduce_scatter | solution.py:278
  193.6 92.7 %collective-permute-start.10 = (f32[512,2048]{1,0:T(8,128)S(1)}, f32[512,2048]{1,0:T(8,128)S(1)}, u32[]{:S(2)}, u32[]{:S(2)}) collective-permute-start(f32[512,2048]{1,0:T(8,128)S(1)} %dynamic-slice_add_fusion.3), channel_id=1, source_target_pairs={{0,2},{2,0},{1,3},{3,1},{4,6},{6,4},{5,7},{7,5},{8,10},{10,8},{9,1... | collective-permute-start | bytes 12582920 | tf_op jit(solution)/shard_map/ppermute | solution.py:265
  378.0 21.6 %collective-permute-start.16 = (f32[9,8,1024]{2,1,0:T(8,128)S(1)}, f32[9,8,1024]{2,1,0:T(8,128)S(1)}, u32[]{:S(2)}, u32[]{:S(2)}) collective-permute-start(f32[9,8,1024]{2,1,0:T(8,128)S(1)} %pad_maximum_fusion.20), channel_id=1, source_target_pairs={{0,4},{4,0},{8,12},{12,8},{16,20},{20,16},{24,28},{28,24},{1,5},{5... | collective-permute-start | bytes 884744 | tf_op jit(solution)/shard_map/ppermute | solution.py:312
  399.7 11.3 collective-permute-start.17
  486.8 21.6 %collective-permute-start.25 = (f32[9,8,1024]{2,1,0:T(8,128)S(1)}, f32[9,8,1024]{2,1,0:T(8,128)S(1)}, u32[]{:S(2)}, u32[]{:S(2)}) collective-permute-start(f32[9,8,1024]{2,1,0:T(8,128)S(1)} %pad_maximum_fusion.23), channel_id=1, source_target_pairs={{24,16},{28,20},{16,8},{20,12},{8,0},{12,4},{25,17},{29,21},{17,9}... | collective-permute-start | bytes 884744 | tf_op jit(solution)/shard_map/ppermute | solution.py:323
  509.7 12.5 collective-permute-start.27
  614.5 704.5 %reduce-scatter.15.cloned.1.call-start = ((), (), s32[]{:S(2)}) async-start(), calls=%async_computation.11 | async-start | bytes 9437184 | tf_op jit(solution)/shard_map/reduce_scatter | solution.py:278
  632.7 686.3 %reduce-scatter.13.cloned.1.call-start = ((), (), s32[]{:S(2)}) async-start(), calls=%async_computation.10 | async-start | bytes 9437184 | tf_op jit(solution)/shard_map/reduce_scatter | solution.py:278
  665.0 23.7 %collective-permute-start.21 = (f32[512,2048]{1,0:T(8,128)}, f32[512,2048]{1,0:T(8,128)}, u32[]{:S(2)}, u32[]{:S(2)}) collective-permute-start(f32[512,2048]{1,0:T(8,128)} %constant_dynamic-slice_fusion.6), channel_id=1, source_target_pairs={{0,1},{1,0},{2,3},{3,2},{4,5},{5,4},{6,7},{7,6},{8,9},{9,8},{10,11... | collective-permute-start | bytes 12582920 | tf_op jit(solution)/shard_map/ppermute | solution.py:264
  691.8 93.4 %collective-permute-start.22 = (f32[512,2048]{1,0:T(8,128)S(1)}, f32[512,2048]{1,0:T(8,128)S(1)}, u32[]{:S(2)}, u32[]{:S(2)}) collective-permute-start(f32[512,2048]{1,0:T(8,128)S(1)} %dynamic-slice_add_fusion.2), channel_id=1, source_target_pairs={{0,2},{2,0},{1,3},{3,1},{4,6},{6,4},{5,7},{7,5},{8,10},{10,8},{9,1... | collective-permute-start | bytes 12582920 | tf_op jit(solution)/shard_map/ppermute | solution.py:265
  698.8 176.1 %collective-permute-start.34 = (f32[512,2048]{1,0:T(8,128)}, f32[512,2048]{1,0:T(8,128)}, u32[]{:S(2)}, u32[]{:S(2)}) collective-permute-start(f32[512,2048]{1,0:T(8,128)} %dynamic-slice_add_fusion.1), channel_id=1, source_target_pairs={{0,2},{2,0},{1,3},{3,1},{4,6},{6,4},{5,7},{7,5},{8,10},{10,8},{9,1... | collective-permute-start | bytes 12582920 | tf_op jit(solution)/shard_map/ppermute | solution.py:265
  787.9 91.4 %collective-permute-start.23 = (f32[512,2048]{1,0:T(8,128)}, f32[512,2048]{1,0:T(8,128)}, u32[]{:S(2)}, u32[]{:S(2)}) collective-permute-start(f32[512,2048]{1,0:T(8,128)} %add.489), channel_id=1, source_target_pairs={{0,1},{1,0},{2,3},{3,2},{4,5},{5,4},{6,7},{7,6},{8,9},{9,8},{10,11... | collective-permute-start | bytes 12582920 | tf_op jit(solution)/shard_map/ppermute | solution.py:266
  794.9 527.2 %reduce-scatter.17.cloned.1.call-start = ((), (), s32[]{:S(2)}) async-start(), calls=%async_computation.12 | async-start | bytes 1474560 | tf_op jit(solution)/shard_map/reduce_scatter | solution.py:278
  942.8 16.3 collective-permute-start.36
  959.2 23.6 %collective-permute-start.37 = (f32[9,8,1024]{2,1,0:T(8,128)S(1)}, f32[9,8,1024]{2,1,0:T(8,128)S(1)}, u32[]{:S(2)}, u32[]{:S(2)}) collective-permute-start(f32[9,8,1024]{2,1,0:T(8,128)S(1)} %pad_maximum_fusion.24), channel_id=1, source_target_pairs={{24,16},{28,20},{16,8},{20,12},{8,0},{12,4},{25,17},{29,21},{17,9}... | collective-permute-start | bytes 884744 | tf_op jit(solution)/shard_map/ppermute | solution.py:323
  984.1 15.9 collective-permute-start.39
  1091.8 297.8 %reduce-scatter.23.cloned.1.call-start = ((), (), s32[]{:S(2)}) async-start(), calls=%async_computation.15 | async-start | bytes 9437184 | tf_op jit(solution)/shard_map/reduce_scatter | solution.py:278
  1103.4 360.3 %reduce-scatter.21.cloned.1.call-start = ((), (), s32[]{:S(2)}) async-start(), calls=%async_computation.14 | async-start | bytes 9437184 | tf_op jit(solution)/shard_map/reduce_scatter | solution.py:278
  1121.8 493.6 %reduce-scatter.11.cloned.1.call-start = ((), (), s32[]{:S(2)}) async-start(), calls=%async_computation.9 | async-start | bytes 9437184 | tf_op jit(solution)/shard_map/reduce_scatter | solution.py:278
  1135.0 632.5 %reduce-scatter.9.cloned.1.call-start = ((), (), s32[]{:S(2)}) async-start(), calls=%async_computation.8 | async-start | bytes 9437184 | tf_op jit(solution)/shard_map/reduce_scatter | solution.py:278
  1188.7 93.0 %collective-permute-start.46 = (f32[512,2048]{1,0:T(8,128)S(1)}, f32[512,2048]{1,0:T(8,128)S(1)}, u32[]{:S(2)}, u32[]{:S(2)}) collective-permute-start(f32[512,2048]{1,0:T(8,128)S(1)} %dynamic-slice_add_fusion), channel_id=1, source_target_pairs={{0,2},{2,0},{1,3},{3,1},{4,6},{6,4},{5,7},{7,5},{8,10},{10,8},{9,1... | collective-permute-start | bytes 12582920 | tf_op jit(solution)/shard_map/ppermute | solution.py:265
  1284.5 40.3 %collective-permute-start.47 = (f32[512,2048]{1,0:T(8,128)}, f32[512,2048]{1,0:T(8,128)}, u32[]{:S(2)}, u32[]{:S(2)}) collective-permute-start(f32[512,2048]{1,0:T(8,128)} %add.531), channel_id=1, source_target_pairs={{0,1},{1,0},{2,3},{3,2},{4,5},{5,4},{6,7},{7,6},{8,9},{9,8},{10,11... | collective-permute-start | bytes 12582920 | tf_op jit(solution)/shard_map/ppermute | solution.py:266
  1345.1 16.1 collective-permute-start.49
  1361.1 23.4 %collective-permute-start.50 = (f32[26,1024]{1,0:T(8,128)S(1)}, f32[26,1024]{1,0:T(8,128)S(1)}, u32[]{:S(2)}, u32[]{:S(2)}) collective-permute-start(f32[26,1024]{1,0:T(8,128)S(1)} %add.534), channel_id=1, source_target_pairs={{0,16},{4,20},{8,24},{12,28},{16,0},{20,4},{24,8},{28,12},{1,17},{... | collective-permute-start | bytes 319496 | tf_op jit(solution)/shard_map/ppermute | solution.py:273
  (177 other events, 3813.1 us)
Sparse Core Ops, SparseCore 0:
  614.6 62.8 reduce-scatter.18
  681.2 147.9 reduce-scatter.14
  833.2 154.1 reduce-scatter.12
  1091.9 62.6 reduce-scatter.16
  1158.1 148.0 reduce-scatter.22
  1310.1 153.5 reduce-scatter.20
  1467.4 147.9 reduce-scatter.10
  1619.5 147.9 reduce-scatter.8

commit v2 on v1

--- a/solution.py
+++ b/solution.py
@@ -255,15 +255,55 @@
     return jnp.concatenate([first, second], axis=0)
 
 
+BESIDE = [(0, 1), (1, 0), (2, 3), (3, 2)]
+ACROSS = [(0, 2), (2, 0), (1, 3), (3, 1)]
+
+
+def paired():
+    return lax.axis_size("tensor") == 4
+
+
 def tensor_sum(array):
-    if lax.axis_size("tensor") != 4:
+    if not paired():
         return lax.psum(array, "tensor")
     core = lax.axis_index("tensor") % 2
-    beside = [(0, 1), (1, 0), (2, 3), (3, 2)]
-    across = [(0, 2), (2, 0), (1, 3), (3, 1)]
-    half = half_of(array, core) + lax.ppermute(half_of(array, 1 - core), "tensor", beside)
-    half = half + lax.ppermute(half, "tensor", across)
-    return ordered(core, half, lax.ppermute(half, "tensor", beside))
+    half = half_of(array, core) + lax.ppermute(half_of(array, 1 - core), "tensor", BESIDE)
+    half = half + lax.ppermute(half, "tensor", ACROSS)
+    return ordered(core, half, lax.ppermute(half, "tensor", BESIDE))
+
+
+def own_rows(array):
+    if not paired():
+        size = array.shape[0] // lax.axis_size("tensor")
+        return lax.dynamic_slice_in_dim(array, lax.axis_index("tensor") * size, size, 0)
+    return half_of(array, lax.axis_index("tensor") % 2)
+
+
+def own_sum(array, beside):
+    if not paired():
+        return lax.psum_scatter(array, "tensor", scatter_dimension=0, tiled=True), beside
+    core = lax.axis_index("tensor") % 2
+    half = half_of(array, core) + lax.ppermute(half_of(array, 1 - core), "tensor", BESIDE)
+    got = lax.ppermute(half, "tensor", ACROSS)
+    got, beside = lax.optimization_barrier((got, beside))
+    return half + got, beside
+
+
+def all_rows(array):
+    if not paired():
+        return lax.optimization_barrier(lax.all_gather(array, "tensor", tiled=True))
+    other = lax.optimization_barrier(lax.ppermute(array, "tensor", BESIDE))
+    return ordered(lax.axis_index("tensor") % 2, array, other)
+
+
+def rows_sum(array):
+    if not paired():
+        return lax.psum(array, "tensor")
+    return array + lax.ppermute(array, "tensor", BESIDE)
+
+
+def chosen(array, axis, index):
+    return lax.dynamic_index_in_dim(array, index, axis, keepdims=False)
 
 
 def blk_sum(array):
@@ -276,6 +316,25 @@
 
 def blk_scatter(array):
     return lax.psum_scatter(array, "blk", scatter_dimension=0, tiled=True)
+
+
+def halved(array, bits):
+    axes = [4, 2, 1]
+    for bit in bits:
+        axis = axes.index(bit)
+        axes.remove(bit)
+        mine = (lax.axis_index("blk") // bit) % 2
+        give = chosen(array, axis, 1 - mine)
+        array = chosen(array, axis, mine) + lax.ppermute(give, "blk", [(j, j ^ bit) for j in range(8)])
+    return array
+
+
+def split_scatter(array):
+    if lax.axis_size("blk") != 8:
+        return blk_scatter(array)
+    array = array.reshape((2, 2, 2, array.shape[0] // 8, array.shape[1]))
+    middle = array.shape[-1] // 2
+    return jnp.concatenate([halved(array[..., :middle], (1, 2, 4)), halved(array[..., middle:], (2, 4, 1))], axis=-1)
 
 
 def neighbour(value, steps):
@@ -380,10 +439,11 @@
         self.out = out_weight[index]
 
 
-def forward_layer(layer, residual, scan_first, conv_first, parts, at_first):
-    width = residual.shape[1]
-    q = lax.rsqrt(jnp.mean(residual * residual, axis=-1, keepdims=True) + EPSILON)
-    normed = (residual * q * layer.gain).astype(jnp.bfloat16)
+def inverse_rms(residual):
+    return lax.rsqrt(jnp.mean(residual * residual, axis=-1, keepdims=True) + EPSILON)
+
+
+def front(layer, normed, conv_first, parts, at_first):
     mixed = dot32(normed, layer.into)
     inner = mixed.shape[-1] // 2
     values, gate = mixed[:, :inner], mixed[:, inner:]
@@ -401,53 +461,75 @@
     before = dot32(dt_low, layer.dt) + layer.dt_bias
     step = jax.nn.softplus(before)
     push = step * inputs.astype(jnp.float32)
-    rate = layer.rate2[:, None]
     local = split_parts(end_states(by_step(step), by_step(push), coef, layer.rate2), parts)
     totals = split_parts(jnp.sum(by_step(step), axis=0), parts)
-    joined, total = local[:, 0], totals[0]
-    for p in range(1, parts):
+    return (window, gate, conv_out, inputs, dt_low, coef, before, step, push, totals), local, tails[:, -1]
+
+
+def join(local, totals, rate, reverse):
+    order = range(local.shape[1])
+    order = list(reversed(order)) if reverse else list(order)
+    joined, total = local[:, order[0]], totals[order[0]]
+    for p in order[1:]:
         joined = local[:, p] + jnp.exp2(totals[p][None] * rate) * joined
         total = total + totals[p]
-    start = entering(total, joined, rate, scan_first, False)
-    starts = [start]
-    for p in range(1, parts):
-        starts.append(local[:, p - 1] + jnp.exp2(totals[p - 1][None] * rate) * starts[-1])
-    start = jnp.stack(starts, axis=1).reshape(STATE, 8, inner)
+    return total, joined
+
+
+def each_part(state, local, totals, rate, reverse):
+    order = range(local.shape[1])
+    order = list(reversed(order)) if reverse else list(order)
+    states = {order[0]: state}
+    for p, following in zip(order[:-1], order[1:]):
+        states[following] = local[:, p] + jnp.exp2(totals[p][None] * rate) * states[p]
+    state = jnp.stack([states[p] for p in range(local.shape[1])], axis=1)
+    return state.reshape(STATE, 8, state.shape[-1])
+
+
+def exchange(layer, local, totals, first, reverse):
+    rate = layer.rate2[:, None]
+    total, joined = join(local, totals, rate, reverse)
+    state = entering(total, joined, rate, first, reverse)
+    return each_part(state, local, totals, rate, reverse)
+
+
+def scanning(layer, kept, start):
+    window, gate, conv_out, inputs, dt_low, coef, before, step, push, totals = kept
     scanned, states, enter, final = scan_forward(by_step(step), by_step(push), coef, layer.rate2, start)
     result = rows(scanned) + layer.skip * inputs.astype(jnp.float32)
     gated = (result * jax.nn.silu(gate)).astype(jnp.bfloat16)
-    branch = tensor_sum(dot32(gated, layer.out))
-    following = residual + branch
-    squares = jnp.stack([jnp.sum(branch * branch), jnp.sum(following * following)])
-    kept = (residual, q, normed, window, gate, conv_out, inputs, dt_low, coef, before, step, push, totals,
-            result, gated, states, enter)
-    return following, squares, split_parts(final, parts)[:, -1], tails[:, -1], kept
-
-
-def backward_layer(layer, grad, kept, parts):
-    (residual, q, normed, window, gate, conv_out, inputs, dt_low, coef, before, step, push, totals,
-     result, gated, states, enter) = kept
+    return dot32(gated, layer.out), (result, gated, states, enter), final
+
+
+def back_front(layer, kept, grad_low):
+    window, gate, conv_out, inputs, dt_low, coef, before, step, push, totals = kept
+    grad_gated = dot_n(grad_low, layer.out)
+    grad_result = grad_gated * jax.nn.silu(gate)
+    local = start_grads(by_step(step), by_step(grad_result), coef, layer.rate2)
+    return (grad_gated, grad_result), split_parts(local, totals.shape[0])
+
+
+def back_side(layer, kept, normed, scans, grads, grad_low):
+    window, gate, conv_out, inputs, dt_low, coef, before, step, push, totals = kept
+    result, gated, states, enter = scans
+    grad_gated, grad_result = grads
+    inner = gate.shape[1]
+    out_grad = dot_t(grad_low, gated)
+    grad_gate = (grad_gated * result * silu_slope(gate)).astype(jnp.bfloat16)
+    gate_grad = dot_t(normed, grad_gate)
+    gate_through = dot_n(grad_gate, layer.into[:, inner:])
+    skip_grad = jnp.sum(grad_result * inputs.astype(jnp.float32), axis=0)
+    return out_grad, gate_grad, gate_through, skip_grad
+
+
+def back_scan(layer, kept, normed, scans, grads, end, gate_through):
+    window, gate, conv_out, inputs, dt_low, coef, before, step, push, totals = kept
+    result, gated, states, enter = scans
+    grad_gated, grad_result = grads
     count, inner = gate.shape
+    parts = totals.shape[0]
     rim = layer.taps.shape[0] - 1
     wide = inputs.astype(jnp.float32)
-    grad_low = grad.astype(jnp.bfloat16)
-    grad_gated = dot_n(grad_low, layer.out)
-    out_grad = dot_t(grad_low, gated)
-    grad_result = grad_gated * jax.nn.silu(gate)
-    grad_gate = (grad_gated * result * silu_slope(gate)).astype(jnp.bfloat16)
-    skip_grad = jnp.sum(grad_result * wide, axis=0)
-    gate_grad = dot_t(normed, grad_gate)
-    rate = layer.rate2[:, None]
-    local = split_parts(start_grads(by_step(step), by_step(grad_result), coef, layer.rate2), parts)
-    joined, total = local[:, -1], totals[-1]
-    for p in reversed(range(parts - 1)):
-        joined = local[:, p] + jnp.exp2(totals[p][None] * rate) * joined
-        total = total + totals[p]
-    end = entering(total, joined, rate, jnp.zeros_like(joined), True)
-    ends = [end]
-    for p in reversed(range(1, parts)):
-        ends.insert(0, local[:, p] + jnp.exp2(totals[p][None] * rate) * ends[0])
-    end = jnp.stack(ends, axis=1).reshape(STATE, 8, inner)
     decays, pushes, coef_grad, start_grad, speed = scan_backward(
         by_step(step), by_step(push), by_step(grad_result), coef, layer.rate2, states, enter, end)
     pushes = rows(pushes)
@@ -456,8 +538,8 @@
     bias_grad = jnp.sum(before_grad, axis=0)
     decay_grad = layer.rate * jnp.sum(speed, axis=1)
     before_low = before_grad.astype(jnp.bfloat16)
+    projected_grad = tensor_sum(jnp.concatenate([dot_n(before_low, layer.dt), rows(coef_grad)], axis=-1))
     dt_grad = dot_t(dt_low, before_low)
-    projected_grad = tensor_sum(jnp.concatenate([dot_n(before_low, layer.dt), rows(coef_grad)], axis=-1))
     high, low = two_parts(projected_grad)
     x_grad = dot_t(high, inputs) + dot_t(low, inputs)
     through = dot_n(jnp.concatenate([high, low], axis=-1), jnp.concatenate([layer.x, layer.x], axis=-1))
@@ -475,19 +557,16 @@
     values_grad = jnp.concatenate([window_grad[8 * rim:count], window_grad[count:] + tail_grad], axis=0)
     values_grad = values_grad.astype(jnp.bfloat16)
     into_grad = dot_t(normed, values_grad)
-    mixed_grad = jnp.concatenate([values_grad, grad_gate], axis=-1)
-    normed_grad = tensor_sum(dot_n(mixed_grad, layer.into))
+    normed_part = dot_n(values_grad, layer.into[:, :inner]) + gate_through
+    grads = (into_grad, taps_grad, shift_grad, x_grad, dt_grad, bias_grad, decay_grad)
+    return normed_part, grads, split_parts(start_grad, parts)[:, 0], prefix_grad[:, 0]
+
+
+def norm_back(layer, normed_grad, residual, q):
     gain_grad = jnp.sum(normed_grad * (residual * q), axis=0)
     scaled = normed_grad * layer.gain
     inner_mean = jnp.mean(scaled * residual, axis=-1, keepdims=True)
-    passed = grad + q * scaled - residual * (q * q * q * inner_mean)
-    grads = (gain_grad, into_grad, gate_grad, taps_grad, shift_grad, x_grad, dt_grad, bias_grad, decay_grad,
-             skip_grad, out_grad)
-    start_first = split_parts(start_grad, parts)[:, 0]
-    return passed, grads, start_first, prefix_grad[:, 0]
-
-
-MICRO = 1
+    return gain_grad, q * scaled - residual * (q * q * q * inner_mean)
 
 
 def on_device(tokens, cotangent, *args):
@@ -496,11 +575,12 @@
     blocks, index = lax.axis_size("blk"), lax.axis_index("blk")
     at_first = index == 0
     layer_total = weights[1].shape[0]
-    seqs = tokens.shape[0] // MICRO
+    seqs = tokens.shape[0]
     parts = 8 // seqs
     length = tokens.shape[1] // parts
     width = tokens.shape[2]
     layers = [Layer(l, weights) for l in range(layer_total)]
+    last = layer_total - 1
 
     def arrange(array):
         return array.reshape(seqs, parts, length, width).transpose(2, 1, 0, 3).reshape(length * 8, width)
@@ -509,79 +589,107 @@
         array = array.reshape(length, parts, seqs, width).transpose(2, 1, 0, 3)
         return array.reshape(seqs, parts * length, width)
 
-    outs, ins = [], []
-    finals, tails, starts, prefixes = ([[None] * MICRO for _ in range(layer_total)] for _ in range(4))
-    sums = [None] * layer_total
-    squares = [0.0] * layer_total
-    input_square = 0.0
-    for m in range(MICRO):
-        part = slice(m * seqs, (m + 1) * seqs)
-        residual = arrange(tokens[part]).astype(jnp.float32)
-        input_square = input_square + jnp.sum(residual * residual)
-        kept = []
-        for l in range(layer_total):
-            residual, square, finals[l][m], tails[l][m], saved = forward_layer(
-                layers[l], residual, jnp.moveaxis(scan_init[l, part], 1, 0),
-                jnp.moveaxis(conv_init[l, part], 1, 0), parts, at_first)
-            squares[l] = squares[l] + square
-            kept.append(saved)
-        outs.append(restore(residual.astype(jnp.bfloat16)))
-        grad = arrange(cotangent[part]).astype(jnp.float32)
-        for l in reversed(range(layer_total)):
-            grad, grads, starts[l][m], prefixes[l][m] = backward_layer(layers[l], grad, kept[l], parts)
-            sums[l] = grads if sums[l] is None else jax.tree.map(jnp.add, sums[l], grads)
-        ins.append(restore(grad.astype(jnp.bfloat16)))
-
-    big, small = [], []
+    residual = arrange(tokens).astype(jnp.float32)
+    normed = (residual * inverse_rms(residual) * layers[0].gain).astype(jnp.bfloat16)
+    residual = own_rows(residual)
+    input_square = jnp.sum(residual * residual)
+    grad = arrange(cotangent).astype(jnp.float32)
+    grad_low = grad.astype(jnp.bfloat16)
+
+    kept, scans, norms, finals, tails, squares = ([None] * layer_total for _ in range(6))
+    starts, prefixes, sums = ([None] * layer_total for _ in range(3))
+    for l, layer in enumerate(layers):
+        norms[l] = (normed, residual)
+        kept[l], local, tails[l] = front(
+            layer, normed, jnp.moveaxis(conv_init[l], 1, 0), parts, at_first)
+        totals = kept[l][-1]
+        if l == last:
+            grads, back_local = back_front(layer, kept[l], grad_low)
+            local, back_local = lax.optimization_barrier((local, back_local))
+            end = exchange(layer, back_local, totals, jnp.zeros_like(back_local[:, 0]), True)
+        start = exchange(layer, local, totals, jnp.moveaxis(scan_init[l], 1, 0), False)
+        partial_sum, scans[l], final = scanning(layer, kept[l], start)
+        finals[l] = split_parts(final, parts)[:, -1]
+        if l < last:
+            branch, layers[l + 1].into = own_sum(partial_sum, layers[l + 1].into)
+        else:
+            branch, _ = own_sum(partial_sum, ())
+        following = residual + branch
+        squares[l] = jnp.stack([jnp.sum(branch * branch), jnp.sum(following * following)])
+        residual = following
+        if l < last:
+            unscaled = all_rows(residual * inverse_rms(residual))
+            normed = (unscaled * layers[l + 1].gain).astype(jnp.bfloat16)
+    out = restore((2.0 * all_rows(0.5 * residual)).astype(jnp.bfloat16))
+
     for l in reversed(range(layer_total)):
-        (gain_grad, into_grad, gate_grad, taps_grad, shift_grad, x_grad, dt_grad, bias_grad, decay_grad,
-         skip_grad, out_grad) = sums[l]
-        into_part, gate_part, out_part = blk_scatter(into_grad), blk_scatter(gate_grad), blk_scatter(out_grad)
+        layer = layers[l]
+        normed, residual = norms[l]
+        if l < last:
+            grads, back_local = back_front(layer, kept[l], grad_low)
+            end = exchange(layer, back_local, kept[l][-1], jnp.zeros_like(back_local[:, 0]), True)
+        side = back_side(layer, kept[l], normed, scans[l], grads, grad_low)
+        end, side = lax.optimization_barrier((end, side))
+        out_grad, gate_grad, gate_through, skip_grad = side
+        normed_part, layer_grads, starts[l], prefixes[l] = back_scan(
+            layer, kept[l], normed, scans[l], grads, end, gate_through)
+        if l == last:
+            normed_part, out = lax.optimization_barrier((normed_part, out))
+        normed_grad, _ = own_sum(normed_part, ())
+        gain_grad, change = norm_back(layer, normed_grad, residual, inverse_rms(residual))
+        grad = grad + all_rows(change)
+        grad_low = grad.astype(jnp.bfloat16)
+        sums[l] = (gain_grad, gate_grad, skip_grad, out_grad) + layer_grads
+    input_grad = restore(grad_low)
+
+    big, small, shared = [], [], []
+    for l in reversed(range(layer_total)):
+        (gain_grad, gate_grad, skip_grad, out_grad, into_grad, taps_grad, shift_grad, x_grad, dt_grad, bias_grad,
+         decay_grad) = sums[l]
+        scatter = blk_scatter if l else split_scatter
+        into_part, gate_part, out_part = scatter(into_grad), scatter(gate_grad), blk_scatter(out_grad)
         thin = jnp.concatenate([x_grad.reshape(blocks, -1, x_grad.shape[-1]),
                                 dt_grad.reshape(blocks, -1, dt_grad.shape[-1])], axis=1)
-        thin = blk_scatter(thin)[0]
+        thin = split_scatter(thin.reshape(-1, thin.shape[-1]))
         cut = x_grad.shape[0] // blocks
         big.insert(0, (jnp.stack([into_part, gate_part], axis=1), out_part.T, thin[:cut].T, thin[cut:]))
-        inner = taps_grad.shape[-1]
-        packed = jnp.concatenate([gain_grad.reshape(-1, inner), taps_grad, shift_grad[None], bias_grad[None],
-                                  skip_grad[None], decay_grad], axis=0)
-        if l == 0:
-            extra = jnp.concatenate([jnp.stack(squares).reshape(-1), input_square.reshape(1)])
-            extra = jnp.pad(extra, (0, inner - extra.shape[0]))[None]
-            packed = jnp.concatenate([packed, extra], axis=0)
-        small.insert(0, blk_sum(packed))
-    rows_gain = width // weights[2].shape[-1]
+        small.insert(0, jnp.concatenate(
+            [taps_grad, shift_grad[None], bias_grad[None], skip_grad[None], decay_grad], axis=0))
+        shared.insert(0, gain_grad)
+    inner = small[0].shape[-1]
+    extra = jnp.concatenate([jnp.stack(squares).reshape(-1), input_square.reshape(1)])
+    extra = jnp.pad(extra, (0, inner - extra.shape[0]))[None]
+    shared = rows_sum(jnp.concatenate([jnp.stack(shared).reshape(-1, inner), extra], axis=0))
+    gain_rows = shared.shape[0] - 1
+    sizes = [part.shape[0] for part in small]
+    packed = blk_sum(jnp.concatenate(small + [shared], axis=0))
+    rest = packed[sum(sizes):]
+    small = packed[:sum(sizes)].reshape(layer_total, sizes[0], inner)
     taps = weights[2].shape[1]
-
-    def unpack(first, count):
-        return jnp.stack([part[first:first + count] for part in small])
-
     row_total = tokens.shape[0] * tokens.shape[1] * width * blocks
-    last = jnp.sqrt(small[0][-1] / row_total)
-    rms_stats = last[:2 * layer_total].reshape(layer_total, 2)
-    input_rms = last[2 * layer_total:2 * layer_total + 1]
-    gain_grad = unpack(0, rows_gain).reshape(layer_total, width)
-    at = rows_gain + taps
-
-    def stacked(lists):
-        return jnp.stack([jnp.moveaxis(jnp.concatenate(parts_, axis=1), 0, 1) for parts_ in lists])[:, :, None]
+    squares = rest[-1] / row_total
+    rms_stats = jnp.sqrt(squares[:2 * layer_total]).reshape(layer_total, 2)
+    input_rms = jnp.sqrt(squares[2 * layer_total:2 * layer_total + 1])
+
+    def stacked(parts_):
+        return jnp.stack([jnp.moveaxis(part, 0, 1) for part in parts_])[:, :, None]
 
     return (
-        jnp.concatenate(outs, axis=0),
+        out,
         stacked(finals),
         stacked(tails),
-        jnp.concatenate(ins, axis=0),
+        input_grad,
         stacked(starts),
         stacked(prefixes),
-        gain_grad,
+        rest[:gain_rows].reshape(layer_total, width),
         jnp.stack([part[0] for part in big]),
-        unpack(rows_gain, taps),
-        unpack(at, 1)[:, 0],
+        small[:, :taps],
+        small[:, taps],
         jnp.stack([part[2] for part in big]),
         jnp.stack([part[3] for part in big]),
-        unpack(at + 1, 1)[:, 0],
-        unpack(at + 3, STATE),
-        unpack(at + 2, 1)[:, 0],
+        small[:, taps + 1],
+        small[:, taps + 3:],
+        small[:, taps + 2],
         jnp.stack([part[1] for part in big]),
         rms_stats,
         input_rms,

time: 1790 us -> 1610 us (0.90)
  waiting for transfers between devices: 939 us -> 698 us
  starting transfers between devices: 76.9 us -> 106 us
  local copies, waits for them, and re-layouts: 115 us -> 139 us
    reduce_scatter x8 -> x4, waiting for transfers between devices: 374 us -> 0.01 us  [blk_scatter(): return lax.psum_scatter(array, 'blk', scatter_dimension=0, tiled=True)]
    ppermute x24 -> x49, waiting for transfers between devices: 398 us -> 613 us  [the longest x24 299 us: halved(): lax.ppermute(give, 'blk', [(j, j ^ bit) for j in range(8)])]
    ppermute x12, waiting for transfers between devices: 79.8 us -> 35.6 us  [along(): lax.ppermute(value, 'blk', [(2 * s + k, 2 * d + k) for s, d in pairs for...]
    ppermute x24 -> x49, starting transfers between devices: 14 us -> 46.2 us  [the longest x24 33.5 us: halved(): lax.ppermute(give, 'blk', [(j, j ^ bit) for j in range(8)])]
    dot_general x8 -> x10, matrix products: 76.9 us -> 100 us  [dot_n(): lax.dot_general(left, right, (((1,), (1,)), ((), ())), preferred_element_...]
    add x10 -> x35, other arithmetic: 17.9 us -> 36.1 us  [the longest x24 20.5 us: halved(): chosen(array, axis, mine)]
    unnamed x293 -> x332, local copies, waits for them, and re-layouts: 65.1 us -> 60.3 us
  transfers between devices with their start and end apart: 62 -> 80, of which waited for: 42 -> 42; matrix products, arithmetic and copies ran while one was open for 19% -> 24% of each run, Pallas kernels for 4% -> 10%
where the time goes in v2:
time: 1610 us; the launch traced here: 1590 us
  waiting for transfers between devices  698 us (43%)
  Pallas kernels  247 us (15%)
  matrix products  205 us (13%)
  other arithmetic  177 us (11%)
  local copies, waits for them, and re-layouts  139 us (9%)
  starting transfers between devices  106 us (7%)
  between operations  19.1 us (1%)
    ppermute x24, waiting for transfers between devices, halved(): lax.ppermute(give, 'blk', [(j, j ^ bit) for j in range(8)])  299 us
    ppermute x4, waiting for transfers between devices, own_sum(): got = lax.ppermute(half, 'tensor', ACROSS)  168 us
    ppermute x4, waiting for transfers between devices, tensor_sum(): half = half + lax.ppermute(half, 'tensor', ACROSS)  120 us
    pallas_call x2, Pallas kernels, scan_backward(): pl.pallas_call(partial(back_body, C // LANES, width), grid=(T // tb,), in...  115 us
    dot_general x10, matrix products, dot_n(): lax.dot_general(left, right, (((1,), (1,)), ((), ())), preferred_element_...  100 us
    pallas_call x2, Pallas kernels, scan_forward(): pl.pallas_call(partial(scan_body, C // LANES, width), grid=(T // tb,), in...  65.3 us
    unnamed x332, local copies, waits for them, and re-layouts  60.3 us
    dot_general x12, matrix products, dot_t(): lax.dot_general(left, right, (((0,), (0,)), ((), ())), preferred_element_...  55.2 us
  transfers between devices with their start and end apart: 80, of which 42 were waited for; matrix products, arithmetic and copies ran while one was open for 24% of the time, Pallas kernels for 10%

profile of v2, /device:TPU:0, one launch (start us, length us, event | category | flops | bytes accessed | tf_op | source)
XLA Modules:
  0.0 1590.7 jit_solution(2521499811981532962)
XLA Ops:
  7.2 14.2 fusion.211
  34.3 12.8 fusion.36
  99.0 16.5 %end_states.2 = f32[16,8,1024]{2,1,0:T(8,128)S(1)} custom-call(f32[128,8,1024]{2,1,0:T(8,128)S(1)} %copy-done, f32[128,8,1024]{2,1,0:T(8,128)S(1)} %copy-done.4, f32[128,8,32]{2,1,0:T(8,128)S(1)} %bitcast.565, f32[16,1024]{1,0:T(8,128)S(1)} %get-tuple-element.248.rate_ref), custom_call_target="tpu_custom_call" | custom-call | tf_op jit(solution)/shard_map/end_states/pallas_call | solution.py:55
  144.4 32.6 %scan_forward.2 = (f32[128,8,1024]{2,1,0:T(8,128)S(1)}, f32[128,16,8,1024]{3,2,1,0:T(8,128)}, f32[16,16,8,1024]{3,2,1,0:T(8,128)}, f32[16,8,1024]{2,1,0:T(8,128)S(1)}) custom-call(f32[128,8,1024]{2,1,0:T(8,128)} %get-tuple-element.207.step_ref, f32[128,8,1024]{2,1,0:T(8,128)} %get-tuple-element.206.push_ref, f32[128,8,32]{2,1,0:T(8,128)S(1)} %bitcast.566, ...), custom_call_target="tpu_custom_call" | custom-call | tf_op jit(solution)/shard_map/scan_forward/pallas_call | solution.py:105
  215.9 76.7 %collective-permute-done.10 = f32[512,2048]{1,0:T(8,128)} collective-permute-done((f32[512,2048]{1,0:T(8,128)}, f32[512,2048]{1,0:T(8,128)}, u32[]{:S(2)}, u32[]{:S(2)}) %collective-permute-start.10) | collective-permute-done | bytes 4194336 | tf_op jit(solution)/shard_map/ppermute | solution.py:287
  308.4 12.7 fusion.221
  363.8 16.5 %end_states.3 = f32[16,8,1024]{2,1,0:T(8,128)S(1)} custom-call(f32[128,8,1024]{2,1,0:T(8,128)S(1)} %get-tuple-element.208.step_ref, f32[128,8,1024]{2,1,0:T(8,128)S(1)} %get-tuple-element.209.push_ref, f32[128,8,32]{2,1,0:T(8,128)S(1)} %bitcast.569, f32[16,1024]{1,0:T(8,128)S(1)} %get-tuple-element.247.rate_ref), custom_call_target="tpu_custom_call" | custom-call | tf_op jit(solution)/shard_map/end_states/pallas_call | solution.py:55
  380.3 16.7 %start_grads.2 = f32[16,8,1024]{2,1,0:T(8,128)S(1)} custom-call(f32[128,8,1024]{2,1,0:T(8,128)S(1)} %get-tuple-element.208.step_ref, f32[128,8,1024]{2,1,0:T(8,128)S(1)} %bitcast.561, f32[128,8,32]{2,1,0:T(8,128)S(1)} %bitcast.570, f32[16,1024]{1,0:T(8,128)S(1)} %get-tuple-element.247.rate_ref), custom_call_target="tpu_custom_call" | custom-call | tf_op jit(solution)/shard_map/start_grads/pallas_call | solution.py:143
  399.5 14.8 collective-permute-start.21
  459.2 32.7 %scan_forward.3 = (f32[128,8,1024]{2,1,0:T(8,128)S(1)}, f32[128,16,8,1024]{3,2,1,0:T(8,128)}, f32[16,16,8,1024]{3,2,1,0:T(8,128)}, f32[16,8,1024]{2,1,0:T(8,128)S(1)}) custom-call(f32[128,8,1024]{2,1,0:T(8,128)} %copy-done.2, f32[128,8,1024]{2,1,0:T(8,128)} %copy-done.3, f32[128,8,32]{2,1,0:T(8,128)S(1)} %bitcast.571, ...), custom_call_target="tpu_custom_call" | custom-call | tf_op jit(solution)/shard_map/scan_forward/pallas_call | solution.py:105
  536.5 57.6 %scan_backward.2 = (f32[128,8,1024]{2,1,0:T(8,128)}, f32[128,8,1024]{2,1,0:T(8,128)}, f32[128,8,32]{2,1,0:T(8,128)S(1)}, f32[16,8,1024]{2,1,0:T(8,128)S(1)}, f32[16,8,1024]{2,1,0:T(8,128)S(1)}) custom-call(f32[128,8,1024]{2,1,0:T(8,128)} %copy-done.2, f32[128,8,1024]{2,1,0:T(8,128)} %copy-done.3, f32[128,8,1024]{2,1,0:T(8,128)} %bitcast.562, ...), custom_call_target="tpu_custom_call" | custom-call | tf_op jit(solution)/shard_map/scan_backward/pallas_call | solution.py:226
  610.6 96.1 %collective-permute-done.27 = f32[512,160]{0,1:T(8,128)S(1)} collective-permute-done((f32[512,160]{0,1:T(8,128)S(1)}, f32[512,160]{0,1:T(8,128)S(1)}, u32[]{:S(2)}, u32[]{:S(2)}) %collective-permute-start.27) | collective-permute-done | bytes 327712 | tf_op jit(solution)/shard_map/ppermute | solution.py:271
  708.7 16.8 %fusion.199 = (f32[1024]{0:T(1024)}, f32[1024]{0:T(1024)}, f32[1024]{0:T(1024)}, f32[1024]{0:T(1024)}, f32[1024]{0:T(1024)}, /*index=5*/f32[1024,1024]{1,0:T(8,128)}) fusion(f32[1024,2048]{1,0:T(8,128)} %copy-done.25, f32[1024,1024]{1,0:T(8,128)} %copy-done.35, f32[24,1024]{1,0:T(8,128)S(1)} %fusion.167, f32[1024,1024]{1,0:T(8,128)} %get-tuple-element.167, ...), kind=kOutput, calls=%fused_computation.499 | convolution fusion | flops 706210816 | bytes 30470144 | tf_op jit(solution)/shard_map/dot_general | solution.py:413
  779.5 91.1 %collective-permute-done.34 = f32[512,2048]{1,0:T(8,128)S(1)} collective-permute-done((f32[512,2048]{1,0:T(8,128)S(1)}, f32[512,2048]{1,0:T(8,128)S(1)}, u32[]{:S(2)}, u32[]{:S(2)}) %collective-permute-start.34) | collective-permute-done | bytes 4194336 | tf_op jit(solution)/shard_map/ppermute | solution.py:287
  953.6 18.2 %fusion.25 = (f32[1024]{0:T(1024)}, f32[1024,1024]{1,0:T(8,128)S(1)}, bf16[1024,1024]{1,0:T(8,128)(2,1)}) fusion(bf16[1024,1024]{1,0:T(8,128)(2,1)} %copy-done.19, f32[1024,2048]{1,0:T(8,128)} %copy-done.45, f32[1024]{0:T(1024)S(1)} %bitcast.651, f32[128,8,1024]{2,1,0:T(8,128)} %copy-done.13, bf16[2,1024,2048]{2,1,0:T(8,128)(2,1)} %param.25, ...), kind=kOutput, calls=%fused_computation.56 | convolution fusion | flops 4321180672 | bytes 33562624 | tf_op jit(solution)/shard_map/dot_general | solution.py:413
  971.9 16.8 %start_grads.3 = f32[16,8,1024]{2,1,0:T(8,128)S(1)} custom-call(f32[128,8,1024]{2,1,0:T(8,128)S(1)} %copy-done.1, f32[128,8,1024]{2,1,0:T(8,128)S(1)} %bitcast.563, f32[128,8,32]{2,1,0:T(8,128)S(1)} %bitcast.567, f32[16,1024]{1,0:T(8,128)S(1)} %copy-done.12), custom_call_target="tpu_custom_call" | custom-call | tf_op jit(solution)/shard_map/start_grads/pallas_call | solution.py:143
  1044.9 57.6 %scan_backward.3 = (f32[128,8,1024]{2,1,0:T(8,128)}, f32[128,8,1024]{2,1,0:T(8,128)}, f32[128,8,32]{2,1,0:T(8,128)S(1)}, f32[16,8,1024]{2,1,0:T(8,128)S(1)}, f32[16,8,1024]{2,1,0:T(8,128)S(1)}) custom-call(f32[128,8,1024]{2,1,0:T(8,128)} %get-tuple-element.207.step_ref, f32[128,8,1024]{2,1,0:T(8,128)} %get-tuple-element.206.push_ref, ...), custom_call_target="tpu_custom_call" | custom-call | tf_op jit(solution)/shard_map/scan_backward/pallas_call | solution.py:226
  1128.9 15.3 fusion.200
  1211.8 43.0 %collective-permute-done.64 = f32[2,2,36,512]{3,2,1,0:T(8,128)} collective-permute-done((f32[2,2,36,512]{3,2,1,0:T(8,128)}, f32[2,2,36,512]{3,2,1,0:T(8,128)}, u32[]{:S(2)}, u32[]{:S(2)}) %collective-permute-start.64) | collective-permute-done | bytes 294944 | tf_op jit(solution)/shard_map/ppermute | solution.py:328
  1257.2 30.4 %collective-permute-done.67 = f32[2,2,36,512]{3,2,1,0:T(8,128)} collective-permute-done((f32[2,2,36,512]{3,2,1,0:T(8,128)}, f32[2,2,36,512]{3,2,1,0:T(8,128)}, u32[]{:S(2)}, u32[]{:S(2)}) %collective-permute-start.67) | collective-permute-done | bytes 294944 | tf_op jit(solution)/shard_map/ppermute | solution.py:328
  1289.5 79.0 %collective-permute-done.65 = f32[2,36,512]{2,1,0:T(8,128)S(1)} collective-permute-done((f32[2,36,512]{2,1,0:T(8,128)S(1)}, f32[2,36,512]{2,1,0:T(8,128)S(1)}, u32[]{:S(2)}, u32[]{:S(2)}) %collective-permute-start.65) | collective-permute-done | bytes 147488 | tf_op jit(solution)/shard_map/ppermute | solution.py:328
  1389.4 41.7 %collective-permute-done.62 = f32[2,256,512]{2,1,0:T(8,128)S(1)} collective-permute-done((f32[2,256,512]{2,1,0:T(8,128)S(1)}, f32[2,256,512]{2,1,0:T(8,128)S(1)}, u32[]{:S(2)}, u32[]{:S(2)}) %collective-permute-start.62) | collective-permute-done | bytes 1048608 | tf_op jit(solution)/shard_map/ppermute | solution.py:328
  1450.7 30.3 %collective-permute-done.60 = f32[256,512]{1,0:T(8,128)} collective-permute-done((f32[256,512]{1,0:T(8,128)}, f32[256,512]{1,0:T(8,128)}, u32[]{:S(2)}, u32[]{:S(2)}) %collective-permute-start.60) | collective-permute-done | bytes 524320 | tf_op jit(solution)/shard_map/ppermute | solution.py:328
  1482.3 21.1 %collective-permute-done.56 = f32[2,256,512]{2,1,0:T(8,128)} collective-permute-done((f32[2,256,512]{2,1,0:T(8,128)}, f32[2,256,512]{2,1,0:T(8,128)}, u32[]{:S(2)}, u32[]{:S(2)}) %collective-permute-start.56) | collective-permute-done | bytes 1048608 | tf_op jit(solution)/shard_map/ppermute | solution.py:328
  (753 shorter events, 710.4 us)
Async XLA Ops:
  7.2 1118.2 %reduce-scatter.7.cloned.1.call-start = ((), (), s32[]{:S(2)}) async-start(), calls=%async_computation.5 | async-start | bytes 9437184 | tf_op jit(solution)/shard_map/reduce_scatter | solution.py:318
  199.7 92.9 %collective-permute-start.10 = (f32[512,2048]{1,0:T(8,128)}, f32[512,2048]{1,0:T(8,128)}, u32[]{:S(2)}, u32[]{:S(2)}) collective-permute-start(f32[512,2048]{1,0:T(8,128)} %dynamic-slice_add_fusion.3), channel_id=1, source_target_pairs={{0,2},{2,0},{1,3},{3,1},{4,6},{6,4},{5,7},{7,5},{8,10},{10,8},{9,1... | collective-permute-start | bytes 12582920 | tf_op jit(solution)/shard_map/ppermute | solution.py:287
  458.1 65.5 %collective-permute-start.25 = (f32[8,8,1024]{2,1,0:T(8,128)}, f32[8,8,1024]{2,1,0:T(8,128)}, u32[]{:S(2)}, u32[]{:S(2)}) collective-permute-start(f32[8,8,1024]{2,1,0:T(8,128)} %get-tuple-element.162), channel_id=1, source_target_pairs={{0,4},{4,0},{8,12},{12,8},{16,20},{20,16},{24,28},{28,24},{1,5},{5... | collective-permute-start | bytes 786440 | tf_op jit(solution)/shard_map/ppermute | solution.py:391
  524.8 600.6 %reduce-scatter.5.cloned.1.call-start = ((), (), s32[]{:S(2)}) async-start(), calls=%async_computation.4 | async-start | bytes 9437184 | tf_op jit(solution)/shard_map/reduce_scatter | solution.py:318
  536.5 67.1 %collective-permute-start.30 = (f32[512,2048]{1,0:T(8,128)}, f32[512,2048]{1,0:T(8,128)}, u32[]{:S(2)}, u32[]{:S(2)}) collective-permute-start(f32[512,2048]{1,0:T(8,128)} %constant_dynamic-slice_fusion.4), channel_id=1, source_target_pairs={{0,1},{1,0},{2,3},{3,2},{4,5},{5,4},{6,7},{7,6},{8,9},{9,8},{10,11... | collective-permute-start | bytes 12582920 | tf_op jit(solution)/shard_map/ppermute | solution.py:286
  606.7 118.8 %collective-permute-start.31 = (f32[512,2048]{1,0:T(8,128)S(1)}, f32[512,2048]{1,0:T(8,128)}, u32[]{:S(2)}, u32[]{:S(2)}) collective-permute-start(f32[512,2048]{1,0:T(8,128)S(1)} %dynamic-slice_add_fusion.2), channel_id=1, source_target_pairs={{0,2},{2,0},{1,3},{3,1},{4,6},{6,4},{5,7},{7,5},{8,10},{10,8},{9,1... | collective-permute-start | bytes 12582920 | tf_op jit(solution)/shard_map/ppermute | solution.py:287
  610.0 96.7 %collective-permute-start.27 = (f32[512,160]{0,1:T(8,128)S(1)}, f32[512,160]{0,1:T(8,128)S(1)}, u32[]{:S(2)}, u32[]{:S(2)}) collective-permute-start(f32[512,160]{0,1:T(8,128)S(1)} %fusion.134), channel_id=1, source_target_pairs={{0,2},{2,0},{1,3},{3,1},{4,6},{6,4},{5,7},{7,5},{8,10},{10,8},{9,1... | collective-permute-start | bytes 983048 | tf_op jit(solution)/shard_map/ppermute | solution.py:271
  749.4 830.4 %reduce-scatter.11.cloned.1.call-start = ((), (), s32[]{:S(2)}) async-start(), calls=%async_computation.7 | async-start | bytes 9437184 | tf_op jit(solution)/shard_map/reduce_scatter | solution.py:318
  777.9 92.7 %collective-permute-start.34 = (f32[512,2048]{1,0:T(8,128)S(1)}, f32[512,2048]{1,0:T(8,128)S(1)}, u32[]{:S(2)}, u32[]{:S(2)}) collective-permute-start(f32[512,2048]{1,0:T(8,128)S(1)} %dynamic-slice_add_fusion.1), channel_id=1, source_target_pairs={{0,2},{2,0},{1,3},{3,1},{4,6},{6,4},{5,7},{7,5},{8,10},{10,8},{9,1... | collective-permute-start | bytes 12582920 | tf_op jit(solution)/shard_map/ppermute | solution.py:287
  875.5 69.6 %collective-permute-start.35 = (f32[512,2048]{1,0:T(8,128)}, f32[512,2048]{1,0:T(8,128)}, u32[]{:S(2)}, u32[]{:S(2)}) collective-permute-start(f32[512,2048]{1,0:T(8,128)} %multiply_subtract_fusion.1), channel_id=1, source_target_pairs={{0,1},{1,0},{2,3},{3,2},{4,5},{5,4},{6,7},{7,6},{8,9},{9,8},{10,11... | collective-permute-start | bytes 12582920 | tf_op jit(solution)/shard_map/ppermute | solution.py:295
  914.3 665.5 %reduce-scatter.9.cloned.1.call-start = ((), (), s32[]{:S(2)}) async-start(), calls=%async_computation.6 | async-start | bytes 9437184 | tf_op jit(solution)/shard_map/reduce_scatter | solution.py:318
  934.0 58.4 %collective-permute-start.74 = (f32[2,36,512]{2,1,0:T(8,128)}, f32[2,36,512]{2,1,0:T(8,128)}, u32[]{:S(2)}, u32[]{:S(2)}) collective-permute-start(f32[2,36,512]{2,1,0:T(8,128)} %dynamic-slice_bitcast_fusion.14), channel_id=1, source_target_pairs={{0,16},{4,20},{8,24},{12,28},{16,0},{20,4},{24,8},{28,12},{1,17},{... | collective-permute-start | bytes 442376 | tf_op jit(solution)/shard_map/ppermute | solution.py:328
  945.1 166.2 %collective-permute-start.72 = (f32[36,512]{1,0:T(8,128)}, f32[36,512]{1,0:T(8,128)}, u32[]{:S(2)}, u32[]{:S(2)}) collective-permute-start(f32[36,512]{1,0:T(8,128)} %dynamic-slice_bitcast_fusion.19), channel_id=1, source_target_pairs={{0,16},{4,20},{8,24},{12,28},{16,0},{20,4},{24,8},{28,12},{1,17},{... | collective-permute-start | bytes 221192 | tf_op jit(solution)/shard_map/ppermute | solution.py:328
  994.1 118.1 %collective-permute-start.75 = (f32[36,512]{1,0:T(8,128)}, f32[36,512]{1,0:T(8,128)}, u32[]{:S(2)}, u32[]{:S(2)}) collective-permute-start(f32[36,512]{1,0:T(8,128)} %dynamic-slice_bitcast_fusion.18), channel_id=1, source_target_pairs={{0,4},{4,0},{8,12},{12,8},{16,20},{20,16},{24,28},{28,24},{1,5},{5... | collective-permute-start | bytes 221192 | tf_op jit(solution)/shard_map/ppermute | solution.py:328
  1183.9 195.2 %collective-permute-start.61 = (f32[2,2,256,512]{3,2,1,0:T(8,128)}, f32[2,2,256,512]{3,2,1,0:T(8,128)}, u32[]{:S(2)}, u32[]{:S(2)}) collective-permute-start(f32[2,2,256,512]{3,2,1,0:T(8,128)} %dynamic-slice_bitcast_fusion), channel_id=1, source_target_pairs={{0,8},{4,12},{8,0},{12,4},{16,24},{20,28},{24,16},{28,20},{1,9},{5... | collective-permute-start | bytes 6291464 | tf_op jit(solution)/shard_map/ppermute | solution.py:328
  1188.2 194.6 %collective-permute-start.58 = (f32[2,2,256,512]{3,2,1,0:T(8,128)}, f32[2,2,256,512]{3,2,1,0:T(8,128)}, u32[]{:S(2)}, u32[]{:S(2)}) collective-permute-start(f32[2,2,256,512]{3,2,1,0:T(8,128)} %dynamic-slice_bitcast_fusion.1), channel_id=1, source_target_pairs={{0,4},{4,0},{8,12},{12,8},{16,20},{20,16},{24,28},{28,24},{1,5},{5... | collective-permute-start | bytes 6291464 | tf_op jit(solution)/shard_map/ppermute | solution.py:328
  1194.2 60.6 %collective-permute-start.64 = (f32[2,2,36,512]{3,2,1,0:T(8,128)}, f32[2,2,36,512]{3,2,1,0:T(8,128)}, u32[]{:S(2)}, u32[]{:S(2)}) collective-permute-start(f32[2,2,36,512]{3,2,1,0:T(8,128)} %dynamic-slice_bitcast_fusion.13), channel_id=1, source_target_pairs={{0,4},{4,0},{8,12},{12,8},{16,20},{20,16},{24,28},{28,24},{1,5},{5... | collective-permute-start | bytes 884744 | tf_op jit(solution)/shard_map/ppermute | solution.py:328
  1195.0 92.7 %collective-permute-start.67 = (f32[2,2,36,512]{3,2,1,0:T(8,128)}, f32[2,2,36,512]{3,2,1,0:T(8,128)}, u32[]{:S(2)}, u32[]{:S(2)}) collective-permute-start(f32[2,2,36,512]{3,2,1,0:T(8,128)} %fusion.120), channel_id=1, source_target_pairs={{0,8},{4,12},{8,0},{12,4},{16,24},{20,28},{24,16},{28,20},{1,9},{5... | collective-permute-start | bytes 884744 | tf_op jit(solution)/shard_map/ppermute | solution.py:328
  1207.2 227.9 %collective-permute-start.55 = (f32[2,2,256,512]{3,2,1,0:T(8,128)S(1)}, f32[2,2,256,512]{3,2,1,0:T(8,128)S(1)}, u32[]{:S(2)}, u32[]{:S(2)}) collective-permute-start(f32[2,2,256,512]{3,2,1,0:T(8,128)S(1)} %dynamic-slice_bitcast_fusion.2), channel_id=1, source_target_pairs={{0,8},{4,12},{8,0},{12,4},{16,24},{20,28},{24,16},{28,20},{1,9},{5... | collective-permute-start | bytes 6291464 | tf_op jit(solution)/shard_map/ppermute | solution.py:328
  1254.8 185.1 %collective-permute-start.46 = (f32[512,2048]{1,0:T(8,128)S(1)}, f32[512,2048]{1,0:T(8,128)S(1)}, u32[]{:S(2)}, u32[]{:S(2)}) collective-permute-start(f32[512,2048]{1,0:T(8,128)S(1)} %dynamic-slice_add_fusion), channel_id=1, source_target_pairs={{0,2},{2,0},{1,3},{3,1},{4,6},{6,4},{5,7},{7,5},{8,10},{10,8},{9,1... | collective-permute-start | bytes 12582920 | tf_op jit(solution)/shard_map/ppermute | solution.py:287
  1287.7 80.8 %collective-permute-start.65 = (f32[2,36,512]{2,1,0:T(8,128)S(1)}, f32[2,36,512]{2,1,0:T(8,128)S(1)}, u32[]{:S(2)}, u32[]{:S(2)}) collective-permute-start(f32[2,36,512]{2,1,0:T(8,128)S(1)} %dynamic-slice_bitcast_fusion.17), channel_id=1, source_target_pairs={{0,8},{4,12},{8,0},{12,4},{16,24},{20,28},{24,16},{28,20},{1,9},{5... | collective-permute-start | bytes 442376 | tf_op jit(solution)/shard_map/ppermute | solution.py:328
  1437.3 66.1 %collective-permute-start.56 = (f32[2,256,512]{2,1,0:T(8,128)}, f32[2,256,512]{2,1,0:T(8,128)}, u32[]{:S(2)}, u32[]{:S(2)}) collective-permute-start(f32[2,256,512]{2,1,0:T(8,128)} %dynamic-slice_bitcast_fusion.6), channel_id=1, source_target_pairs={{0,16},{4,20},{8,24},{12,28},{16,0},{20,4},{24,8},{28,12},{1,17},{... | collective-permute-start | bytes 3145736 | tf_op jit(solution)/shard_map/ppermute | solution.py:328
  1445.8 114.6 %collective-permute-start.47 = (f32[512,2048]{1,0:T(8,128)}, f32[512,2048]{1,0:T(8,128)}, u32[]{:S(2)}, u32[]{:S(2)}) collective-permute-start(f32[512,2048]{1,0:T(8,128)} %multiply_subtract_fusion), channel_id=1, source_target_pairs={{0,1},{1,0},{2,3},{3,2},{4,5},{5,4},{6,7},{7,6},{8,9},{9,8},{10,11... | collective-permute-start | bytes 12582920 | tf_op jit(solution)/shard_map/ppermute | solution.py:295
  1448.0 59.2 %collective-permute-start.53 = (f32[2,256,512]{2,1,0:T(8,128)S(1)}, f32[2,256,512]{2,1,0:T(8,128)S(1)}, u32[]{:S(2)}, u32[]{:S(2)}) collective-permute-start(f32[2,256,512]{2,1,0:T(8,128)S(1)} %dynamic-slice_bitcast_fusion.7), channel_id=1, source_target_pairs={{0,8},{4,12},{8,0},{12,4},{16,24},{20,28},{24,16},{28,20},{1,9},{5... | collective-permute-start | bytes 3145736 | tf_op jit(solution)/shard_map/ppermute | solution.py:328
  (216 other events, 3873.9 us)
Sparse Core Ops, SparseCore 0:
  524.9 159.4 reduce-scatter.6
  749.5 159.6 reduce-scatter.4
  914.4 167.1 reduce-scatter.10
  1160.1 210.8 reduce-scatter.8

commit v3 on v2

--- a/solution.py
+++ b/solution.py
@@ -13,6 +13,9 @@
 EPSILON = 1e-05
 LANES=128
 LOG2E=math.log2(math.e)
+
+def cost(step, passes):
+    return pl.CostEstimate(flops=passes * STATE * step.size, bytes_accessed=passes * STATE * step.size, transcendentals=0)
 
 def cp(limit):
     return pltpu.CompilerParams(dimension_semantics=("arbitrary",), vmem_limit_bytes=limit)
@@ -60,15 +63,14 @@
         out_specs=pl.BlockSpec((STATE, 8, C), lambda i: (0, 0, 0)),
         out_shape=jax.ShapeDtypeStruct((STATE, 8, C), jnp.float32),
         scratch_shapes=[pltpu.VMEM((tb, STATE, 8, LANES), jnp.float32)],
-        compiler_params=cp(limit), name="end_states")(step, push, coef, rate)
-
-def scan_body(blocks, width, step_ref, push_ref, coef_ref, rate_ref, start_ref, out_ref, states_ref, enter_ref, final_ref, write, read):
+        compiler_params=cp(limit), cost_estimate=cost(step, 4), name="end_states")(step, push, coef, rate)
+
+def scan_body(blocks, width, step_ref, push_ref, coef_ref, rate_ref, start_ref, out_ref, states_ref, final_ref, write, read):
     @pl.when(pl.program_id(0) == 0)
     def _():
         final_ref[...] = start_ref[...]
     spread(coef_ref, write, 0)
     spread(coef_ref, read, STATE)
-    enter_ref[0] = final_ref[...]
     def group(g, _):
         cols = [pl.ds(pl.multiple_of((g * width + k) * LANES, LANES), LANES) for k in range(width)]
         for low in range(0, STATE, STATE // width):
@@ -106,11 +108,11 @@
         partial(scan_body, C // LANES, width),
         grid=(T // tb,),
         in_specs=[row, row, pl.BlockSpec((tb, 8, 2 * STATE), lambda i: (i, 0, 0)), pl.BlockSpec((STATE, C), lambda i: (0, 0)), whole],
-        out_specs=[row, pl.BlockSpec((tb, STATE, 8, C), lambda i: (i, 0, 0, 0)), pl.BlockSpec((1, STATE, 8, C), lambda i: (i, 0, 0, 0)), whole],
+        out_specs=[row, pl.BlockSpec((tb, STATE, 8, C), lambda i: (i, 0, 0, 0)), whole],
         out_shape=[jax.ShapeDtypeStruct((T, 8, C), f32), jax.ShapeDtypeStruct((T, STATE, 8, C), f32),
-                   jax.ShapeDtypeStruct((T // tb, STATE, 8, C), f32), jax.ShapeDtypeStruct((STATE, 8, C), f32)],
+                   jax.ShapeDtypeStruct((STATE, 8, C), f32)],
         scratch_shapes=[pltpu.VMEM((tb, STATE, 8, LANES), f32)] * 2,
-        compiler_params=cp(limit), name="scan_forward")(step, push, coef, rate, start)
+        compiler_params=cp(limit), cost_estimate=cost(step, 7), name="scan_forward")(step, push, coef, rate, start)
 
 def start_body(blocks, width, step_ref, grad_ref, coef_ref, rate_ref, start_ref, read):
     @pl.when(pl.program_id(0) == 0)
@@ -147,9 +149,9 @@
         out_specs=pl.BlockSpec((STATE, 8, C), lambda i: (0, 0, 0)),
         out_shape=jax.ShapeDtypeStruct((STATE, 8, C), jnp.float32),
         scratch_shapes=[pltpu.VMEM((tb, STATE, 8, LANES), jnp.float32)],
-        compiler_params=cp(limit), name="start_grads")(step, grad, coef, rate)
-
-def back_body(blocks, width, step_ref, push_ref, grad_ref, coef_ref, rate_ref, states_ref, enter_ref, end_ref,
+        compiler_params=cp(limit), cost_estimate=cost(step, 4), name="start_grads")(step, grad, coef, rate)
+
+def back_body(blocks, width, step_ref, push_ref, grad_ref, coef_ref, rate_ref, states_ref, prior_ref, begin_ref, end_ref,
               decay_out, push_out, coef_out, start_ref, speed_ref, write, read, write_sum, read_sum):
     @pl.when(pl.program_id(0) == 0)
     def _():
@@ -158,6 +160,7 @@
     spread(coef_ref, write, 0)
     spread(coef_ref, read, STATE)
     tb = step_ref.shape[0]
+    begins = pl.program_id(0) == pl.num_programs(0) - 1
     def group(g, first):
         cols = [pl.ds(pl.multiple_of((g * width + k) * LANES, LANES), LANES) for k in range(width)]
         for low in range(0, STATE, STATE // width):
@@ -165,6 +168,8 @@
             carry = {(k, n): start_ref[n, :, cols[k]] for k in range(width) for n in span}
             speed = {(k, n): speed_ref[n, :, cols[k]] for k in range(width) for n in span}
             rate = {(k, n): rates(rate_ref, cols[k], n) for k in range(width) for n in span}
+            enter = {(k, n): jnp.where(begins, begin_ref[n, :, cols[k]], prior_ref[0, n, :, cols[k]])
+                     for k in range(width) for n in span}
             for t in reversed(range(tb)):
                 step = [step_ref[t, :, c] for c in cols]
                 push = [push_ref[t, :, c] for c in cols]
@@ -175,7 +180,7 @@
                     w, r = write[t, n], read[t, n]
                     wsum, rsum = None, None
                     for k in range(width):
-                        before = states_ref[t - 1, n, :, cols[k]] if t else enter_ref[0, n, :, cols[k]]
+                        before = states_ref[t - 1, n, :, cols[k]] if t else enter[k, n]
                         back = carry[k, n] + r * grad[k]
                         held = jnp.exp2(step[k] * rate[k, n]) * back
                         carry[k, n] = held
@@ -216,7 +221,7 @@
             row = jnp.where(lane == STATE + n, jnp.sum(read_sum[t, n], axis=-1, keepdims=True), row)
         coef_out[t] = row
 
-def scan_backward(step, push, grad, coef, rate, states, enter, end, tb=8, width=2, limit=48*2**20):
+def scan_backward(step, push, grad, coef, rate, states, begin, end, tb=8, width=2, limit=48*2**20):
     T, _, C = step.shape
     last = T // tb - 1
     f32 = jnp.float32
@@ -228,12 +233,12 @@
         grid=(T // tb,),
         in_specs=[row, row, row, thin, pl.BlockSpec((STATE, C), lambda i: (0, 0)),
                   pl.BlockSpec((tb, STATE, 8, C), lambda i: (last - i, 0, 0, 0)),
-                  pl.BlockSpec((1, STATE, 8, C), lambda i: (last - i, 0, 0, 0)), whole],
+                  pl.BlockSpec((1, STATE, 8, C), lambda i: (jnp.maximum((last - i) * tb - 1, 0), 0, 0, 0)), whole, whole],
         out_specs=[row, row, thin, whole, whole],
         out_shape=[jax.ShapeDtypeStruct((T, 8, C), f32)] * 2 + [jax.ShapeDtypeStruct((T, 8, 2 * STATE), f32)]
           + [jax.ShapeDtypeStruct((STATE, 8, C), f32)] * 2,
         scratch_shapes=[pltpu.VMEM((tb, STATE, 8, LANES), f32)] * 4,
-        compiler_params=cp(limit), name="scan_backward")(step, push, grad, coef, rate, states, enter, end)
+        compiler_params=cp(limit), cost_estimate=cost(step, 13), name="scan_backward")(step, push, grad, coef, rate, states, states, begin, end)
 
 
 HALVES_OF_CHIP = 2
@@ -279,14 +284,21 @@
     return half_of(array, lax.axis_index("tensor") % 2)
 
 
-def own_sum(array, beside):
+def ordered_after(value, *others):
+    return lax.optimization_barrier((value,) + others)[0]
+
+
+def core_sum(array):
     if not paired():
-        return lax.psum_scatter(array, "tensor", scatter_dimension=0, tiled=True), beside
+        return lax.psum_scatter(array, "tensor", scatter_dimension=0, tiled=True)
     core = lax.axis_index("tensor") % 2
-    half = half_of(array, core) + lax.ppermute(half_of(array, 1 - core), "tensor", BESIDE)
-    got = lax.ppermute(half, "tensor", ACROSS)
-    got, beside = lax.optimization_barrier((got, beside))
-    return half + got, beside
+    return half_of(array, core) + lax.ppermute(half_of(array, 1 - core), "tensor", BESIDE)
+
+
+def across(half):
+    if not paired():
+        return jnp.zeros_like(half)
+    return lax.ppermute(half, "tensor", ACROSS)
 
 
 def all_rows(array):
@@ -318,23 +330,192 @@
     return lax.psum_scatter(array, "blk", scatter_dimension=0, tiled=True)
 
 
-def halved(array, bits):
-    axes = [4, 2, 1]
-    for bit in bits:
-        axis = axes.index(bit)
-        axes.remove(bit)
-        mine = (lax.axis_index("blk") // bit) % 2
-        give = chosen(array, axis, 1 - mine)
-        array = chosen(array, axis, mine) + lax.ppermute(give, "blk", [(j, j ^ bit) for j in range(8)])
-    return array
-
-
-def split_scatter(array):
-    if lax.axis_size("blk") != 8:
-        return blk_scatter(array)
-    array = array.reshape((2, 2, 2, array.shape[0] // 8, array.shape[1]))
-    middle = array.shape[-1] // 2
-    return jnp.concatenate([halved(array[..., :middle], (1, 2, 4)), halved(array[..., middle:], (2, 4, 1))], axis=-1)
+def add_rows(total, other, count):
+    slab = 8
+
+    def body(i, _):
+        at = pl.ds(pl.multiple_of(i * slab, slab), slab)
+        total[at, :] = total[at, :] + other[at, :]
+        return 0
+
+    lax.fori_loop(0, count // slab, body, 0)
+
+
+def remote(src, dst, sends, recvs, at, device):
+    return pltpu.make_async_remote_copy(
+        src_ref=src, dst_ref=dst, send_sem=sends.at[at], recv_sem=recvs.at[at], device_id=device,
+        device_id_type=pl.DeviceIdType.MESH)
+
+
+def joint_body(plan, chunks, sum_ref, *refs):
+    count = 1 + max(job[0] for job in plan)
+    thick_refs, small_ref, refs = refs[:count], refs[count], refs[count + 1:]
+    half_out, thick_outs, small_out, refs = refs[0], refs[1:1 + count], refs[1 + count], refs[2 + count:]
+    own_half, core_half, far_half, small_in, refs = refs[0], refs[1], refs[2], refs[3], refs[4:]
+    core_send, core_recv, far_send, far_recv, local_sem, out_sem, small_send, small_recv = refs[:8]
+    refs = refs[8:]
+    blk, tensor = lax.axis_index("blk"), lax.axis_index("tensor")
+    bits = {1: blk % 2, 2: (blk // 2) % 2, 4: blk // 4}
+    core = tensor % 2
+    beside = (blk, tensor + 1 - 2 * core)
+    far = (blk, (tensor + 2) % 4)
+    peers = {bit: (blk + bit - 2 * bit * bits[bit], tensor) for bit in bits}
+    barrier = pltpu.get_barrier_semaphore()
+    for device in (beside, far, peers[1], peers[2], peers[4]):
+        pl.semaphore_signal(barrier, inc=1, device_id=device, device_id_type=pl.DeviceIdType.MESH)
+    pl.semaphore_wait(barrier, 5)
+
+    rows_each = half_out.shape[0] // chunks
+    smalls, core_copies, local_copies, far_copies, outs = [], [], [], [], []
+
+    def small_step(i):
+        copy = remote(small_out, small_in.at[i], small_send, small_recv, i, peers[1 << i])
+        copy.start()
+        smalls.append(copy)
+
+    def small_end(i):
+        smalls[i].wait()
+        small_out[...] = small_out[...] + small_in[i]
+
+    small_out[...] = small_ref[...]
+    small_step(0)
+    for k in range(chunks):
+        give = pl.ds(pl.multiple_of((1 - core) * rows_each * chunks + k * rows_each, rows_each), rows_each)
+        keep = pl.ds(pl.multiple_of(core * rows_each * chunks + k * rows_each, rows_each), rows_each)
+        copy = remote(sum_ref.at[give], core_half.at[k], core_send, core_recv, k, beside)
+        copy.start()
+        core_copies.append(copy)
+        copy = pltpu.make_async_copy(sum_ref.at[keep], own_half.at[k], local_sem.at[k])
+        copy.start()
+        local_copies.append(copy)
+
+    class Job:
+        def __init__(self, which, low, wide, order, refs):
+            (self.own, self.first, self.second, self.third, self.sems) = refs[0], refs[1], refs[2], refs[3], refs[4:]
+            self.order = order
+            self.count = thick_refs[which].shape[3]
+            self.out = thick_outs[which].at[:, pl.ds(low, wide)]
+            lead, (u, v) = bits[order[0]], (bits[order[1]], bits[order[2]])
+            self.parts = [(1 - u, 1 - v), (1 - u, v), (u, 1 - v), (u, v)]
+            self.firsts, self.owns, self.seconds = [], [], []
+            for i, part in enumerate(self.parts):
+                at = {order[1]: part[0], order[2]: part[1]}
+
+                def source(mine):
+                    index = dict(at)
+                    index[order[0]] = mine
+                    return thick_refs[which].at[index[4], index[2], index[1], :, pl.ds(low, wide)]
+
+                copy = remote(source(1 - lead), self.first.at[part], self.sems[0], self.sems[1], i, peers[order[0]])
+                copy.start()
+                self.firsts.append(copy)
+                copy = pltpu.make_async_copy(source(lead), self.own.at[part], self.sems[2].at[i])
+                copy.start()
+                self.owns.append(copy)
+
+        def first_end(self, i):
+            self.owns[i].wait()
+            self.firsts[i].wait_recv()
+            add_rows(self.own.at[self.parts[i]], self.first.at[self.parts[i]], self.count)
+            if i < 2:
+                copy = remote(self.own.at[self.parts[i]], self.second.at[i], self.sems[3], self.sems[4], i,
+                              peers[self.order[1]])
+                copy.start()
+                self.seconds.append(copy)
+                return
+            self.seconds[i - 2].wait_recv()
+            add_rows(self.own.at[self.parts[i]], self.second.at[i - 2], self.count)
+            if i == 2:
+                self.last = remote(self.own.at[self.parts[i]], self.third, self.sems[5], self.sems[6], 0,
+                                   peers[self.order[2]])
+                self.last.start()
+
+        def end(self):
+            self.last.wait_recv()
+            add_rows(self.own.at[self.parts[3]], self.third, self.count)
+            copy = pltpu.make_async_copy(self.own.at[self.parts[3]], self.out, self.sems[7].at[0])
+            copy.start()
+            outs.append(copy)
+
+        def sent(self):
+            return self.firsts + self.seconds + [self.last]
+
+    jobs = [Job(*job, refs[12 * i:12 * i + 12]) for i, job in enumerate(plan)]
+
+    def core_end(k):
+        local_copies[k].wait()
+        core_copies[k].wait()
+        add_rows(own_half.at[k], core_half.at[k], rows_each)
+        copy = remote(own_half.at[k], far_half.at[k], far_send, far_recv, k, far)
+        copy.start()
+        far_copies.append(copy)
+
+    def far_end(k):
+        far_copies[k].wait_recv()
+        add_rows(far_half.at[k], own_half.at[k], rows_each)
+        copy = pltpu.make_async_copy(
+            far_half.at[k], half_out.at[pl.ds(k * rows_each, rows_each)], out_sem.at[k])
+        copy.start()
+        outs.append(copy)
+
+    for k in range(chunks):
+        core_end(k)
+    small_end(0)
+    small_step(1)
+    for i in range(4):
+        for job in jobs:
+            job.first_end(i)
+        if i in (0, 1):
+            small_end(i + 1)
+            if i == 0:
+                small_step(2)
+        far_end(i)
+    for job in jobs:
+        job.end()
+    for copy in far_copies + [each for job in jobs for each in job.sent()]:
+        copy.wait_send()
+    for copy in outs:
+        copy.wait()
+
+
+def joint_sums(array, thick, small, collective_id):
+    if not paired() or lax.axis_size("blk") != 8:
+        return (lax.psum_scatter(array, "tensor", scatter_dimension=0, tiled=True),
+                [blk_scatter(part) for part in thick], lax.psum(small, "blk"))
+    R, N = array.shape
+    C = thick[0].shape[1]
+    chunks = 4
+    f32 = jnp.float32
+    dma = pltpu.SemaphoreType.DMA
+    any_spec = pl.BlockSpec(memory_space=pl.ANY)
+    vmem_spec = pl.BlockSpec(memory_space=pltpu.VMEM)
+    cut = C - 128 if len(thick) == 1 else C
+    plan = [(0, 0, cut, (1, 2, 4))]
+    if cut < C:
+        plan.append((0, cut, C - cut, (2, 4, 1)))
+    plan += [(i, 0, C, (2, 4, 1)) for i in range(1, len(thick))]
+    scratch = []
+    for which, _, wide, _ in plan:
+        count = thick[which].shape[0] // 8
+        scratch += [pltpu.VMEM((2, 2, count, wide), f32), pltpu.VMEM((2, 2, count, wide), f32),
+                    pltpu.VMEM((2, count, wide), f32), pltpu.VMEM((count, wide), f32),
+                    dma((4,)), dma((4,)), dma((4,)), dma((2,)), dma((2,)), dma((1,)), dma((1,)), dma((1,))]
+    half = pltpu.VMEM((chunks, R // 2 // chunks, N), f32)
+    out = pl.pallas_call(
+        partial(joint_body, plan, chunks),
+        in_specs=[any_spec] * (1 + len(thick)) + [vmem_spec],
+        out_specs=[any_spec] * (1 + len(thick)) + [vmem_spec],
+        out_shape=[jax.ShapeDtypeStruct((R // 2, N), f32)]
+        + [jax.ShapeDtypeStruct((part.shape[0] // 8, C), f32) for part in thick]
+        + [jax.ShapeDtypeStruct(small.shape, f32)],
+        scratch_shapes=[half, half, half, pltpu.VMEM((3,) + small.shape, f32)]
+        + [dma((chunks,))] * 5 + [dma((chunks,)), dma((3,)), dma((3,))] + scratch,
+        compiler_params=pltpu.CompilerParams(
+            collective_id=collective_id, has_side_effects=True, vmem_limit_bytes=52 * 2**20),
+        cost_estimate=pl.CostEstimate(flops=0, bytes_accessed=50 * R * N * 4, transcendentals=0),
+        name="joint_sums",
+    )(array, *[part.reshape(2, 2, 2, part.shape[0] // 8, C) for part in thick], small)
+    return out[0], list(out[1:-1]), out[-1]
 
 
 def neighbour(value, steps):
@@ -427,7 +608,7 @@
         (norm_gain, in_weight, conv_weight, conv_bias, x_weight, dt_weight, dt_bias, decay_log,
          skip_weight, out_weight) = args
         self.gain = norm_gain[index]
-        self.into = in_weight[index].reshape(in_weight.shape[1], -1)
+        self.raw = in_weight[index]
         self.taps = conv_weight[index]
         self.shift = conv_bias[index]
         self.x = x_weight[index]
@@ -444,9 +625,9 @@
 
 
 def front(layer, normed, conv_first, parts, at_first):
-    mixed = dot32(normed, layer.into)
-    inner = mixed.shape[-1] // 2
-    values, gate = mixed[:, :inner], mixed[:, inner:]
+    mixed = jnp.einsum("rd,dkc->krc", normed, layer.raw, preferred_element_type=jnp.float32)
+    values, gate = mixed[0], mixed[1]
+    inner = values.shape[-1]
     count = values.shape[0]
     rim = layer.taps.shape[0] - 1
     tails = split_parts(by_step(values[count - 8 * rim:]), parts)
@@ -458,12 +639,11 @@
     projected = tensor_sum(dot32(inputs, layer.x))
     dt_low = projected[:, :RANK].astype(jnp.bfloat16)
     coef = by_step(projected[:, RANK:])
-    before = dot32(dt_low, layer.dt) + layer.dt_bias
-    step = jax.nn.softplus(before)
+    step = jax.nn.softplus(dot32(dt_low, layer.dt) + layer.dt_bias)
     push = step * inputs.astype(jnp.float32)
     local = split_parts(end_states(by_step(step), by_step(push), coef, layer.rate2), parts)
     totals = split_parts(jnp.sum(by_step(step), axis=0), parts)
-    return (window, gate, conv_out, inputs, dt_low, coef, before, step, push, totals), local, tails[:, -1]
+    return (window, gate, conv_out, inputs, dt_low, coef, step, push, totals), local, tails[:, -1]
 
 
 def join(local, totals, rate, reverse):
@@ -494,54 +674,61 @@
 
 
 def scanning(layer, kept, start):
-    window, gate, conv_out, inputs, dt_low, coef, before, step, push, totals = kept
-    scanned, states, enter, final = scan_forward(by_step(step), by_step(push), coef, layer.rate2, start)
+    window, gate, conv_out, inputs, dt_low, coef, step, push, totals = kept
+    scanned, states, final = scan_forward(by_step(step), by_step(push), coef, layer.rate2, start)
     result = rows(scanned) + layer.skip * inputs.astype(jnp.float32)
     gated = (result * jax.nn.silu(gate)).astype(jnp.bfloat16)
-    return dot32(gated, layer.out), (result, gated, states, enter), final
-
-
-def back_front(layer, kept, grad_low):
-    window, gate, conv_out, inputs, dt_low, coef, before, step, push, totals = kept
+    return dot32(gated, layer.out), (result, gated, states, start), final
+
+
+def back_gated(layer, kept, grad_low):
+    gate = kept[1]
     grad_gated = dot_n(grad_low, layer.out)
-    grad_result = grad_gated * jax.nn.silu(gate)
+    return grad_gated, grad_gated * jax.nn.silu(gate)
+
+
+def back_local(layer, kept, grad_result):
+    window, gate, conv_out, inputs, dt_low, coef, step, push, totals = kept
     local = start_grads(by_step(step), by_step(grad_result), coef, layer.rate2)
-    return (grad_gated, grad_result), split_parts(local, totals.shape[0])
+    return split_parts(local, totals.shape[0])
 
 
 def back_side(layer, kept, normed, scans, grads, grad_low):
-    window, gate, conv_out, inputs, dt_low, coef, before, step, push, totals = kept
-    result, gated, states, enter = scans
+    window, gate, conv_out, inputs, dt_low, coef, step, push, totals = kept
+    result, gated, states, start = scans
     grad_gated, grad_result = grads
     inner = gate.shape[1]
-    out_grad = dot_t(grad_low, gated)
     grad_gate = (grad_gated * result * silu_slope(gate)).astype(jnp.bfloat16)
     gate_grad = dot_t(normed, grad_gate)
     gate_through = dot_n(grad_gate, layer.into[:, inner:])
     skip_grad = jnp.sum(grad_result * inputs.astype(jnp.float32), axis=0)
-    return out_grad, gate_grad, gate_through, skip_grad
-
-
-def back_scan(layer, kept, normed, scans, grads, end, gate_through):
-    window, gate, conv_out, inputs, dt_low, coef, before, step, push, totals = kept
-    result, gated, states, enter = scans
+    return gate_grad, gate_through, skip_grad
+
+
+def back_scan(layer, kept, scans, grads, end):
+    window, gate, conv_out, inputs, dt_low, coef, step, push, totals = kept
+    result, gated, states, start = scans
+    grad_gated, grad_result = grads
+    return scan_backward(
+        by_step(step), by_step(push), by_step(grad_result), coef, layer.rate2, states, start, end)
+
+
+def back_rest(layer, kept, grads, scan_out, gate_through):
+    window, gate, conv_out, inputs, dt_low, coef, step, push, totals = kept
     grad_gated, grad_result = grads
     count, inner = gate.shape
     parts = totals.shape[0]
     rim = layer.taps.shape[0] - 1
     wide = inputs.astype(jnp.float32)
-    decays, pushes, coef_grad, start_grad, speed = scan_backward(
-        by_step(step), by_step(push), by_step(grad_result), coef, layer.rate2, states, enter, end)
+    decays, pushes, coef_grad, start_grad, speed = scan_out
     pushes = rows(pushes)
     step_grad = rows(decays) * (1.0 / LOG2E) + wide * pushes
-    before_grad = step_grad * jax.nn.sigmoid(before)
+    before_grad = step_grad * -jnp.expm1(-step)
     bias_grad = jnp.sum(before_grad, axis=0)
     decay_grad = layer.rate * jnp.sum(speed, axis=1)
     before_low = before_grad.astype(jnp.bfloat16)
     projected_grad = tensor_sum(jnp.concatenate([dot_n(before_low, layer.dt), rows(coef_grad)], axis=-1))
-    dt_grad = dot_t(dt_low, before_low)
     high, low = two_parts(projected_grad)
-    x_grad = dot_t(high, inputs) + dot_t(low, inputs)
     through = dot_n(jnp.concatenate([high, low], axis=-1), jnp.concatenate([layer.x, layer.x], axis=-1))
     inputs_grad = grad_result * layer.skip + step * pushes + through
     conv_grad = inputs_grad * silu_slope(conv_out)
@@ -556,10 +743,22 @@
     tail_grad = jnp.concatenate([prefix_grad[:, 1:], arrived[:, None]], axis=1).reshape(8 * rim, inner)
     values_grad = jnp.concatenate([window_grad[8 * rim:count], window_grad[count:] + tail_grad], axis=0)
     values_grad = values_grad.astype(jnp.bfloat16)
-    into_grad = dot_t(normed, values_grad)
     normed_part = dot_n(values_grad, layer.into[:, :inner]) + gate_through
-    grads = (into_grad, taps_grad, shift_grad, x_grad, dt_grad, bias_grad, decay_grad)
-    return normed_part, grads, split_parts(start_grad, parts)[:, 0], prefix_grad[:, 0]
+    small = jnp.concatenate([taps_grad, shift_grad[None], bias_grad[None], decay_grad], axis=0)
+    return normed_part, small, (values_grad, before_low, high, low), split_parts(start_grad, parts)[:, 0], prefix_grad[:, 0]
+
+
+def thick_grads(kept, normed, lows):
+    inputs, dt_low = kept[3], kept[4]
+    values_grad, before_low, high, low = lows
+    blocks = lax.axis_size("blk")
+    x_grad = dot_t(high, inputs) + dot_t(low, inputs)
+    return [eights(part.reshape(blocks, -1, part.shape[-1]))
+            for part in (dot_t(normed, values_grad), x_grad, dot_t(dt_low, before_low))]
+
+
+def eights(array):
+    return jnp.pad(array, ((0, 0), (0, -array.shape[1] % 8), (0, 0)))
 
 
 def norm_back(layer, normed_grad, residual, q):
@@ -597,79 +796,104 @@
     grad_low = grad.astype(jnp.bfloat16)
 
     kept, scans, norms, finals, tails, squares = ([None] * layer_total for _ in range(6))
-    starts, prefixes, sums = ([None] * layer_total for _ in range(3))
+    starts, prefixes, smalls, gains = ([None] * layer_total for _ in range(4))
     for l, layer in enumerate(layers):
         norms[l] = (normed, residual)
         kept[l], local, tails[l] = front(
             layer, normed, jnp.moveaxis(conv_init[l], 1, 0), parts, at_first)
         totals = kept[l][-1]
         if l == last:
-            grads, back_local = back_front(layer, kept[l], grad_low)
-            local, back_local = lax.optimization_barrier((local, back_local))
-            end = exchange(layer, back_local, totals, jnp.zeros_like(back_local[:, 0]), True)
+            grads = back_gated(layer, kept[l], grad_low)
+            local, late = lax.optimization_barrier((local, back_local(layer, kept[l], grads[1])))
+            end = exchange(layer, late, totals, jnp.zeros_like(late[:, 0]), True)
         start = exchange(layer, local, totals, jnp.moveaxis(scan_init[l], 1, 0), False)
         partial_sum, scans[l], final = scanning(layer, kept[l], start)
         finals[l] = split_parts(final, parts)[:, -1]
+        half = core_sum(partial_sum)
         if l < last:
-            branch, layers[l + 1].into = own_sum(partial_sum, layers[l + 1].into)
-        else:
-            branch, _ = own_sum(partial_sum, ())
-        following = residual + branch
-        squares[l] = jnp.stack([jnp.sum(branch * branch), jnp.sum(following * following)])
-        residual = following
-        if l < last:
+            half, stored = lax.optimization_barrier((half, weights[1]))
+            into = [stored[k].reshape(width, -1) for k in range(layer_total)]
+            got, into, grad_low = lax.optimization_barrier((across(half), into, grad_low))
+            for each, array in zip(layers, into):
+                each.into = array
+            branch = half + got
+            following = residual + branch
+            squares[l] = jnp.stack([jnp.sum(branch * branch), jnp.sum(following * following)])
+            residual = following
             unscaled = all_rows(residual * inverse_rms(residual))
             normed = (unscaled * layers[l + 1].gain).astype(jnp.bfloat16)
-    out = restore((2.0 * all_rows(0.5 * residual)).astype(jnp.bfloat16))
-
+
+    thins, scattered = [], [None] * layer_total
     for l in reversed(range(layer_total)):
         layer = layers[l]
-        normed, residual = norms[l]
+        normed, base = norms[l]
         if l < last:
-            grads, back_local = back_front(layer, kept[l], grad_low)
-            end = exchange(layer, back_local, kept[l][-1], jnp.zeros_like(back_local[:, 0]), True)
+            grads = back_gated(layer, kept[l], grad_low)
+            late = back_local(layer, kept[l], grads[1])
+            end = exchange(layer, late, kept[l][-1], jnp.zeros_like(late[:, 0]), True)
+        out_grad = dot_t(grad_low, scans[l][1])
         side = back_side(layer, kept[l], normed, scans[l], grads, grad_low)
-        end, side = lax.optimization_barrier((end, side))
-        out_grad, gate_grad, gate_through, skip_grad = side
-        normed_part, layer_grads, starts[l], prefixes[l] = back_scan(
-            layer, kept[l], normed, scans[l], grads, end, gate_through)
+        middle = half.shape[0] // 2
         if l == last:
-            normed_part, out = lax.optimization_barrier((normed_part, out))
-        normed_grad, _ = own_sum(normed_part, ())
-        gain_grad, change = norm_back(layer, normed_grad, residual, inverse_rms(residual))
+            end, side, out_grad, half = lax.optimization_barrier((end, side, out_grad, half))
+            scattered[l] = [blk_scatter(out_grad), blk_scatter(side[0])]
+            scan_out, got = lax.optimization_barrier(
+                (back_scan(layer, kept[l], scans[l], grads, end), across(half[:middle])))
+        else:
+            end, side, out_grad, half, scattered[last] = lax.optimization_barrier(
+                (end, side, out_grad, half, scattered[last]))
+            scattered[l] = [blk_scatter(out_grad), blk_scatter(side[0])]
+            scan_out, got_rest = lax.optimization_barrier(
+                (back_scan(layer, kept[l], scans[l], grads, end), across(half[middle:])))
+            branch = half + jnp.concatenate([got, got_rest], axis=0)
+            following = residual + branch
+            squares[last] = jnp.stack([jnp.sum(branch * branch), jnp.sum(following * following)])
+            out = restore((2.0 * all_rows(0.5 * following)).astype(jnp.bfloat16))
+        gate_grad, gate_through, skip_grad = side
+        normed_part, smalls[l], lows, starts[l], prefixes[l] = back_rest(
+            layer, kept[l], grads, scan_out, gate_through)
+        smalls[l] = jnp.concatenate([smalls[l], skip_grad[None]], axis=0)
+        thick = thick_grads(kept[l], normed, lows)
+        inner = smalls[l].shape[-1]
+        if l == last:
+            thins = thick[1:] + thins
+            normed_grad, thick, smalls[l] = joint_sums(normed_part, [rows(thick[0])], smalls[l], l)
+            scattered[l].append(thick[0])
+        else:
+            thins = thick[1:] + thins
+            cuts = [part.shape[1] for part in thins]
+            extra = jnp.concatenate([jnp.stack(squares).reshape(-1), input_square.reshape(1)])
+            extra = jnp.pad(extra, (0, inner - extra.shape[0]))[None]
+            shared = rows_sum(jnp.concatenate(
+                [extra] + [gain.reshape(-1, inner) for gain in gains[1:]], axis=0))
+            own_count = smalls[l].shape[0]
+            small = jnp.concatenate([smalls[l], shared], axis=0)
+            small = jnp.pad(small, ((0, -small.shape[0] % 8), (0, 0)))
+            normed_part, thins, out = lax.optimization_barrier((normed_part, thins, out))
+            normed_grad, thick, small = joint_sums(
+                normed_part, [rows(thick[0]), rows(jnp.concatenate(thins, axis=1))], small, l)
+            scattered[l].append(thick[0])
+            smalls[l], rest = small[:own_count], small[own_count:]
+        gains[l], change = norm_back(layer, normed_grad, base, inverse_rms(base))
         grad = grad + all_rows(change)
         grad_low = grad.astype(jnp.bfloat16)
-        sums[l] = (gain_grad, gate_grad, skip_grad, out_grad) + layer_grads
+    first_gain = blk_sum(rows_sum(gains[0].reshape(-1, inner)))
     input_grad = restore(grad_low)
 
-    big, small, shared = [], [], []
-    for l in reversed(range(layer_total)):
-        (gain_grad, gate_grad, skip_grad, out_grad, into_grad, taps_grad, shift_grad, x_grad, dt_grad, bias_grad,
-         decay_grad) = sums[l]
-        scatter = blk_scatter if l else split_scatter
-        into_part, gate_part, out_part = scatter(into_grad), scatter(gate_grad), blk_scatter(out_grad)
-        thin = jnp.concatenate([x_grad.reshape(blocks, -1, x_grad.shape[-1]),
-                                dt_grad.reshape(blocks, -1, dt_grad.shape[-1])], axis=1)
-        thin = split_scatter(thin.reshape(-1, thin.shape[-1]))
-        cut = x_grad.shape[0] // blocks
-        big.insert(0, (jnp.stack([into_part, gate_part], axis=1), out_part.T, thin[:cut].T, thin[cut:]))
-        small.insert(0, jnp.concatenate(
-            [taps_grad, shift_grad[None], bias_grad[None], skip_grad[None], decay_grad], axis=0))
-        shared.insert(0, gain_grad)
-    inner = small[0].shape[-1]
-    extra = jnp.concatenate([jnp.stack(squares).reshape(-1), input_square.reshape(1)])
-    extra = jnp.pad(extra, (0, inner - extra.shape[0]))[None]
-    shared = rows_sum(jnp.concatenate([jnp.stack(shared).reshape(-1, inner), extra], axis=0))
-    gain_rows = shared.shape[0] - 1
-    sizes = [part.shape[0] for part in small]
-    packed = blk_sum(jnp.concatenate(small + [shared], axis=0))
-    rest = packed[sum(sizes):]
-    small = packed[:sum(sizes)].reshape(layer_total, sizes[0], inner)
+    small = jnp.stack(smalls)
+    gain_rows = first_gain.shape[0] * layer_total
+    gain_grad = jnp.concatenate([first_gain, rest[1:1 + gain_rows - first_gain.shape[0]]], axis=0)
+    gain_grad = gain_grad.reshape(layer_total, width)
     taps = weights[2].shape[1]
     row_total = tokens.shape[0] * tokens.shape[1] * width * blocks
-    squares = rest[-1] / row_total
+    squares = rest[0] / row_total
     rms_stats = jnp.sqrt(squares[:2 * layer_total]).reshape(layer_total, 2)
     input_rms = jnp.sqrt(squares[2 * layer_total:2 * layer_total + 1])
+    pieces, at = [], 0
+    for cut in cuts:
+        pieces.append(thick[1][at:at + cut])
+        at += cut
+    into_out = jnp.stack([jnp.stack([part[2], part[1]], axis=1) for part in scattered])
 
     def stacked(parts_):
         return jnp.stack([jnp.moveaxis(part, 0, 1) for part in parts_])[:, :, None]
@@ -681,16 +905,16 @@
         input_grad,
         stacked(starts),
         stacked(prefixes),
-        rest[:gain_rows].reshape(layer_total, width),
-        jnp.stack([part[0] for part in big]),
+        gain_grad,
+        into_out,
         small[:, :taps],
         small[:, taps],
-        jnp.stack([part[2] for part in big]),
-        jnp.stack([part[3] for part in big]),
+        jnp.stack([part[:weights[4].shape[-1] // blocks].T for part in pieces[0::2]]),
+        jnp.stack([part[:RANK // blocks] for part in pieces[1::2]]),
         small[:, taps + 1],
-        small[:, taps + 3:],
-        small[:, taps + 2],
-        jnp.stack([part[1] for part in big]),
+        small[:, taps + 2:-1],
+        small[:, -1],
+        jnp.stack([part[0].T for part in scattered]),
         rms_stats,
         input_rms,
     )

time: 1610 us -> 1400 us (0.87)
  waiting for transfers between devices: 698 us -> 209 us
  Pallas kernels: 247 us -> 592 us
  starting transfers between devices: 106 us -> 70.9 us
  other arithmetic: 177 us -> 158 us
    ppermute x32 -> x5, waiting for transfers between devices: 481 us -> 54.9 us  [the longest x3 47.7 us: across(): return lax.ppermute(half, 'tensor', ACROSS)]
    pallas_call x0 -> x2, Pallas kernels: none -> 343 us  [joint_sums(): pl.pallas_call(partial(joint_body, plan, chunks), in_specs=[any_spec] * (...]
    ppermute x4, waiting for transfers between devices: 120 us -> 33.4 us  [tensor_sum(): half = half + lax.ppermute(half, 'tensor', ACROSS)]
    ppermute x32 -> x5, starting transfers between devices: 40 us -> 4.63 us  [the longest x3 4.56 us: across(): return lax.ppermute(half, 'tensor', ACROSS)]
    dot_general x8 -> x6, matrix products: 49.5 us -> 20.1 us  [dot32(): return jnp.dot(left, right, preferred_element_type=jnp.float32)]
    dot_general x0 -> x2, matrix products: none -> 23 us  [front(): jnp.einsum('rd,dkc->krc', normed, layer.raw, preferred_element_type=jnp.f...]
    add x30 -> x4, other arithmetic: 35.9 us -> 14.3 us  [the longest x2 9.44 us: core_sum(): half_of(array, core)]
    dot_general x12, matrix products: 55.2 us -> 73.3 us  [dot_t(): lax.dot_general(left, right, (((0,), (0,)), ((), ())), preferred_element_...]
  transfers between devices with their start and end apart: 80 -> 54, of which waited for: 42 -> 29; matrix products, arithmetic and copies ran while one was open for 24% -> 27% of each run, Pallas kernels for 10% -> 37%
where the time goes in v3:
time: 1400 us; the launch traced here: 1390 us
  Pallas kernels  592 us (42%)
  matrix products  213 us (15%)
  waiting for transfers between devices  209 us (15%)
  other arithmetic  158 us (11%)
  local copies, waits for them, and re-layouts  126 us (9%)
  starting transfers between devices  70.9 us (5%)
  between operations  18.4 us (1%)
    pallas_call x2, Pallas kernels, joint_sums(): pl.pallas_call(partial(joint_body, plan, chunks), in_specs=[any_spec] * (...  343 us
    pallas_call x2, Pallas kernels, scan_backward(): pl.pallas_call(partial(back_body, C // LANES, width), grid=(T // tb,), in...  119 us
    dot_general x10, matrix products, dot_n(): lax.dot_general(left, right, (((1,), (1,)), ((), ())), preferred_element_...  96.7 us
    dot_general x12, matrix products, dot_t(): lax.dot_general(left, right, (((0,), (0,)), ((), ())), preferred_element_...  73.3 us
    pallas_call x2, Pallas kernels, scan_forward(): pl.pallas_call(partial(scan_body, C // LANES, width), grid=(T // tb,), in...  63.8 us
    unnamed x292, local copies, waits for them, and re-layouts  58.6 us
    ppermute x3, waiting for transfers between devices, across(): return lax.ppermute(half, 'tensor', ACROSS)  47.7 us
    ppermute x12, waiting for transfers between devices, along(): lax.ppermute(value, 'blk', [(2 * s + k, 2 * d + k) for s, d in pairs for...  37.6 us
  transfers between devices with their start and end apart: 54, of which 29 were waited for; matrix products, arithmetic and copies ran while one was open for 27% of the time, Pallas kernels for 37%

profile of v3, /device:TPU:0, one launch (start us, length us, event | category | flops | bytes accessed | tf_op | source)
XLA Modules:
  0.0 1388.0 jit_solution(7353436807925210799)
XLA Ops:
  8.1 14.1 %fusion.192 = (bf16[1,2048,2,1024]{3,2,1,0:T(2,128)(2,1)}, bf16[1,2048,2,1024]{3,2,1,0:T(2,128)(2,1)S(1)}) fusion(bf16[2,2048,2,1024]{3,2,1,0:T(2,128)(2,1)} %param.17), kind=kLoop, calls=%fused_computation.431 | loop fusion | bytes 33554432 | tf_op jit(solution)/shard_map/slice | solution.py:611
  76.2 16.5 %end_states.2 = f32[16,8,1024]{2,1,0:T(8,128)S(1)} custom-call(f32[128,8,1024]{2,1,0:T(8,128)S(1)} %bitcast.506, f32[128,8,1024]{2,1,0:T(8,128)S(1)} %fusion.25.push_ref, f32[128,8,32]{2,1,0:T(8,128)S(1)} %bitcast.518, f32[16,1024]{1,0:T(8,128)S(1)} %get-tuple-element.305.rate_ref), custom_call_target="tpu_custom_call" | custom-call | flops 67108864 | bytes 67108864 | tf_op jit(solution)/shard_map/end_states/pallas_call | solution.py:58
  125.4 32.2 %scan_forward.2 = (f32[128,8,1024]{2,1,0:T(8,128)S(1)}, f32[128,16,8,1024]{3,2,1,0:T(8,128)}, f32[16,8,1024]{2,1,0:T(8,128)S(1)}) custom-call(f32[128,8,1024]{2,1,0:T(8,128)} %bitcast.507, f32[128,8,1024]{2,1,0:T(8,128)} %copy-done.5, f32[128,8,32]{2,1,0:T(8,128)S(1)} %bitcast.519, f32[16,1024]{1,0:T(8,128)S(1)} %get-tuple-element.305.rate_ref, ...), custom_call_target="tpu_custom_call" | custom-call | flops 117440512 | bytes 117440512 | tf_op jit(solution)/shard_map/scan_forward/pallas_call | solution.py:107
  191.0 13.1 fusion.193
  224.7 47.7 %collective-permute-done.10 = f32[512,2048]{1,0:T(8,128)} collective-permute-done((f32[512,2048]{1,0:T(8,128)}, f32[512,2048]{1,0:T(8,128)}, u32[]{:S(2)}, u32[]{:S(2)}) %collective-permute-start.10) | collective-permute-done | bytes 4194336 | tf_op jit(solution)/shard_map/ppermute | solution.py:301
  290.5 13.0 fusion.81
  345.9 16.7 %start_grads.2 = f32[16,8,1024]{2,1,0:T(8,128)S(1)} custom-call(f32[128,8,1024]{2,1,0:T(8,128)S(1)} %bitcast.510, f32[128,8,1024]{2,1,0:T(8,128)S(1)} %bitcast.514, f32[128,8,32]{2,1,0:T(8,128)S(1)} %bitcast.522, f32[16,1024]{1,0:T(8,128)S(1)} %get-tuple-element.304.rate_ref), custom_call_target="tpu_custom_call" | custom-call | flops 67108864 | bytes 67108864 | tf_op jit(solution)/shard_map/start_grads/pallas_call | solution.py:145
  362.6 16.5 %end_states.3 = f32[16,8,1024]{2,1,0:T(8,128)S(1)} custom-call(f32[128,8,1024]{2,1,0:T(8,128)S(1)} %bitcast.511, f32[128,8,1024]{2,1,0:T(8,128)S(1)} %get-tuple-element.264.push_ref, f32[128,8,32]{2,1,0:T(8,128)S(1)} %bitcast.523, f32[16,1024]{1,0:T(8,128)S(1)} %get-tuple-element.304.rate_ref), custom_call_target="tpu_custom_call" | custom-call | flops 67108864 | bytes 67108864 | tf_op jit(solution)/shard_map/end_states/pallas_call | solution.py:58
  379.7 14.9 %collective-permute-start.16 = (f32[9,8,1024]{2,1,0:T(8,128)S(1)}, f32[9,8,1024]{2,1,0:T(8,128)S(1)}, u32[]{:S(2)}, u32[]{:S(2)}) collective-permute-start(f32[9,8,1024]{2,1,0:T(8,128)S(1)} %get-tuple-element.315), channel_id=1, source_target_pairs={{0,4},{4,0},{8,12},{12,8},{16,20},{20,16},{24,28},{28,24},{1,5},{5... | collective-permute-start | bytes 884744 | tf_op jit(solution)/shard_map/ppermute | solution.py:552
  439.1 31.7 %scan_forward.3 = (f32[128,8,1024]{2,1,0:T(8,128)S(1)}, f32[128,16,8,1024]{3,2,1,0:T(8,128)}, f32[16,8,1024]{2,1,0:T(8,128)S(1)}) custom-call(f32[128,8,1024]{2,1,0:T(8,128)} %bitcast.512, f32[128,8,1024]{2,1,0:T(8,128)} %copy-done.6, f32[128,8,32]{2,1,0:T(8,128)S(1)} %bitcast.524, f32[16,1024]{1,0:T(8,128)S(1)} %get-tuple-element.304.rate_ref, ...), custom_call_target="tpu_custom_call" | custom-call | flops 117440512 | bytes 117440512 | tf_op jit(solution)/shard_map/scan_forward/pallas_call | solution.py:107
  505.6 10.7 fusion.200
  536.9 59.5 %scan_backward.2 = (f32[128,8,1024]{2,1,0:T(8,128)}, f32[128,8,1024]{2,1,0:T(8,128)}, f32[128,8,32]{2,1,0:T(8,128)S(1)}, f32[16,8,1024]{2,1,0:T(8,128)S(1)}, f32[16,8,1024]{2,1,0:T(8,128)S(1)}) custom-call(f32[128,8,1024]{2,1,0:T(8,128)} %bitcast.513, f32[128,8,1024]{2,1,0:T(8,128)} %copy-done.6, f32[128,8,1024]{2,1,0:T(8,128)} %bitcast.515, ...), custom_call_target="tpu_custom_call" | custom-call | flops 218103808 | bytes 218103808 | tf_op jit(solution)/shard_map/scan_backward/pallas_call | solution.py:231
  620.8 13.3 fusion.181
  665.1 157.1 %joint_sums.2 = (f32[512,2048]{1,0:T(8,128)}, f32[256,1024]{1,0:T(8,128)S(1)}, f32[23,1024]{1,0:T(8,128)S(1)}) custom-call(f32[1024,2048]{1,0:T(8,128)} %fusion.68.sum_ref, f32[2,2,2,256,1024]{4,3,2,1,0:T(8,128)} %bitcast.552, f32[23,1024]{1,0:T(8,128)S(1)} %concatenate.157.refs_1_), custom_call_target="tpu_custom_call" | custom-call | bytes 419430400 | tf_op jit(solution)/shard_map/joint_sums/pallas_call | solution.py:504
  838.7 17.6 %fusion.27 = (f32[1024]{0:T(1024)S(1)}, f32[1024,1024]{1,0:T(8,128)S(1)}, bf16[1024,1024]{1,0:T(8,128)(2,1)}) fusion(bf16[1024,1024]{1,0:T(8,128)(2,1)} %copy-done.28, f32[2,1024,1024]{2,1,0:T(8,128)} %copy-done.50, f32[1024]{0:T(1024)S(1)} %bitcast.598, f32[128,8,1024]{2,1,0:T(8,128)} %copy-done.15, bf16[2,1024,2048]{2,1,0:T(8,128)(2,1)} %param.25, ...), kind=kOutput, calls=%fused_computation.59 | convolution fusion | flops 4321180672 | bytes 33562624 | tf_op jit(solution)/shard_map/dot_general | solution.py:594
  856.3 16.8 %start_grads.3 = f32[16,8,1024]{2,1,0:T(8,128)S(1)} custom-call(f32[128,8,1024]{2,1,0:T(8,128)S(1)} %bitcast.509, f32[128,8,1024]{2,1,0:T(8,128)S(1)} %bitcast.516, f32[128,8,32]{2,1,0:T(8,128)S(1)} %bitcast.520, f32[16,1024]{1,0:T(8,128)S(1)} %copy-done.14), custom_call_target="tpu_custom_call" | custom-call | flops 67108864 | bytes 67108864 | tf_op jit(solution)/shard_map/start_grads/pallas_call | solution.py:145
  875.1 15.1 %collective-permute-done.33 = f32[9,8,1024]{2,1,0:T(8,128)S(1)} collective-permute-done((f32[9,8,1024]{2,1,0:T(8,128)S(1)}, f32[9,8,1024]{2,1,0:T(8,128)S(1)}, u32[]{:S(2)}, u32[]{:S(2)}) %collective-permute-start.33) | collective-permute-done | bytes 294944 | tf_op jit(solution)/shard_map/ppermute | solution.py:552
  893.0 14.9 %fusion.35 = f32[2048,1024]{1,0:T(8,128)} fusion(bf16[1024,1024]{1,0:T(8,128)(2,1)} %copy-done.64, f32[512,2048]{1,0:T(8,128)} %get-tuple-element.257, f32[512,2048]{1,0:T(8,128)} %get-tuple-element.256, bf16[8,128,2048]{2,1,0:T(8,128)(2,1)} %param.15), kind=kOutput, calls=%fused_computation.67 | convolution fusion | flops 4303355904 | bytes 23068672 | tf_op jit(solution)/shard_map/dot_general | solution.py:590
  915.2 12.3 fusion.98
  939.8 10.7 fusion.58
  980.0 59.2 %scan_backward.3 = (f32[128,8,1024]{2,1,0:T(8,128)}, f32[128,8,1024]{2,1,0:T(8,128)}, f32[128,8,32]{2,1,0:T(8,128)S(1)}, f32[16,8,1024]{2,1,0:T(8,128)S(1)}, f32[16,8,1024]{2,1,0:T(8,128)S(1)}) custom-call(f32[128,8,1024]{2,1,0:T(8,128)} %bitcast.508, f32[128,8,1024]{2,1,0:T(8,128)} %copy-done.5, f32[128,8,1024]{2,1,0:T(8,128)} %bitcast.517, ...), custom_call_target="tpu_custom_call" | custom-call | flops 218103808 | bytes 218103808 | tf_op jit(solution)/shard_map/scan_backward/pallas_call | solution.py:231
  1075.1 11.9 fusion.180
  1098.2 11.0 fusion.86.refs_0_
  1130.6 185.9 %joint_sums.3 = (f32[512,2048]{1,0:T(8,128)}, f32[256,1024]{1,0:T(8,128)S(1)}, f32[80,1024]{1,0:T(8,128)S(1)}, f32[32,1024]{1,0:T(8,128)S(1)}) custom-call(f32[1024,2048]{1,0:T(8,128)} %fusion.71.sum_ref, f32[2,2,2,256,1024]{4,3,2,1,0:T(8,128)} %fusion.86.refs_0_, f32[2,2,2,80,1024]{4,3,2,1,0:T(8,128)} %bitcast.547, f32[32,1024]{1,0:T(8,128)S(1)} %pad.22.refs_2_), custom_call_target="tpu_custom_call" | custom-call | bytes 419430400 | tf_op jit(solution)/shard_map/joint_sums/pallas_call | solution.py:504
  (612 shorter events, 557.1 us)
Async XLA Ops:
  7.2 943.5 %reduce-scatter.5.cloned.1.call-start = ((), (), s32[]{:S(2)}) async-start(), calls=%async_computation.4 | async-start | bytes 9437184 | tf_op jit(solution)/shard_map/reduce_scatter | solution.py:330
  179.5 92.9 %collective-permute-start.10 = (f32[512,2048]{1,0:T(8,128)}, f32[512,2048]{1,0:T(8,128)}, u32[]{:S(2)}, u32[]{:S(2)}) collective-permute-start(f32[512,2048]{1,0:T(8,128)} %dynamic-slice_add_fusion.1), channel_id=1, source_target_pairs={{0,2},{2,0},{1,3},{3,1},{4,6},{6,4},{5,7},{7,5},{8,10},{10,8},{9,1... | collective-permute-start | bytes 12582920 | tf_op jit(solution)/shard_map/ppermute | solution.py:301
  379.7 22.8 %collective-permute-start.16 = (f32[9,8,1024]{2,1,0:T(8,128)S(1)}, f32[9,8,1024]{2,1,0:T(8,128)S(1)}, u32[]{:S(2)}, u32[]{:S(2)}) collective-permute-start(f32[9,8,1024]{2,1,0:T(8,128)S(1)} %get-tuple-element.315), channel_id=1, source_target_pairs={{0,4},{4,0},{8,12},{12,8},{16,20},{20,16},{24,28},{28,24},{1,5},{5... | collective-permute-start | bytes 884744 | tf_op jit(solution)/shard_map/ppermute | solution.py:552
  394.6 14.0 %collective-permute-start.21 = (f32[9,8,1024]{2,1,0:T(8,128)S(1)}, f32[9,8,1024]{2,1,0:T(8,128)S(1)}, u32[]{:S(2)}, u32[]{:S(2)}) collective-permute-start(f32[9,8,1024]{2,1,0:T(8,128)S(1)} %get-tuple-element.316), channel_id=1, source_target_pairs={{0,4},{4,0},{8,12},{12,8},{16,20},{20,16},{24,28},{28,24},{1,5},{5... | collective-permute-start | bytes 884744 | tf_op jit(solution)/shard_map/ppermute | solution.py:552
  408.8 11.7 collective-permute-start.17
  421.2 13.0 collective-permute-start.22
  423.4 15.2 %collective-permute-start.20 = (f32[8,8,1024]{2,1,0:T(8,128)S(1)}, f32[8,8,1024]{2,1,0:T(8,128)S(1)}, u32[]{:S(2)}, u32[]{:S(2)}) collective-permute-start(f32[8,8,1024]{2,1,0:T(8,128)S(1)} %get-tuple-element.219), channel_id=1, source_target_pairs={{0,4},{4,0},{8,12},{12,8},{16,20},{20,16},{24,28},{28,24},{1,5},{5... | collective-permute-start | bytes 786440 | tf_op jit(solution)/shard_map/ppermute | solution.py:572
  435.8 52.8 %collective-permute-start.24 = (f32[8,8,1024]{2,1,0:T(8,128)}, f32[8,8,1024]{2,1,0:T(8,128)}, u32[]{:S(2)}, u32[]{:S(2)}) collective-permute-start(f32[8,8,1024]{2,1,0:T(8,128)} %slice.504), channel_id=1, source_target_pairs={{16,0},{20,4},{17,1},{21,5},{18,2},{22,6},{19,3},{23,7}} | collective-permute-start | bytes 786440 | tf_op jit(solution)/shard_map/ppermute | solution.py:563
  437.1 50.6 %collective-permute-start.23 = (f32[9,8,1024]{2,1,0:T(8,128)}, f32[9,8,1024]{2,1,0:T(8,128)}, u32[]{:S(2)}, u32[]{:S(2)}) collective-permute-start(f32[9,8,1024]{2,1,0:T(8,128)} %collective-permute-done.22), channel_id=1, source_target_pairs={{16,8},{20,12},{8,0},{12,4},{17,9},{21,13},{9,1},{13,5},{18,10},{2... | collective-permute-start | bytes 884744 | tf_op jit(solution)/shard_map/ppermute | solution.py:563
  486.8 40.2 %collective-permute-start.26 = (f32[512,2048]{1,0:T(8,128)}, f32[512,2048]{1,0:T(8,128)}, u32[]{:S(2)}, u32[]{:S(2)}) collective-permute-start(f32[512,2048]{1,0:T(8,128)} %constant_dynamic-slice_fusion.2), channel_id=1, source_target_pairs={{0,1},{1,0},{2,3},{3,2},{4,5},{5,4},{6,7},{7,6},{8,9},{9,8},{10,11... | collective-permute-start | bytes 12582920 | tf_op jit(solution)/shard_map/ppermute | solution.py:295
  533.5 417.2 %reduce-scatter.7.cloned.1.call-start = ((), (), s32[]{:S(2)}) async-start(), calls=%async_computation.5 | async-start | bytes 9437184 | tf_op jit(solution)/shard_map/reduce_scatter | solution.py:330
  535.4 61.9 %collective-permute-start.27 = (f32[256,2048]{1,0:T(8,128)S(1)}, f32[256,2048]{1,0:T(8,128)}, u32[]{:S(2)}, u32[]{:S(2)}) collective-permute-start(f32[256,2048]{1,0:T(8,128)S(1)} %slice.437), channel_id=1, source_target_pairs={{0,2},{2,0},{1,3},{3,1},{4,6},{6,4},{5,7},{7,5},{8,10},{10,8},{9,1... | collective-permute-start | bytes 6291464 | tf_op jit(solution)/shard_map/ppermute | solution.py:301
  619.8 748.9 %reduce-scatter.11.cloned.1.call-start = ((), (), s32[]{:S(2)}) async-start(), calls=%async_computation.7 | async-start | bytes 9437184 | tf_op jit(solution)/shard_map/reduce_scatter | solution.py:330
  874.2 16.0 %collective-permute-start.33 = (f32[9,8,1024]{2,1,0:T(8,128)S(1)}, f32[9,8,1024]{2,1,0:T(8,128)S(1)}, u32[]{:S(2)}, u32[]{:S(2)}) collective-permute-start(f32[9,8,1024]{2,1,0:T(8,128)S(1)} %pad_maximum_fusion.18), channel_id=1, source_target_pairs={{0,4},{4,0},{8,12},{12,8},{16,20},{20,16},{24,28},{28,24},{1,5},{5... | collective-permute-start | bytes 884744 | tf_op jit(solution)/shard_map/ppermute | solution.py:552
  891.3 22.7 %collective-permute-start.34 = (f32[9,8,1024]{2,1,0:T(8,128)S(1)}, f32[9,8,1024]{2,1,0:T(8,128)S(1)}, u32[]{:S(2)}, u32[]{:S(2)}) collective-permute-start(f32[9,8,1024]{2,1,0:T(8,128)S(1)} %pad_maximum_fusion.25), channel_id=1, source_target_pairs={{24,16},{28,20},{16,8},{20,12},{8,0},{12,4},{25,17},{29,21},{17,9}... | collective-permute-start | bytes 884744 | tf_op jit(solution)/shard_map/ppermute | solution.py:563
  913.9 14.9 %collective-permute-start.35 = (f32[9,8,1024]{2,1,0:T(8,128)S(1)}, f32[9,8,1024]{2,1,0:T(8,128)S(1)}, u32[]{:S(2)}, u32[]{:S(2)}) collective-permute-start(f32[9,8,1024]{2,1,0:T(8,128)S(1)} %collective-permute-done.34), channel_id=1, source_target_pairs={{16,8},{20,12},{8,0},{12,4},{17,9},{21,13},{9,1},{13,5},{18,10},{2... | collective-permute-start | bytes 884744 | tf_op jit(solution)/shard_map/ppermute | solution.py:563
  927.5 10.5 collective-permute-start.36
  938.2 12.3 collective-permute-start.37
  950.7 421.7 %reduce-scatter.9.cloned.1.call-start = ((), (), s32[]{:S(2)}) async-start(), calls=%async_computation.6 | async-start | bytes 9437184 | tf_op jit(solution)/shard_map/reduce_scatter | solution.py:330
  954.3 84.9 %collective-permute-start.38 = (f32[256,2048]{1,0:T(8,128)}, f32[256,2048]{1,0:T(8,128)}, u32[]{:S(2)}, u32[]{:S(2)}) collective-permute-start(f32[256,2048]{1,0:T(8,128)} %slice.451), channel_id=1, source_target_pairs={{0,2},{2,0},{1,3},{3,1},{4,6},{6,4},{5,7},{7,5},{8,10},{10,8},{9,1... | collective-permute-start | bytes 6291464 | tf_op jit(solution)/shard_map/ppermute | solution.py:301
  1048.2 11.9 collective-permute-start.39
  1062.5 11.4 collective-permute-start.44
  1073.3 46.5 %collective-permute-start.43 = (f32[512,2048]{1,0:T(8,128)}, f32[512,2048]{1,0:T(8,128)}, u32[]{:S(2)}, u32[]{:S(2)}) collective-permute-start(f32[512,2048]{1,0:T(8,128)} %get-tuple-element.244), channel_id=1, source_target_pairs={{0,1},{1,0},{2,3},{3,2},{4,5},{5,4},{6,7},{7,6},{8,9},{9,8},{10,11... | collective-permute-start | bytes 12582920 | tf_op jit(solution)/shard_map/ppermute | solution.py:307
  1322.8 25.0 %collective-permute-start.45 = (f32[512,2048]{1,0:T(8,128)}, f32[512,2048]{1,0:T(8,128)}, u32[]{:S(2)}, u32[]{:S(2)}) collective-permute-start(f32[512,2048]{1,0:T(8,128)} %multiply_subtract_fusion), channel_id=1, source_target_pairs={{0,1},{1,0},{2,3},{3,2},{4,5},{5,4},{6,7},{7,6},{8,9},{9,8},{10,11... | collective-permute-start | bytes 12582920 | tf_op jit(solution)/shard_map/ppermute | solution.py:307
  (169 other events, 3478.1 us)
Sparse Core Ops, SparseCore 0:
  533.6 163.1 reduce-scatter.4
  700.9 215.2 reduce-scatter.6
  950.8 147.4 reduce-scatter.10
  1102.3 228.3 reduce-scatter.8

commit v4 on v3

--- a/solution.py
+++ b/solution.py
@@ -284,10 +284,6 @@
     return half_of(array, lax.axis_index("tensor") % 2)
 
 
-def ordered_after(value, *others):
-    return lax.optimization_barrier((value,) + others)[0]
-
-
 def core_sum(array):
     if not paired():
         return lax.psum_scatter(array, "tensor", scatter_dimension=0, tiled=True)
@@ -312,10 +308,6 @@
     if not paired():
         return lax.psum(array, "tensor")
     return array + lax.ppermute(array, "tensor", BESIDE)
-
-
-def chosen(array, axis, index):
-    return lax.dynamic_index_in_dim(array, index, axis, keepdims=False)
 
 
 def blk_sum(array):
@@ -478,7 +470,7 @@
         copy.wait()
 
 
-def joint_sums(array, thick, small, collective_id):
+def joint_sums(array, thick, late, small, collective_id):
     if not paired() or lax.axis_size("blk") != 8:
         return (lax.psum_scatter(array, "tensor", scatter_dimension=0, tiled=True),
                 [blk_scatter(part) for part in thick], lax.psum(small, "blk"))
@@ -489,11 +481,8 @@
     dma = pltpu.SemaphoreType.DMA
     any_spec = pl.BlockSpec(memory_space=pl.ANY)
     vmem_spec = pl.BlockSpec(memory_space=pltpu.VMEM)
-    cut = C - 128 if len(thick) == 1 else C
-    plan = [(0, 0, cut, (1, 2, 4))]
-    if cut < C:
-        plan.append((0, cut, C - cut, (2, 4, 1)))
-    plan += [(i, 0, C, (2, 4, 1)) for i in range(1, len(thick))]
+    plan = [(i, 0, C - each, (1, 2, 4)) for i, each in enumerate(late) if each < C]
+    plan += [(i, C - each, each, (2, 4, 1)) for i, each in enumerate(late) if each]
     scratch = []
     for which, _, wide, _ in plan:
         count = thick[which].shape[0] // 8
@@ -536,42 +525,131 @@
     return lax.fori_loop(0, peers, step, first)
 
 
-def entering(total, local, rate, first, reverse):
-    if lax.axis_size("blk") != 8:
-        return entering_any(total, local, rate, first, reverse)
-    index = lax.axis_index("blk")
-    y, z = index % 2, index // 2
-    pair = [(j, j ^ 1) for j in range(8)]
-    if reverse:
-        y, z = 1 - y, 3 - z
-    sign = -1 if reverse else 1
-    at_a = y == 0
-    decay = jnp.exp2(total[None] * rate)
-    own = local + jnp.where(jnp.logical_and(z == 0, at_a), decay * first, 0.0)
-    mine, give = half_of(own, y), half_of(own, 1 - y)
-    got = lax.ppermute(jnp.concatenate([give, total[None]], axis=0), "blk", pair)
-    got, got_total = got[:-1], got[-1]
-    rate_half = half_of(rate, y)
-    local_a, local_b = jnp.where(at_a, mine, got), jnp.where(at_a, got, mine)
-    total_a, total_b = jnp.where(at_a, total, got_total), jnp.where(at_a, got_total, total)
-    joined = local_b + jnp.exp2(total_b[None] * rate_half) * local_a
-    message = jnp.concatenate([joined, (total_a + total_b)[None]], axis=0)
-
-    def along(value, pairs):
-        if reverse:
-            pairs = [(3 - s, 3 - d) for s, d in pairs]
-        return lax.ppermute(value, "blk", [(2 * s + k, 2 * d + k) for s, d in pairs for k in (0, 1)])
-
-    one = along(message, [(0, 1), (1, 2), (2, 3)])
-    two = along(one, [(1, 2), (2, 3)])
-    three = along(one[:-1], [(1, 3)])
-    enter = one[:-1] + jnp.exp2(one[-1:] * rate_half) * (
-        two[:-1] + jnp.exp2(two[-1:] * rate_half) * three
-    )
-    after_a = local_a + jnp.exp2(total_a[None] * rate_half) * enter
-    other = lax.ppermute(jnp.where(at_a, after_a, enter), "blk", pair)
-    state = ordered(y, jnp.where(at_a, enter, after_a), other)
-    return jnp.where(jnp.logical_and(z == 0, at_a), first, state)
+def hop_body(reverses, groups, total_ref, rate_ref, *refs):
+    ways = len(reverses)
+    locals_, first_ref, refs = refs[:ways], refs[ways], refs[ways + 1:]
+    outs, refs = refs[:ways], refs[ways:]
+    beside_total, total_send, total_recv, refs = refs[0], refs[1], refs[2], refs[3:]
+    blk, tensor = lax.axis_index("blk"), lax.axis_index("tensor")
+    y, z = blk % 2, blk // 2
+    beside = (blk + 1 - 2 * y, tensor)
+    up, down = ((blk + 2) % 8, tensor), ((blk + 6) % 8, tensor)
+    barrier = pltpu.get_barrier_semaphore()
+
+    def greet(device):
+        pl.semaphore_signal(barrier, inc=1, device_id=device, device_id_type=pl.DeviceIdType.MESH)
+
+    greet(beside)
+    pl.when(z < 3)(lambda: greet(up))
+    pl.when(z > 0)(lambda: greet(down))
+    pl.semaphore_wait(barrier, 3 - z // 3 - (3 - z) // 3)
+
+    total = total_ref[...]
+    copy_total = remote(total_ref, beside_total, total_send, total_recv, 0, beside)
+    copy_total.start()
+    size = STATE // 2 // groups
+
+    class Way:
+        def __init__(self, reverse, local, out, refs):
+            self.own, self.other, self.came, self.goes, self.gives, self.gets = refs[:6]
+            self.sems, self.out, self.reverse = refs[6:], out, reverse
+            self.y, self.z = (1 - y, 3 - z) if reverse else (y, z)
+            self.following = down if reverse else up
+            self.at_a, self.begins = self.y == 0, self.z == 0
+            self.firsts = []
+            for n in range(STATE):
+                value = local[n]
+                if not reverse:
+                    decay = jnp.exp2(total * rate_ref[pl.ds(n, 1), :])
+                    value = value + jnp.where(jnp.logical_and(self.begins, self.at_a), decay * first_ref[n], 0.0)
+                self.own[n] = value
+            for k in range(groups):
+                give = pl.ds((1 - self.y) * (STATE // 2) + k * size, size)
+                copy = remote(self.own.at[give], self.other.at[pl.ds(k * size, size)], self.sems[0], self.sems[1], k, beside)
+                copy.start()
+                self.firsts.append(copy)
+
+        def chain(self, k):
+            part = pl.ds(k * size, size)
+            return remote(self.goes.at[part], self.came.at[part], self.sems[2], self.sems[3], k, self.following)
+
+        def middle(self, k, total_a, total_b):
+            self.firsts[k].wait()
+            pl.when(self.z > 0)(lambda: self.chain(k).wait_recv())
+            for i in range(k * size, k * size + size):
+                n = self.y * (STATE // 2) + i
+                rate = rate_ref[pl.ds(n, 1), :]
+                mine, got = self.own[n], self.other[i]
+                local_a, local_b = jnp.where(self.at_a, mine, got), jnp.where(self.at_a, got, mine)
+                enter = jnp.where(self.begins, 0.0, self.came[i])
+                after_a = local_a + jnp.exp2(total_a * rate) * enter
+                self.goes[i] = local_b + jnp.exp2(total_b * rate) * after_a
+                self.gives[i] = jnp.where(self.at_a, after_a, enter)
+                self.out[n] = jnp.where(self.at_a, enter, after_a)
+            pl.when(self.z < 3)(lambda: self.chain(k).start())
+            self.last(k).start()
+
+        def last(self, k):
+            part = pl.ds(k * size, size)
+            return remote(self.gives.at[part], self.gets.at[part], self.sems[4], self.sems[5], k, beside)
+
+        def all(self):
+            other_total = beside_total[...]
+            total_a, total_b = jnp.where(self.at_a, total, other_total), jnp.where(self.at_a, other_total, total)
+            for k in range(groups):
+                self.middle(k, total_a, total_b)
+
+        def end(self, k):
+            self.last(k).wait()
+            for i in range(k * size, k * size + size):
+                self.out[(1 - self.y) * (STATE // 2) + i] = self.gets[i]
+            pl.when(self.z < 3)(lambda: self.chain(k).wait_send())
+
+        def begin(self):
+            starts = jnp.logical_and(self.begins, self.at_a)
+            for n in range(STATE):
+                first = 0.0 if self.reverse else first_ref[n]
+                self.out[n] = jnp.where(starts, first, self.out[n])
+
+    each = 6 + 6
+    jobs = [Way(reverse, locals_[i], outs[i], refs[each * i:each * i + each]) for i, reverse in enumerate(reverses)]
+    copy_total.wait()
+    if ways == 1:
+        jobs[0].all()
+    else:
+
+        def in_turn(order):
+            for job in order:
+                job.all()
+
+        pl.when(z < 2)(lambda: in_turn(jobs))
+        pl.when(z >= 2)(lambda: in_turn(jobs[::-1]))
+    for k in range(groups):
+        for job in jobs:
+            job.end(k)
+    for job in jobs:
+        job.begin()
+
+
+def hops(total, locals_, rate, first, reverses, collective_id):
+    C = total.shape[-1]
+    groups = 4
+    f32 = jnp.float32
+    dma = pltpu.SemaphoreType.DMA
+    spec = pl.BlockSpec(memory_space=pltpu.VMEM)
+    whole, half = pltpu.VMEM((STATE, 8, C), f32), pltpu.VMEM((STATE // 2, 8, C), f32)
+    return pl.pallas_call(
+        partial(hop_body, reverses, groups),
+        in_specs=[spec] * (3 + len(locals_)),
+        out_specs=[spec] * len(locals_),
+        out_shape=[jax.ShapeDtypeStruct((STATE, 8, C), f32)] * len(locals_),
+        scratch_shapes=[pltpu.VMEM((8, C), f32), dma((1,)), dma((1,))]
+        + ([whole] + [half] * 5 + [dma((groups,))] * 6) * len(locals_),
+        compiler_params=pltpu.CompilerParams(
+            collective_id=collective_id, has_side_effects=True, vmem_limit_bytes=32 * 2**20),
+        cost_estimate=pl.CostEstimate(flops=0, bytes_accessed=100 * total.size * 32, transcendentals=0),
+        name="hops",
+    )(total, rate, *locals_, first)
 
 
 def rows(array):
@@ -608,7 +686,7 @@
         (norm_gain, in_weight, conv_weight, conv_bias, x_weight, dt_weight, dt_bias, decay_log,
          skip_weight, out_weight) = args
         self.gain = norm_gain[index]
-        self.raw = in_weight[index]
+        self.raw = in_weight[index] if index == 0 else None
         self.taps = conv_weight[index]
         self.shift = conv_bias[index]
         self.x = x_weight[index]
@@ -666,11 +744,16 @@
     return state.reshape(STATE, 8, state.shape[-1])
 
 
-def exchange(layer, local, totals, first, reverse):
+def exchange(layer, locals_, totals, first, reverses, collective_id):
     rate = layer.rate2[:, None]
-    total, joined = join(local, totals, rate, reverse)
-    state = entering(total, joined, rate, first, reverse)
-    return each_part(state, local, totals, rate, reverse)
+    if lax.axis_size("blk") == 8 and totals.shape[0] == 1:
+        return hops(totals[0], [local[:, 0] for local in locals_], layer.rate2, first, reverses, collective_id)
+    states = []
+    for local, reverse in zip(locals_, reverses):
+        total, joined = join(local, totals, rate, reverse)
+        state = entering_any(total, joined, rate, jnp.zeros_like(first) if reverse else first, reverse)
+        states.append(each_part(state, local, totals, rate, reverse))
+    return states
 
 
 def scanning(layer, kept, start):
@@ -802,17 +885,20 @@
         kept[l], local, tails[l] = front(
             layer, normed, jnp.moveaxis(conv_init[l], 1, 0), parts, at_first)
         totals = kept[l][-1]
+        first = jnp.moveaxis(scan_init[l], 1, 0)
         if l == last:
             grads = back_gated(layer, kept[l], grad_low)
-            local, late = lax.optimization_barrier((local, back_local(layer, kept[l], grads[1])))
-            end = exchange(layer, late, totals, jnp.zeros_like(late[:, 0]), True)
-        start = exchange(layer, local, totals, jnp.moveaxis(scan_init[l], 1, 0), False)
+            late = back_local(layer, kept[l], grads[1])
+            start, end = exchange(layer, [local, late], totals, first, (False, True), layer_total + l)
+        else:
+            start, = exchange(layer, [local], totals, first, (False,), layer_total + l)
         partial_sum, scans[l], final = scanning(layer, kept[l], start)
         finals[l] = split_parts(final, parts)[:, -1]
         half = core_sum(partial_sum)
         if l < last:
             half, stored = lax.optimization_barrier((half, weights[1]))
             into = [stored[k].reshape(width, -1) for k in range(layer_total)]
+            layers[l + 1].raw = stored[l + 1]
             got, into, grad_low = lax.optimization_barrier((across(half), into, grad_low))
             for each, array in zip(layers, into):
                 each.into = array
@@ -828,21 +914,23 @@
         layer = layers[l]
         normed, base = norms[l]
         if l < last:
-            grads = back_gated(layer, kept[l], grad_low)
+            grads, out_grad, scattered[last] = lax.optimization_barrier(
+                (back_gated(layer, kept[l], grad_low), dot_t(grad_low, scans[l][1]), scattered[last]))
+            scattered[l] = [blk_scatter(out_grad)]
             late = back_local(layer, kept[l], grads[1])
-            end = exchange(layer, late, kept[l][-1], jnp.zeros_like(late[:, 0]), True)
-        out_grad = dot_t(grad_low, scans[l][1])
+            end, = exchange(layer, [late], kept[l][-1], jnp.zeros_like(late[:, 0]), (True,), 2 + 2 * layer_total + l)
+        else:
+            out_grad = dot_t(grad_low, scans[l][1])
         side = back_side(layer, kept[l], normed, scans[l], grads, grad_low)
         middle = half.shape[0] // 2
         if l == last:
             end, side, out_grad, half = lax.optimization_barrier((end, side, out_grad, half))
-            scattered[l] = [blk_scatter(out_grad), blk_scatter(side[0])]
+            scattered[l] = [blk_scatter(out_grad)]
             scan_out, got = lax.optimization_barrier(
                 (back_scan(layer, kept[l], scans[l], grads, end), across(half[:middle])))
         else:
-            end, side, out_grad, half, scattered[last] = lax.optimization_barrier(
-                (end, side, out_grad, half, scattered[last]))
-            scattered[l] = [blk_scatter(out_grad), blk_scatter(side[0])]
+            end, side, half = lax.optimization_barrier((end, side, half))
+            scattered[l].append(blk_scatter(side[0]))
             scan_out, got_rest = lax.optimization_barrier(
                 (back_scan(layer, kept[l], scans[l], grads, end), across(half[middle:])))
             branch = half + jnp.concatenate([got, got_rest], axis=0)
@@ -857,8 +945,9 @@
         inner = smalls[l].shape[-1]
         if l == last:
             thins = thick[1:] + thins
-            normed_grad, thick, smalls[l] = joint_sums(normed_part, [rows(thick[0])], smalls[l], l)
-            scattered[l].append(thick[0])
+            normed_grad, thick, smalls[l] = joint_sums(
+                normed_part, [rows(thick[0]), side[0]], (128, 128), smalls[l], l)
+            scattered[l] += [thick[1], thick[0]]
         else:
             thins = thick[1:] + thins
             cuts = [part.shape[1] for part in thins]
@@ -871,7 +960,7 @@
             small = jnp.pad(small, ((0, -small.shape[0] % 8), (0, 0)))
             normed_part, thins, out = lax.optimization_barrier((normed_part, thins, out))
             normed_grad, thick, small = joint_sums(
-                normed_part, [rows(thick[0]), rows(jnp.concatenate(thins, axis=1))], small, l)
+                normed_part, [rows(thick[0]), rows(jnp.concatenate(thins, axis=1))], (0, inner), small, l)
             scattered[l].append(thick[0])
             smalls[l], rest = small[:own_count], small[own_count:]
         gains[l], change = norm_back(layer, normed_grad, base, inverse_rms(base))

time: 1400 us -> 1420 us (1.014)
  Pallas kernels: 592 us -> 760 us
  waiting for transfers between devices: 209 us -> 103 us
  starting transfers between devices: 70.9 us -> 29.3 us
  matrix products: 213 us -> 194 us
  local copies, waits for them, and re-layouts: 126 us -> 142 us
    pallas_call x0 -> x3, Pallas kernels: none -> 97.7 us  [hops(): pl.pallas_call(partial(hop_body, reverses, groups), in_specs=[spec] * (3...]
    ppermute x20 -> x0, waiting for transfers between devices: 87.4 us -> none  [the longest x12 37.6 us: along(): lax.ppermute(value, 'blk', [(2 * s + k, 2 * d + k) for s, d in pairs for...]
    pallas_call x2, Pallas kernels: 343 us -> 414 us  [joint_sums(): pl.pallas_call(partial(joint_body, plan, chunks), in_specs=[any_spec] * (...]
    ppermute x20 -> x0, starting transfers between devices: 41.7 us -> none  [the longest x12 20.2 us: along(): lax.ppermute(value, 'blk', [(2 * s + k, 2 * d + k) for s, d in pairs for...]
    ppermute x3, waiting for transfers between devices: 47.7 us -> 33.5 us  [across(): return lax.ppermute(half, 'tensor', ACROSS)]
    unnamed x292 -> x287, local copies, waits for them, and re-layouts: 58.6 us -> 61.3 us
  transfers between devices with their start and end apart: 54 -> 33, of which waited for: 29 -> 18; matrix products, arithmetic and copies ran while one was open for 27% -> 24% of each run, Pallas kernels for 37% -> 42%
where the time goes in v4:
time: 1420 us; the launch traced here: 1410 us
  Pallas kernels  760 us (54%)
  matrix products  194 us (14%)
  other arithmetic  165 us (12%)
  local copies, waits for them, and re-layouts  142 us (10%)
  waiting for transfers between devices  103 us (7%)
  starting transfers between devices  29.3 us (2%)
  between operations  18.1 us (1%)
    pallas_call x2, Pallas kernels, joint_sums(): pl.pallas_call(partial(joint_body, plan, chunks), in_specs=[any_spec] * (...  414 us
    pallas_call x2, Pallas kernels, scan_backward(): pl.pallas_call(partial(back_body, C // LANES, width), grid=(T // tb,), in...  119 us
    pallas_call x3, Pallas kernels, hops(): pl.pallas_call(partial(hop_body, reverses, groups), in_specs=[spec] * (3...  97.7 us
    dot_general x10, matrix products, dot_n(): lax.dot_general(left, right, (((1,), (1,)), ((), ())), preferred_element_...  86 us
    dot_general x12, matrix products, dot_t(): lax.dot_general(left, right, (((0,), (0,)), ((), ())), preferred_element_...  66 us
    pallas_call x2, Pallas kernels, scan_forward(): pl.pallas_call(partial(scan_body, C // LANES, width), grid=(T // tb,), in...  63.6 us
    unnamed x287, local copies, waits for them, and re-layouts  61.3 us
    ppermute x3, waiting for transfers between devices, across(): return lax.ppermute(half, 'tensor', ACROSS)  33.5 us
  transfers between devices with their start and end apart: 33, of which 18 were waited for; matrix products, arithmetic and copies ran while one was open for 24% of the time, Pallas kernels for 42%

profile of v4, /device:TPU:0, one launch (start us, length us, event | category | flops | bytes accessed | tf_op | source)
XLA Modules:
  0.0 1411.8 jit_solution(11478013038557393775)
XLA Ops:
  68.8 16.5 %end_states.2.refs_0_ = f32[16,8,1024]{2,1,0:T(8,128)S(1)} custom-call(f32[128,8,1024]{2,1,0:T(8,128)S(1)} %bitcast.444, f32[128,8,1024]{2,1,0:T(8,128)S(1)} %fusion.26.push_ref, f32[128,8,32]{2,1,0:T(8,128)S(1)} %bitcast.456, f32[16,1024]{1,0:T(8,128)S(1)} %get-tuple-element.270.rate_ref), custom_call_target="tpu_custom_call" | custom-call | flops 67108864 | bytes 67108864 | tf_op jit(solution)/shard_map/end_states/pallas_call | solution.py:58
  85.2 16.2 %hops.3.start_ref.begin_ref = f32[16,8,1024]{2,1,0:T(8,128)S(1)} custom-call(f32[8,1024]{1,0:T(8,128)S(1)} %get-tuple-element.287.total_ref, f32[16,1024]{1,0:T(8,128)S(1)} %get-tuple-element.270.rate_ref, f32[16,8,1024]{2,1,0:T(8,128)S(1)} %end_states.2.refs_0_, f32[16,8,1024]{2,1,0:T(8,128)S(1)} %get-tuple-element.296.refs_1_), custom_call_target="tpu_custom_call" | custom-call | bytes 26214400 | tf_op jit(solution)/shard_map/hops/pallas_call | solution.py:641
  101.5 31.7 %scan_forward.2 = (f32[128,8,1024]{2,1,0:T(8,128)S(1)}, f32[128,16,8,1024]{3,2,1,0:T(8,128)}, f32[16,8,1024]{2,1,0:T(8,128)S(1)}) custom-call(f32[128,8,1024]{2,1,0:T(8,128)} %bitcast.445, f32[128,8,1024]{2,1,0:T(8,128)} %copy-done.6, f32[128,8,32]{2,1,0:T(8,128)S(1)} %bitcast.457, f32[16,1024]{1,0:T(8,128)S(1)} %get-tuple-element.270.rate_ref, ...), custom_call_target="tpu_custom_call" | custom-call | flops 117440512 | bytes 117440512 | tf_op jit(solution)/shard_map/scan_forward/pallas_call | solution.py:107
  172.8 11.2 copy.60
  198.8 11.7 copy.61
  220.8 33.5 %collective-permute-done.5 = f32[512,2048]{1,0:T(8,128)} collective-permute-done((f32[512,2048]{1,0:T(8,128)}, f32[512,2048]{1,0:T(8,128)}, u32[]{:S(2)}, u32[]{:S(2)}) %collective-permute-start.5) | collective-permute-done | bytes 4194336 | tf_op jit(solution)/shard_map/ppermute | solution.py:297
  280.8 11.1 fusion.79
  331.6 16.7 %start_grads.2.refs_1_ = f32[16,8,1024]{2,1,0:T(8,128)S(1)} custom-call(f32[128,8,1024]{2,1,0:T(8,128)S(1)} %bitcast.448, f32[128,8,1024]{2,1,0:T(8,128)S(1)} %bitcast.454, f32[128,8,32]{2,1,0:T(8,128)S(1)} %bitcast.460, f32[16,1024]{1,0:T(8,128)S(1)} %get-tuple-element.269.rate_ref), custom_call_target="tpu_custom_call" | custom-call | flops 67108864 | bytes 67108864 | tf_op jit(solution)/shard_map/start_grads/pallas_call | solution.py:145
  348.3 16.5 %end_states.3.refs_0_ = f32[16,8,1024]{2,1,0:T(8,128)S(1)} custom-call(f32[128,8,1024]{2,1,0:T(8,128)S(1)} %bitcast.449, f32[128,8,1024]{2,1,0:T(8,128)S(1)} %get-tuple-element.249.push_ref, f32[128,8,32]{2,1,0:T(8,128)S(1)} %bitcast.461, f32[16,1024]{1,0:T(8,128)S(1)} %get-tuple-element.269.rate_ref), custom_call_target="tpu_custom_call" | custom-call | flops 67108864 | bytes 67108864 | tf_op jit(solution)/shard_map/end_states/pallas_call | solution.py:58
  364.8 39.0 %hops.4 = (f32[16,8,1024]{2,1,0:T(8,128)S(1)}, f32[16,8,1024]{2,1,0:T(8,128)S(1)}) custom-call(f32[8,1024]{1,0:T(8,128)S(1)} %get-tuple-element.289.total_ref, f32[16,1024]{1,0:T(8,128)S(1)} %get-tuple-element.269.rate_ref, f32[16,8,1024]{2,1,0:T(8,128)S(1)} %end_states.3.refs_0_, f32[16,8,1024]{2,1,0:T(8,128)S(1)} %start_grads.2.refs_1_, ...), custom_call_target="tpu_custom_call" | custom-call | bytes 26214400 | tf_op jit(solution)/shard_map/hops/pallas_call | solution.py:641
  403.8 31.9 %scan_forward.3 = (f32[128,8,1024]{2,1,0:T(8,128)S(1)}, f32[128,16,8,1024]{3,2,1,0:T(8,128)}, f32[16,8,1024]{2,1,0:T(8,128)S(1)}) custom-call(f32[128,8,1024]{2,1,0:T(8,128)} %bitcast.450, f32[128,8,1024]{2,1,0:T(8,128)} %copy-done.7, f32[128,8,32]{2,1,0:T(8,128)S(1)} %bitcast.462, f32[16,1024]{1,0:T(8,128)S(1)} %get-tuple-element.269.rate_ref, ...), custom_call_target="tpu_custom_call" | custom-call | flops 117440512 | bytes 117440512 | tf_op jit(solution)/shard_map/scan_forward/pallas_call | solution.py:107
  459.6 10.9 fusion.169
  484.8 59.3 %scan_backward.2 = (f32[128,8,1024]{2,1,0:T(8,128)}, f32[128,8,1024]{2,1,0:T(8,128)}, f32[128,8,32]{2,1,0:T(8,128)S(1)}, f32[16,8,1024]{2,1,0:T(8,128)S(1)}, f32[16,8,1024]{2,1,0:T(8,128)S(1)}) custom-call(f32[128,8,1024]{2,1,0:T(8,128)} %bitcast.451, f32[128,8,1024]{2,1,0:T(8,128)} %copy-done.7, f32[128,8,1024]{2,1,0:T(8,128)} %bitcast.455, ...), custom_call_target="tpu_custom_call" | custom-call | flops 218103808 | bytes 218103808 | tf_op jit(solution)/shard_map/scan_backward/pallas_call | solution.py:231
  567.1 12.9 fusion.157
  591.2 10.9 fusion.91
  602.1 10.7 fusion.69.sum_ref
  612.8 261.5 %joint_sums.2 = (f32[512,2048]{1,0:T(8,128)}, f32[256,1024]{1,0:T(8,128)S(1)}, f32[256,1024]{1,0:T(8,128)}, f32[23,1024]{1,0:T(8,128)S(1)}) custom-call(f32[1024,2048]{1,0:T(8,128)} %fusion.69.sum_ref, f32[2,2,2,256,1024]{4,3,2,1,0:T(8,128)} %bitcast.490, f32[2,2,2,256,1024]{4,3,2,1,0:T(8,128)} %bitcast.489, f32[23,1024]{1,0:T(8,128)S(1)} %concatenate.112.refs_2_), custom_call_target="tpu_custom_call" | custom-call | bytes 419430400 | tf_op jit(solution)/shard_map/joint_sums/pallas_call | solution.py:493
  901.3 16.1 %fusion.120 = (f32[1024,1024]{1,0:T(8,128)}, f32[1024,1024]{1,0:T(8,128)}) fusion(f32[2,1024,1024]{2,1,0:T(8,128)} %copy-done.44, bf16[2,1024,2048]{2,1,0:T(8,128)(2,1)} %param.25, f32[512,2048]{1,0:T(8,128)} %copy-done.51, f32[512,2048]{1,0:T(8,128)} %copy-done.49, bf16[8,128,2048]{2,1,0:T(8,128)(2,1)} %param.15), kind=kOutput, calls=%fused_computation.228 | convolution fusion | flops 4308598784 | bytes 29360128 | tf_op jit(solution)/shard_map/dot_general | solution.py:672
  922.7 16.7 %start_grads.3.refs_0_ = f32[16,8,1024]{2,1,0:T(8,128)S(1)} custom-call(f32[128,8,1024]{2,1,0:T(8,128)S(1)} %bitcast.447, f32[128,8,1024]{2,1,0:T(8,128)S(1)} %bitcast.453, f32[128,8,32]{2,1,0:T(8,128)S(1)} %bitcast.458, f32[16,1024]{1,0:T(8,128)S(1)} %copy-done.15), custom_call_target="tpu_custom_call" | custom-call | flops 67108864 | bytes 67108864 | tf_op jit(solution)/shard_map/start_grads/pallas_call | solution.py:145
  939.5 42.5 %hops.5.end_ref = f32[16,8,1024]{2,1,0:T(8,128)S(1)} custom-call(f32[8,1024]{1,0:T(8,128)S(1)} %copy-done.27, f32[16,1024]{1,0:T(8,128)S(1)} %copy-done.15, f32[16,8,1024]{2,1,0:T(8,128)S(1)} %start_grads.3.refs_0_, f32[16,8,1024]{2,1,0:T(8,128)S(1)} %broadcast_in_dim.45.refs_1_), custom_call_target="tpu_custom_call" | custom-call | bytes 26214400 | tf_op jit(solution)/shard_map/hops/pallas_call | solution.py:641
  1035.2 59.3 %scan_backward.3 = (f32[128,8,1024]{2,1,0:T(8,128)}, f32[128,8,1024]{2,1,0:T(8,128)}, f32[128,8,32]{2,1,0:T(8,128)S(1)}, f32[16,8,1024]{2,1,0:T(8,128)S(1)}, f32[16,8,1024]{2,1,0:T(8,128)S(1)}) custom-call(f32[128,8,1024]{2,1,0:T(8,128)} %bitcast.446, f32[128,8,1024]{2,1,0:T(8,128)} %copy-done.6, f32[128,8,1024]{2,1,0:T(8,128)} %bitcast.452, ...), custom_call_target="tpu_custom_call" | custom-call | flops 218103808 | bytes 218103808 | tf_op jit(solution)/shard_map/scan_backward/pallas_call | solution.py:231
  1127.7 12.0 fusion.156
  1153.4 11.0 fusion.89.refs_0_
  1186.1 152.6 %joint_sums.3 = (f32[512,2048]{1,0:T(8,128)}, f32[256,1024]{1,0:T(8,128)S(1)}, f32[80,1024]{1,0:T(8,128)S(1)}, f32[32,1024]{1,0:T(8,128)S(1)}) custom-call(f32[1024,2048]{1,0:T(8,128)} %fusion.72.sum_ref, f32[2,2,2,256,1024]{4,3,2,1,0:T(8,128)} %fusion.89.refs_0_, f32[2,2,2,80,1024]{4,3,2,1,0:T(8,128)} %bitcast.482, f32[32,1024]{1,0:T(8,128)S(1)} %pad.22.refs_2_), custom_call_target="tpu_custom_call" | custom-call | bytes 419430400 | tf_op jit(solution)/shard_map/joint_sums/pallas_call | solution.py:493
  (529 shorter events, 481.4 us)
Async XLA Ops:
  7.2 910.1 %reduce-scatter.4.cloned.1.call-start = ((), (), s32[]{:S(2)}) async-start(), calls=%async_computation.3 | async-start | bytes 9437184 | tf_op jit(solution)/shard_map/reduce_scatter | solution.py:322
  27.8 7.9 collective-permute-start
  48.6 9.8 collective-permute-start.2
  148.9 7.2 collective-permute-start.4
  161.3 92.9 %collective-permute-start.5 = (f32[512,2048]{1,0:T(8,128)}, f32[512,2048]{1,0:T(8,128)}, u32[]{:S(2)}, u32[]{:S(2)}) collective-permute-start(f32[512,2048]{1,0:T(8,128)} %dynamic-slice_add_fusion.1), channel_id=1, source_target_pairs={{0,2},{2,0},{1,3},{3,1},{4,6},{6,4},{5,7},{7,5},{8,10},{10,8},{9,1... | collective-permute-start | bytes 12582920 | tf_op jit(solution)/shard_map/ppermute | solution.py:297
  262.8 7.3 collective-permute-start.6
  293.5 6.1 collective-permute-start.7
  306.8 9.8 collective-permute-start.9
  316.7 6.3 collective-permute-start.10
  452.8 27.0 %collective-permute-start.11 = (f32[512,2048]{1,0:T(8,128)}, f32[512,2048]{1,0:T(8,128)}, u32[]{:S(2)}, u32[]{:S(2)}) collective-permute-start(f32[512,2048]{1,0:T(8,128)} %constant_dynamic-slice_fusion), channel_id=1, source_target_pairs={{0,1},{1,0},{2,3},{3,2},{4,5},{5,4},{6,7},{7,6},{8,9},{9,8},{10,11... | collective-permute-start | bytes 12582920 | tf_op jit(solution)/shard_map/ppermute | solution.py:291
  482.9 61.2 %collective-permute-start.12 = (f32[256,2048]{1,0:T(8,128)S(1)}, f32[256,2048]{1,0:T(8,128)S(1)}, u32[]{:S(2)}, u32[]{:S(2)}) collective-permute-start(f32[256,2048]{1,0:T(8,128)S(1)} %slice.340), channel_id=1, source_target_pairs={{0,2},{2,0},{1,3},{3,1},{4,6},{6,4},{5,7},{7,5},{8,10},{10,8},{9,1... | collective-permute-start | bytes 6291464 | tf_op jit(solution)/shard_map/ppermute | solution.py:297
  555.1 10.1 collective-permute-start.14
  556.7 832.6 %reduce-scatter.8.cloned.1.call-start = ((), (), s32[]{:S(2)}) async-start(), calls=%async_computation.5 | async-start | bytes 9437184 | tf_op jit(solution)/shard_map/reduce_scatter | solution.py:322
  583.6 6.7 collective-permute-start.16
  878.5 7.4 collective-permute-start.17
  917.4 477.8 %reduce-scatter.6.cloned.1.call-start = ((), (), s32[]{:S(2)}) async-start(), calls=%async_computation.4 | async-start | bytes 9437184 | tf_op jit(solution)/shard_map/reduce_scatter | solution.py:322
  1005.3 89.1 %collective-permute-start.18 = (f32[256,2048]{1,0:T(8,128)}, f32[256,2048]{1,0:T(8,128)}, u32[]{:S(2)}, u32[]{:S(2)}) collective-permute-start(f32[256,2048]{1,0:T(8,128)} %slice.348), channel_id=1, source_target_pairs={{0,2},{2,0},{1,3},{3,1},{4,6},{6,4},{5,7},{7,5},{8,10},{10,8},{9,1... | collective-permute-start | bytes 6291464 | tf_op jit(solution)/shard_map/ppermute | solution.py:297
  1103.1 11.5 collective-permute-start.19
  1114.6 10.1 collective-permute-start.20
  1115.3 11.1 collective-permute-start.24
  1125.9 49.1 %collective-permute-start.23 = (f32[512,2048]{1,0:T(8,128)}, f32[512,2048]{1,0:T(8,128)}, u32[]{:S(2)}, u32[]{:S(2)}) collective-permute-start(f32[512,2048]{1,0:T(8,128)} %get-tuple-element.227), channel_id=1, source_target_pairs={{0,1},{1,0},{2,3},{3,2},{4,5},{5,4},{6,7},{7,6},{8,9},{9,8},{10,11... | collective-permute-start | bytes 12582920 | tf_op jit(solution)/shard_map/ppermute | solution.py:303
  1143.2 9.2 collective-permute-start.22
  1344.9 23.4 %collective-permute-start.25 = (f32[512,2048]{1,0:T(8,128)}, f32[512,2048]{1,0:T(8,128)}, u32[]{:S(2)}, u32[]{:S(2)}) collective-permute-start(f32[512,2048]{1,0:T(8,128)} %multiply_subtract_fusion), channel_id=1, source_target_pairs={{0,1},{1,0},{2,3},{3,2},{4,5},{5,4},{6,7},{7,6},{8,9},{9,8},{10,11... | collective-permute-start | bytes 12582920 | tf_op jit(solution)/shard_map/ppermute | solution.py:303
  1360.9 6.7 collective-permute-start.29
  (147 other events, 2932.7 us)
Sparse Core Ops, SparseCore 0:
  556.8 182.6 reduce-scatter.3
  917.5 152.7 reduce-scatter.7
  1073.9 174.7 reduce-scatter.5

commit v5 on v4

--- a/solution.py
+++ b/solution.py
@@ -322,6 +322,46 @@
     return lax.psum_scatter(array, "blk", scatter_dimension=0, tiled=True)
 
 
+def chosen(array, axis, index):
+    return lax.dynamic_index_in_dim(array, index, axis, keepdims=False)
+
+
+class Halving:
+    def __init__(self, array, bits=(1, 2, 4)):
+        self.got = None
+        if lax.axis_size("blk") != 8:
+            self.array, self.bits = blk_scatter(array), []
+            return
+        self.array = array.reshape((2, 2, 2, array.shape[0] // 8, array.shape[1]))
+        self.axes, self.bits = [4, 2, 1], list(bits)
+
+    def start(self):
+        if self.bits:
+            bit = self.bits.pop(0)
+            axis = self.axes.index(bit)
+            self.axes.remove(bit)
+            mine = (lax.axis_index("blk") // bit) % 2
+            self.keep = chosen(self.array, axis, mine)
+            give = chosen(self.array, axis, 1 - mine)
+            self.got = lax.ppermute(give, "blk", [(j, j ^ bit) for j in range(8)])
+        return self
+
+
+def meet(jobs, values, more=True):
+    jobs = [job for job in jobs if job.got is not None]
+    gots, values = lax.optimization_barrier((tuple(job.got for job in jobs), values))
+    for job, got in zip(jobs, gots):
+        job.array, job.got = job.keep + got, None
+        if more:
+            job.start()
+    return values
+
+
+def halvings(array):
+    middle = array.shape[1] // 2
+    return [Halving(array[:, :middle]).start(), Halving(array[:, middle:], (2, 4, 1)).start()]
+
+
 def add_rows(total, other, count):
     slab = 8
 
@@ -914,9 +954,8 @@
         layer = layers[l]
         normed, base = norms[l]
         if l < last:
-            grads, out_grad, scattered[last] = lax.optimization_barrier(
-                (back_gated(layer, kept[l], grad_low), dot_t(grad_low, scans[l][1]), scattered[last]))
-            scattered[l] = [blk_scatter(out_grad)]
+            grads = back_gated(layer, kept[l], grad_low)
+            out_grad = dot_t(grad_low, scans[l][1])
             late = back_local(layer, kept[l], grads[1])
             end, = exchange(layer, [late], kept[l][-1], jnp.zeros_like(late[:, 0]), (True,), 2 + 2 * layer_total + l)
         else:
@@ -925,14 +964,15 @@
         middle = half.shape[0] // 2
         if l == last:
             end, side, out_grad, half = lax.optimization_barrier((end, side, out_grad, half))
-            scattered[l] = [blk_scatter(out_grad)]
-            scan_out, got = lax.optimization_barrier(
-                (back_scan(layer, kept[l], scans[l], grads, end), across(half[:middle])))
+            jobs = [halvings(out_grad)]
+            scattered[l] = [blk_scatter(side[0])]
+            scan_out, got = meet(jobs[0], (back_scan(layer, kept[l], scans[l], grads, end), across(half[:middle])))
         else:
-            end, side, half = lax.optimization_barrier((end, side, half))
-            scattered[l].append(blk_scatter(side[0]))
-            scan_out, got_rest = lax.optimization_barrier(
-                (back_scan(layer, kept[l], scans[l], grads, end), across(half[middle:])))
+            end, side, out_grad, half = lax.optimization_barrier((end, side, out_grad, half))
+            jobs.append(halvings(out_grad))
+            scattered[l] = [blk_scatter(side[0])]
+            scan_out, got_rest = meet(
+                jobs[0] + jobs[1], (back_scan(layer, kept[l], scans[l], grads, end), across(half[middle:])))
             branch = half + jnp.concatenate([got, got_rest], axis=0)
             following = residual + branch
             squares[last] = jnp.stack([jnp.sum(branch * branch), jnp.sum(following * following)])
@@ -945,9 +985,10 @@
         inner = smalls[l].shape[-1]
         if l == last:
             thins = thick[1:] + thins
-            normed_grad, thick, smalls[l] = joint_sums(
-                normed_part, [rows(thick[0]), side[0]], (128, 128), smalls[l], l)
-            scattered[l] += [thick[1], thick[0]]
+            normed_part, scattered[l] = lax.optimization_barrier((normed_part, scattered[l]))
+            normed_grad, thick, smalls[l] = meet(
+                jobs[0], joint_sums(normed_part, [rows(thick[0])], (128,), smalls[l], l))
+            scattered[l].append(thick[0])
         else:
             thins = thick[1:] + thins
             cuts = [part.shape[1] for part in thins]
@@ -959,13 +1000,15 @@
             small = jnp.concatenate([smalls[l], shared], axis=0)
             small = jnp.pad(small, ((0, -small.shape[0] % 8), (0, 0)))
             normed_part, thins, out = lax.optimization_barrier((normed_part, thins, out))
-            normed_grad, thick, small = joint_sums(
-                normed_part, [rows(thick[0]), rows(jnp.concatenate(thins, axis=1))], (0, inner), small, l)
+            normed_grad, thick, small = meet(jobs[1], joint_sums(
+                normed_part, [rows(thick[0]), rows(jnp.concatenate(thins, axis=1))], (0, inner), small, l))
             scattered[l].append(thick[0])
             smalls[l], rest = small[:own_count], small[own_count:]
         gains[l], change = norm_back(layer, normed_grad, base, inverse_rms(base))
         grad = grad + all_rows(change)
         grad_low = grad.astype(jnp.bfloat16)
+    meet(jobs[1], ())
+    out_grads = [jnp.concatenate([job.array.T for job in each], axis=0) for each in reversed(jobs)]
     first_gain = blk_sum(rows_sum(gains[0].reshape(-1, inner)))
     input_grad = restore(grad_low)
 
@@ -982,7 +1025,7 @@
     for cut in cuts:
         pieces.append(thick[1][at:at + cut])
         at += cut
-    into_out = jnp.stack([jnp.stack([part[2], part[1]], axis=1) for part in scattered])
+    into_out = jnp.stack([jnp.stack([part[1], part[0]], axis=1) for part in scattered])
 
     def stacked(parts_):
         return jnp.stack([jnp.moveaxis(part, 0, 1) for part in parts_])[:, :, None]
@@ -1003,7 +1046,7 @@
         small[:, taps + 1],
         small[:, taps + 2:-1],
         small[:, -1],
-        jnp.stack([part[0].T for part in scattered]),
+        jnp.stack(out_grads),
         rms_stats,
         input_rms,
     )

time: 1420 us -> 1450 us (1.021)
  Pallas kernels: 760 us -> 635 us
  waiting for transfers between devices: 103 us -> 190 us
  local copies, waits for them, and re-layouts: 142 us -> 181 us
  other arithmetic: 165 us -> 181 us
    pallas_call x2, Pallas kernels: 414 us -> 306 us  [joint_sums(): pl.pallas_call(partial(joint_body, plan, chunks), in_specs=[any_spec] * (...]
    ppermute x0 -> x12, waiting for transfers between devices: none -> 68.4 us  [start(): self.got = lax.ppermute(give, 'blk', [(j, j ^ bit) for j in range(8)])]
    reduce_scatter x3 -> x2, waiting for transfers between devices: 0.02 us -> 24.5 us  [blk_scatter(): return lax.psum_scatter(array, 'blk', scatter_dimension=0, tiled=True)]
    dynamic_slice x0 -> x12, local copies, waits for them, and re-layouts: none -> 17.3 us  [chosen(): return lax.dynamic_index_in_dim(array, index, axis, keepdims=False)]
    pallas_call x3, Pallas kernels: 97.7 us -> 80.7 us  [hops(): pl.pallas_call(partial(hop_body, reverses, groups), in_specs=[spec] * (3...]
    add x0 -> x8, other arithmetic: none -> 15.2 us  [meet(): job.array, job.got = (job.keep + got, None)]
    unnamed x287 -> x326, local copies, waits for them, and re-layouts: 61.3 us -> 62.6 us
  transfers between devices with their start and end apart: 33 -> 44, of which waited for: 18 -> 16; matrix products, arithmetic and copies ran while one was open for 24% -> 24% of each run, Pallas kernels for 42% -> 29%
where the time goes in v5:
time: 1450 us; the launch traced here: 1440 us
  Pallas kernels  635 us (44%)
  matrix products  205 us (14%)
  waiting for transfers between devices  190 us (13%)
  local copies, waits for them, and re-layouts  181 us (12%)
  other arithmetic  181 us (12%)
  starting transfers between devices  32.7 us (2%)
  between operations  18.6 us (1%)
    pallas_call x2, Pallas kernels, joint_sums(): pl.pallas_call(partial(joint_body, plan, chunks), in_specs=[any_spec] * (...  306 us
    pallas_call x2, Pallas kernels, scan_backward(): pl.pallas_call(partial(back_body, C // LANES, width), grid=(T // tb,), in...  119 us
    dot_general x10, matrix products, dot_n(): lax.dot_general(left, right, (((1,), (1,)), ((), ())), preferred_element_...  98.5 us
    pallas_call x3, Pallas kernels, hops(): pl.pallas_call(partial(hop_body, reverses, groups), in_specs=[spec] * (3...  80.7 us
    ppermute x12, waiting for transfers between devices, start(): self.got = lax.ppermute(give, 'blk', [(j, j ^ bit) for j in range(8)])  68.4 us
    pallas_call x2, Pallas kernels, scan_forward(): pl.pallas_call(partial(scan_body, C // LANES, width), grid=(T // tb,), in...  63.2 us
    unnamed x326, local copies, waits for them, and re-layouts  62.6 us
    dot_general x12, matrix products, dot_t(): lax.dot_general(left, right, (((0,), (0,)), ((), ())), preferred_element_...  62.1 us
  transfers between devices with their start and end apart: 44, of which 16 were waited for; matrix products, arithmetic and copies ran while one was open for 24% of the time, Pallas kernels for 29%

profile of v5, /device:TPU:0, one launch (start us, length us, event | category | flops | bytes accessed | tf_op | source)
XLA Modules:
  0.0 1443.0 jit_solution(6810062352348580152)
XLA Ops:
  69.0 16.5 %end_states.2.refs_0_ = f32[16,8,1024]{2,1,0:T(8,128)S(1)} custom-call(f32[128,8,1024]{2,1,0:T(8,128)S(1)} %bitcast.506, f32[128,8,1024]{2,1,0:T(8,128)S(1)} %fusion.26.push_ref, f32[128,8,32]{2,1,0:T(8,128)S(1)} %bitcast.518, f32[16,1024]{1,0:T(8,128)S(1)} %get-tuple-element.313.rate_ref), custom_call_target="tpu_custom_call" | custom-call | flops 67108864 | bytes 67108864 | tf_op jit(solution)/shard_map/end_states/pallas_call | solution.py:58
  85.5 16.1 %hops.3.start_ref.begin_ref = f32[16,8,1024]{2,1,0:T(8,128)S(1)} custom-call(f32[8,1024]{1,0:T(8,128)S(1)} %get-tuple-element.330.total_ref, f32[16,1024]{1,0:T(8,128)S(1)} %get-tuple-element.313.rate_ref, f32[16,8,1024]{2,1,0:T(8,128)S(1)} %end_states.2.refs_0_, f32[16,8,1024]{2,1,0:T(8,128)S(1)} %get-tuple-element.337.refs_1_), custom_call_target="tpu_custom_call" | custom-call | bytes 26214400 | tf_op jit(solution)/shard_map/hops/pallas_call | solution.py:681
  101.6 31.5 %scan_forward.2 = (f32[128,8,1024]{2,1,0:T(8,128)S(1)}, f32[128,16,8,1024]{3,2,1,0:T(8,128)}, f32[16,8,1024]{2,1,0:T(8,128)S(1)}) custom-call(f32[128,8,1024]{2,1,0:T(8,128)} %bitcast.507, f32[128,8,1024]{2,1,0:T(8,128)} %copy-done.5, f32[128,8,32]{2,1,0:T(8,128)S(1)} %bitcast.519, f32[16,1024]{1,0:T(8,128)S(1)} %get-tuple-element.313.rate_ref, ...), custom_call_target="tpu_custom_call" | custom-call | flops 117440512 | bytes 117440512 | tf_op jit(solution)/shard_map/scan_forward/pallas_call | solution.py:107
  172.8 11.4 copy.67
  199.0 11.7 copy.68
  221.1 33.1 %collective-permute-done.5 = f32[512,2048]{1,0:T(8,128)} collective-permute-done((f32[512,2048]{1,0:T(8,128)}, f32[512,2048]{1,0:T(8,128)}, u32[]{:S(2)}, u32[]{:S(2)}) %collective-permute-start.5) | collective-permute-done | bytes 4194336 | tf_op jit(solution)/shard_map/ppermute | solution.py:297
  332.4 16.7 %start_grads.2.refs_1_ = f32[16,8,1024]{2,1,0:T(8,128)S(1)} custom-call(f32[128,8,1024]{2,1,0:T(8,128)S(1)} %bitcast.510, f32[128,8,1024]{2,1,0:T(8,128)S(1)} %bitcast.514, f32[128,8,32]{2,1,0:T(8,128)S(1)} %bitcast.522, f32[16,1024]{1,0:T(8,128)S(1)} %get-tuple-element.312.rate_ref), custom_call_target="tpu_custom_call" | custom-call | flops 67108864 | bytes 67108864 | tf_op jit(solution)/shard_map/start_grads/pallas_call | solution.py:145
  349.1 16.5 %end_states.3.refs_0_ = f32[16,8,1024]{2,1,0:T(8,128)S(1)} custom-call(f32[128,8,1024]{2,1,0:T(8,128)S(1)} %bitcast.511, f32[128,8,1024]{2,1,0:T(8,128)S(1)} %get-tuple-element.292.push_ref, f32[128,8,32]{2,1,0:T(8,128)S(1)} %bitcast.523, f32[16,1024]{1,0:T(8,128)S(1)} %get-tuple-element.312.rate_ref), custom_call_target="tpu_custom_call" | custom-call | flops 67108864 | bytes 67108864 | tf_op jit(solution)/shard_map/end_states/pallas_call | solution.py:58
  365.6 39.3 %hops.4 = (f32[16,8,1024]{2,1,0:T(8,128)S(1)}, f32[16,8,1024]{2,1,0:T(8,128)S(1)}) custom-call(f32[8,1024]{1,0:T(8,128)S(1)} %get-tuple-element.332.total_ref, f32[16,1024]{1,0:T(8,128)S(1)} %get-tuple-element.312.rate_ref, f32[16,8,1024]{2,1,0:T(8,128)S(1)} %end_states.3.refs_0_, f32[16,8,1024]{2,1,0:T(8,128)S(1)} %start_grads.2.refs_1_, ...), custom_call_target="tpu_custom_call" | custom-call | bytes 26214400 | tf_op jit(solution)/shard_map/hops/pallas_call | solution.py:681
  404.9 31.7 %scan_forward.3 = (f32[128,8,1024]{2,1,0:T(8,128)S(1)}, f32[128,16,8,1024]{3,2,1,0:T(8,128)}, f32[16,8,1024]{2,1,0:T(8,128)S(1)}) custom-call(f32[128,8,1024]{2,1,0:T(8,128)} %bitcast.512, f32[128,8,1024]{2,1,0:T(8,128)} %copy-done.6, f32[128,8,32]{2,1,0:T(8,128)S(1)} %bitcast.524, f32[16,1024]{1,0:T(8,128)S(1)} %get-tuple-element.312.rate_ref, ...), custom_call_target="tpu_custom_call" | custom-call | flops 117440512 | bytes 117440512 | tf_op jit(solution)/shard_map/scan_forward/pallas_call | solution.py:107
  498.3 59.5 %scan_backward.2 = (f32[128,8,1024]{2,1,0:T(8,128)}, f32[128,8,1024]{2,1,0:T(8,128)}, f32[128,8,32]{2,1,0:T(8,128)S(1)}, f32[16,8,1024]{2,1,0:T(8,128)S(1)}, f32[16,8,1024]{2,1,0:T(8,128)S(1)}) custom-call(f32[128,8,1024]{2,1,0:T(8,128)} %bitcast.513, f32[128,8,1024]{2,1,0:T(8,128)} %copy-done.6, f32[128,8,1024]{2,1,0:T(8,128)} %bitcast.515, ...), custom_call_target="tpu_custom_call" | custom-call | flops 218103808 | bytes 218103808 | tf_op jit(solution)/shard_map/scan_backward/pallas_call | solution.py:231
  558.7 45.5 %collective-permute-done.13 = f32[2,2,256,512]{3,2,1,0:T(8,128)} collective-permute-done((f32[2,2,256,512]{3,2,1,0:T(8,128)}, f32[2,2,256,512]{3,2,1,0:T(8,128)}, u32[]{:S(2)}, u32[]{:S(2)}) %collective-permute-start.13) | collective-permute-done | bytes 2097184 | tf_op jit(solution)/shard_map/ppermute | solution.py:346
  630.7 13.0 fusion.161
  663.5 13.2 fusion.69.sum_ref
  683.6 24.5 %reduce-scatter.3.cloned.1.call-done = f32[256,1024]{1,0:T(8,128)} async-done(((f32[2048,1024]{1,0:T(8,128)}), f32[256,1024]{1,0:T(8,128)}) %reduce-scatter.3.cloned.1.call-update) | async-done | bytes 1048592 | tf_op jit(solution)/shard_map/reduce_scatter | solution.py:322
  708.1 123.6 %joint_sums.2 = (f32[512,2048]{1,0:T(8,128)}, f32[256,1024]{1,0:T(8,128)S(1)}, f32[23,1024]{1,0:T(8,128)S(1)}) custom-call(f32[1024,2048]{1,0:T(8,128)} %fusion.69.sum_ref, f32[2,2,2,256,1024]{4,3,2,1,0:T(8,128)} %bitcast.557, f32[23,1024]{1,0:T(8,128)S(1)} %concatenate.118.refs_1_), custom_call_target="tpu_custom_call" | custom-call | bytes 419430400 | tf_op jit(solution)/shard_map/joint_sums/pallas_call | solution.py:533
  871.2 17.0 %fusion.28 = (f32[1024]{0:T(1024)S(1)}, f32[1024,1024]{1,0:T(8,128)}, bf16[1024,1024]{1,0:T(8,128)(2,1)}) fusion(bf16[1024,1024]{1,0:T(8,128)(2,1)S(1)} %copy-done.29, f32[2,1024,1024]{2,1,0:T(8,128)} %copy-done.59, f32[1024]{0:T(1024)S(1)} %bitcast.601, f32[128,8,1024]{2,1,0:T(8,128)S(1)} %copy-done.13, bf16[2,1024,2048]{2,1,0:T(8,128)(2,1)} %param.25, ...), kind=kOutput, calls=%fused_computation.59 | convolution fusion | flops 4321180672 | bytes 33562624 | tf_op jit(solution)/shard_map/dot_general | solution.py:712
  888.2 12.4 fusion.101
  911.5 16.7 %start_grads.3.refs_0_ = f32[16,8,1024]{2,1,0:T(8,128)S(1)} custom-call(f32[128,8,1024]{2,1,0:T(8,128)S(1)} %bitcast.509, f32[128,8,1024]{2,1,0:T(8,128)S(1)} %bitcast.517, f32[128,8,32]{2,1,0:T(8,128)S(1)} %bitcast.520, f32[16,1024]{1,0:T(8,128)S(1)} %copy-done.15), custom_call_target="tpu_custom_call" | custom-call | flops 67108864 | bytes 67108864 | tf_op jit(solution)/shard_map/start_grads/pallas_call | solution.py:145
  928.3 25.4 %hops.5.end_ref = f32[16,8,1024]{2,1,0:T(8,128)S(1)} custom-call(f32[8,1024]{1,0:T(8,128)S(1)} %copy-done.23, f32[16,1024]{1,0:T(8,128)S(1)} %copy-done.15, f32[16,8,1024]{2,1,0:T(8,128)S(1)} %start_grads.3.refs_0_, f32[16,8,1024]{2,1,0:T(8,128)S(1)} %broadcast_in_dim.45.refs_1_), custom_call_target="tpu_custom_call" | custom-call | bytes 26214400 | tf_op jit(solution)/shard_map/hops/pallas_call | solution.py:681
  987.9 59.5 %scan_backward.3 = (f32[128,8,1024]{2,1,0:T(8,128)}, f32[128,8,1024]{2,1,0:T(8,128)}, f32[128,8,32]{2,1,0:T(8,128)S(1)}, f32[16,8,1024]{2,1,0:T(8,128)S(1)}, f32[16,8,1024]{2,1,0:T(8,128)S(1)}) custom-call(f32[128,8,1024]{2,1,0:T(8,128)} %bitcast.508, f32[128,8,1024]{2,1,0:T(8,128)} %copy-done.5, f32[128,8,1024]{2,1,0:T(8,128)} %bitcast.516, ...), custom_call_target="tpu_custom_call" | custom-call | flops 218103808 | bytes 218103808 | tf_op jit(solution)/shard_map/scan_backward/pallas_call | solution.py:231
  1047.4 22.9 %collective-permute-done.25 = f32[2,2,256,512]{3,2,1,0:T(8,128)} collective-permute-done((f32[2,2,256,512]{3,2,1,0:T(8,128)}, f32[2,2,256,512]{3,2,1,0:T(8,128)}, u32[]{:S(2)}, u32[]{:S(2)}) %collective-permute-start.25) | collective-permute-done | bytes 2097184 | tf_op jit(solution)/shard_map/ppermute | solution.py:346
  1109.3 15.2 %fusion.160 = (f32[1024]{0:T(1024)S(1)}, f32[1024]{0:T(1024)S(1)}, f32[1024]{0:T(1024)S(1)}, f32[1024]{0:T(1024)S(1)}, f32[1024]{0:T(1024)S(1)}, /*index=5*/f32[1024,1024]{1,0:T(8,128)S(1)}) fusion(f32[2,1024,1024]{2,1,0:T(8,128)} %copy-done.59, f32[1024,1024]{1,0:T(8,128)} %slice_bitcast_fusion.3, f32[24,1024]{1,0:T(8,128)S(1)} %copy-done.103, ...), kind=kOutput, calls=%fused_computation.368 | convolution fusion | flops 698870784 | bytes 30466048 | tf_op jit(solution)/shard_map/dot_general | solution.py:712
  1168.9 182.1 %joint_sums.3 = (f32[512,2048]{1,0:T(8,128)}, f32[256,1024]{1,0:T(8,128)S(1)}, f32[80,1024]{1,0:T(8,128)S(1)}, f32[32,1024]{1,0:T(8,128)S(1)}) custom-call(f32[1024,2048]{1,0:T(8,128)} %fusion.72.sum_ref, f32[2,2,2,256,1024]{4,3,2,1,0:T(8,128)} %fusion.89.refs_0_, f32[2,2,2,80,1024]{4,3,2,1,0:T(8,128)} %bitcast.552, f32[32,1024]{1,0:T(8,128)S(1)} %pad.22.refs_2_), custom_call_target="tpu_custom_call" | custom-call | bytes 419430400 | tf_op jit(solution)/shard_map/joint_sums/pallas_call | solution.py:533
  (623 shorter events, 569.5 us)
Async XLA Ops:
  7.2 700.9 %reduce-scatter.3.cloned.1.call-start = ((), (), s32[]{:S(2)}) async-start(), calls=%async_computation.2 | async-start | bytes 9437184 | tf_op jit(solution)/shard_map/reduce_scatter | solution.py:322
  161.2 92.9 %collective-permute-start.5 = (f32[512,2048]{1,0:T(8,128)}, f32[512,2048]{1,0:T(8,128)}, u32[]{:S(2)}, u32[]{:S(2)}) collective-permute-start(f32[512,2048]{1,0:T(8,128)} %dynamic-slice_add_fusion.1), channel_id=1, source_target_pairs={{0,2},{2,0},{1,3},{3,1},{4,6},{6,4},{5,7},{7,5},{8,10},{10,8},{9,1... | collective-permute-start | bytes 12582920 | tf_op jit(solution)/shard_map/ppermute | solution.py:297
  453.5 24.5 %collective-permute-start.11 = (f32[512,2048]{1,0:T(8,128)}, f32[512,2048]{1,0:T(8,128)}, u32[]{:S(2)}, u32[]{:S(2)}) collective-permute-start(f32[512,2048]{1,0:T(8,128)} %constant_dynamic-slice_fusion.8), channel_id=1, source_target_pairs={{0,1},{1,0},{2,3},{3,2},{4,5},{5,4},{6,7},{7,6},{8,9},{9,8},{10,11... | collective-permute-start | bytes 12582920 | tf_op jit(solution)/shard_map/ppermute | solution.py:291
  483.1 943.9 %reduce-scatter.5.cloned.1.call-start = ((), (), s32[]{:S(2)}) async-start(), calls=%async_computation.3 | async-start | bytes 9437184 | tf_op jit(solution)/shard_map/reduce_scatter | solution.py:322
  489.2 115.0 %collective-permute-start.13 = (f32[2,2,256,512]{3,2,1,0:T(8,128)}, f32[2,2,256,512]{3,2,1,0:T(8,128)}, u32[]{:S(2)}, u32[]{:S(2)}) collective-permute-start(f32[2,2,256,512]{3,2,1,0:T(8,128)} %dynamic-slice_bitcast_fusion.2), channel_id=1, source_target_pairs={{0,8},{4,12},{8,0},{12,4},{16,24},{20,28},{24,16},{28,20},{1,9},{5... | collective-permute-start | bytes 6291464 | tf_op jit(solution)/shard_map/ppermute | solution.py:346
  493.2 111.0 %collective-permute-start.12 = (f32[2,2,256,512]{3,2,1,0:T(8,128)}, f32[2,2,256,512]{3,2,1,0:T(8,128)}, u32[]{:S(2)}, u32[]{:S(2)}) collective-permute-start(f32[2,2,256,512]{3,2,1,0:T(8,128)} %dynamic-slice_bitcast_fusion.3), channel_id=1, source_target_pairs={{0,4},{4,0},{8,12},{12,8},{16,20},{20,16},{24,28},{28,24},{1,5},{5... | collective-permute-start | bytes 6291464 | tf_op jit(solution)/shard_map/ppermute | solution.py:346
  495.9 108.2 %collective-permute-start.14 = (f32[256,2048]{1,0:T(8,128)}, f32[256,2048]{1,0:T(8,128)}, u32[]{:S(2)}, u32[]{:S(2)}) collective-permute-start(f32[256,2048]{1,0:T(8,128)} %slice.354), channel_id=1, source_target_pairs={{0,2},{2,0},{1,3},{3,1},{4,6},{6,4},{5,7},{7,5},{8,10},{10,8},{9,1... | collective-permute-start | bytes 6291464 | tf_op jit(solution)/shard_map/ppermute | solution.py:297
  619.1 212.6 %collective-permute-start.16 = (f32[2,256,512]{1,2,0:T(8,128)}, f32[2,256,512]{1,2,0:T(8,128)}, u32[]{:S(2)}, u32[]{:S(2)}) collective-permute-start(f32[2,256,512]{1,2,0:T(8,128)} %bitcast.566), channel_id=1, source_target_pairs={{0,16},{4,20},{8,24},{12,28},{16,0},{20,4},{24,8},{28,12},{1,17},{... | collective-permute-start | bytes 3145736 | tf_op jit(solution)/shard_map/ppermute | solution.py:346
  649.5 13.1 collective-permute-start.20
  654.9 176.8 %collective-permute-start.15 = (f32[2,256,512]{1,2,0:T(8,128)}, f32[2,256,512]{1,2,0:T(8,128)S(1)}, u32[]{:S(2)}, u32[]{:S(2)}) collective-permute-start(f32[2,256,512]{1,2,0:T(8,128)} %bitcast.70), channel_id=1, source_target_pairs={{0,8},{4,12},{8,0},{12,4},{16,24},{20,28},{24,16},{28,20},{1,9},{5... | collective-permute-start | bytes 3145736 | tf_op jit(solution)/shard_map/ppermute | solution.py:346
  838.3 14.8 %collective-permute-start.21 = (f32[512,2048]{1,0:T(8,128)}, f32[512,2048]{1,0:T(8,128)}, u32[]{:S(2)}, u32[]{:S(2)}) collective-permute-start(f32[512,2048]{1,0:T(8,128)} %multiply_subtract_fusion.1), channel_id=1, source_target_pairs={{0,1},{1,0},{2,3},{3,2},{4,5},{5,4},{6,7},{7,6},{8,9},{9,8},{10,11... | collective-permute-start | bytes 12582920 | tf_op jit(solution)/shard_map/ppermute | solution.py:303
  959.7 110.6 %collective-permute-start.25 = (f32[2,2,256,512]{3,2,1,0:T(8,128)}, f32[2,2,256,512]{3,2,1,0:T(8,128)}, u32[]{:S(2)}, u32[]{:S(2)}) collective-permute-start(f32[2,2,256,512]{3,2,1,0:T(8,128)} %dynamic-slice_bitcast_fusion), channel_id=1, source_target_pairs={{0,8},{4,12},{8,0},{12,4},{16,24},{20,28},{24,16},{28,20},{1,9},{5... | collective-permute-start | bytes 6291464 | tf_op jit(solution)/shard_map/ppermute | solution.py:346
  964.0 106.3 %collective-permute-start.24 = (f32[2,2,256,512]{3,2,1,0:T(8,128)}, f32[2,2,256,512]{3,2,1,0:T(8,128)}, u32[]{:S(2)}, u32[]{:S(2)}) collective-permute-start(f32[2,2,256,512]{3,2,1,0:T(8,128)} %dynamic-slice_bitcast_fusion.1), channel_id=1, source_target_pairs={{0,4},{4,0},{8,12},{12,8},{16,20},{20,16},{24,28},{28,24},{1,5},{5... | collective-permute-start | bytes 6291464 | tf_op jit(solution)/shard_map/ppermute | solution.py:346
  966.5 103.8 %collective-permute-start.26 = (f32[256,2048]{1,0:T(8,128)}, f32[256,2048]{1,0:T(8,128)}, u32[]{:S(2)}, u32[]{:S(2)}) collective-permute-start(f32[256,2048]{1,0:T(8,128)} %slice.364), channel_id=1, source_target_pairs={{0,2},{2,0},{1,3},{3,1},{4,6},{6,4},{5,7},{7,5},{8,10},{10,8},{9,1... | collective-permute-start | bytes 6291464 | tf_op jit(solution)/shard_map/ppermute | solution.py:297
  977.8 69.6 %collective-permute-start.23 = (f32[256,512]{0,1:T(8,128)}, f32[256,512]{0,1:T(8,128)}, u32[]{:S(2)}, u32[]{:S(2)}) collective-permute-start(f32[256,512]{0,1:T(8,128)} %dynamic-slice_bitcast_fusion.6), channel_id=1, source_target_pairs={{0,4},{4,0},{8,12},{12,8},{16,20},{20,16},{24,28},{28,24},{1,5},{5... | collective-permute-start | bytes 1572872 | tf_op jit(solution)/shard_map/ppermute | solution.py:346
  980.1 67.3 %collective-permute-start.22 = (f32[256,512]{0,1:T(8,128)}, f32[256,512]{0,1:T(8,128)}, u32[]{:S(2)}, u32[]{:S(2)}) collective-permute-start(f32[256,512]{0,1:T(8,128)} %dynamic-slice_bitcast_fusion.7), channel_id=1, source_target_pairs={{0,16},{4,20},{8,24},{12,28},{16,0},{20,4},{24,8},{28,12},{1,17},{... | collective-permute-start | bytes 1572872 | tf_op jit(solution)/shard_map/ppermute | solution.py:346
  1087.0 20.4 %collective-permute-start.34 = (f32[3,1024]{1,0:T(4,128)S(1)}, f32[3,1024]{1,0:T(4,128)}, u32[]{:S(2)}, u32[]{:S(2)}) collective-permute-start(f32[3,1024]{1,0:T(4,128)S(1)} %pad_maximum_fusion.23), channel_id=1, source_target_pairs={{0,1},{1,0},{2,3},{3,2},{4,5},{5,4},{6,7},{7,6},{8,9},{9,8},{10,11... | collective-permute-start | bytes 36872 | tf_op jit(solution)/shard_map/ppermute | solution.py:310
  1088.7 69.3 %collective-permute-start.31 = (f32[512,2048]{1,0:T(8,128)}, f32[512,2048]{1,0:T(8,128)}, u32[]{:S(2)}, u32[]{:S(2)}) collective-permute-start(f32[512,2048]{1,0:T(8,128)} %get-tuple-element.260), channel_id=1, source_target_pairs={{0,1},{1,0},{2,3},{3,2},{4,5},{5,4},{6,7},{7,6},{8,9},{9,8},{10,11... | collective-permute-start | bytes 12582920 | tf_op jit(solution)/shard_map/ppermute | solution.py:303
  1093.0 258.0 %collective-permute-start.33 = (f32[2,256,512]{1,2,0:T(8,128)}, f32[2,256,512]{1,2,0:T(8,128)}, u32[]{:S(2)}, u32[]{:S(2)}) collective-permute-start(f32[2,256,512]{1,2,0:T(8,128)} %bitcast.564), channel_id=1, source_target_pairs={{0,16},{4,20},{8,24},{12,28},{16,0},{20,4},{24,8},{28,12},{1,17},{... | collective-permute-start | bytes 3145736 | tf_op jit(solution)/shard_map/ppermute | solution.py:346
  1094.0 10.8 collective-permute-start.28
  1107.4 243.6 %collective-permute-start.32 = (f32[2,256,512]{1,2,0:T(8,128)}, f32[2,256,512]{1,2,0:T(8,128)}, u32[]{:S(2)}, u32[]{:S(2)}) collective-permute-start(f32[2,256,512]{1,2,0:T(8,128)} %bitcast.565), channel_id=1, source_target_pairs={{0,8},{4,12},{8,0},{12,4},{16,24},{20,28},{24,16},{28,20},{1,9},{5... | collective-permute-start | bytes 3145736 | tf_op jit(solution)/shard_map/ppermute | solution.py:346
  1357.2 48.7 %collective-permute-start.35 = (f32[512,2048]{1,0:T(8,128)}, f32[512,2048]{1,0:T(8,128)}, u32[]{:S(2)}, u32[]{:S(2)}) collective-permute-start(f32[512,2048]{1,0:T(8,128)} %multiply_subtract_fusion), channel_id=1, source_target_pairs={{0,1},{1,0},{2,3},{3,2},{4,5},{5,4},{6,7},{7,6},{8,9},{9,8},{10,11... | collective-permute-start | bytes 12582920 | tf_op jit(solution)/shard_map/ppermute | solution.py:303
  1371.9 30.0 %collective-permute-start.41 = (f32[256,512]{0,1:T(8,128)}, f32[256,512]{0,1:T(8,128)}, u32[]{:S(2)}, u32[]{:S(2)}) collective-permute-start(f32[256,512]{0,1:T(8,128)} %dynamic-slice_bitcast_fusion.4), channel_id=1, source_target_pairs={{0,4},{4,0},{8,12},{12,8},{16,20},{20,16},{24,28},{28,24},{1,5},{5... | collective-permute-start | bytes 1572872 | tf_op jit(solution)/shard_map/ppermute | solution.py:346
  1374.1 27.7 %collective-permute-start.40 = (f32[256,512]{0,1:T(8,128)}, f32[256,512]{0,1:T(8,128)}, u32[]{:S(2)}, u32[]{:S(2)}) collective-permute-start(f32[256,512]{0,1:T(8,128)} %dynamic-slice_bitcast_fusion.5), channel_id=1, source_target_pairs={{0,16},{4,20},{8,24},{12,28},{16,0},{20,4},{24,8},{28,12},{1,17},{... | collective-permute-start | bytes 1572872 | tf_op jit(solution)/shard_map/ppermute | solution.py:346
  (178 other events, 3885.8 us)
Sparse Core Ops, SparseCore 0:
  483.2 224.8 reduce-scatter.2
  987.0 205.5 reduce-scatter.4

commit v6 on v4

--- a/solution.py
+++ b/solution.py
@@ -339,13 +339,15 @@
         device_id_type=pl.DeviceIdType.MESH)
 
 
-def joint_body(plan, chunks, sum_ref, *refs):
+def joint_body(plan, chunks, sum_ref, base_ref, gain_ref, *refs):
     count = 1 + max(job[0] for job in plan)
     thick_refs, small_ref, refs = refs[:count], refs[count], refs[count + 1:]
-    half_out, thick_outs, small_out, refs = refs[0], refs[1:1 + count], refs[1 + count], refs[2 + count:]
-    own_half, core_half, far_half, small_in, refs = refs[0], refs[1], refs[2], refs[3], refs[4:]
-    core_send, core_recv, far_send, far_recv, local_sem, out_sem, small_send, small_recv = refs[:8]
-    refs = refs[8:]
+    change_out, gain_out, refs = refs[0], refs[1], refs[2:]
+    thick_outs, small_out, refs = refs[:count], refs[count], refs[1 + count:]
+    own_half, core_half, far_half, base, came, small_in, refs = refs[0], refs[1], refs[2], refs[3], refs[4], refs[5], refs[6:]
+    core_send, core_recv, far_send, far_recv, back_send, back_recv, local_sem, base_sem, out_sem, came_sem = refs[:10]
+    small_send, small_recv = refs[10:12]
+    refs = refs[12:]
     blk, tensor = lax.axis_index("blk"), lax.axis_index("tensor")
     bits = {1: blk % 2, 2: (blk // 2) % 2, 4: blk // 4}
     core = tensor % 2
@@ -357,8 +359,8 @@
         pl.semaphore_signal(barrier, inc=1, device_id=device, device_id_type=pl.DeviceIdType.MESH)
     pl.semaphore_wait(barrier, 5)
 
-    rows_each = half_out.shape[0] // chunks
-    smalls, core_copies, local_copies, far_copies, outs = [], [], [], [], []
+    rows_each, width = own_half.shape[1:]
+    smalls, core_copies, local_copies, base_copies, far_copies, back_copies, outs = [], [], [], [], [], [], []
 
     def small_step(i):
         copy = remote(small_out, small_in.at[i], small_send, small_recv, i, peers[1 << i])
@@ -380,6 +382,10 @@
         copy = pltpu.make_async_copy(sum_ref.at[keep], own_half.at[k], local_sem.at[k])
         copy.start()
         local_copies.append(copy)
+        copy = pltpu.make_async_copy(base_ref.at[pl.ds(k * rows_each, rows_each)], base.at[k], base_sem.at[k])
+        copy.start()
+        base_copies.append(copy)
+    gain_out[...] = jnp.zeros_like(gain_out)
 
     class Job:
         def __init__(self, which, low, wide, order, refs):
@@ -444,9 +450,33 @@
 
     def far_end(k):
         far_copies[k].wait_recv()
-        add_rows(far_half.at[k], own_half.at[k], rows_each)
-        copy = pltpu.make_async_copy(
-            far_half.at[k], half_out.at[pl.ds(k * rows_each, rows_each)], out_sem.at[k])
+        base_copies[k].wait()
+
+        def slab(i, _):
+            at = pl.ds(pl.multiple_of(i * 8, 8), 8)
+            residual = base[k, at, :]
+            normed_grad = far_half[k, at, :] + own_half[k, at, :]
+            q = lax.rsqrt(jnp.sum(residual * residual, axis=-1, keepdims=True) * (1.0 / width) + EPSILON)
+            part = residual * q
+            gain_out[...] += normed_grad * part
+            scaled = normed_grad * gain_ref[...]
+            inner = jnp.sum(scaled * part, axis=-1, keepdims=True) * (1.0 / width)
+            far_half[k, at, :] = q * (scaled - part * inner)
+            return 0
+
+        lax.fori_loop(0, rows_each // 8, slab, 0)
+        copy = remote(far_half.at[k], came.at[k], back_send, back_recv, k, beside)
+        copy.start()
+        back_copies.append(copy)
+        own_rows_at = pl.ds(pl.multiple_of((core * chunks + k) * rows_each, rows_each), rows_each)
+        copy = pltpu.make_async_copy(far_half.at[k], change_out.at[own_rows_at], out_sem.at[k])
+        copy.start()
+        outs.append(copy)
+
+    def back_end(k):
+        back_copies[k].wait_recv()
+        other_rows_at = pl.ds(pl.multiple_of(((1 - core) * chunks + k) * rows_each, rows_each), rows_each)
+        copy = pltpu.make_async_copy(came.at[k], change_out.at[other_rows_at], came_sem.at[k])
         copy.start()
         outs.append(copy)
 
@@ -462,18 +492,21 @@
             if i == 0:
                 small_step(2)
         far_end(i)
+    for k in range(chunks):
+        back_end(k)
     for job in jobs:
         job.end()
-    for copy in far_copies + [each for job in jobs for each in job.sent()]:
+    for copy in far_copies + back_copies + [each for job in jobs for each in job.sent()]:
         copy.wait_send()
     for copy in outs:
         copy.wait()
 
 
-def joint_sums(array, thick, late, small, collective_id):
+def joint_sums(array, base, gain, thick, late, small, collective_id):
     if not paired() or lax.axis_size("blk") != 8:
-        return (lax.psum_scatter(array, "tensor", scatter_dimension=0, tiled=True),
-                [blk_scatter(part) for part in thick], lax.psum(small, "blk"))
+        normed_grad = lax.psum_scatter(array, "tensor", scatter_dimension=0, tiled=True)
+        gain_grad, change = norm_back(gain, normed_grad, base, inverse_rms(base))
+        return all_rows(change), gain_grad, [blk_scatter(part) for part in thick], lax.psum(small, "blk")
     R, N = array.shape
     C = thick[0].shape[1]
     chunks = 4
@@ -492,19 +525,19 @@
     half = pltpu.VMEM((chunks, R // 2 // chunks, N), f32)
     out = pl.pallas_call(
         partial(joint_body, plan, chunks),
-        in_specs=[any_spec] * (1 + len(thick)) + [vmem_spec],
-        out_specs=[any_spec] * (1 + len(thick)) + [vmem_spec],
-        out_shape=[jax.ShapeDtypeStruct((R // 2, N), f32)]
+        in_specs=[any_spec, any_spec, vmem_spec] + [any_spec] * len(thick) + [vmem_spec],
+        out_specs=[any_spec, vmem_spec] + [any_spec] * len(thick) + [vmem_spec],
+        out_shape=[jax.ShapeDtypeStruct((R, N), f32), jax.ShapeDtypeStruct((8, N), f32)]
         + [jax.ShapeDtypeStruct((part.shape[0] // 8, C), f32) for part in thick]
         + [jax.ShapeDtypeStruct(small.shape, f32)],
-        scratch_shapes=[half, half, half, pltpu.VMEM((3,) + small.shape, f32)]
-        + [dma((chunks,))] * 5 + [dma((chunks,)), dma((3,)), dma((3,))] + scratch,
+        scratch_shapes=[half] * 5 + [pltpu.VMEM((3,) + small.shape, f32)]
+        + [dma((chunks,))] * 10 + [dma((3,)), dma((3,))] + scratch,
         compiler_params=pltpu.CompilerParams(
             collective_id=collective_id, has_side_effects=True, vmem_limit_bytes=52 * 2**20),
         cost_estimate=pl.CostEstimate(flops=0, bytes_accessed=50 * R * N * 4, transcendentals=0),
         name="joint_sums",
-    )(array, *[part.reshape(2, 2, 2, part.shape[0] // 8, C) for part in thick], small)
-    return out[0], list(out[1:-1]), out[-1]
+    )(array, base, gain[None], *[part.reshape(2, 2, 2, part.shape[0] // 8, C) for part in thick], small)
+    return out[0], jnp.sum(out[1], axis=0), list(out[2:-1]), out[-1]
 
 
 def neighbour(value, steps):
@@ -764,9 +797,8 @@
     return dot32(gated, layer.out), (result, gated, states, start), final
 
 
-def back_gated(layer, kept, grad_low):
+def back_gated(kept, grad_gated):
     gate = kept[1]
-    grad_gated = dot_n(grad_low, layer.out)
     return grad_gated, grad_gated * jax.nn.silu(gate)
 
 
@@ -844,9 +876,9 @@
     return jnp.pad(array, ((0, 0), (0, -array.shape[1] % 8), (0, 0)))
 
 
-def norm_back(layer, normed_grad, residual, q):
+def norm_back(gain, normed_grad, residual, q):
     gain_grad = jnp.sum(normed_grad * (residual * q), axis=0)
-    scaled = normed_grad * layer.gain
+    scaled = normed_grad * gain
     inner_mean = jnp.mean(scaled * residual, axis=-1, keepdims=True)
     return gain_grad, q * scaled - residual * (q * q * q * inner_mean)
 
@@ -872,7 +904,7 @@
         return array.reshape(seqs, parts * length, width)
 
     residual = arrange(tokens).astype(jnp.float32)
-    normed = (residual * inverse_rms(residual) * layers[0].gain).astype(jnp.bfloat16)
+    normed = lax.optimization_barrier((residual * inverse_rms(residual) * layers[0].gain).astype(jnp.bfloat16))
     residual = own_rows(residual)
     input_square = jnp.sum(residual * residual)
     grad = arrange(cotangent).astype(jnp.float32)
@@ -887,7 +919,7 @@
         totals = kept[l][-1]
         first = jnp.moveaxis(scan_init[l], 1, 0)
         if l == last:
-            grads = back_gated(layer, kept[l], grad_low)
+            grads = back_gated(kept[l], late_gated)
             late = back_local(layer, kept[l], grads[1])
             start, end = exchange(layer, [local, late], totals, first, (False, True), layer_total + l)
         else:
@@ -899,7 +931,8 @@
             half, stored = lax.optimization_barrier((half, weights[1]))
             into = [stored[k].reshape(width, -1) for k in range(layer_total)]
             layers[l + 1].raw = stored[l + 1]
-            got, into, grad_low = lax.optimization_barrier((across(half), into, grad_low))
+            late_gated = dot_n(grad_low, layers[last].out)
+            got, into, grad_low, late_gated = lax.optimization_barrier((across(half), into, grad_low, late_gated))
             for each, array in zip(layers, into):
                 each.into = array
             branch = half + got
@@ -914,8 +947,8 @@
         layer = layers[l]
         normed, base = norms[l]
         if l < last:
-            grads, out_grad, scattered[last] = lax.optimization_barrier(
-                (back_gated(layer, kept[l], grad_low), dot_t(grad_low, scans[l][1]), scattered[last]))
+            grads, out_grad = lax.optimization_barrier(
+                (back_gated(kept[l], dot_n(grad_low, layer.out)), dot_t(grad_low, scans[l][1])))
             scattered[l] = [blk_scatter(out_grad)]
             late = back_local(layer, kept[l], grads[1])
             end, = exchange(layer, [late], kept[l][-1], jnp.zeros_like(late[:, 0]), (True,), 2 + 2 * layer_total + l)
@@ -925,11 +958,11 @@
         middle = half.shape[0] // 2
         if l == last:
             end, side, out_grad, half = lax.optimization_barrier((end, side, out_grad, half))
-            scattered[l] = [blk_scatter(out_grad)]
+            scattered[l] = [blk_scatter(out_grad), blk_scatter(side[0])]
             scan_out, got = lax.optimization_barrier(
                 (back_scan(layer, kept[l], scans[l], grads, end), across(half[:middle])))
         else:
-            end, side, half = lax.optimization_barrier((end, side, half))
+            end, side, half, scattered[last] = lax.optimization_barrier((end, side, half, scattered[last]))
             scattered[l].append(blk_scatter(side[0]))
             scan_out, got_rest = lax.optimization_barrier(
                 (back_scan(layer, kept[l], scans[l], grads, end), across(half[middle:])))
@@ -945,9 +978,10 @@
         inner = smalls[l].shape[-1]
         if l == last:
             thins = thick[1:] + thins
-            normed_grad, thick, smalls[l] = joint_sums(
-                normed_part, [rows(thick[0]), side[0]], (128, 128), smalls[l], l)
-            scattered[l] += [thick[1], thick[0]]
+            joint, scattered[l][0] = lax.optimization_barrier((joint_sums(
+                normed_part, base, layer.gain, [rows(thick[0])], (128,), smalls[l], l), scattered[l][0]))
+            change, gains[l], thick, smalls[l] = joint
+            scattered[l].append(thick[0])
         else:
             thins = thick[1:] + thins
             cuts = [part.shape[1] for part in thins]
@@ -959,12 +993,12 @@
             small = jnp.concatenate([smalls[l], shared], axis=0)
             small = jnp.pad(small, ((0, -small.shape[0] % 8), (0, 0)))
             normed_part, thins, out = lax.optimization_barrier((normed_part, thins, out))
-            normed_grad, thick, small = joint_sums(
-                normed_part, [rows(thick[0]), rows(jnp.concatenate(thins, axis=1))], (0, inner), small, l)
+            change, gains[l], thick, small = joint_sums(
+                normed_part, base, layer.gain, [rows(thick[0]), rows(jnp.concatenate(thins, axis=1))], (0, inner),
+                small, l)
             scattered[l].append(thick[0])
             smalls[l], rest = small[:own_count], small[own_count:]
-        gains[l], change = norm_back(layer, normed_grad, base, inverse_rms(base))
-        grad = grad + all_rows(change)
+        grad = grad + change
         grad_low = grad.astype(jnp.bfloat16)
     first_gain = blk_sum(rows_sum(gains[0].reshape(-1, inner)))
     input_grad = restore(grad_low)

time: 1420 us -> 1310 us (0.923)
  Pallas kernels: 760 us -> 684 us
  other arithmetic: 165 us -> 144 us
    pallas_call x2, Pallas kernels: 414 us -> 347 us  [joint_sums(): pl.pallas_call(partial(joint_body, plan, chunks), in_specs=[any_spec, any...]
    ppermute x3, waiting for transfers between devices: 33.5 us -> 18 us  [across(): return lax.ppermute(half, 'tensor', ACROSS)]
    unnamed x287 -> x257, local copies, waits for them, and re-layouts: 61.3 us -> 47.6 us
  transfers between devices with their start and end apart: 33 -> 32, of which waited for: 18 -> 17; matrix products, arithmetic and copies ran while one was open for 24% -> 25% of each run, Pallas kernels for 42% -> 40%
where the time goes in v6:
time: 1310 us; the launch traced here: 1300 us
  Pallas kernels  684 us (52%)
  matrix products  200 us (15%)
  other arithmetic  144 us (11%)
  local copies, waits for them, and re-layouts  139 us (11%)
  waiting for transfers between devices  90.8 us (7%)
  starting transfers between devices  20.9 us (2%)
  between operations  18 us (1%)
    pallas_call x2, Pallas kernels, joint_sums(): pl.pallas_call(partial(joint_body, plan, chunks), in_specs=[any_spec, any...  347 us
    pallas_call x2, Pallas kernels, scan_backward(): pl.pallas_call(partial(back_body, C // LANES, width), grid=(T // tb,), in...  120 us
    dot_general x10, matrix products, dot_n(): lax.dot_general(left, right, (((1,), (1,)), ((), ())), preferred_element_...  95.3 us
    pallas_call x3, Pallas kernels, hops(): pl.pallas_call(partial(hop_body, reverses, groups), in_specs=[spec] * (3...  87.5 us
    dot_general x12, matrix products, dot_t(): lax.dot_general(left, right, (((0,), (0,)), ((), ())), preferred_element_...  64 us
    pallas_call x2, Pallas kernels, scan_forward(): pl.pallas_call(partial(scan_body, C // LANES, width), grid=(T // tb,), in...  62.9 us
    unnamed x257, local copies, waits for them, and re-layouts  47.6 us
    pallas_call x2, Pallas kernels, start_grads(): pl.pallas_call(partial(start_body, C // LANES, width), grid=(T // tb,), i...  33.4 us
  transfers between devices with their start and end apart: 32, of which 17 were waited for; matrix products, arithmetic and copies ran while one was open for 25% of the time, Pallas kernels for 40%

profile of v6, /device:TPU:0, one launch (start us, length us, event | category | flops | bytes accessed | tf_op | source)
XLA Modules:
  0.0 1296.5 jit_solution(1426351337135919299)
XLA Ops:
  79.5 16.5 %end_states.2.refs_0_ = f32[16,8,1024]{2,1,0:T(8,128)S(1)} custom-call(f32[128,8,1024]{2,1,0:T(8,128)S(1)} %bitcast.380, f32[128,8,1024]{2,1,0:T(8,128)S(1)} %fusion.17.push_ref, f32[128,8,32]{2,1,0:T(8,128)S(1)} %bitcast.392, f32[16,1024]{1,0:T(8,128)S(1)} %get-tuple-element.292.rate_ref), custom_call_target="tpu_custom_call" | custom-call | flops 67108864 | bytes 67108864 | tf_op jit(solution)/shard_map/end_states/pallas_call | solution.py:58
  96.0 16.1 %hops.3.start_ref.begin_ref = f32[16,8,1024]{2,1,0:T(8,128)S(1)} custom-call(f32[8,1024]{1,0:T(8,128)S(1)} %get-tuple-element.309.total_ref, f32[16,1024]{1,0:T(8,128)S(1)} %get-tuple-element.292.rate_ref, f32[16,8,1024]{2,1,0:T(8,128)S(1)} %end_states.2.refs_0_, f32[16,8,1024]{2,1,0:T(8,128)S(1)} %get-tuple-element.318.refs_1_), custom_call_target="tpu_custom_call" | custom-call | bytes 26214400 | tf_op jit(solution)/shard_map/hops/pallas_call | solution.py:674
  112.1 31.5 %scan_forward.2 = (f32[128,8,1024]{2,1,0:T(8,128)S(1)}, f32[128,16,8,1024]{3,2,1,0:T(8,128)}, f32[16,8,1024]{2,1,0:T(8,128)S(1)}) custom-call(f32[128,8,1024]{2,1,0:T(8,128)} %bitcast.381, f32[128,8,1024]{2,1,0:T(8,128)} %copy-done.4, f32[128,8,32]{2,1,0:T(8,128)S(1)} %bitcast.393, f32[16,1024]{1,0:T(8,128)S(1)} %get-tuple-element.292.rate_ref, ...), custom_call_target="tpu_custom_call" | custom-call | flops 117440512 | bytes 117440512 | tf_op jit(solution)/shard_map/scan_forward/pallas_call | solution.py:107
  183.4 10.8 fusion.38
  194.2 11.3 copy.79
  220.0 11.6 copy.80
  241.9 18.0 %collective-permute-done.5 = f32[512,2048]{1,0:T(8,128)} collective-permute-done((f32[512,2048]{1,0:T(8,128)}, f32[512,2048]{1,0:T(8,128)}, u32[]{:S(2)}, u32[]{:S(2)}) %collective-permute-start.5) | collective-permute-done | bytes 4194336 | tf_op jit(solution)/shard_map/ppermute | solution.py:297
  285.5 11.1 fusion.65
  330.7 16.7 %start_grads.2.refs_1_ = f32[16,8,1024]{2,1,0:T(8,128)S(1)} custom-call(f32[128,8,1024]{2,1,0:T(8,128)S(1)} %bitcast.384, f32[128,8,1024]{2,1,0:T(8,128)S(1)} %bitcast.390, f32[128,8,32]{2,1,0:T(8,128)S(1)} %bitcast.396, f32[16,1024]{1,0:T(8,128)S(1)} %get-tuple-element.291.rate_ref), custom_call_target="tpu_custom_call" | custom-call | flops 67108864 | bytes 67108864 | tf_op jit(solution)/shard_map/start_grads/pallas_call | solution.py:145
  347.4 16.5 %end_states.3.refs_0_ = f32[16,8,1024]{2,1,0:T(8,128)S(1)} custom-call(f32[128,8,1024]{2,1,0:T(8,128)S(1)} %bitcast.385, f32[128,8,1024]{2,1,0:T(8,128)S(1)} %get-tuple-element.271.push_ref, f32[128,8,32]{2,1,0:T(8,128)S(1)} %bitcast.397, f32[16,1024]{1,0:T(8,128)S(1)} %get-tuple-element.291.rate_ref), custom_call_target="tpu_custom_call" | custom-call | flops 67108864 | bytes 67108864 | tf_op jit(solution)/shard_map/end_states/pallas_call | solution.py:58
  363.9 38.8 %hops.4 = (f32[16,8,1024]{2,1,0:T(8,128)S(1)}, f32[16,8,1024]{2,1,0:T(8,128)S(1)}) custom-call(f32[8,1024]{1,0:T(8,128)S(1)} %get-tuple-element.311.total_ref, f32[16,1024]{1,0:T(8,128)S(1)} %get-tuple-element.291.rate_ref, f32[16,8,1024]{2,1,0:T(8,128)S(1)} %end_states.3.refs_0_, f32[16,8,1024]{2,1,0:T(8,128)S(1)} %start_grads.2.refs_1_, ...), custom_call_target="tpu_custom_call" | custom-call | bytes 26214400 | tf_op jit(solution)/shard_map/hops/pallas_call | solution.py:674
  402.7 31.4 %scan_forward.3 = (f32[128,8,1024]{2,1,0:T(8,128)S(1)}, f32[128,16,8,1024]{3,2,1,0:T(8,128)}, f32[16,8,1024]{2,1,0:T(8,128)S(1)}) custom-call(f32[128,8,1024]{2,1,0:T(8,128)} %bitcast.386, f32[128,8,1024]{2,1,0:T(8,128)} %copy-done.5, f32[128,8,32]{2,1,0:T(8,128)S(1)} %bitcast.398, f32[16,1024]{1,0:T(8,128)S(1)} %get-tuple-element.291.rate_ref, ...), custom_call_target="tpu_custom_call" | custom-call | flops 117440512 | bytes 117440512 | tf_op jit(solution)/shard_map/scan_forward/pallas_call | solution.py:107
  468.9 10.8 fusion.51
  488.9 60.1 %scan_backward.2 = (f32[128,8,1024]{2,1,0:T(8,128)}, f32[128,8,1024]{2,1,0:T(8,128)}, f32[128,8,32]{2,1,0:T(8,128)S(1)}, f32[16,8,1024]{2,1,0:T(8,128)S(1)}, f32[16,8,1024]{2,1,0:T(8,128)S(1)}) custom-call(f32[128,8,1024]{2,1,0:T(8,128)} %bitcast.387, f32[128,8,1024]{2,1,0:T(8,128)} %copy-done.5, f32[128,8,1024]{2,1,0:T(8,128)} %bitcast.391, ...), custom_call_target="tpu_custom_call" | custom-call | flops 218103808 | bytes 218103808 | tf_op jit(solution)/shard_map/scan_backward/pallas_call | solution.py:231
  573.5 13.0 %fusion.137 = (f32[1024]{0:T(1024)S(1)}, f32[1024]{0:T(1024)S(1)}, f32[1024]{0:T(1024)S(1)}, f32[1024]{0:T(1024)S(1)}, f32[1024]{0:T(1024)S(1)}, /*index=5*/f32[1024,1024]{1,0:T(8,128)S(1)}) fusion(f32[2,1024,1024]{2,1,0:T(8,128)} %fusion.65, f32[1024,1024]{1,0:T(8,128)} %copy-done.48, f32[24,1024]{1,0:T(8,128)S(1)} %fusion.120, ...), kind=kOutput, calls=%fused_computation.302 | convolution fusion | flops 698870784 | bytes 30466048 | tf_op jit(solution)/shard_map/dot_general | solution.py:705
  598.4 10.9 fusion.74
  619.9 161.6 %joint_sums.2 = (f32[1024,2048]{1,0:T(8,128)}, f32[8,2048]{1,0:T(8,128)S(1)}, f32[256,1024]{1,0:T(8,128)S(1)}, f32[23,1024]{1,0:T(8,128)S(1)}) custom-call(f32[1024,2048]{1,0:T(8,128)} %fusion.55.sum_ref, f32[512,2048]{1,0:T(8,128)} %copy-done.35, f32[1,2048]{1,0:T(1,128)S(1)} %copy-done.30, f32[2,2,2,256,1024]{4,3,2,1,0:T(8,128)} %bitcast.434, ...), custom_call_target="tpu_custom_call" | custom-call | bytes 419430400 | tf_op jit(solution)/shard_map/joint_sums/pallas_call | solution.py:526
  781.6 15.2 %fusion.132 = f32[2048,1024]{1,0:T(8,128)} fusion(bf16[1024,1024]{1,0:T(8,128)(2,1)} %copy-done.66, f32[1024,2048]{1,0:T(8,128)} %get-tuple-element.121, bf16[128,1,8,2048]{3,0,2,1:T(8,128)(2,1)} %bitcast.423), kind=kOutput, calls=%fused_computation.299 | convolution fusion | flops 4301258752 | bytes 23068672 | tf_op jit(solution)/shard_map/dot_general | solution.py:701
  796.7 16.0 %fusion.101 = (f32[1024,1024]{1,0:T(8,128)}, f32[1024,1024]{1,0:T(8,128)}) fusion(f32[2,1024,1024]{2,1,0:T(8,128)} %copy-done.41, bf16[2,1024,2048]{2,1,0:T(8,128)(2,1)} %param.25, f32[1024,2048]{1,0:T(8,128)} %get-tuple-element.121, bf16[128,1,8,2048]{3,0,2,1:T(8,128)(2,1)} %bitcast.424), kind=kOutput, calls=%fused_computation.200 | convolution fusion | flops 4306501632 | bytes 29360128 | tf_op jit(solution)/shard_map/dot_general | solution.py:705
  818.3 16.7 %start_grads.3.refs_0_ = f32[16,8,1024]{2,1,0:T(8,128)S(1)} custom-call(f32[128,8,1024]{2,1,0:T(8,128)S(1)} %bitcast.383, f32[128,8,1024]{2,1,0:T(8,128)S(1)} %bitcast.389, f32[128,8,32]{2,1,0:T(8,128)S(1)} %bitcast.394, f32[16,1024]{1,0:T(8,128)S(1)} %copy-done.14), custom_call_target="tpu_custom_call" | custom-call | flops 67108864 | bytes 67108864 | tf_op jit(solution)/shard_map/start_grads/pallas_call | solution.py:145
  835.1 32.6 %hops.5.end_ref = f32[16,8,1024]{2,1,0:T(8,128)S(1)} custom-call(f32[8,1024]{1,0:T(8,128)S(1)} %copy-done.26, f32[16,1024]{1,0:T(8,128)S(1)} %copy-done.14, f32[16,8,1024]{2,1,0:T(8,128)S(1)} %start_grads.3.refs_0_, f32[16,8,1024]{2,1,0:T(8,128)S(1)} %broadcast_in_dim.41.refs_1_), custom_call_target="tpu_custom_call" | custom-call | bytes 26214400 | tf_op jit(solution)/shard_map/hops/pallas_call | solution.py:674
  906.5 59.8 %scan_backward.3 = (f32[128,8,1024]{2,1,0:T(8,128)}, f32[128,8,1024]{2,1,0:T(8,128)}, f32[128,8,32]{2,1,0:T(8,128)S(1)}, f32[16,8,1024]{2,1,0:T(8,128)S(1)}, f32[16,8,1024]{2,1,0:T(8,128)S(1)}) custom-call(f32[128,8,1024]{2,1,0:T(8,128)} %bitcast.382, f32[128,8,1024]{2,1,0:T(8,128)} %copy-done.4, f32[128,8,1024]{2,1,0:T(8,128)} %bitcast.388, ...), custom_call_target="tpu_custom_call" | custom-call | flops 218103808 | bytes 218103808 | tf_op jit(solution)/shard_map/scan_backward/pallas_call | solution.py:231
  1001.4 12.1 fusion.136
  1059.2 185.6 %joint_sums.3 = (f32[1024,2048]{1,0:T(8,128)}, f32[8,2048]{1,0:T(8,128)S(1)}, f32[256,1024]{1,0:T(8,128)S(1)}, f32[80,1024]{1,0:T(8,128)S(1)}, f32[32,1024]{1,0:T(8,128)S(1)}) custom-call(f32[1024,2048]{1,0:T(8,128)} %fusion.58.sum_ref, f32[512,2048]{1,0:T(8,128)} %get-tuple-element.240.base_ref, f32[1,2048]{1,0:T(1,128)S(1)} %copy-done.28, ...), custom_call_target="tpu_custom_call" | custom-call | bytes 419430400 | tf_op jit(solution)/shard_map/joint_sums/pallas_call | solution.py:526
  (494 shorter events, 453.9 us)
Async XLA Ops:
  7.2 774.4 %reduce-scatter.5.cloned.1.call-start = ((), (), s32[]{:S(2)}) async-start(), calls=%async_computation.4 | async-start | bytes 9437184 | tf_op jit(solution)/shard_map/reduce_scatter | solution.py:322
  39.2 8.8 collective-permute-start
  61.4 9.8 collective-permute-start.2
  157.0 7.2 collective-permute-start.4
  166.9 92.9 %collective-permute-start.5 = (f32[512,2048]{1,0:T(8,128)}, f32[512,2048]{1,0:T(8,128)}, u32[]{:S(2)}, u32[]{:S(2)}) collective-permute-start(f32[512,2048]{1,0:T(8,128)} %dynamic-slice_add_fusion.1), channel_id=1, source_target_pairs={{0,2},{2,0},{1,3},{3,1},{4,6},{6,4},{5,7},{7,5},{8,10},{10,8},{9,1... | collective-permute-start | bytes 12582920 | tf_op jit(solution)/shard_map/ppermute | solution.py:297
  267.3 7.4 collective-permute-start.6
  298.1 5.3 collective-permute-start.7
  310.4 9.8 collective-permute-start.9
  451.1 28.5 %collective-permute-start.11 = (f32[512,2048]{1,0:T(8,128)}, f32[512,2048]{1,0:T(8,128)}, u32[]{:S(2)}, u32[]{:S(2)}) collective-permute-start(f32[512,2048]{1,0:T(8,128)} %constant_dynamic-slice_fusion), channel_id=1, source_target_pairs={{0,1},{1,0},{2,3},{3,2},{4,5},{5,4},{6,7},{7,6},{8,9},{9,8},{10,11... | collective-permute-start | bytes 12582920 | tf_op jit(solution)/shard_map/ppermute | solution.py:291
  484.7 406.5 %reduce-scatter.7.cloned.1.call-start = ((), (), s32[]{:S(2)}) async-start(), calls=%async_computation.5 | async-start | bytes 9437184 | tf_op jit(solution)/shard_map/reduce_scatter | solution.py:322
  485.5 788.8 %reduce-scatter.11.cloned.1.call-start = ((), (), s32[]{:S(2)}) async-start(), calls=%async_computation.7 | async-start | bytes 9437184 | tf_op jit(solution)/shard_map/reduce_scatter | solution.py:322
  487.3 62.4 %collective-permute-start.12 = (f32[256,2048]{1,0:T(8,128)S(1)}, f32[256,2048]{1,0:T(8,128)}, u32[]{:S(2)}, u32[]{:S(2)}) collective-permute-start(f32[256,2048]{1,0:T(8,128)S(1)} %slice.340), channel_id=1, source_target_pairs={{0,2},{2,0},{1,3},{3,1},{4,6},{6,4},{5,7},{7,5},{8,10},{10,8},{9,1... | collective-permute-start | bytes 6291464 | tf_op jit(solution)/shard_map/ppermute | solution.py:297
  561.6 10.0 collective-permute-start.14
  590.1 7.4 collective-permute-start.16
  812.8 467.1 %reduce-scatter.9.cloned.1.call-start = ((), (), s32[]{:S(2)}) async-start(), calls=%async_computation.6 | async-start | bytes 9437184 | tf_op jit(solution)/shard_map/reduce_scatter | solution.py:322
  894.3 73.8 %collective-permute-start.17 = (f32[256,2048]{1,0:T(8,128)}, f32[256,2048]{1,0:T(8,128)}, u32[]{:S(2)}, u32[]{:S(2)}) collective-permute-start(f32[256,2048]{1,0:T(8,128)} %slice.348), channel_id=1, source_target_pairs={{0,2},{2,0},{1,3},{3,1},{4,6},{6,4},{5,7},{7,5},{8,10},{10,8},{9,1... | collective-permute-start | bytes 6291464 | tf_op jit(solution)/shard_map/ppermute | solution.py:297
  977.2 9.3 collective-permute-start.18
  985.9 13.3 %collective-permute-start.23 = (f32[3,1024]{1,0:T(4,128)S(1)}, f32[3,1024]{1,0:T(4,128)S(1)}, u32[]{:S(2)}, u32[]{:S(2)}) collective-permute-start(f32[3,1024]{1,0:T(4,128)S(1)} %pad_maximum_fusion.22), channel_id=1, source_target_pairs={{0,1},{1,0},{2,3},{3,2},{4,5},{5,4},{6,7},{7,6},{8,9},{9,8},{10,11... | collective-permute-start | bytes 36872 | tf_op jit(solution)/shard_map/ppermute | solution.py:310
  987.5 9.8 collective-permute-start.19
  988.0 60.5 %collective-permute-start.22 = (f32[512,2048]{1,0:T(8,128)}, f32[512,2048]{1,0:T(8,128)}, u32[]{:S(2)}, u32[]{:S(2)}) collective-permute-start(f32[512,2048]{1,0:T(8,128)} %get-tuple-element.255), channel_id=1, source_target_pairs={{0,1},{1,0},{2,3},{3,2},{4,5},{5,4},{6,7},{7,6},{8,9},{9,8},{10,11... | collective-permute-start | bytes 12582920 | tf_op jit(solution)/shard_map/ppermute | solution.py:303
  1020.7 10.7 collective-permute-start.21
  1244.9 10.6 collective-permute-start.24
  1255.5 3.7 collective-permute-start.25
  1262.9 10.7 collective-permute-start.27
  (132 other events, 1558.4 us)
Sparse Core Ops, SparseCore 0:
  484.8 151.1 reduce-scatter.4
  640.1 212.9 reduce-scatter.6
  856.8 154.6 reduce-scatter.10
  1015.4 231.9 reduce-scatter.8

commit v7 on v6

--- a/solution.py
+++ b/solution.py
@@ -21,23 +21,22 @@
     return pltpu.CompilerParams(dimension_semantics=("arbitrary",), vmem_limit_bytes=limit)
 
 def spread(ref_value, out, first):
-    for t in range(out.shape[0]):
-        row = ref_value[t]
-        for n in range(STATE):
-            out[t, n] = jnp.broadcast_to(row[:, first + n:first + n + 1], out.shape[2:])
+    for n in range(STATE):
+        for t in range(out.shape[0]):
+            out[t, n] = jnp.broadcast_to(ref_value[t, :, first + n:first + n + 1], out.shape[2:])
 
 def rates(rate_ref, lanes, n):
     return jnp.broadcast_to(rate_ref[pl.ds(n, 1), lanes], (8, LANES))
 
-def end_body(blocks, width, step_ref, push_ref, coef_ref, rate_ref, end_ref, write):
+def end_body(blocks, width, held, step_ref, push_ref, coef_ref, rate_ref, end_ref, write):
     @pl.when(pl.program_id(0) == 0)
     def _():
         end_ref[...] = jnp.zeros_like(end_ref)
     spread(coef_ref, write, 0)
     def group(g, _):
         cols = [pl.ds(pl.multiple_of((g * width + k) * LANES, LANES), LANES) for k in range(width)]
-        for low in range(0, STATE, STATE // width):
-            span = range(low, low + STATE // width)
+        for low in range(0, STATE, held):
+            span = range(low, low + held)
             state = {(k, n): end_ref[n, :, cols[k]] for k in range(width) for n in span}
             rate = {(k, n): rates(rate_ref, cols[k], n) for k in range(width) for n in span}
             for t in range(step_ref.shape[0]):
@@ -53,10 +52,10 @@
         return 0
     lax.fori_loop(0, blocks // width, group, 0)
 
-def end_states(step, push, coef, rate, tb=8, width=2, limit=40*2**20):
+def end_states(step, push, coef, rate, tb=16, width=2, held=8, limit=48*2**20):
     T, _, C = step.shape
     return pl.pallas_call(
-        partial(end_body, C // LANES, width),
+        partial(end_body, C // LANES, width, held),
         grid=(T // tb,),
         in_specs=[pl.BlockSpec((tb, 8, C), lambda i: (i, 0, 0)), pl.BlockSpec((tb, 8, C), lambda i: (i, 0, 0)),
                   pl.BlockSpec((tb, 8, 2 * STATE), lambda i: (i, 0, 0)), pl.BlockSpec((STATE, C), lambda i: (0, 0))],
@@ -65,7 +64,7 @@
         scratch_shapes=[pltpu.VMEM((tb, STATE, 8, LANES), jnp.float32)],
         compiler_params=cp(limit), cost_estimate=cost(step, 4), name="end_states")(step, push, coef, rate)
 
-def scan_body(blocks, width, step_ref, push_ref, coef_ref, rate_ref, start_ref, out_ref, states_ref, final_ref, write, read):
+def scan_body(blocks, width, held, step_ref, push_ref, coef_ref, rate_ref, start_ref, out_ref, states_ref, final_ref, write, read):
     @pl.when(pl.program_id(0) == 0)
     def _():
         final_ref[...] = start_ref[...]
@@ -73,8 +72,8 @@
     spread(coef_ref, read, STATE)
     def group(g, _):
         cols = [pl.ds(pl.multiple_of((g * width + k) * LANES, LANES), LANES) for k in range(width)]
-        for low in range(0, STATE, STATE // width):
-            span = range(low, low + STATE // width)
+        for low in range(0, STATE, held):
+            span = range(low, low + held)
             state = {(k, n): final_ref[n, :, cols[k]] for k in range(width) for n in span}
             rate = {(k, n): rates(rate_ref, cols[k], n) for k in range(width) for n in span}
             for t in range(step_ref.shape[0]):
@@ -99,13 +98,13 @@
         return 0
     lax.fori_loop(0, blocks // width, group, 0)
 
-def scan_forward(step, push, coef, rate, start, tb=8, width=2, limit=48*2**20):
+def scan_forward(step, push, coef, rate, start, tb=16, width=2, held=8, limit=48*2**20):
     T, _, C = step.shape
     row = pl.BlockSpec((tb, 8, C), lambda i: (i, 0, 0))
     whole = pl.BlockSpec((STATE, 8, C), lambda i: (0, 0, 0))
     f32 = jnp.float32
     return pl.pallas_call(
-        partial(scan_body, C // LANES, width),
+        partial(scan_body, C // LANES, width, held),
         grid=(T // tb,),
         in_specs=[row, row, pl.BlockSpec((tb, 8, 2 * STATE), lambda i: (i, 0, 0)), pl.BlockSpec((STATE, C), lambda i: (0, 0)), whole],
         out_specs=[row, pl.BlockSpec((tb, STATE, 8, C), lambda i: (i, 0, 0, 0)), whole],
@@ -114,15 +113,15 @@
         scratch_shapes=[pltpu.VMEM((tb, STATE, 8, LANES), f32)] * 2,
         compiler_params=cp(limit), cost_estimate=cost(step, 7), name="scan_forward")(step, push, coef, rate, start)
 
-def start_body(blocks, width, step_ref, grad_ref, coef_ref, rate_ref, start_ref, read):
+def start_body(blocks, width, held, step_ref, grad_ref, coef_ref, rate_ref, start_ref, read):
     @pl.when(pl.program_id(0) == 0)
     def _():
         start_ref[...] = jnp.zeros_like(start_ref)
     spread(coef_ref, read, STATE)
     def group(g, _):
         cols = [pl.ds(pl.multiple_of((g * width + k) * LANES, LANES), LANES) for k in range(width)]
-        for low in range(0, STATE, STATE // width):
-            span = range(low, low + STATE // width)
+        for low in range(0, STATE, held):
+            span = range(low, low + held)
             state = {(k, n): start_ref[n, :, cols[k]] for k in range(width) for n in span}
             rate = {(k, n): rates(rate_ref, cols[k], n) for k in range(width) for n in span}
             for t in reversed(range(step_ref.shape[0])):
@@ -138,12 +137,12 @@
         return 0
     lax.fori_loop(0, blocks // width, group, 0)
 
-def start_grads(step, grad, coef, rate, tb=8, width=2, limit=40*2**20):
+def start_grads(step, grad, coef, rate, tb=16, width=2, held=8, limit=48*2**20):
     T, _, C = step.shape
     last = T // tb - 1
     row = pl.BlockSpec((tb, 8, C), lambda i: (last - i, 0, 0))
     return pl.pallas_call(
-        partial(start_body, C // LANES, width),
+        partial(start_body, C // LANES, width, held),
         grid=(T // tb,),
         in_specs=[row, row, pl.BlockSpec((tb, 8, 2 * STATE), lambda i: (last - i, 0, 0)), pl.BlockSpec((STATE, C), lambda i: (0, 0))],
         out_specs=pl.BlockSpec((STATE, 8, C), lambda i: (0, 0, 0)),
@@ -151,7 +150,7 @@
         scratch_shapes=[pltpu.VMEM((tb, STATE, 8, LANES), jnp.float32)],
         compiler_params=cp(limit), cost_estimate=cost(step, 4), name="start_grads")(step, grad, coef, rate)
 
-def back_body(blocks, width, step_ref, push_ref, grad_ref, coef_ref, rate_ref, states_ref, prior_ref, begin_ref, end_ref,
+def back_body(blocks, width, held, step_ref, push_ref, grad_ref, coef_ref, rate_ref, states_ref, prior_ref, begin_ref, end_ref,
               decay_out, push_out, coef_out, start_ref, speed_ref, write, read, write_sum, read_sum):
     @pl.when(pl.program_id(0) == 0)
     def _():
@@ -162,9 +161,10 @@
     tb = step_ref.shape[0]
     begins = pl.program_id(0) == pl.num_programs(0) - 1
     def group(g, first):
-        cols = [pl.ds(pl.multiple_of((g * width + k) * LANES, LANES), LANES) for k in range(width)]
-        for low in range(0, STATE, STATE // width):
-            span = range(low, low + STATE // width)
+        cols = [pl.ds((g * width + k) * LANES if first else pl.multiple_of((g * width + k) * LANES, LANES), LANES)
+                for k in range(width)]
+        for low in range(0, STATE, held):
+            span = range(low, low + held)
             carry = {(k, n): start_ref[n, :, cols[k]] for k in range(width) for n in span}
             speed = {(k, n): speed_ref[n, :, cols[k]] for k in range(width) for n in span}
             rate = {(k, n): rates(rate_ref, cols[k], n) for k in range(width) for n in span}
@@ -182,9 +182,9 @@
                     for k in range(width):
                         before = states_ref[t - 1, n, :, cols[k]] if t else enter[k, n]
                         back = carry[k, n] + r * grad[k]
-                        held = jnp.exp2(step[k] * rate[k, n]) * back
-                        carry[k, n] = held
-                        q = held * before
+                        onward = jnp.exp2(step[k] * rate[k, n]) * back
+                        carry[k, n] = onward
+                        q = onward * before
                         speed[k, n] = speed[k, n] + step[k] * q
                         rq, bw = rate[k, n] * q, back * w
                         decays[k] = rq if decays[k] is None else decays[k] + rq
@@ -210,9 +210,8 @@
                     start_ref[n, :, cols[k]] = carry[k, n]
                     speed_ref[n, :, cols[k]] = speed[k, n]
         return 0
-    write_sum[...] = jnp.zeros_like(write_sum)
-    read_sum[...] = jnp.zeros_like(read_sum)
-    lax.fori_loop(0, blocks // width, lambda g, _: group(g, False), 0)
+    group(0, True)
+    lax.fori_loop(1, blocks // width, lambda g, _: group(g, False), 0)
     lane = lax.broadcasted_iota(jnp.int32, (8, 2 * STATE), 1)
     for t in range(tb):
         row = jnp.zeros((8, 2 * STATE), jnp.float32)
@@ -221,7 +220,7 @@
             row = jnp.where(lane == STATE + n, jnp.sum(read_sum[t, n], axis=-1, keepdims=True), row)
         coef_out[t] = row
 
-def scan_backward(step, push, grad, coef, rate, states, begin, end, tb=8, width=2, limit=48*2**20):
+def scan_backward(step, push, grad, coef, rate, states, begin, end, tb=8, width=2, held=4, limit=48*2**20):
     T, _, C = step.shape
     last = T // tb - 1
     f32 = jnp.float32
@@ -229,7 +228,7 @@
     thin = pl.BlockSpec((tb, 8, 2 * STATE), lambda i: (last - i, 0, 0))
     whole = pl.BlockSpec((STATE, 8, C), lambda i: (0, 0, 0))
     return pl.pallas_call(
-        partial(back_body, C // LANES, width),
+        partial(back_body, C // LANES, width, held),
         grid=(T // tb,),
         in_specs=[row, row, row, thin, pl.BlockSpec((STATE, C), lambda i: (0, 0)),
                   pl.BlockSpec((tb, STATE, 8, C), lambda i: (last - i, 0, 0, 0)),
@@ -794,7 +793,7 @@
     scanned, states, final = scan_forward(by_step(step), by_step(push), coef, layer.rate2, start)
     result = rows(scanned) + layer.skip * inputs.astype(jnp.float32)
     gated = (result * jax.nn.silu(gate)).astype(jnp.bfloat16)
-    return dot32(gated, layer.out), (result, gated, states, start), final
+    return (result, gated, states, start), final
 
 
 def back_gated(kept, grad_gated):
@@ -924,7 +923,11 @@
             start, end = exchange(layer, [local, late], totals, first, (False, True), layer_total + l)
         else:
             start, = exchange(layer, [local], totals, first, (False,), layer_total + l)
-        partial_sum, scans[l], final = scanning(layer, kept[l], start)
+        scans[l], final = scanning(layer, kept[l], start)
+        gated = scans[l][1]
+        if l == last:
+            gated, late_out = lax.optimization_barrier((gated, dot_t(grad_low, gated)))
+        partial_sum = dot32(gated, layer.out)
         finals[l] = split_parts(final, parts)[:, -1]
         half = core_sum(partial_sum)
         if l < last:
@@ -953,17 +956,18 @@
             late = back_local(layer, kept[l], grads[1])
             end, = exchange(layer, [late], kept[l][-1], jnp.zeros_like(late[:, 0]), (True,), 2 + 2 * layer_total + l)
         else:
-            out_grad = dot_t(grad_low, scans[l][1])
+            out_grad = late_out
         side = back_side(layer, kept[l], normed, scans[l], grads, grad_low)
         middle = half.shape[0] // 2
         if l == last:
-            end, side, out_grad, half = lax.optimization_barrier((end, side, out_grad, half))
             scattered[l] = [blk_scatter(out_grad), blk_scatter(side[0])]
+            end, side, half = lax.optimization_barrier((end, side, half))
             scan_out, got = lax.optimization_barrier(
                 (back_scan(layer, kept[l], scans[l], grads, end), across(half[:middle])))
         else:
+            scattered[l].append(blk_scatter(side[0]))
             end, side, half, scattered[last] = lax.optimization_barrier((end, side, half, scattered[last]))
-            scattered[l].append(blk_scatter(side[0]))
+            stacked_last = jnp.stack([scattered[last][2], scattered[last][1]], axis=1)
             scan_out, got_rest = lax.optimization_barrier(
                 (back_scan(layer, kept[l], scans[l], grads, end), across(half[middle:])))
             branch = half + jnp.concatenate([got, got_rest], axis=0)
@@ -979,7 +983,7 @@
         if l == last:
             thins = thick[1:] + thins
             joint, scattered[l][0] = lax.optimization_barrier((joint_sums(
-                normed_part, base, layer.gain, [rows(thick[0])], (128,), smalls[l], l), scattered[l][0]))
+                normed_part, base, layer.gain, [rows(thick[0])], (0,), smalls[l], l), scattered[l][0]))
             change, gains[l], thick, smalls[l] = joint
             scattered[l].append(thick[0])
         else:
@@ -992,7 +996,7 @@
             own_count = smalls[l].shape[0]
             small = jnp.concatenate([smalls[l], shared], axis=0)
             small = jnp.pad(small, ((0, -small.shape[0] % 8), (0, 0)))
-            normed_part, thins, out = lax.optimization_barrier((normed_part, thins, out))
+            normed_part, thins, out, stacked_last = lax.optimization_barrier((normed_part, thins, out, stacked_last))
             change, gains[l], thick, small = joint_sums(
                 normed_part, base, layer.gain, [rows(thick[0]), rows(jnp.concatenate(thins, axis=1))], (0, inner),
                 small, l)
@@ -1000,6 +1004,8 @@
             smalls[l], rest = small[:own_count], small[own_count:]
         grad = grad + change
         grad_low = grad.astype(jnp.bfloat16)
+        if l:
+            grad_low = lax.optimization_barrier(grad_low)
     first_gain = blk_sum(rows_sum(gains[0].reshape(-1, inner)))
     input_grad = restore(grad_low)
 
@@ -1016,7 +1022,7 @@
     for cut in cuts:
         pieces.append(thick[1][at:at + cut])
         at += cut
-    into_out = jnp.stack([jnp.stack([part[2], part[1]], axis=1) for part in scattered])
+    into_out = jnp.stack([jnp.stack([part[2], part[1]], axis=1) for part in scattered[:-1]] + [stacked_last])
 
     def stacked(parts_):
         return jnp.stack([jnp.moveaxis(part, 0, 1) for part in parts_])[:, :, None]

time: 1310 us -> 1260 us (0.962)
  Pallas kernels: 684 us -> 639 us
    pallas_call x2, Pallas kernels: 347 us -> 318 us  [joint_sums(): pl.pallas_call(partial(joint_body, plan, chunks), in_specs=[any_spec, any...]
    pallas_call x8, Pallas kernels: 249 us -> 222 us  [the longest x2 103 us: scan_backward(): pl.pallas_call(partial(back_body, C // LANES, width, held), grid=(T // tb...]
  transfers between devices with their start and end apart: 32 -> 32, of which waited for: 17 -> 17; matrix products, arithmetic and copies ran while one was open for 25% -> 27% of each run, Pallas kernels for 40% -> 39%
where the time goes in v7:
time: 1260 us; the launch traced here: 1250 us
  Pallas kernels  639 us (51%)
  matrix products  187 us (15%)
  other arithmetic  157 us (12%)
  local copies, waits for them, and re-layouts  139 us (11%)
  waiting for transfers between devices  80.4 us (6%)
  starting transfers between devices  25.9 us (2%)
  between operations  17.9 us (1%)
    pallas_call x2, Pallas kernels, joint_sums(): pl.pallas_call(partial(joint_body, plan, chunks), in_specs=[any_spec, any...  318 us
    pallas_call x2, Pallas kernels, scan_backward(): pl.pallas_call(partial(back_body, C // LANES, width, held), grid=(T // tb...  103 us
    pallas_call x3, Pallas kernels, hops(): pl.pallas_call(partial(hop_body, reverses, groups), in_specs=[spec] * (3...  99.2 us
    dot_general x10, matrix products, dot_n(): lax.dot_general(left, right, (((1,), (1,)), ((), ())), preferred_element_...  93.8 us
    pallas_call x2, Pallas kernels, scan_forward(): pl.pallas_call(partial(scan_body, C // LANES, width, held), grid=(T // tb...  56.4 us
    dot_general x12, matrix products, dot_t(): lax.dot_general(left, right, (((0,), (0,)), ((), ())), preferred_element_...  51.8 us
    unnamed x257, local copies, waits for them, and re-layouts  48.5 us
    pallas_call x2, Pallas kernels, start_grads(): pl.pallas_call(partial(start_body, C // LANES, width, held), grid=(T // t...  31.3 us
  transfers between devices with their start and end apart: 32, of which 17 were waited for; matrix products, arithmetic and copies ran while one was open for 27% of the time, Pallas kernels for 39%

profile of v7, /device:TPU:0, one launch (start us, length us, event | category | flops | bytes accessed | tf_op | source)
XLA Modules:
  0.0 1247.1 jit_solution(4648983324794854582)
XLA Ops:
  80.8 15.6 %end_states.2.refs_0_ = f32[16,8,1024]{2,1,0:T(8,128)S(1)} custom-call(f32[128,8,1024]{2,1,0:T(8,128)S(1)} %bitcast.375, f32[128,8,1024]{2,1,0:T(8,128)} %fusion.17.push_ref, f32[128,8,32]{2,1,0:T(8,128)S(1)} %bitcast.383, f32[16,1024]{1,0:T(8,128)S(1)} %get-tuple-element.292.rate_ref), custom_call_target="tpu_custom_call" | custom-call | flops 67108864 | bytes 67108864 | tf_op jit(solution)/shard_map/end_states/pallas_call | solution.py:57
  96.4 16.1 %hops.3.start_ref.begin_ref = f32[16,8,1024]{2,1,0:T(8,128)S(1)} custom-call(f32[8,1024]{1,0:T(8,128)S(1)} %get-tuple-element.309.total_ref, f32[16,1024]{1,0:T(8,128)S(1)} %get-tuple-element.292.rate_ref, f32[16,8,1024]{2,1,0:T(8,128)S(1)} %end_states.2.refs_0_, f32[16,8,1024]{2,1,0:T(8,128)S(1)} %get-tuple-element.318.refs_1_), custom_call_target="tpu_custom_call" | custom-call | bytes 26214400 | tf_op jit(solution)/shard_map/hops/pallas_call | solution.py:673
  112.5 28.2 %scan_forward.2 = (f32[128,8,1024]{2,1,0:T(8,128)S(1)}, f32[128,16,8,1024]{3,2,1,0:T(8,128)}, f32[16,8,1024]{2,1,0:T(8,128)S(1)}) custom-call(f32[128,8,1024]{2,1,0:T(8,128)} %bitcast.376, f32[128,8,1024]{2,1,0:T(8,128)} %fusion.17.push_ref, f32[128,8,32]{2,1,0:T(8,128)S(1)} %bitcast.384, f32[16,1024]{1,0:T(8,128)S(1)} %get-tuple-element.292.rate_ref, ...), custom_call_target="tpu_custom_call" | custom-call | flops 117440512 | bytes 117440512 | tf_op jit(solution)/shard_map/scan_forward/pallas_call | solution.py:106
  181.9 12.6 %fusion.38 = f32[1024,1024]{1,0:T(8,128)} fusion(bf16[2,1024,2048]{2,1,0:T(8,128)(2,1)} %param.25, bf16[128,1,8,2048]{3,0,2,1:T(8,128)(2,1)S(1)} %bitcast.417), kind=kOutput, calls=%fused_computation.79 | convolution fusion | flops 4294967296 | bytes 12582912 | tf_op jit(solution)/shard_map/dot_general | solution.py:704
  201.4 11.2 copy.79
  230.6 11.9 copy.80
  242.5 14.6 %collective-permute-done.5 = f32[512,2048]{1,0:T(8,128)} collective-permute-done((f32[512,2048]{1,0:T(8,128)}, f32[512,2048]{1,0:T(8,128)}, u32[]{:S(2)}, u32[]{:S(2)}) %collective-permute-start.5) | collective-permute-done | bytes 4194336 | tf_op jit(solution)/shard_map/ppermute | solution.py:296
  282.6 11.1 fusion.65
  329.7 15.6 %start_grads.2.refs_1_ = f32[16,8,1024]{2,1,0:T(8,128)S(1)} custom-call(f32[128,8,1024]{2,1,0:T(8,128)S(1)} %bitcast.379, f32[128,8,1024]{2,1,0:T(8,128)} %bitcast.410, f32[128,8,32]{2,1,0:T(8,128)S(1)} %bitcast.387, f32[16,1024]{1,0:T(8,128)S(1)} %get-tuple-element.291.rate_ref), custom_call_target="tpu_custom_call" | custom-call | flops 67108864 | bytes 67108864 | tf_op jit(solution)/shard_map/start_grads/pallas_call | solution.py:144
  345.3 15.6 %end_states.3.refs_0_ = f32[16,8,1024]{2,1,0:T(8,128)S(1)} custom-call(f32[128,8,1024]{2,1,0:T(8,128)S(1)} %bitcast.380, f32[128,8,1024]{2,1,0:T(8,128)} %get-tuple-element.271.push_ref, f32[128,8,32]{2,1,0:T(8,128)S(1)} %bitcast.388, f32[16,1024]{1,0:T(8,128)S(1)} %get-tuple-element.291.rate_ref), custom_call_target="tpu_custom_call" | custom-call | flops 67108864 | bytes 67108864 | tf_op jit(solution)/shard_map/end_states/pallas_call | solution.py:57
  360.9 39.1 %hops.4 = (f32[16,8,1024]{2,1,0:T(8,128)S(1)}, f32[16,8,1024]{2,1,0:T(8,128)S(1)}) custom-call(f32[8,1024]{1,0:T(8,128)S(1)} %get-tuple-element.311.total_ref, f32[16,1024]{1,0:T(8,128)S(1)} %get-tuple-element.291.rate_ref, f32[16,8,1024]{2,1,0:T(8,128)S(1)} %end_states.3.refs_0_, f32[16,8,1024]{2,1,0:T(8,128)S(1)} %start_grads.2.refs_1_, ...), custom_call_target="tpu_custom_call" | custom-call | bytes 26214400 | tf_op jit(solution)/shard_map/hops/pallas_call | solution.py:673
  400.0 28.2 %scan_forward.3 = (f32[128,8,1024]{2,1,0:T(8,128)S(1)}, f32[128,16,8,1024]{3,2,1,0:T(8,128)}, f32[16,8,1024]{2,1,0:T(8,128)S(1)}) custom-call(f32[128,8,1024]{2,1,0:T(8,128)} %bitcast.381, f32[128,8,1024]{2,1,0:T(8,128)} %get-tuple-element.271.push_ref, f32[128,8,32]{2,1,0:T(8,128)S(1)} %bitcast.389, f32[16,1024]{1,0:T(8,128)S(1)} %get-tuple-element.291.rate_ref, ...), custom_call_target="tpu_custom_call" | custom-call | flops 117440512 | bytes 117440512 | tf_op jit(solution)/shard_map/scan_forward/pallas_call | solution.py:106
  462.8 10.7 fusion.51
  479.9 51.4 %scan_backward.2 = (f32[128,8,1024]{2,1,0:T(8,128)}, f32[128,8,1024]{2,1,0:T(8,128)}, f32[128,8,32]{2,1,0:T(8,128)S(1)}, f32[16,8,1024]{2,1,0:T(8,128)S(1)}, f32[16,8,1024]{2,1,0:T(8,128)S(1)}) custom-call(f32[128,8,1024]{2,1,0:T(8,128)} %bitcast.382, f32[128,8,1024]{2,1,0:T(8,128)} %get-tuple-element.271.push_ref, f32[128,8,1024]{2,1,0:T(8,128)} %bitcast.411, ...), custom_call_target="tpu_custom_call" | custom-call | flops 218103808 | bytes 218103808 | tf_op jit(solution)/shard_map/scan_backward/pallas_call | solution.py:230
  555.6 13.0 %fusion.134 = (f32[1024]{0:T(1024)S(1)}, f32[1024]{0:T(1024)S(1)}, f32[1024]{0:T(1024)S(1)}, f32[1024]{0:T(1024)S(1)}, f32[1024]{0:T(1024)S(1)}, /*index=5*/f32[1024,1024]{1,0:T(8,128)S(1)}) fusion(f32[2,1024,1024]{2,1,0:T(8,128)} %fusion.65, f32[1024,1024]{1,0:T(8,128)} %copy-done.46, f32[24,1024]{1,0:T(8,128)S(1)} %fusion.120, ...), kind=kOutput, calls=%fused_computation.301 | convolution fusion | flops 698870784 | bytes 30466048 | tf_op jit(solution)/shard_map/dot_general | solution.py:704
  579.8 10.9 fusion.74
  601.4 148.1 %joint_sums.2 = (f32[1024,2048]{1,0:T(8,128)}, f32[8,2048]{1,0:T(8,128)S(1)}, f32[256,1024]{1,0:T(8,128)S(1)}, f32[23,1024]{1,0:T(8,128)S(1)}) custom-call(f32[1024,2048]{1,0:T(8,128)} %fusion.55.sum_ref, f32[512,2048]{1,0:T(8,128)} %copy-done.30, f32[1,2048]{1,0:T(1,128)S(1)} %copy-done.25, f32[2,2,2,256,1024]{4,3,2,1,0:T(8,128)} %bitcast.428, ...), custom_call_target="tpu_custom_call" | custom-call | bytes 419430400 | tf_op jit(solution)/shard_map/joint_sums/pallas_call | solution.py:525
  765.9 12.9 %fusion.101 = (f32[1024,1024]{1,0:T(8,128)}, f32[1024,1024]{1,0:T(8,128)}) fusion(f32[2,1024,1024]{2,1,0:T(8,128)} %copy-done.39, bf16[1024,2048]{1,0:T(8,128)(2,1)} %copy-done.56, bf16[2,1024,2048]{2,1,0:T(8,128)(2,1)} %param.25), kind=kOutput, calls=%fused_computation.200 | convolution fusion | flops 4300210176 | bytes 20971520 | tf_op jit(solution)/shard_map/dot_general | solution.py:704
  781.9 15.7 %start_grads.3.refs_0_ = f32[16,8,1024]{2,1,0:T(8,128)S(1)} custom-call(f32[128,8,1024]{2,1,0:T(8,128)S(1)} %bitcast.378, f32[128,8,1024]{2,1,0:T(8,128)} %bitcast.408, f32[128,8,32]{2,1,0:T(8,128)S(1)} %bitcast.385, f32[16,1024]{1,0:T(8,128)S(1)} %copy-done.9), custom_call_target="tpu_custom_call" | custom-call | flops 67108864 | bytes 67108864 | tf_op jit(solution)/shard_map/start_grads/pallas_call | solution.py:144
  797.6 44.0 %hops.5.end_ref = f32[16,8,1024]{2,1,0:T(8,128)S(1)} custom-call(f32[8,1024]{1,0:T(8,128)S(1)} %copy-done.21, f32[16,1024]{1,0:T(8,128)S(1)} %copy-done.9, f32[16,8,1024]{2,1,0:T(8,128)S(1)} %start_grads.3.refs_0_, f32[16,8,1024]{2,1,0:T(8,128)S(1)} %broadcast_in_dim.41.refs_1_), custom_call_target="tpu_custom_call" | custom-call | bytes 26214400 | tf_op jit(solution)/shard_map/hops/pallas_call | solution.py:673
  856.1 10.8 fusion.47
  883.9 51.7 %scan_backward.3 = (f32[128,8,1024]{2,1,0:T(8,128)}, f32[128,8,1024]{2,1,0:T(8,128)}, f32[128,8,32]{2,1,0:T(8,128)S(1)}, f32[16,8,1024]{2,1,0:T(8,128)S(1)}, f32[16,8,1024]{2,1,0:T(8,128)S(1)}) custom-call(f32[128,8,1024]{2,1,0:T(8,128)} %bitcast.377, f32[128,8,1024]{2,1,0:T(8,128)} %fusion.17.push_ref, f32[128,8,1024]{2,1,0:T(8,128)} %bitcast.409, ...), custom_call_target="tpu_custom_call" | custom-call | flops 218103808 | bytes 218103808 | tf_op jit(solution)/shard_map/scan_backward/pallas_call | solution.py:230
  970.4 12.6 %fusion.133 = (f32[1024]{0:T(1024)S(1)}, f32[1024]{0:T(1024)S(1)}, f32[1024]{0:T(1024)S(1)}, f32[1024]{0:T(1024)S(1)}, f32[1024]{0:T(1024)S(1)}, /*index=5*/f32[1024,1024]{1,0:T(8,128)}) fusion(f32[2,1024,1024]{2,1,0:T(8,128)} %copy-done.39, f32[1024,1024]{1,0:T(8,128)} %slice_bitcast_fusion.3, f32[24,1024]{1,0:T(8,128)S(1)} %copy-done.85, ...), kind=kOutput, calls=%fused_computation.300 | convolution fusion | flops 698870784 | bytes 30466048 | tf_op jit(solution)/shard_map/dot_general | solution.py:704
  1025.6 170.2 %joint_sums.3 = (f32[1024,2048]{1,0:T(8,128)}, f32[8,2048]{1,0:T(8,128)S(1)}, f32[256,1024]{1,0:T(8,128)S(1)}, f32[80,1024]{1,0:T(8,128)S(1)}, f32[32,1024]{1,0:T(8,128)S(1)}) custom-call(f32[1024,2048]{1,0:T(8,128)} %fusion.58.sum_ref, f32[512,2048]{1,0:T(8,128)} %get-tuple-element.240.base_ref, f32[1,2048]{1,0:T(1,128)S(1)} %copy-done.23, ...), custom_call_target="tpu_custom_call" | custom-call | bytes 419430400 | tf_op jit(solution)/shard_map/joint_sums/pallas_call | solution.py:525
  (495 shorter events, 457.6 us)
Async XLA Ops:
  7.2 742.4 %reduce-scatter.5.cloned.1.call-start = ((), (), s32[]{:S(2)}) async-start(), calls=%async_computation.4 | async-start | bytes 9437184 | tf_op jit(solution)/shard_map/reduce_scatter | solution.py:321
  39.3 8.8 collective-permute-start
  61.6 9.8 collective-permute-start.2
  154.2 7.2 collective-permute-start.4
  164.1 92.9 %collective-permute-start.5 = (f32[512,2048]{1,0:T(8,128)}, f32[512,2048]{1,0:T(8,128)}, u32[]{:S(2)}, u32[]{:S(2)}) collective-permute-start(f32[512,2048]{1,0:T(8,128)} %dynamic-slice_add_fusion.1), channel_id=1, source_target_pairs={{0,2},{2,0},{1,3},{3,1},{4,6},{6,4},{5,7},{7,5},{8,10},{10,8},{9,1... | collective-permute-start | bytes 12582920 | tf_op jit(solution)/shard_map/ppermute | solution.py:296
  264.5 7.4 collective-permute-start.6
  295.3 5.3 collective-permute-start.7
  307.7 9.8 collective-permute-start.9
  441.6 425.3 %reduce-scatter.7.cloned.1.call-start = ((), (), s32[]{:S(2)}) async-start(), calls=%async_computation.5 | async-start | bytes 9437184 | tf_op jit(solution)/shard_map/reduce_scatter | solution.py:321
  454.9 18.6 %collective-permute-start.11 = (f32[512,2048]{1,0:T(8,128)}, f32[512,2048]{1,0:T(8,128)}, u32[]{:S(2)}, u32[]{:S(2)}) collective-permute-start(f32[512,2048]{1,0:T(8,128)} %constant_dynamic-slice_fusion), channel_id=1, source_target_pairs={{0,1},{1,0},{2,3},{3,2},{4,5},{5,4},{6,7},{7,6},{8,9},{9,8},{10,11... | collective-permute-start | bytes 12582920 | tf_op jit(solution)/shard_map/ppermute | solution.py:290
  462.8 762.1 %reduce-scatter.11.cloned.1.call-start = ((), (), s32[]{:S(2)}) async-start(), calls=%async_computation.7 | async-start | bytes 9437184 | tf_op jit(solution)/shard_map/reduce_scatter | solution.py:321
  478.0 54.2 %collective-permute-start.12 = (f32[256,2048]{1,0:T(8,128)S(1)}, f32[256,2048]{1,0:T(8,128)}, u32[]{:S(2)}, u32[]{:S(2)}) collective-permute-start(f32[256,2048]{1,0:T(8,128)S(1)} %slice.340), channel_id=1, source_target_pairs={{0,2},{2,0},{1,3},{3,1},{4,6},{6,4},{5,7},{7,5},{8,10},{10,8},{9,1... | collective-permute-start | bytes 6291464 | tf_op jit(solution)/shard_map/ppermute | solution.py:296
  543.8 9.8 collective-permute-start.14
  572.2 6.7 collective-permute-start.16
  778.8 451.7 %reduce-scatter.9.cloned.1.call-start = ((), (), s32[]{:S(2)}) async-start(), calls=%async_computation.6 | async-start | bytes 9437184 | tf_op jit(solution)/shard_map/reduce_scatter | solution.py:321
  870.1 67.2 %collective-permute-start.17 = (f32[256,2048]{1,0:T(8,128)}, f32[256,2048]{1,0:T(8,128)}, u32[]{:S(2)}, u32[]{:S(2)}) collective-permute-start(f32[256,2048]{1,0:T(8,128)} %slice.348), channel_id=1, source_target_pairs={{0,2},{2,0},{1,3},{3,1},{4,6},{6,4},{5,7},{7,5},{8,10},{10,8},{9,1... | collective-permute-start | bytes 6291464 | tf_op jit(solution)/shard_map/ppermute | solution.py:296
  946.2 9.2 collective-permute-start.18
  954.8 13.8 %collective-permute-start.23 = (f32[3,1024]{1,0:T(4,128)S(1)}, f32[3,1024]{1,0:T(4,128)S(1)}, u32[]{:S(2)}, u32[]{:S(2)}) collective-permute-start(f32[3,1024]{1,0:T(4,128)S(1)} %pad_maximum_fusion.23), channel_id=1, source_target_pairs={{0,1},{1,0},{2,3},{3,2},{4,5},{5,4},{6,7},{7,6},{8,9},{9,8},{10,11... | collective-permute-start | bytes 36872 | tf_op jit(solution)/shard_map/ppermute | solution.py:309
  956.5 9.8 collective-permute-start.19
  968.1 45.8 %collective-permute-start.22 = (f32[512,2048]{1,0:T(8,128)}, f32[512,2048]{1,0:T(8,128)}, u32[]{:S(2)}, u32[]{:S(2)}) collective-permute-start(f32[512,2048]{1,0:T(8,128)} %get-tuple-element.255), channel_id=1, source_target_pairs={{0,1},{1,0},{2,3},{3,2},{4,5},{5,4},{6,7},{7,6},{8,9},{9,8},{10,11... | collective-permute-start | bytes 12582920 | tf_op jit(solution)/shard_map/ppermute | solution.py:302
  990.4 7.3 collective-permute-start.21
  1195.8 11.7 collective-permute-start.24
  1207.5 3.7 collective-permute-start.25
  1214.9 9.3 collective-permute-start.27
  (132 other events, 1485.0 us)
Sparse Core Ops, SparseCore 0:
  441.8 149.4 reduce-scatter.4
  595.3 191.6 reduce-scatter.6
  790.7 151.4 reduce-scatter.10
  946.1 194.3 reduce-scatter.8

commit v8 on v7

--- a/solution.py
+++ b/solution.py
@@ -276,6 +276,68 @@
     return ordered(core, half, lax.ppermute(half, "tensor", BESIDE))
 
 
+def pair_body(chunks, count, *refs):
+    ins, outs, refs = refs[:count], refs[count:2 * count], refs[2 * count:]
+    buffers, sems = refs[:5 * count], refs[5 * count:]
+    blk, tensor = lax.axis_index("blk"), lax.axis_index("tensor")
+    core = tensor % 2
+    beside, far = (blk, tensor + 1 - 2 * core), (blk, (tensor + 2) % 4)
+    barrier = pltpu.get_barrier_semaphore()
+    for device in (beside, far):
+        pl.semaphore_signal(barrier, inc=1, device_id=device, device_id_type=pl.DeviceIdType.MESH)
+    pl.semaphore_wait(barrier, 2)
+    parts = [(k, i) for k in range(chunks) for i in range(count)]
+    firsts, seconds, thirds = {}, {}, {}
+
+    def rows_of(i, k, side):
+        size = ins[i].shape[0] // 2 // chunks
+        return pl.ds(pl.multiple_of((side * chunks + k) * size, size), size)
+
+    for at, (k, i) in enumerate(parts):
+        firsts[k, i] = remote(ins[i].at[rows_of(i, k, 1 - core)], buffers[5 * i].at[k], sems[0], sems[1], at, beside)
+        firsts[k, i].start()
+    for at, (k, i) in enumerate(parts):
+        firsts[k, i].wait_recv()
+        buffers[5 * i + 1][k] = ins[i][rows_of(i, k, core), :] + buffers[5 * i][k]
+        seconds[k, i] = remote(buffers[5 * i + 1].at[k], buffers[5 * i + 2].at[k], sems[2], sems[3], at, far)
+        seconds[k, i].start()
+    for at, (k, i) in enumerate(parts):
+        seconds[k, i].wait_recv()
+        total = buffers[5 * i + 1][k] + buffers[5 * i + 2][k]
+        buffers[5 * i + 3][k] = total
+        outs[i][rows_of(i, k, core), :] = total
+        thirds[k, i] = remote(buffers[5 * i + 3].at[k], buffers[5 * i + 4].at[k], sems[4], sems[5], at, beside)
+        thirds[k, i].start()
+    for k, i in parts:
+        thirds[k, i].wait_recv()
+        outs[i][rows_of(i, k, 1 - core), :] = buffers[5 * i + 4][k]
+    for group in (firsts, seconds, thirds):
+        for copy in group.values():
+            copy.wait_send()
+
+
+def pair_sums(arrays, collective_id):
+    if not paired() or lax.axis_size("blk") != 8:
+        return [lax.psum(array, "tensor") for array in arrays]
+    chunks, count = 2, len(arrays)
+    f32 = jnp.float32
+    spec = pl.BlockSpec(memory_space=pltpu.VMEM)
+    scratch = []
+    for array in arrays:
+        scratch += [pltpu.VMEM((chunks, array.shape[0] // 2 // chunks, array.shape[1]), f32)] * 5
+    return pl.pallas_call(
+        partial(pair_body, chunks, count),
+        in_specs=[spec] * count,
+        out_specs=[spec] * count,
+        out_shape=[jax.ShapeDtypeStruct(array.shape, f32) for array in arrays],
+        scratch_shapes=scratch + [pltpu.SemaphoreType.DMA((chunks * count,))] * 6,
+        compiler_params=pltpu.CompilerParams(
+            collective_id=collective_id, has_side_effects=True, vmem_limit_bytes=24 * 2**20),
+        cost_estimate=pl.CostEstimate(flops=0, bytes_accessed=40 * 2**20, transcendentals=0),
+        name="pair_sums",
+    )(*arrays)
+
+
 def own_rows(array):
     if not paired():
         size = array.shape[0] // lax.axis_size("tensor")
@@ -296,11 +358,11 @@
     return lax.ppermute(half, "tensor", ACROSS)
 
 
-def all_rows(array):
+def all_rows(array, finish=lambda part: part):
     if not paired():
-        return lax.optimization_barrier(lax.all_gather(array, "tensor", tiled=True))
+        return finish(lax.optimization_barrier(lax.all_gather(array, "tensor", tiled=True)))
     other = lax.optimization_barrier(lax.ppermute(array, "tensor", BESIDE))
-    return ordered(lax.axis_index("tensor") % 2, array, other)
+    return ordered(lax.axis_index("tensor") % 2, finish(array), finish(other))
 
 
 def rows_sum(array):
@@ -344,6 +406,7 @@
     change_out, gain_out, refs = refs[0], refs[1], refs[2:]
     thick_outs, small_out, refs = refs[:count], refs[count], refs[1 + count:]
     own_half, core_half, far_half, base, came, small_in, refs = refs[0], refs[1], refs[2], refs[3], refs[4], refs[5], refs[6:]
+    gain_in, gain_send, gain_recv, refs = refs[0], refs[1], refs[2], refs[3:]
     core_send, core_recv, far_send, far_recv, back_send, back_recv, local_sem, base_sem, out_sem, came_sem = refs[:10]
     small_send, small_recv = refs[10:12]
     refs = refs[12:]
@@ -438,6 +501,17 @@
             return self.firsts + self.seconds + [self.last]
 
     jobs = [Job(*job, refs[12 * i:12 * i + 12]) for i, job in enumerate(plan)]
+    gains = []
+
+    def gain_step(i):
+        device = beside if i == 0 else peers[1 << (i - 1)]
+        copy = remote(gain_out, gain_in.at[i], gain_send, gain_recv, i, device)
+        copy.start()
+        gains.append(copy)
+
+    def gain_end(i):
+        gains[i].wait()
+        gain_out[...] = gain_out[...] + gain_in[i]
 
     def core_end(k):
         local_copies[k].wait()
@@ -491,8 +565,13 @@
             if i == 0:
                 small_step(2)
         far_end(i)
+    gain_step(0)
     for k in range(chunks):
         back_end(k)
+    for i in range(4):
+        gain_end(i)
+        if i < 3:
+            gain_step(i + 1)
     for job in jobs:
         job.end()
     for copy in far_copies + back_copies + [each for job in jobs for each in job.sent()]:
@@ -505,7 +584,7 @@
     if not paired() or lax.axis_size("blk") != 8:
         normed_grad = lax.psum_scatter(array, "tensor", scatter_dimension=0, tiled=True)
         gain_grad, change = norm_back(gain, normed_grad, base, inverse_rms(base))
-        return all_rows(change), gain_grad, [blk_scatter(part) for part in thick], lax.psum(small, "blk")
+        return all_rows(change), lax.psum(rows_sum(gain_grad), "blk"), [blk_scatter(part) for part in thick], lax.psum(small, "blk")
     R, N = array.shape
     C = thick[0].shape[1]
     chunks = 4
@@ -529,7 +608,7 @@
         out_shape=[jax.ShapeDtypeStruct((R, N), f32), jax.ShapeDtypeStruct((8, N), f32)]
         + [jax.ShapeDtypeStruct((part.shape[0] // 8, C), f32) for part in thick]
         + [jax.ShapeDtypeStruct(small.shape, f32)],
-        scratch_shapes=[half] * 5 + [pltpu.VMEM((3,) + small.shape, f32)]
+        scratch_shapes=[half] * 5 + [pltpu.VMEM((3,) + small.shape, f32), pltpu.VMEM((4, 8, N), f32), dma((4,)), dma((4,))]
         + [dma((chunks,))] * 10 + [dma((3,)), dma((3,))] + scratch,
         compiler_params=pltpu.CompilerParams(
             collective_id=collective_id, has_side_effects=True, vmem_limit_bytes=52 * 2**20),
@@ -734,7 +813,7 @@
     return lax.rsqrt(jnp.mean(residual * residual, axis=-1, keepdims=True) + EPSILON)
 
 
-def front(layer, normed, conv_first, parts, at_first):
+def front(layer, normed, conv_first, parts, at_first, collective_id):
     mixed = jnp.einsum("rd,dkc->krc", normed, layer.raw, preferred_element_type=jnp.float32)
     values, gate = mixed[0], mixed[1]
     inner = values.shape[-1]
@@ -746,9 +825,11 @@
     window = jnp.concatenate([prefix, values], axis=0)
     conv_out = layer.shift + sum(layer.taps[k] * window[8 * k:8 * k + count] for k in range(rim + 1))
     inputs = lax.optimization_barrier(jax.nn.silu(conv_out).astype(jnp.bfloat16))
-    projected = tensor_sum(dot32(inputs, layer.x))
-    dt_low = projected[:, :RANK].astype(jnp.bfloat16)
-    coef = by_step(projected[:, RANK:])
+    ranks, coef = pair_sums(
+        [dot32(inputs, layer.x[:, :RANK]), lax.dot_general(
+            layer.x[:, RANK:], inputs, (((0,), (1,)), ((), ())), preferred_element_type=jnp.float32)], collective_id)
+    dt_low = ranks.astype(jnp.bfloat16)
+    coef = by_step(coef.T)
     step = jax.nn.softplus(dot32(dt_low, layer.dt) + layer.dt_bias)
     push = step * inputs.astype(jnp.float32)
     local = split_parts(end_states(by_step(step), by_step(push), coef, layer.rate2), parts)
@@ -827,7 +908,7 @@
         by_step(step), by_step(push), by_step(grad_result), coef, layer.rate2, states, start, end)
 
 
-def back_rest(layer, kept, grads, scan_out, gate_through):
+def back_rest(layer, kept, grads, scan_out, gate_through, collective_id):
     window, gate, conv_out, inputs, dt_low, coef, step, push, totals = kept
     grad_gated, grad_result = grads
     count, inner = gate.shape
@@ -841,8 +922,8 @@
     bias_grad = jnp.sum(before_grad, axis=0)
     decay_grad = layer.rate * jnp.sum(speed, axis=1)
     before_low = before_grad.astype(jnp.bfloat16)
-    projected_grad = tensor_sum(jnp.concatenate([dot_n(before_low, layer.dt), rows(coef_grad)], axis=-1))
-    high, low = two_parts(projected_grad)
+    ranks_grad, coef_grad = pair_sums([dot_n(before_low, layer.dt), rows(coef_grad).T], collective_id)
+    high, low = two_parts(jnp.concatenate([ranks_grad, coef_grad.T], axis=-1))
     through = dot_n(jnp.concatenate([high, low], axis=-1), jnp.concatenate([layer.x, layer.x], axis=-1))
     inputs_grad = grad_result * layer.skip + step * pushes + through
     conv_grad = inputs_grad * silu_slope(conv_out)
@@ -914,7 +995,7 @@
     for l, layer in enumerate(layers):
         norms[l] = (normed, residual)
         kept[l], local, tails[l] = front(
-            layer, normed, jnp.moveaxis(conv_init[l], 1, 0), parts, at_first)
+            layer, normed, jnp.moveaxis(conv_init[l], 1, 0), parts, at_first, 4 * layer_total + l)
         totals = kept[l][-1]
         first = jnp.moveaxis(scan_init[l], 1, 0)
         if l == last:
@@ -942,41 +1023,40 @@
             following = residual + branch
             squares[l] = jnp.stack([jnp.sum(branch * branch), jnp.sum(following * following)])
             residual = following
-            unscaled = all_rows(residual * inverse_rms(residual))
-            normed = (unscaled * layers[l + 1].gain).astype(jnp.bfloat16)
+            gain = layers[l + 1].gain
+            normed = all_rows(residual * inverse_rms(residual), lambda part: (part * gain).astype(jnp.bfloat16))
 
     thins, scattered = [], [None] * layer_total
     for l in reversed(range(layer_total)):
         layer = layers[l]
         normed, base = norms[l]
         if l < last:
-            grads, out_grad = lax.optimization_barrier(
-                (back_gated(kept[l], dot_n(grad_low, layer.out)), dot_t(grad_low, scans[l][1])))
+            grads, out_grad, half = lax.optimization_barrier(
+                (back_gated(kept[l], dot_n(grad_low, layer.out)), dot_t(grad_low, scans[l][1]), half))
             scattered[l] = [blk_scatter(out_grad)]
             late = back_local(layer, kept[l], grads[1])
             end, = exchange(layer, [late], kept[l][-1], jnp.zeros_like(late[:, 0]), (True,), 2 + 2 * layer_total + l)
+            end, got_rest = lax.optimization_barrier((end, across(half[half.shape[0] // 2:])))
+            branch = half + jnp.concatenate([got, got_rest], axis=0)
+            following = residual + branch
+            squares[last] = jnp.stack([jnp.sum(branch * branch), jnp.sum(following * following)])
+            out = restore(all_rows(0.5 * following, lambda part: (2.0 * part).astype(jnp.bfloat16)))
         else:
             out_grad = late_out
         side = back_side(layer, kept[l], normed, scans[l], grads, grad_low)
-        middle = half.shape[0] // 2
         if l == last:
             scattered[l] = [blk_scatter(out_grad), blk_scatter(side[0])]
             end, side, half = lax.optimization_barrier((end, side, half))
             scan_out, got = lax.optimization_barrier(
-                (back_scan(layer, kept[l], scans[l], grads, end), across(half[:middle])))
+                (back_scan(layer, kept[l], scans[l], grads, end), across(half[:half.shape[0] // 2])))
         else:
             scattered[l].append(blk_scatter(side[0]))
-            end, side, half, scattered[last] = lax.optimization_barrier((end, side, half, scattered[last]))
+            end, side, scattered[last] = lax.optimization_barrier((end, side, scattered[last]))
             stacked_last = jnp.stack([scattered[last][2], scattered[last][1]], axis=1)
-            scan_out, got_rest = lax.optimization_barrier(
-                (back_scan(layer, kept[l], scans[l], grads, end), across(half[middle:])))
-            branch = half + jnp.concatenate([got, got_rest], axis=0)
-            following = residual + branch
-            squares[last] = jnp.stack([jnp.sum(branch * branch), jnp.sum(following * following)])
-            out = restore((2.0 * all_rows(0.5 * following)).astype(jnp.bfloat16))
+            scan_out = lax.optimization_barrier(back_scan(layer, kept[l], scans[l], grads, end))
         gate_grad, gate_through, skip_grad = side
         normed_part, smalls[l], lows, starts[l], prefixes[l] = back_rest(
-            layer, kept[l], grads, scan_out, gate_through)
+            layer, kept[l], grads, scan_out, gate_through, 5 * layer_total + l)
         smalls[l] = jnp.concatenate([smalls[l], skip_grad[None]], axis=0)
         thick = thick_grads(kept[l], normed, lows)
         inner = smalls[l].shape[-1]
@@ -991,8 +1071,7 @@
             cuts = [part.shape[1] for part in thins]
             extra = jnp.concatenate([jnp.stack(squares).reshape(-1), input_square.reshape(1)])
             extra = jnp.pad(extra, (0, inner - extra.shape[0]))[None]
-            shared = rows_sum(jnp.concatenate(
-                [extra] + [gain.reshape(-1, inner) for gain in gains[1:]], axis=0))
+            shared = rows_sum(extra)
             own_count = smalls[l].shape[0]
             small = jnp.concatenate([smalls[l], shared], axis=0)
             small = jnp.pad(small, ((0, -small.shape[0] % 8), (0, 0)))
@@ -1006,13 +1085,10 @@
         grad_low = grad.astype(jnp.bfloat16)
         if l:
             grad_low = lax.optimization_barrier(grad_low)
-    first_gain = blk_sum(rows_sum(gains[0].reshape(-1, inner)))
     input_grad = restore(grad_low)
 
     small = jnp.stack(smalls)
-    gain_rows = first_gain.shape[0] * layer_total
-    gain_grad = jnp.concatenate([first_gain, rest[1:1 + gain_rows - first_gain.shape[0]]], axis=0)
-    gain_grad = gain_grad.reshape(layer_total, width)
+    gain_grad = jnp.stack(gains)
     taps = weights[2].shape[1]
     row_total = tokens.shape[0] * tokens.shape[1] * width * blocks
     squares = rest[0] / row_total

time: 1260 us -> 1270 us (level)
  Pallas kernels: 639 us -> 697 us
  waiting for transfers between devices: 80.4 us -> 35.6 us
    pallas_call x0 -> x4, Pallas kernels: none -> 48.5 us  [pair_sums(): pl.pallas_call(partial(pair_body, chunks, count), in_specs=[spec] * count...]
    ppermute x15 -> x0, waiting for transfers between devices: 43.3 us -> none  [the longest x4 29.2 us: tensor_sum(): half = half + lax.ppermute(half, 'tensor', ACROSS)]
    pallas_call x2, Pallas kernels: 318 us -> 332 us  [joint_sums(): pl.pallas_call(partial(joint_body, plan, chunks), in_specs=[any_spec, any...]
    unnamed x257 -> x251, local copies, waits for them, and re-layouts: 48.5 us -> 45.7 us
  transfers between devices with their start and end apart: 32 -> 16, of which waited for: 17 -> 5; matrix products, arithmetic and copies ran while one was open for 27% -> 27% of each run, Pallas kernels for 39% -> 41%
where the time goes in v8:
time: 1270 us; the launch traced here: 1260 us
  Pallas kernels  697 us (55%)
  matrix products  199 us (16%)
  other arithmetic  163 us (13%)
  local copies, waits for them, and re-layouts  135 us (11%)
  waiting for transfers between devices  35.6 us (3%)
  between operations  17.8 us (1%)
  starting transfers between devices  15.2 us (1%)
    pallas_call x2, Pallas kernels, joint_sums(): pl.pallas_call(partial(joint_body, plan, chunks), in_specs=[any_spec, any...  332 us
    pallas_call x2, Pallas kernels, scan_backward(): pl.pallas_call(partial(back_body, C // LANES, width, held), grid=(T // tb...  103 us
    dot_general x10, matrix products, dot_n(): lax.dot_general(left, right, (((1,), (1,)), ((), ())), preferred_element_...  96.2 us
    pallas_call x3, Pallas kernels, hops(): pl.pallas_call(partial(hop_body, reverses, groups), in_specs=[spec] * (3...  94.9 us
    dot_general x12, matrix products, dot_t(): lax.dot_general(left, right, (((0,), (0,)), ((), ())), preferred_element_...  58.7 us
    pallas_call x2, Pallas kernels, scan_forward(): pl.pallas_call(partial(scan_body, C // LANES, width, held), grid=(T // tb...  56.4 us
    pallas_call x4, Pallas kernels, pair_sums(): pl.pallas_call(partial(pair_body, chunks, count), in_specs=[spec] * count...  48.5 us
    unnamed x251, local copies, waits for them, and re-layouts  45.7 us
  transfers between devices with their start and end apart: 16, of which 5 were waited for; matrix products, arithmetic and copies ran while one was open for 27% of the time, Pallas kernels for 41%

profile of v8, /device:TPU:0, one launch (start us, length us, event | category | flops | bytes accessed | tf_op | source)
XLA Modules:
  0.0 1261.9 jit_solution(16020482826849057791)
XLA Ops:
  60.6 12.4 pair_sums.4
  79.4 15.6 %end_states.2.refs_0_ = f32[16,8,1024]{2,1,0:T(8,128)S(1)} custom-call(f32[128,8,1024]{2,1,0:T(8,128)S(1)} %bitcast.381, f32[128,8,1024]{2,1,0:T(8,128)} %fusion.15.push_ref, f32[128,8,32]{2,1,0:T(8,128)S(1)} %bitcast.389, f32[16,1024]{1,0:T(8,128)S(1)} %get-tuple-element.292.rate_ref), custom_call_target="tpu_custom_call" | custom-call | flops 67108864 | bytes 67108864 | tf_op jit(solution)/shard_map/end_states/pallas_call | solution.py:57
  95.0 16.3 %hops.3.start_ref.begin_ref = f32[16,8,1024]{2,1,0:T(8,128)S(1)} custom-call(f32[8,1024]{1,0:T(8,128)S(1)} %get-tuple-element.309.total_ref, f32[16,1024]{1,0:T(8,128)S(1)} %get-tuple-element.292.rate_ref, f32[16,8,1024]{2,1,0:T(8,128)S(1)} %end_states.2.refs_0_, f32[16,8,1024]{2,1,0:T(8,128)S(1)} %get-tuple-element.318.refs_1_), custom_call_target="tpu_custom_call" | custom-call | bytes 26214400 | tf_op jit(solution)/shard_map/hops/pallas_call | solution.py:752
  111.4 28.2 %scan_forward.2 = (f32[128,8,1024]{2,1,0:T(8,128)S(1)}, f32[128,16,8,1024]{3,2,1,0:T(8,128)}, f32[16,8,1024]{2,1,0:T(8,128)S(1)}) custom-call(f32[128,8,1024]{2,1,0:T(8,128)} %bitcast.382, f32[128,8,1024]{2,1,0:T(8,128)} %fusion.15.push_ref, f32[128,8,32]{2,1,0:T(8,128)S(1)} %bitcast.390, f32[16,1024]{1,0:T(8,128)S(1)} %get-tuple-element.292.rate_ref, ...), custom_call_target="tpu_custom_call" | custom-call | flops 117440512 | bytes 117440512 | tf_op jit(solution)/shard_map/scan_forward/pallas_call | solution.py:106
  187.8 12.6 fusion.35
  236.7 11.9 copy.84
  248.7 15.2 %collective-permute-done.2 = f32[512,2048]{1,0:T(8,128)} collective-permute-done((f32[512,2048]{1,0:T(8,128)}, f32[512,2048]{1,0:T(8,128)}, u32[]{:S(2)}, u32[]{:S(2)}) %collective-permute-start.2) | collective-permute-done | bytes 4194336 | tf_op jit(solution)/shard_map/ppermute | solution.py:358
  286.6 12.7 %fusion.62 = f32[2,1024,1024]{2,1,0:T(8,128)S(1)} fusion(bf16[512,2048]{1,0:T(8,128)(2,1)S(1)} %get-tuple-element.264, bf16[512,2048]{1,0:T(8,128)(2,1)S(1)} %get-tuple-element.263, bf16[2,2048,2,1024]{3,1,2,0:T(8,128)(2,1)} %copy.83), kind=kOutput, calls=%fused_computation.135 | convolution fusion | flops 8598323200 | bytes 20971520 | tf_op jit(solution)/shard_map/rd,dkc->krc/dot_general | solution.py:817
  332.6 15.6 %start_grads.2.refs_1_ = f32[16,8,1024]{2,1,0:T(8,128)S(1)} custom-call(f32[128,8,1024]{2,1,0:T(8,128)S(1)} %bitcast.385, f32[128,8,1024]{2,1,0:T(8,128)} %bitcast.420, f32[128,8,32]{2,1,0:T(8,128)S(1)} %bitcast.393, f32[16,1024]{1,0:T(8,128)S(1)} %get-tuple-element.291.rate_ref), custom_call_target="tpu_custom_call" | custom-call | flops 67108864 | bytes 67108864 | tf_op jit(solution)/shard_map/start_grads/pallas_call | solution.py:144
  348.2 15.6 %end_states.3.refs_0_ = f32[16,8,1024]{2,1,0:T(8,128)S(1)} custom-call(f32[128,8,1024]{2,1,0:T(8,128)S(1)} %bitcast.386, f32[128,8,1024]{2,1,0:T(8,128)} %get-tuple-element.279.push_ref, f32[128,8,32]{2,1,0:T(8,128)S(1)} %bitcast.394, f32[16,1024]{1,0:T(8,128)S(1)} %get-tuple-element.291.rate_ref), custom_call_target="tpu_custom_call" | custom-call | flops 67108864 | bytes 67108864 | tf_op jit(solution)/shard_map/end_states/pallas_call | solution.py:57
  363.7 39.3 %hops.4 = (f32[16,8,1024]{2,1,0:T(8,128)S(1)}, f32[16,8,1024]{2,1,0:T(8,128)S(1)}) custom-call(f32[8,1024]{1,0:T(8,128)S(1)} %get-tuple-element.311.total_ref, f32[16,1024]{1,0:T(8,128)S(1)} %get-tuple-element.291.rate_ref, f32[16,8,1024]{2,1,0:T(8,128)S(1)} %end_states.3.refs_0_, f32[16,8,1024]{2,1,0:T(8,128)S(1)} %start_grads.2.refs_1_, ...), custom_call_target="tpu_custom_call" | custom-call | bytes 26214400 | tf_op jit(solution)/shard_map/hops/pallas_call | solution.py:752
  403.1 28.1 %scan_forward.3 = (f32[128,8,1024]{2,1,0:T(8,128)S(1)}, f32[128,16,8,1024]{3,2,1,0:T(8,128)}, f32[16,8,1024]{2,1,0:T(8,128)S(1)}) custom-call(f32[128,8,1024]{2,1,0:T(8,128)} %bitcast.387, f32[128,8,1024]{2,1,0:T(8,128)} %get-tuple-element.279.push_ref, f32[128,8,32]{2,1,0:T(8,128)S(1)} %bitcast.395, f32[16,1024]{1,0:T(8,128)S(1)} %get-tuple-element.291.rate_ref, ...), custom_call_target="tpu_custom_call" | custom-call | flops 117440512 | bytes 117440512 | tf_op jit(solution)/shard_map/scan_forward/pallas_call | solution.py:106
  483.0 51.6 %scan_backward.2 = (f32[128,8,1024]{2,1,0:T(8,128)}, f32[128,8,1024]{2,1,0:T(8,128)}, f32[128,8,32]{2,1,0:T(8,128)S(1)}, f32[16,8,1024]{2,1,0:T(8,128)S(1)}, f32[16,8,1024]{2,1,0:T(8,128)S(1)}) custom-call(f32[128,8,1024]{2,1,0:T(8,128)} %bitcast.388, f32[128,8,1024]{2,1,0:T(8,128)} %get-tuple-element.279.push_ref, f32[128,8,1024]{2,1,0:T(8,128)} %bitcast.421, ...), custom_call_target="tpu_custom_call" | custom-call | flops 218103808 | bytes 218103808 | tf_op jit(solution)/shard_map/scan_backward/pallas_call | solution.py:230
  545.1 12.4 pair_sums.6
  558.1 15.0 %fusion.132 = (f32[1024]{0:T(1024)S(1)}, f32[1024]{0:T(1024)S(1)}, f32[1024]{0:T(1024)S(1)}, f32[1024]{0:T(1024)S(1)}, f32[1024]{0:T(1024)S(1)}, /*index=5*/f32[1024,1024]{1,0:T(8,128)S(1)}) fusion(f32[2,1024,1024]{2,1,0:T(8,128)} %copy-done.43, f32[1024,1024]{1,0:T(8,128)} %copy-done.48, f32[24,1024]{1,0:T(8,128)S(1)} %fusion.117, ...), kind=kOutput, calls=%fused_computation.277 | convolution fusion | flops 698870784 | bytes 30466048 | tf_op jit(solution)/shard_map/dot_general | solution.py:783
  606.1 164.8 %joint_sums.2 = (f32[1024,2048]{1,0:T(8,128)}, f32[8,2048]{1,0:T(8,128)S(1)}, f32[256,1024]{1,0:T(8,128)S(1)}, f32[23,1024]{1,0:T(8,128)S(1)}) custom-call(f32[1024,2048]{1,0:T(8,128)} %fusion.52.sum_ref, f32[512,2048]{1,0:T(8,128)} %copy-done.35, f32[1,2048]{1,0:T(1,128)S(1)} %copy-done.27, f32[2,2,2,256,1024]{4,3,2,1,0:T(8,128)} %bitcast.433, ...), custom_call_target="tpu_custom_call" | custom-call | bytes 419430400 | tf_op jit(solution)/shard_map/joint_sums/pallas_call | solution.py:604
  788.0 12.7 %fusion.96 = (f32[1024,1024]{1,0:T(8,128)}, f32[1024,1024]{1,0:T(8,128)}) fusion(f32[2,1024,1024]{2,1,0:T(8,128)} %copy-done.42, bf16[1024,2048]{1,0:T(8,128)(2,1)} %copy-done.57, bf16[2,1024,2048]{2,1,0:T(8,128)(2,1)} %param.25), kind=kOutput, calls=%fused_computation.188 | convolution fusion | flops 4300210176 | bytes 20971520 | tf_op jit(solution)/shard_map/dot_general | solution.py:783
  834.4 15.7 %start_grads.3.refs_0_ = f32[16,8,1024]{2,1,0:T(8,128)S(1)} custom-call(f32[128,8,1024]{2,1,0:T(8,128)S(1)} %bitcast.384, f32[128,8,1024]{2,1,0:T(8,128)} %bitcast.418, f32[128,8,32]{2,1,0:T(8,128)S(1)} %bitcast.391, f32[16,1024]{1,0:T(8,128)S(1)} %copy-done.8), custom_call_target="tpu_custom_call" | custom-call | flops 67108864 | bytes 67108864 | tf_op jit(solution)/shard_map/start_grads/pallas_call | solution.py:144
  850.2 39.3 %hops.5.end_ref = f32[16,8,1024]{2,1,0:T(8,128)S(1)} custom-call(f32[8,1024]{1,0:T(8,128)S(1)} %copy-done.23, f32[16,1024]{1,0:T(8,128)S(1)} %copy-done.8, f32[16,8,1024]{2,1,0:T(8,128)S(1)} %start_grads.3.refs_0_, f32[16,8,1024]{2,1,0:T(8,128)S(1)} %broadcast_in_dim.41.refs_1_), custom_call_target="tpu_custom_call" | custom-call | bytes 26214400 | tf_op jit(solution)/shard_map/hops/pallas_call | solution.py:752
  912.9 51.8 %scan_backward.3 = (f32[128,8,1024]{2,1,0:T(8,128)}, f32[128,8,1024]{2,1,0:T(8,128)}, f32[128,8,32]{2,1,0:T(8,128)S(1)}, f32[16,8,1024]{2,1,0:T(8,128)S(1)}, f32[16,8,1024]{2,1,0:T(8,128)S(1)}) custom-call(f32[128,8,1024]{2,1,0:T(8,128)} %bitcast.383, f32[128,8,1024]{2,1,0:T(8,128)} %fusion.15.push_ref, f32[128,8,1024]{2,1,0:T(8,128)} %bitcast.419, ...), custom_call_target="tpu_custom_call" | custom-call | flops 218103808 | bytes 218103808 | tf_op jit(solution)/shard_map/scan_backward/pallas_call | solution.py:230
  976.1 12.4 pair_sums.7
  989.0 12.9 %fusion.131 = (f32[1024]{0:T(1024)S(1)}, f32[1024]{0:T(1024)S(1)}, f32[1024]{0:T(1024)S(1)}, f32[1024]{0:T(1024)S(1)}, f32[1024]{0:T(1024)S(1)}, /*index=5*/f32[1024,1024]{1,0:T(8,128)S(1)}) fusion(f32[2,1024,1024]{2,1,0:T(8,128)} %copy-done.42, f32[1024,1024]{1,0:T(8,128)} %slice_bitcast_fusion.3, f32[24,1024]{1,0:T(8,128)S(1)} %copy-done.92, ...), kind=kOutput, calls=%fused_computation.276 | convolution fusion | flops 698870784 | bytes 30466048 | tf_op jit(solution)/shard_map/dot_general | solution.py:783
  1048.3 166.7 %joint_sums.3 = (f32[1024,2048]{1,0:T(8,128)}, f32[8,2048]{1,0:T(8,128)S(1)}, f32[256,1024]{1,0:T(8,128)S(1)}, f32[80,1024]{1,0:T(8,128)S(1)}, f32[24,1024]{1,0:T(8,128)S(1)}) custom-call(f32[1024,2048]{1,0:T(8,128)} %fusion.55.sum_ref, f32[512,2048]{1,0:T(8,128)} %get-tuple-element.249.base_ref, f32[1,2048]{1,0:T(1,128)S(1)} %copy-done.25, ...), custom_call_target="tpu_custom_call" | custom-call | bytes 419430400 | tf_op jit(solution)/shard_map/joint_sums/pallas_call | solution.py:604
  1215.0 13.0 %fusion.25 = bf16[128,1,8,2048]{3,2,0,1:T(8,128)(2,1)S(1)} fusion(f32[1024,2048]{1,0:T(8,128)} %get-tuple-element.162, f32[1024,2048]{1,0:T(8,128)} %get-tuple-element.132, bf16[128,1,8,2048]{3,0,2,1:T(8,128)(2,1)S(1)} %bitcast.425), kind=kLoop, calls=%fused_computation.54 | loop fusion | flops 8388608 | bytes 25165824 | tf_op jit(solution)/shard_map/reshape | solution.py:983
  (432 shorter events, 452.4 us)
Async XLA Ops:
  7.2 764.4 %reduce-scatter.5.cloned.1.call-start = ((), (), s32[]{:S(2)}) async-start(), calls=%async_computation.4 | async-start | bytes 9437184 | tf_op jit(solution)/shard_map/reduce_scatter | solution.py:383
  15.1 266.6 %copy-start.26 = (f32[1,2048]{1,0:T(1,128)}, f32[1,2048]{1,0:T(1,128)S(1)}, u32[]{:S(2)}) copy-start(f32[1,2048]{1,0:T(1,128)S(1)} %get-tuple-element.301.gain_ref) | copy-start | bytes 24580
  39.4 10.8 collective-permute-start
  48.7 62.6 %copy-start.7 = (f32[16,1024]{1,0:T(8,128)}, f32[16,1024]{1,0:T(8,128)S(1)}, u32[]{:S(2)}) copy-start(f32[16,1024]{1,0:T(8,128)S(1)} %get-tuple-element.292.rate_ref) | copy-start | bytes 196612
  48.8 261.3 %copy-start.78 = (bf16[1024,160]{0,1:T(8,128)(2,1)}, bf16[1024,160]{0,1:T(8,128)(2,1)S(1)}, u32[]{:S(2)}) copy-start(bf16[1024,160]{0,1:T(8,128)(2,1)S(1)} %get-tuple-element.282) | copy-start | bytes 983044
  50.1 89.5 %copy-start.105 = (f32[1,1024]{1,0:T(1,128)}, f32[1,1024]{1,0:T(1,128)S(1)}, u32[]{:S(2)}) copy-start(f32[1,1024]{1,0:T(1,128)S(1)} %get-tuple-element.304) | copy-start | bytes 12292
  111.3 28.2 %copy-start.5 = (f32[16,8,1024]{2,1,0:T(8,128)}, f32[16,8,1024]{2,1,0:T(8,128)S(1)}, u32[]{:S(2)}) copy-start(f32[16,8,1024]{2,1,0:T(8,128)S(1)} %hops.3.start_ref.begin_ref) | copy-start | bytes 1572868
  156.8 7.5 collective-permute-start.1
  170.9 92.9 %collective-permute-start.2 = (f32[512,2048]{1,0:T(8,128)}, f32[512,2048]{1,0:T(8,128)}, u32[]{:S(2)}, u32[]{:S(2)}) collective-permute-start(f32[512,2048]{1,0:T(8,128)} %dynamic-slice_add_fusion.1), channel_id=1, source_target_pairs={{0,2},{2,0},{1,3},{3,1},{4,6},{6,4},{5,7},{7,5},{8,10},{10,8},{9,1... | collective-permute-start | bytes 12582920 | tf_op jit(solution)/shard_map/ppermute | solution.py:358
  274.2 7.5 collective-permute-start.3
  300.1 4.9 collective-permute-start.4
  403.1 28.1 %copy-start.110 = (f32[1,1024]{1,0:T(1,128)S(1)}, f32[1,1024]{1,0:T(1,128)}, u32[]{:S(2)}) copy-start(f32[1,1024]{1,0:T(1,128)} %get-tuple-element.303) | copy-start | bytes 12292
  444.6 468.3 %reduce-scatter.7.cloned.1.call-start = ((), (), s32[]{:S(2)}) async-start(), calls=%async_computation.5 | async-start | bytes 9437184 | tf_op jit(solution)/shard_map/reduce_scatter | solution.py:383
  457.9 18.7 %collective-permute-start.5 = (f32[512,2048]{1,0:T(8,128)}, f32[512,2048]{1,0:T(8,128)}, u32[]{:S(2)}, u32[]{:S(2)}) collective-permute-start(f32[512,2048]{1,0:T(8,128)} %constant_dynamic-slice_fusion), channel_id=1, source_target_pairs={{0,1},{1,0},{2,3},{3,2},{4,5},{5,4},{6,7},{7,6},{8,9},{9,8},{10,11... | collective-permute-start | bytes 12582920 | tf_op jit(solution)/shard_map/ppermute | solution.py:352
  465.9 773.7 %reduce-scatter.11.cloned.1.call-start = ((), (), s32[]{:S(2)}) async-start(), calls=%async_computation.7 | async-start | bytes 9437184 | tf_op jit(solution)/shard_map/reduce_scatter | solution.py:383
  481.0 54.3 %collective-permute-start.6 = (f32[256,2048]{1,0:T(8,128)S(1)}, f32[256,2048]{1,0:T(8,128)S(1)}, u32[]{:S(2)}, u32[]{:S(2)}) collective-permute-start(f32[256,2048]{1,0:T(8,128)S(1)} %slice.332), channel_id=1, source_target_pairs={{0,2},{2,0},{1,3},{3,1},{4,6},{6,4},{5,7},{7,5},{8,10},{10,8},{9,1... | collective-permute-start | bytes 6291464 | tf_op jit(solution)/shard_map/ppermute | solution.py:358
  576.7 6.9 collective-permute-start.7
  800.8 444.4 %reduce-scatter.9.cloned.1.call-start = ((), (), s32[]{:S(2)}) async-start(), calls=%async_computation.6 | async-start | bytes 9437184 | tf_op jit(solution)/shard_map/reduce_scatter | solution.py:383
  808.6 90.5 %collective-permute-start.8 = (f32[256,2048]{1,0:T(8,128)}, f32[256,2048]{1,0:T(8,128)}, u32[]{:S(2)}, u32[]{:S(2)}) collective-permute-start(f32[256,2048]{1,0:T(8,128)} %slice.339), channel_id=1, source_target_pairs={{0,2},{2,0},{1,3},{3,1},{4,6},{6,4},{5,7},{7,5},{8,10},{10,8},{9,1... | collective-permute-start | bytes 6291464 | tf_op jit(solution)/shard_map/ppermute | solution.py:358
  834.4 55.1 %copy-start.63 = (bf16[1024,1024]{1,0:T(8,128)(2,1)S(1)}, bf16[1024,1024]{1,0:T(8,128)(2,1)}, u32[]{:S(2)}) copy-start(bf16[1024,1024]{1,0:T(8,128)(2,1)} %copy-done.62) | copy-start | bytes 6291460
  907.6 108.0 %collective-permute-start.11 = (f32[1,1024]{1,0:T(1,128)S(1)}, f32[1,1024]{1,0:T(1,128)S(1)}, u32[]{:S(2)}, u32[]{:S(2)}) collective-permute-start(f32[1,1024]{1,0:T(1,128)S(1)} %bitcast.474), channel_id=1, source_target_pairs={{0,1},{1,0},{2,3},{3,2},{4,5},{5,4},{6,7},{7,6},{8,9},{9,8},{10,11... | collective-permute-start | bytes 12296 | tf_op jit(solution)/shard_map/ppermute | solution.py:371
  912.5 125.8 %collective-permute-start.10 = (f32[512,2048]{1,0:T(8,128)}, f32[512,2048]{1,0:T(8,128)}, u32[]{:S(2)}, u32[]{:S(2)}) collective-permute-start(f32[512,2048]{1,0:T(8,128)} %broadcast_multiply_fusion), channel_id=1, source_target_pairs={{0,1},{1,0},{2,3},{3,2},{4,5},{5,4},{6,7},{7,6},{8,9},{9,8},{10,11... | collective-permute-start | bytes 12582920 | tf_op jit(solution)/shard_map/ppermute | solution.py:364
  1005.8 10.0 collective-permute-start.9
  1048.3 166.7 %copy-start.41 = (bf16[8,128,2048]{2,1,0:T(8,128)(2,1)S(1)}, bf16[8,128,2048]{2,1,0:T(8,128)(2,1)}, u32[]{:S(2)}) copy-start(bf16[8,128,2048]{2,1,0:T(8,128)(2,1)} %param.15) | copy-start | bytes 12582916
  (113 other events, 784.7 us)
Sparse Core Ops, SparseCore 0:
  444.7 150.7 reduce-scatter.4
  599.6 194.5 reduce-scatter.6
  800.9 151.8 reduce-scatter.10
  956.6 184.9 reduce-scatter.8

commit v9 on v8

--- a/solution.py
+++ b/solution.py
@@ -318,7 +318,9 @@
 
 def pair_sums(arrays, collective_id):
     if not paired() or lax.axis_size("blk") != 8:
-        return [lax.psum(array, "tensor") for array in arrays]
+        first, second = arrays
+        total = lax.psum(jnp.concatenate([first, second.T], axis=-1), "tensor")
+        return [total[:, :first.shape[1]], total[:, first.shape[1]:].T]
     chunks, count = 2, len(arrays)
     f32 = jnp.float32
     spec = pl.BlockSpec(memory_space=pltpu.VMEM)
@@ -400,7 +402,7 @@
         device_id_type=pl.DeviceIdType.MESH)
 
 
-def joint_body(plan, chunks, sum_ref, base_ref, gain_ref, *refs):
+def joint_body(plan, chunks, sum_gain, sum_ref, base_ref, gain_ref, *refs):
     count = 1 + max(job[0] for job in plan)
     thick_refs, small_ref, refs = refs[:count], refs[count], refs[count + 1:]
     change_out, gain_out, refs = refs[0], refs[1], refs[2:]
@@ -565,13 +567,15 @@
             if i == 0:
                 small_step(2)
         far_end(i)
-    gain_step(0)
+    if sum_gain:
+        gain_step(0)
     for k in range(chunks):
         back_end(k)
-    for i in range(4):
-        gain_end(i)
-        if i < 3:
-            gain_step(i + 1)
+    if sum_gain:
+        for i in range(4):
+            gain_end(i)
+            if i < 3:
+                gain_step(i + 1)
     for job in jobs:
         job.end()
     for copy in far_copies + back_copies + [each for job in jobs for each in job.sent()]:
@@ -580,11 +584,13 @@
         copy.wait()
 
 
-def joint_sums(array, base, gain, thick, late, small, collective_id):
+def joint_sums(array, base, gain, thick, late, small, sum_gain, collective_id):
     if not paired() or lax.axis_size("blk") != 8:
         normed_grad = lax.psum_scatter(array, "tensor", scatter_dimension=0, tiled=True)
         gain_grad, change = norm_back(gain, normed_grad, base, inverse_rms(base))
-        return all_rows(change), lax.psum(rows_sum(gain_grad), "blk"), [blk_scatter(part) for part in thick], lax.psum(small, "blk")
+        if sum_gain:
+            gain_grad = lax.psum(rows_sum(gain_grad), "blk")
+        return all_rows(change), gain_grad, [blk_scatter(part) for part in thick], lax.psum(small, "blk")
     R, N = array.shape
     C = thick[0].shape[1]
     chunks = 4
@@ -602,7 +608,7 @@
                     dma((4,)), dma((4,)), dma((4,)), dma((2,)), dma((2,)), dma((1,)), dma((1,)), dma((1,))]
     half = pltpu.VMEM((chunks, R // 2 // chunks, N), f32)
     out = pl.pallas_call(
-        partial(joint_body, plan, chunks),
+        partial(joint_body, plan, chunks, sum_gain),
         in_specs=[any_spec, any_spec, vmem_spec] + [any_spec] * len(thick) + [vmem_spec],
         out_specs=[any_spec, vmem_spec] + [any_spec] * len(thick) + [vmem_spec],
         out_shape=[jax.ShapeDtypeStruct((R, N), f32), jax.ShapeDtypeStruct((8, N), f32)]
@@ -807,6 +813,27 @@
         self.rate2 = self.rate * LOG2E
         self.skip = skip_weight[index]
         self.out = out_weight[index]
+
+
+def norm_body(rows_ref, gain_ref, out_ref):
+    value = rows_ref[...].astype(jnp.float32)
+    q = lax.rsqrt(jnp.mean(value * value, axis=-1, keepdims=True) + EPSILON)
+    out_ref[...] = (value * q * gain_ref[...]).astype(jnp.bfloat16)
+
+
+def norm_rows(array, gain):
+    R, N = array.shape
+    block = 128
+    return pl.pallas_call(
+        norm_body,
+        grid=(R // block,),
+        in_specs=[pl.BlockSpec((block, N), lambda i: (i, 0)), pl.BlockSpec((1, N), lambda i: (0, 0))],
+        out_specs=pl.BlockSpec((block, N), lambda i: (i, 0)),
+        out_shape=jax.ShapeDtypeStruct((R, N), jnp.bfloat16),
+        compiler_params=cp(24 * 2**20),
+        cost_estimate=pl.CostEstimate(flops=4 * R * N, bytes_accessed=4 * R * N, transcendentals=R),
+        name="norm_rows",
+    )(array, gain[None])
 
 
 def inverse_rms(residual):
@@ -892,12 +919,10 @@
     window, gate, conv_out, inputs, dt_low, coef, step, push, totals = kept
     result, gated, states, start = scans
     grad_gated, grad_result = grads
-    inner = gate.shape[1]
     grad_gate = (grad_gated * result * silu_slope(gate)).astype(jnp.bfloat16)
     gate_grad = dot_t(normed, grad_gate)
-    gate_through = dot_n(grad_gate, layer.into[:, inner:])
     skip_grad = jnp.sum(grad_result * inputs.astype(jnp.float32), axis=0)
-    return gate_grad, gate_through, skip_grad
+    return gate_grad, grad_gate, skip_grad
 
 
 def back_scan(layer, kept, scans, grads, end):
@@ -908,7 +933,7 @@
         by_step(step), by_step(push), by_step(grad_result), coef, layer.rate2, states, start, end)
 
 
-def back_rest(layer, kept, grads, scan_out, gate_through, collective_id):
+def back_rest(layer, kept, grads, scan_out, grad_gate, collective_id):
     window, gate, conv_out, inputs, dt_low, coef, step, push, totals = kept
     grad_gated, grad_result = grads
     count, inner = gate.shape
@@ -938,7 +963,7 @@
     tail_grad = jnp.concatenate([prefix_grad[:, 1:], arrived[:, None]], axis=1).reshape(8 * rim, inner)
     values_grad = jnp.concatenate([window_grad[8 * rim:count], window_grad[count:] + tail_grad], axis=0)
     values_grad = values_grad.astype(jnp.bfloat16)
-    normed_part = dot_n(values_grad, layer.into[:, :inner]) + gate_through
+    normed_part = dot_n(jnp.concatenate([values_grad, grad_gate], axis=-1), layer.into)
     small = jnp.concatenate([taps_grad, shift_grad[None], bias_grad[None], decay_grad], axis=0)
     return normed_part, small, (values_grad, before_low, high, low), split_parts(start_grad, parts)[:, 0], prefix_grad[:, 0]
 
@@ -983,10 +1008,9 @@
         array = array.reshape(length, parts, seqs, width).transpose(2, 1, 0, 3)
         return array.reshape(seqs, parts * length, width)
 
-    residual = arrange(tokens).astype(jnp.float32)
-    normed = lax.optimization_barrier((residual * inverse_rms(residual) * layers[0].gain).astype(jnp.bfloat16))
-    residual = own_rows(residual)
-    input_square = jnp.sum(residual * residual)
+    rows_low = arrange(tokens)
+    normed = norm_rows(rows_low, layers[0].gain)
+    residual = own_rows(rows_low).astype(jnp.float32)
     grad = arrange(cotangent).astype(jnp.float32)
     grad_low = grad.astype(jnp.bfloat16)
 
@@ -1012,11 +1036,15 @@
         finals[l] = split_parts(final, parts)[:, -1]
         half = core_sum(partial_sum)
         if l < last:
+            if l == 0:
+                half, residual = lax.optimization_barrier((half, residual))
+                input_square = jnp.sum(residual * residual)
             half, stored = lax.optimization_barrier((half, weights[1]))
             into = [stored[k].reshape(width, -1) for k in range(layer_total)]
             layers[l + 1].raw = stored[l + 1]
             late_gated = dot_n(grad_low, layers[last].out)
-            got, into, grad_low, late_gated = lax.optimization_barrier((across(half), into, grad_low, late_gated))
+            got, into, grad_low, late_gated, input_square = lax.optimization_barrier(
+                (across(half), into, grad_low, late_gated, input_square))
             for each, array in zip(layers, into):
                 each.into = array
             branch = half + got
@@ -1054,16 +1082,16 @@
             end, side, scattered[last] = lax.optimization_barrier((end, side, scattered[last]))
             stacked_last = jnp.stack([scattered[last][2], scattered[last][1]], axis=1)
             scan_out = lax.optimization_barrier(back_scan(layer, kept[l], scans[l], grads, end))
-        gate_grad, gate_through, skip_grad = side
+        gate_grad, grad_gate, skip_grad = side
         normed_part, smalls[l], lows, starts[l], prefixes[l] = back_rest(
-            layer, kept[l], grads, scan_out, gate_through, 5 * layer_total + l)
+            layer, kept[l], grads, scan_out, grad_gate, 5 * layer_total + l)
         smalls[l] = jnp.concatenate([smalls[l], skip_grad[None]], axis=0)
         thick = thick_grads(kept[l], normed, lows)
         inner = smalls[l].shape[-1]
         if l == last:
             thins = thick[1:] + thins
             joint, scattered[l][0] = lax.optimization_barrier((joint_sums(
-                normed_part, base, layer.gain, [rows(thick[0])], (0,), smalls[l], l), scattered[l][0]))
+                normed_part, base, layer.gain, [rows(thick[0])], (0,), smalls[l], False, l), scattered[l][0]))
             change, gains[l], thick, smalls[l] = joint
             scattered[l].append(thick[0])
         else:
@@ -1071,14 +1099,15 @@
             cuts = [part.shape[1] for part in thins]
             extra = jnp.concatenate([jnp.stack(squares).reshape(-1), input_square.reshape(1)])
             extra = jnp.pad(extra, (0, inner - extra.shape[0]))[None]
-            shared = rows_sum(extra)
+            shared = rows_sum(jnp.concatenate(
+                [extra] + [gain.reshape(-1, inner) for gain in gains[1:]], axis=0))
             own_count = smalls[l].shape[0]
             small = jnp.concatenate([smalls[l], shared], axis=0)
             small = jnp.pad(small, ((0, -small.shape[0] % 8), (0, 0)))
             normed_part, thins, out, stacked_last = lax.optimization_barrier((normed_part, thins, out, stacked_last))
             change, gains[l], thick, small = joint_sums(
                 normed_part, base, layer.gain, [rows(thick[0]), rows(jnp.concatenate(thins, axis=1))], (0, inner),
-                small, l)
+                small, True, l)
             scattered[l].append(thick[0])
             smalls[l], rest = small[:own_count], small[own_count:]
         grad = grad + change
@@ -1088,7 +1117,9 @@
     input_grad = restore(grad_low)
 
     small = jnp.stack(smalls)
-    gain_grad = jnp.stack(gains)
+    gain_rows = width // inner
+    gain_grad = jnp.concatenate([gains[0].reshape(-1, inner), rest[1:1 + gain_rows * last]], axis=0)
+    gain_grad = gain_grad.reshape(layer_total, width)
     taps = weights[2].shape[1]
     row_total = tokens.shape[0] * tokens.shape[1] * width * blocks
     squares = rest[0] / row_total

time: 1270 us -> 1260 us (level)
  matrix products: 199 us -> 178 us
    dot_general x10 -> x8, matrix products: 96.2 us -> 78.4 us  [dot_n(): lax.dot_general(left, right, (((1,), (1,)), ((), ())), preferred_element_...]
    unnamed x251 -> x277, local copies, waits for them, and re-layouts: 45.7 us -> 49.9 us
    pallas_call x2 -> x3, Pallas kernels: 332 us -> 335 us  [the longest x2 333 us: joint_sums(): pl.pallas_call(partial(joint_body, plan, chunks, sum_gain), in_specs=[any...]
  transfers between devices with their start and end apart: 16 -> 16, of which waited for: 5 -> 6; matrix products, arithmetic and copies ran while one was open for 27% -> 26% of each run, Pallas kernels for 41% -> 42%
where the time goes in v9:
time: 1260 us; the launch traced here: 1250 us
  Pallas kernels  705 us (56%)
  matrix products  178 us (14%)
  other arithmetic  151 us (12%)
  local copies, waits for them, and re-layouts  138 us (11%)
  waiting for transfers between devices  41.3 us (3%)
  between operations  17.6 us (1%)
  starting transfers between devices  16.2 us (1%)
    pallas_call x2, Pallas kernels, joint_sums(): pl.pallas_call(partial(joint_body, plan, chunks, sum_gain), in_specs=[any...  333 us
    pallas_call x2, Pallas kernels, scan_backward(): pl.pallas_call(partial(back_body, C // LANES, width, held), grid=(T // tb...  103 us
    pallas_call x3, Pallas kernels, hops(): pl.pallas_call(partial(hop_body, reverses, groups), in_specs=[spec] * (3...  99.9 us
    dot_general x8, matrix products, dot_n(): lax.dot_general(left, right, (((1,), (1,)), ((), ())), preferred_element_...  78.4 us
    pallas_call x2, Pallas kernels, scan_forward(): pl.pallas_call(partial(scan_body, C // LANES, width, held), grid=(T // tb...  56.5 us
    dot_general x12, matrix products, dot_t(): lax.dot_general(left, right, (((0,), (0,)), ((), ())), preferred_element_...  56.4 us
    unnamed x277, local copies, waits for them, and re-layouts  49.9 us
    pallas_call x4, Pallas kernels, pair_sums(): pl.pallas_call(partial(pair_body, chunks, count), in_specs=[spec] * count...  48.5 us
  transfers between devices with their start and end apart: 16, of which 6 were waited for; matrix products, arithmetic and copies ran while one was open for 26% of the time, Pallas kernels for 42%

profile of v9, /device:TPU:0, one launch (start us, length us, event | category | flops | bytes accessed | tf_op | source)
XLA Modules:
  0.0 1246.9 jit_solution(8579810023558494523)
XLA Ops:
  49.1 12.4 pair_sums.4
  67.7 15.6 %end_states.2.refs_0_ = f32[16,8,1024]{2,1,0:T(8,128)S(1)} custom-call(f32[128,8,1024]{2,1,0:T(8,128)S(1)} %bitcast.373, f32[128,8,1024]{2,1,0:T(8,128)} %fusion.14.push_ref, f32[128,8,32]{2,1,0:T(8,128)S(1)} %bitcast.383, f32[16,1024]{1,0:T(8,128)S(1)} %get-tuple-element.278.rate_ref), custom_call_target="tpu_custom_call" | custom-call | flops 67108864 | bytes 67108864 | tf_op jit(solution)/shard_map/end_states/pallas_call | solution.py:57
  83.3 16.6 %hops.3.start_ref.begin_ref = f32[16,8,1024]{2,1,0:T(8,128)S(1)} custom-call(f32[8,1024]{1,0:T(8,128)S(1)} %get-tuple-element.295.total_ref, f32[16,1024]{1,0:T(8,128)S(1)} %get-tuple-element.278.rate_ref, f32[16,8,1024]{2,1,0:T(8,128)S(1)} %end_states.2.refs_0_, f32[16,8,1024]{2,1,0:T(8,128)S(1)} %get-tuple-element.304.refs_1_), custom_call_target="tpu_custom_call" | custom-call | bytes 26214400 | tf_op jit(solution)/shard_map/hops/pallas_call | solution.py:758
  99.9 28.2 %scan_forward.2 = (f32[128,8,1024]{2,1,0:T(8,128)S(1)}, f32[128,16,8,1024]{3,2,1,0:T(8,128)}, f32[16,8,1024]{2,1,0:T(8,128)S(1)}) custom-call(f32[128,8,1024]{2,1,0:T(8,128)} %bitcast.374, f32[128,8,1024]{2,1,0:T(8,128)} %fusion.14.push_ref, f32[128,8,32]{2,1,0:T(8,128)S(1)} %bitcast.384, f32[16,1024]{1,0:T(8,128)S(1)} %get-tuple-element.278.rate_ref, ...), custom_call_target="tpu_custom_call" | custom-call | flops 117440512 | bytes 117440512 | tf_op jit(solution)/shard_map/scan_forward/pallas_call | solution.py:106
  164.0 12.4 fusion.46
  228.8 23.4 %collective-permute-done.2 = f32[512,2048]{1,0:T(8,128)} collective-permute-done((f32[512,2048]{1,0:T(8,128)}, f32[512,2048]{1,0:T(8,128)}, u32[]{:S(2)}, u32[]{:S(2)}) %collective-permute-start.2) | collective-permute-done | bytes 4194336 | tf_op jit(solution)/shard_map/ppermute | solution.py:360
  274.2 12.7 %fusion.59 = f32[2,1024,1024]{2,1,0:T(8,128)S(1)} fusion(bf16[512,2048]{1,0:T(8,128)(2,1)S(1)} %get-tuple-element.250, bf16[512,2048]{1,0:T(8,128)(2,1)S(1)} %get-tuple-element.249, bf16[2,2048,2,1024]{3,1,2,0:T(8,128)(2,1)} %copy.60), kind=kOutput, calls=%fused_computation.133 | convolution fusion | flops 8598323200 | bytes 20971520 | tf_op jit(solution)/shard_map/rd,dkc->krc/dot_general | solution.py:844
  320.1 15.5 %start_grads.2.refs_1_ = f32[16,8,1024]{2,1,0:T(8,128)S(1)} custom-call(f32[128,8,1024]{2,1,0:T(8,128)S(1)} %bitcast.377, f32[128,8,1024]{2,1,0:T(8,128)} %bitcast.413, f32[128,8,32]{2,1,0:T(8,128)S(1)} %bitcast.387, f32[16,1024]{1,0:T(8,128)S(1)} %get-tuple-element.277.rate_ref), custom_call_target="tpu_custom_call" | custom-call | flops 67108864 | bytes 67108864 | tf_op jit(solution)/shard_map/start_grads/pallas_call | solution.py:144
  335.7 15.6 %end_states.3.refs_0_ = f32[16,8,1024]{2,1,0:T(8,128)S(1)} custom-call(f32[128,8,1024]{2,1,0:T(8,128)S(1)} %bitcast.378, f32[128,8,1024]{2,1,0:T(8,128)} %get-tuple-element.265.push_ref, f32[128,8,32]{2,1,0:T(8,128)S(1)} %bitcast.388, f32[16,1024]{1,0:T(8,128)S(1)} %get-tuple-element.277.rate_ref), custom_call_target="tpu_custom_call" | custom-call | flops 67108864 | bytes 67108864 | tf_op jit(solution)/shard_map/end_states/pallas_call | solution.py:57
  351.2 39.3 %hops.4 = (f32[16,8,1024]{2,1,0:T(8,128)S(1)}, f32[16,8,1024]{2,1,0:T(8,128)S(1)}) custom-call(f32[8,1024]{1,0:T(8,128)S(1)} %get-tuple-element.297.total_ref, f32[16,1024]{1,0:T(8,128)S(1)} %get-tuple-element.277.rate_ref, f32[16,8,1024]{2,1,0:T(8,128)S(1)} %end_states.3.refs_0_, f32[16,8,1024]{2,1,0:T(8,128)S(1)} %start_grads.2.refs_1_, ...), custom_call_target="tpu_custom_call" | custom-call | bytes 26214400 | tf_op jit(solution)/shard_map/hops/pallas_call | solution.py:758
  390.6 28.2 %scan_forward.3 = (f32[128,8,1024]{2,1,0:T(8,128)S(1)}, f32[128,16,8,1024]{3,2,1,0:T(8,128)}, f32[16,8,1024]{2,1,0:T(8,128)S(1)}) custom-call(f32[128,8,1024]{2,1,0:T(8,128)} %bitcast.379, f32[128,8,1024]{2,1,0:T(8,128)} %get-tuple-element.265.push_ref, f32[128,8,32]{2,1,0:T(8,128)S(1)} %bitcast.389, f32[16,1024]{1,0:T(8,128)S(1)} %get-tuple-element.277.rate_ref, ...), custom_call_target="tpu_custom_call" | custom-call | flops 117440512 | bytes 117440512 | tf_op jit(solution)/shard_map/scan_forward/pallas_call | solution.py:106
  459.8 51.6 %scan_backward.2 = (f32[128,8,1024]{2,1,0:T(8,128)}, f32[128,8,1024]{2,1,0:T(8,128)}, f32[128,8,32]{2,1,0:T(8,128)S(1)}, f32[16,8,1024]{2,1,0:T(8,128)S(1)}, f32[16,8,1024]{2,1,0:T(8,128)S(1)}) custom-call(f32[128,8,1024]{2,1,0:T(8,128)} %bitcast.380, f32[128,8,1024]{2,1,0:T(8,128)} %get-tuple-element.265.push_ref, f32[128,8,1024]{2,1,0:T(8,128)} %bitcast.414, ...), custom_call_target="tpu_custom_call" | custom-call | flops 218103808 | bytes 218103808 | tf_op jit(solution)/shard_map/scan_backward/pallas_call | solution.py:230
  522.6 12.4 pair_sums.6
  536.2 13.1 %fusion.136 = (f32[1024]{0:T(1024)S(1)}, f32[1024]{0:T(1024)S(1)}, f32[1024]{0:T(1024)S(1)}, f32[1024]{0:T(1024)S(1)}, f32[1024]{0:T(1024)S(1)}, /*index=5*/f32[1024,1024]{1,0:T(8,128)S(1)}) fusion(f32[2,1024,1024]{2,1,0:T(8,128)} %copy-done.48, f32[1024,1024]{1,0:T(8,128)} %copy-done.52, f32[24,1024]{1,0:T(8,128)S(1)} %copy-done.100, ...), kind=kOutput, calls=%fused_computation.280 | convolution fusion | flops 698870784 | bytes 30466048 | tf_op jit(solution)/shard_map/dot_general | solution.py:789
  571.4 13.2 %fusion.25.sum_ref = f32[1024,2048]{1,0:T(8,128)} fusion(bf16[2048,2048]{0,1:T(8,128)(2,1)} %bitcast.422, bf16[1024,1024]{1,0:T(8,128)(2,1)S(1)} %copy-done.68, bf16[24,1024]{1,0:T(8,128)(2,1)S(1)} %fusion.119, bf16[1000,1024]{1,0:T(8,128)(2,1)S(1)} %copy-done.83), kind=kOutput, calls=%fused_computation.57 | convolution fusion | flops 8602517504 | bytes 20971520 | tf_op jit(solution)/shard_map/dot_general | solution.py:789
  584.6 158.9 %joint_sums.2 = (f32[1024,2048]{1,0:T(8,128)}, f32[8,2048]{1,0:T(8,128)S(1)}, f32[256,1024]{1,0:T(8,128)S(1)}, f32[23,1024]{1,0:T(8,128)S(1)}) custom-call(f32[1024,2048]{1,0:T(8,128)} %fusion.25.sum_ref, f32[512,2048]{1,0:T(8,128)} %copy-done.39, f32[1,2048]{1,0:T(1,128)S(1)} %copy-done.31, f32[2,2,2,256,1024]{4,3,2,1,0:T(8,128)} %bitcast.424, ...), custom_call_target="tpu_custom_call" | custom-call | bytes 419430400 | tf_op jit(solution)/shard_map/joint_sums/pallas_call | solution.py:610
  760.1 12.9 %fusion.99 = (f32[1024,1024]{1,0:T(8,128)}, f32[1024,1024]{1,0:T(8,128)}) fusion(f32[2,1024,1024]{2,1,0:T(8,128)} %copy-done.47, bf16[1024,2048]{1,0:T(8,128)(2,1)} %copy-done.61, bf16[2,1024,2048]{2,1,0:T(8,128)(2,1)} %param.25), kind=kOutput, calls=%fused_computation.191 | convolution fusion | flops 4300210176 | bytes 20971520 | tf_op jit(solution)/shard_map/dot_general | solution.py:789
  809.7 15.7 %start_grads.3.refs_0_ = f32[16,8,1024]{2,1,0:T(8,128)S(1)} custom-call(f32[128,8,1024]{2,1,0:T(8,128)S(1)} %bitcast.376, f32[128,8,1024]{2,1,0:T(8,128)} %bitcast.411, f32[128,8,32]{2,1,0:T(8,128)S(1)} %bitcast.385, f32[16,1024]{1,0:T(8,128)S(1)} %copy-done.12), custom_call_target="tpu_custom_call" | custom-call | flops 67108864 | bytes 67108864 | tf_op jit(solution)/shard_map/start_grads/pallas_call | solution.py:144
  825.5 44.0 %hops.5.end_ref = f32[16,8,1024]{2,1,0:T(8,128)S(1)} custom-call(f32[8,1024]{1,0:T(8,128)S(1)} %copy-done.27, f32[16,1024]{1,0:T(8,128)S(1)} %copy-done.12, f32[16,8,1024]{2,1,0:T(8,128)S(1)} %start_grads.3.refs_0_, f32[16,8,1024]{2,1,0:T(8,128)S(1)} %broadcast_in_dim.40.refs_1_), custom_call_target="tpu_custom_call" | custom-call | bytes 26214400 | tf_op jit(solution)/shard_map/hops/pallas_call | solution.py:758
  883.6 51.3 %scan_backward.3 = (f32[128,8,1024]{2,1,0:T(8,128)}, f32[128,8,1024]{2,1,0:T(8,128)}, f32[128,8,32]{2,1,0:T(8,128)S(1)}, f32[16,8,1024]{2,1,0:T(8,128)S(1)}, f32[16,8,1024]{2,1,0:T(8,128)S(1)}) custom-call(f32[128,8,1024]{2,1,0:T(8,128)} %bitcast.375, f32[128,8,1024]{2,1,0:T(8,128)} %fusion.14.push_ref, f32[128,8,1024]{2,1,0:T(8,128)} %bitcast.412, ...), custom_call_target="tpu_custom_call" | custom-call | flops 218103808 | bytes 218103808 | tf_op jit(solution)/shard_map/scan_backward/pallas_call | solution.py:230
  946.8 12.4 pair_sums.7
  1002.5 13.8 %fusion.31.sum_ref = f32[1024,2048]{1,0:T(8,128)} fusion(bf16[2048,2048]{1,0:T(8,128)(2,1)} %bitcast.421, bf16[1024,1024]{1,0:T(8,128)(2,1)S(1)} %copy-done.65, bf16[24,1024]{1,0:T(8,128)(2,1)S(1)} %fusion.118, bf16[1000,1024]{1,0:T(8,128)(2,1)S(1)} %copy-done.82), kind=kOutput, calls=%fused_computation.63 | convolution fusion | flops 8602517504 | bytes 20971520 | tf_op jit(solution)/shard_map/dot_general | solution.py:789
  1026.3 174.0 %joint_sums.3 = (f32[1024,2048]{1,0:T(8,128)}, f32[8,2048]{1,0:T(8,128)S(1)}, f32[256,1024]{1,0:T(8,128)S(1)}, f32[80,1024]{1,0:T(8,128)S(1)}, f32[32,1024]{1,0:T(8,128)S(1)}) custom-call(f32[1024,2048]{1,0:T(8,128)} %fusion.31.sum_ref, f32[512,2048]{1,0:T(8,128)} %dynamic-slice_convert_fusion.base_ref, f32[1,2048]{1,0:T(1,128)S(1)} %copy-done.29, ...), custom_call_target="tpu_custom_call" | custom-call | bytes 419430400 | tf_op jit(solution)/shard_map/joint_sums/pallas_call | solution.py:610
  1200.3 12.5 %fusion.24 = bf16[128,1,8,2048]{3,2,0,1:T(8,128)(2,1)S(1)} fusion(f32[1024,2048]{1,0:T(8,128)} %get-tuple-element.169, f32[1024,2048]{1,0:T(8,128)} %get-tuple-element.137, bf16[128,1,8,2048]{3,0,2,1:T(8,128)(2,1)S(1)} %bitcast.418), kind=kLoop, calls=%fused_computation.49 | loop fusion | flops 8388608 | bytes 25165824 | tf_op jit(solution)/shard_map/reshape | solution.py:1008
  (458 shorter events, 423.7 us)
Async XLA Ops:
  7.2 736.4 %reduce-scatter.5.cloned.1.call-start = ((), (), s32[]{:S(2)}) async-start(), calls=%async_computation.4 | async-start | bytes 9437184 | tf_op jit(solution)/shard_map/reduce_scatter | solution.py:385
  8.1 261.3 %copy-start.30 = (f32[1,2048]{1,0:T(1,128)}, f32[1,2048]{1,0:T(1,128)S(1)}, u32[]{:S(2)}) copy-start(f32[1,2048]{1,0:T(1,128)S(1)} %get-tuple-element.287.gain_ref) | copy-start | bytes 24580
  27.6 11.2 collective-permute-start
  37.4 62.5 %copy-start.11 = (f32[16,1024]{1,0:T(8,128)}, f32[16,1024]{1,0:T(8,128)S(1)}, u32[]{:S(2)}) copy-start(f32[16,1024]{1,0:T(8,128)S(1)} %get-tuple-element.278.rate_ref) | copy-start | bytes 196612
  38.8 89.4 %copy-start.114 = (f32[1,1024]{1,0:T(1,128)}, f32[1,1024]{1,0:T(1,128)S(1)}, u32[]{:S(2)}) copy-start(f32[1,1024]{1,0:T(1,128)S(1)} %get-tuple-element.290) | copy-start | bytes 12292
  99.9 28.3 %copy-start.7 = (f32[16,8,1024]{2,1,0:T(8,128)}, f32[16,8,1024]{2,1,0:T(8,128)S(1)}, u32[]{:S(2)}) copy-start(f32[16,8,1024]{2,1,0:T(8,128)S(1)} %hops.3.start_ref.begin_ref) | copy-start | bytes 1572868
  145.2 7.5 collective-permute-start.1
  159.3 92.9 %collective-permute-start.2 = (f32[512,2048]{1,0:T(8,128)}, f32[512,2048]{1,0:T(8,128)}, u32[]{:S(2)}, u32[]{:S(2)}) collective-permute-start(f32[512,2048]{1,0:T(8,128)} %dynamic-slice_add_fusion.1), channel_id=1, source_target_pairs={{0,2},{2,0},{1,3},{3,1},{4,6},{6,4},{5,7},{7,5},{8,10},{10,8},{9,1... | collective-permute-start | bytes 12582920 | tf_op jit(solution)/shard_map/ppermute | solution.py:360
  261.9 7.5 collective-permute-start.3
  287.7 4.9 collective-permute-start.4
  390.6 28.2 %copy-start.122 = (f32[1,1024]{1,0:T(1,128)S(1)}, f32[1,1024]{1,0:T(1,128)}, u32[]{:S(2)}) copy-start(f32[1,1024]{1,0:T(1,128)} %get-tuple-element.289) | copy-start | bytes 12292
  432.2 451.4 %reduce-scatter.7.cloned.1.call-start = ((), (), s32[]{:S(2)}) async-start(), calls=%async_computation.5 | async-start | bytes 9437184 | tf_op jit(solution)/shard_map/reduce_scatter | solution.py:385
  445.5 8.0 collective-permute-start.5
  453.5 770.9 %reduce-scatter.11.cloned.1.call-start = ((), (), s32[]{:S(2)}) async-start(), calls=%async_computation.7 | async-start | bytes 9437184 | tf_op jit(solution)/shard_map/reduce_scatter | solution.py:385
  458.0 54.2 %collective-permute-start.6 = (f32[256,2048]{1,0:T(8,128)S(1)}, f32[256,2048]{1,0:T(8,128)S(1)}, u32[]{:S(2)}, u32[]{:S(2)}) collective-permute-start(f32[256,2048]{1,0:T(8,128)S(1)} %slice.325), channel_id=1, source_target_pairs={{0,2},{2,0},{1,3},{3,1},{4,6},{6,4},{5,7},{7,5},{8,10},{10,8},{9,1... | collective-permute-start | bytes 6291464 | tf_op jit(solution)/shard_map/ppermute | solution.py:360
  552.9 7.2 collective-permute-start.7
  773.1 457.3 %reduce-scatter.9.cloned.1.call-start = ((), (), s32[]{:S(2)}) async-start(), calls=%async_computation.6 | async-start | bytes 9437184 | tf_op jit(solution)/shard_map/reduce_scatter | solution.py:385
  780.9 88.7 %collective-permute-start.8 = (f32[256,2048]{1,0:T(8,128)}, f32[256,2048]{1,0:T(8,128)}, u32[]{:S(2)}, u32[]{:S(2)}) collective-permute-start(f32[256,2048]{1,0:T(8,128)} %slice.331), channel_id=1, source_target_pairs={{0,2},{2,0},{1,3},{3,1},{4,6},{6,4},{5,7},{7,5},{8,10},{10,8},{9,1... | collective-permute-start | bytes 6291464 | tf_op jit(solution)/shard_map/ppermute | solution.py:360
  809.7 59.8 %copy-start.40 = (f32[512,2048]{1,0:T(8,128)S(1)}, f32[512,2048]{1,0:T(8,128)}, u32[]{:S(2)}) copy-start(f32[512,2048]{1,0:T(8,128)} %copy-done.39) | copy-start | bytes 12582916
  809.7 59.8 %copy-start.43 = (f32[512,2048]{1,0:T(8,128)S(1)}, f32[512,2048]{1,0:T(8,128)}, u32[]{:S(2)}) copy-start(f32[512,2048]{1,0:T(8,128)} %copy-done.42) | copy-start | bytes 12582916
  878.2 109.7 %collective-permute-start.11 = (f32[3,1024]{1,0:T(4,128)}, f32[3,1024]{1,0:T(4,128)}, u32[]{:S(2)}, u32[]{:S(2)}) collective-permute-start(f32[3,1024]{1,0:T(4,128)} %pad_maximum_fusion.19), channel_id=1, source_target_pairs={{0,1},{1,0},{2,3},{3,2},{4,5},{5,4},{6,7},{7,6},{8,9},{9,8},{10,11... | collective-permute-start | bytes 36872 | tf_op jit(solution)/shard_map/ppermute | solution.py:373
  883.3 133.0 %collective-permute-start.10 = (f32[512,2048]{1,0:T(8,128)}, f32[512,2048]{1,0:T(8,128)}, u32[]{:S(2)}, u32[]{:S(2)}) collective-permute-start(f32[512,2048]{1,0:T(8,128)} %broadcast_multiply_fusion), channel_id=1, source_target_pairs={{0,1},{1,0},{2,3},{3,2},{4,5},{5,4},{6,7},{7,6},{8,9},{9,8},{10,11... | collective-permute-start | bytes 12582920 | tf_op jit(solution)/shard_map/ppermute | solution.py:366
  982.9 7.7 collective-permute-start.9
  1026.3 174.0 %copy-start.46 = (bf16[8,128,2048]{2,1,0:T(8,128)(2,1)S(1)}, bf16[8,128,2048]{2,1,0:T(8,128)(2,1)}, u32[]{:S(2)}) copy-start(bf16[8,128,2048]{2,1,0:T(8,128)(2,1)} %param.15) | copy-start | bytes 12582916
  (126 other events, 862.0 us)
Sparse Core Ops, SparseCore 0:
  432.4 150.6 reduce-scatter.4
  587.2 192.1 reduce-scatter.6
  783.0 152.6 reduce-scatter.10
  939.6 188.5 reduce-scatter.8
